TPU v7x, 32 devices: a whole 2x2x4 slice. The times are simulated.
32 devices in a mesh: row: 4 (over y, core), col: 8 (over z, x).
Axes of the slice: x: 2, y: 2, z: 4, core: 2. Of those that a mesh axis runs over, the one named last changes fastest.
Arguments:
- features: bfloat16 [16384, 256], P(('row', 'col')), may hold values from -6 to 6
- tile_values: bfloat16 [64, 64, 256, 256], P('col', 'row'), may hold values from 0 to 1, as said below
- tile_cols: int32 [64, 64], P('col', 'row'), may hold values from 0 to 15
- tile_counts: int32 [64, 4], P('col', 'row'), may hold values from 1 to 16, as said below
- weight: bfloat16 [256, 256], replicated, may hold values from -0.375 to 0.375
- bias: float32 [256], replicated, may hold values from -3 to 3
- cotangent: bfloat16 [16384, 256], P(('col', 'row')), may hold values from -6 to 6
Outputs:
- layer_out: bfloat16 [16384, 256], P(('col', 'row'))
- feature_grad: bfloat16 [16384, 256], P(('row', 'col'))
- weight_grad: float32 [256, 256], replicated
- bias_grad: float32 [256], replicated
Inputs may be any that keep to these rules, and one draw needn't show every extreme that they name: `tile_values`: nonnegative edge weights. `tile_counts`: every draw has some entry equal to 16; the loads differ between the devices' blocks.
All inputs are finite; a program needn't handle non-finite values.
Results may differ from a plain program's by a relative error of at most 0.025.
Values may be sent and summed in bfloat16 or wider, within the bound.
No kernel may reach another device: no remote copies, remote signals or barrier semaphores. Data moves between devices by JAX's collectives and lax.ppermute only.
A program may use at most 128 MiB of HBM per device.

v0:
```python
import math

import jax
import jax.numpy as jnp
from jax import lax
from jax.sharding import PartitionSpec as P


def dense_part(hidden, weight, bias, cotangent):
    preact = jnp.dot(hidden, weight, preferred_element_type=jnp.float32) + bias
    output = jax.nn.silu(preact).astype(jnp.bfloat16)
    sigmoid_value = jax.nn.sigmoid(preact)
    slope = sigmoid_value * (1.0 + preact * (1.0 - sigmoid_value))
    preact_grad = (cotangent.astype(jnp.float32) * slope).astype(jnp.bfloat16)
    weight_grad = lax.dot_general(
        hidden, preact_grad, (((0,), (0,)), ((), ())), preferred_element_type=jnp.float32
    )
    bias_grad = jnp.sum(preact_grad.astype(jnp.float32), axis=0)
    hidden_grad = lax.dot_general(
        preact_grad, weight, (((1,), (1,)), ((), ())), preferred_element_type=jnp.float32
    ).astype(jnp.bfloat16)
    return (output, weight_grad, bias_grad, hidden_grad)


def per_device(features, tile_values, tile_cols, tile_counts, weight, bias, cotangent):
    node_dev, width = features.shape
    row_tiles, slot_count, tile_size, _ = tile_values.shape
    column_block = lax.all_gather(features, "col", axis=0, tiled=True)
    column_tiles = column_block.shape[0] // tile_size
    x_tiles = column_block.reshape(column_tiles, tile_size, width)
    live_counts = tile_counts[:, 0]
    slot_top = jnp.max(live_counts)

    def slot_data(slot):
        values = lax.dynamic_index_in_dim(tile_values, slot, 1, keepdims=False)
        columns = lax.dynamic_index_in_dim(tile_cols, slot, 1, keepdims=False)
        live = slot < live_counts
        return (values, columns, live)

    def forward_slot(slot, running):
        values, columns, live = slot_data(slot)
        picked = jnp.take(x_tiles, columns, axis=0) * live[:, None, None].astype(jnp.bfloat16)
        return running + jnp.einsum(
            "tij,tjf->tif", values, picked, preferred_element_type=jnp.float32
        )

    partial_value = lax.fori_loop(
        0, slot_top, forward_slot, jnp.zeros((row_tiles, tile_size, width), jnp.float32)
    )
    partial_value = partial_value.reshape(row_tiles * tile_size, width)
    node_total = node_dev * lax.axis_size("row") * lax.axis_size("col")
    grad_scale = 1.0 / math.sqrt(node_total)
    own_rows = lax.psum_scatter(
        partial_value.astype(jnp.bfloat16), "row", scatter_dimension=0, tiled=True
    )
    layer_out, weight_grad, bias_grad, hidden_grad = dense_part(own_rows, weight, bias, cotangent)
    weight_grad, bias_grad = lax.psum((weight_grad, bias_grad), ("row", "col"))
    grad_block = lax.all_gather(hidden_grad, "row", axis=0, tiled=True)
    grad_tiles = grad_block.reshape(row_tiles, tile_size, width)

    def backward_slot(slot, running):
        values, columns, live = slot_data(slot)
        contrib = jnp.einsum("tij,tif->tjf", values, grad_tiles, preferred_element_type=jnp.float32)
        contrib = contrib * live[:, None, None].astype(jnp.float32)
        return running.at[columns].add(contrib)

    summed = lax.fori_loop(
        0, slot_top, backward_slot, jnp.zeros((column_tiles, tile_size, width), jnp.float32)
    )
    summed = summed.reshape(column_tiles * tile_size, width)
    feature_grad = lax.psum_scatter(
        summed.astype(jnp.bfloat16), "col", scatter_dimension=0, tiled=True
    )
    return (layer_out, feature_grad, weight_grad * grad_scale, bias_grad * grad_scale)


def solution(mesh):
    placed = (
        P(("row", "col"), None),
        P("col", "row", None, None),
        P("col", "row"),
        P("col", "row"),
        P(),
        P(),
        P(("col", "row"), None),
    )
    return jax.shard_map(
        per_device,
        mesh=mesh,
        in_specs=placed,
        out_specs=(P(("col", "row"), None), P(("row", "col"), None), P(), P()),
        check_vma=False,
    )
```

profile of v0, /device:TPU:0, one launch (start us, length us, event | category | flops | bytes accessed | tf_op | source)
XLA Modules:
  0.0 396.9 jit_solution(18309459428129167916)
XLA Ops:
  7.2 0.0 copy-start
  7.2 0.0 copy-start.5
  7.2 0.0 all-gather.3.cloned.1.call-start
  7.2 0.7 all-gather.3.cloned.1.call-update
  7.9 0.0 reduce-scatter.3.cloned.1.call-start
  8.0 0.8 copy.12
  8.7 1.3 reduce_max.9
  10.0 52.1 %all-gather.3.cloned.1.call-done = bf16[4096,256]{1,0:T(8,128)(2,1)} async-done(((bf16[512,256]{1,0:T(8,128)(2,1)}), bf16[4096,256]{1,0:T(8,128)(2,1)}) %all-gather.3.cloned.1.call-update) | async-done | bytes 2097168 | tf_op jit(solution)/shard_map/all_gather | solution.py:28
  62.2 0.2 broadcast_in_dim.20
  62.4 20.8 %while.20 = (s32[]{:T(128)}, f32[8,256,256]{2,1,0:T(8,128)S(1)}, s32[]{:T(128)}, bf16[8,16,256,256]{3,2,1,0:T(8,128)(2,1)}, s32[8,16]{0,1:T(8,128)S(1)}, /*index...) while((s32[]{:T(128)}, f32[8,256,256]{2,1,0:T(8,128)S(1)}, s32[]{:T(128)}, ...), condition=%wide.region_2.3_spmd, body=%wide.region_1.2_spmd.sunk | while | flops 270009408 | bytes 8393067 | solution.py:47
  63.0 2.2 gather_fusion
  65.3 2.1 convolution_add_fusion.3
  68.1 2.2 gather_fusion
  70.3 2.1 convolution_add_fusion.3
  73.1 2.2 gather_fusion
  75.3 2.1 convolution_add_fusion.3
  78.2 2.2 gather_fusion
  80.4 2.1 convolution_add_fusion.3
  83.1 0.0 copy-start.3
  83.1 0.0 copy-start.4
  83.2 1.1 convert_element_type.43
  84.2 0.0 reduce-scatter.3.cloned.1.call-update
  84.3 0.0 all-gather.5.cloned.1.call-start
  84.3 83.0 %reduce-scatter.3.cloned.1.call-done = bf16[512,256]{1,0:T(8,128)(2,1)} async-done(((bf16[2048,256]{1,0:T(8,128)(2,1)}), bf16[512,256]{1,0:T(8,128)(2,1)}) %reduce-scatter.3.cloned.1.call-update) | async-done | bytes 262160 | tf_op jit(solution)/shard_map/reduce_scatter | solution.py:53
  167.3 2.1 convert_reduce_fusion
  169.5 1.0 convolution_convert_fusion
  170.4 0.0 all-gather.5.cloned.1.call-update
  170.5 0.0 all-reduce.2.cloned.1.call-start
  170.5 1.0 fusion.13
  171.5 0.0 all-reduce.2.cloned.1.call-update
  171.5 0.0 reduce-scatter.5.cloned.1.call-start
  171.6 15.8 %all-gather.5.cloned.1.call-done = bf16[2048,256]{1,0:T(8,128)(2,1)} async-done(((bf16[512,256]{1,0:T(8,128)(2,1)}), bf16[2048,256]{1,0:T(8,128)(2,1)}) %all-gather.5.cloned.1.call-update) | async-done | bytes 1048592 | tf_op jit(solution)/shard_map/all_gather | solution.py:58
  187.3 2.4 broadcast_in_dim.21
  189.7 27.7 %while.21 = (s32[]{:T(128)}, f32[16,256,256]{2,1,0:T(8,128)}, s32[]{:T(128)}, s32[8,16]{0,1:T(8,128)S(1)}, bf16[8,16,256,256]{3,2,1,0:T(8,128)(2,1)}, /*index=5*...) while((s32[]{:T(128)}, f32[16,256,256]{2,1,0:T(8,128)}, s32[]{:T(128)}, ...), condition=%wide.region_6.7_spmd, body=%wide.region_4.6_spmd.sunk | while | flops 269484064 | bytes 10486107 | solution.py:67
  190.4 1.8 convolution_multiply_fusion.2
  192.2 4.3 %scatter_fusion = f32[16,256,256]{2,1,0:T(8,128)} fusion(f32[16,256,256]{2,1,0:T(8,128)} %get-tuple-element.262, s32[8]{0:T(128)S(1)} %fusion.30, f32[8,256,256]{2,1,0:T(8,128)S(1)} %convolution_multiply_fusion.2), kind=kCustom, calls=%fused_computation.1.clone.1 | custom fusion | flops 524288 | bytes 6291488 | tf_op jit(solution)/shard_map/while/body/scatter-add | solution.py:65
  197.2 1.8 convolution_multiply_fusion.2
  199.0 4.4 %scatter_fusion = f32[16,256,256]{2,1,0:T(8,128)} fusion(f32[16,256,256]{2,1,0:T(8,128)} %get-tuple-element.262, s32[8]{0:T(128)S(1)} %fusion.30, f32[8,256,256]{2,1,0:T(8,128)S(1)} %convolution_multiply_fusion.2), kind=kCustom, calls=%fused_computation.1.clone.1 | custom fusion | flops 524288 | bytes 6291488 | tf_op jit(solution)/shard_map/while/body/scatter-add | solution.py:65
  204.1 1.8 convolution_multiply_fusion.2
  205.9 4.2 %scatter_fusion = f32[16,256,256]{2,1,0:T(8,128)} fusion(f32[16,256,256]{2,1,0:T(8,128)} %get-tuple-element.262, s32[8]{0:T(128)S(1)} %fusion.30, f32[8,256,256]{2,1,0:T(8,128)S(1)} %convolution_multiply_fusion.2), kind=kCustom, calls=%fused_computation.1.clone.1 | custom fusion | flops 524288 | bytes 6291488 | tf_op jit(solution)/shard_map/while/body/scatter-add | solution.py:65
  210.7 1.8 convolution_multiply_fusion.2
  212.5 4.3 %scatter_fusion = f32[16,256,256]{2,1,0:T(8,128)} fusion(f32[16,256,256]{2,1,0:T(8,128)} %get-tuple-element.262, s32[8]{0:T(128)S(1)} %fusion.30, f32[8,256,256]{2,1,0:T(8,128)S(1)} %convolution_multiply_fusion.2), kind=kCustom, calls=%fused_computation.1.clone.1 | custom fusion | flops 524288 | bytes 6291488 | tf_op jit(solution)/shard_map/while/body/scatter-add | solution.py:65
  217.4 3.8 convert_element_type.49
  221.2 0.0 reduce-scatter.5.cloned.1.call-update
  221.3 119.5 %psum.15 = f32[256]{0:T(256)S(1)} all-reduce(f32[256]{0:T(256)S(1)} %get-tuple-element.126), channel_id=1, replica_groups=mesh['row'=4,'col'=8] {'row','col'}, use_global_device_ids=true, to_apply=%region_10.11 | all-reduce | flops 256 | bytes 2048 | tf_op jit(solution)/shard_map/psum | solution.py:57
  340.8 0.6 broadcast_multiply_fusion.1
  341.4 1.7 broadcast_multiply_fusion
  343.0 47.3 %reduce-scatter.5.cloned.1.call-done = bf16[512,256]{1,0:T(8,128)(2,1)} async-done(((bf16[4096,256]{1,0:T(8,128)(2,1)}), bf16[512,256]{1,0:T(8,128)(2,1)}) %reduce-scatter.5.cloned.1.call-update) | async-done | bytes 262160 | tf_op jit(solution)/shard_map/reduce_scatter | solution.py:71
  (29 shorter events, 0.2 us)
Async XLA Ops:
  7.2 160.2 %copy-start = (bf16[256,256]{1,0:T(8,128)(2,1)S(1)}, bf16[256,256]{1,0:T(8,128)(2,1)}, u32[]{:S(2)}) copy-start(bf16[256,256]{1,0:T(8,128)(2,1)} %param.15) | copy-start | bytes 393220
  7.2 55.2 %copy-start.5 = (s32[8,1]{0,1:T(1,128)S(1)}, s32[8,1]{0,1:T(1,128)}, u32[]{:S(2)}) copy-start(s32[8,1]{0,1:T(1,128)} %param.14) | copy-start | bytes 100
  7.2 55.0 %all-gather.3.cloned.1.call-start = ((), (), s32[]{:S(2)}) async-start(), calls=%async_computation.2 | async-start | bytes 2359296 | tf_op jit(solution)/shard_map/all_gather | solution.py:28
  7.9 159.4 %reduce-scatter.3.cloned.1.call-start = ((), (), s32[]{:S(2)}) async-start(), calls=%async_computation.3 | async-start | bytes 1310720 | tf_op jit(solution)/shard_map/reduce_scatter | solution.py:53
  83.1 84.2 %copy-start.3 = (bf16[512,256]{1,0:T(8,128)(2,1)S(1)}, bf16[512,256]{1,0:T(8,128)(2,1)}, u32[]{:S(2)}) copy-start(bf16[512,256]{1,0:T(8,128)(2,1)} %param.17) | copy-start | bytes 786436
  83.1 84.2 %copy-start.4 = (f32[256]{0:T(256)S(1)}, f32[256]{0:T(256)}, u32[]{:S(2)}) copy-start(f32[256]{0:T(256)} %param.16) | copy-start | bytes 3076
  84.3 103.1 %all-gather.5.cloned.1.call-start = ((), (), s32[]{:S(2)}) async-start(), calls=%async_computation.4 | async-start | bytes 1310720 | tf_op jit(solution)/shard_map/all_gather | solution.py:58
  167.3 3.2 copy-start.2
  170.5 170.9 %all-reduce.2.cloned.1.call-start = ((), (), s32[]{:S(2)}) async-start(), calls=%async_computation.6 | async-start | bytes 524288 | tf_op jit(solution)/shard_map/psum | solution.py:57
  171.5 218.8 %reduce-scatter.5.cloned.1.call-start = ((), (), s32[]{:S(2)}) async-start(), calls=%async_computation.5 | async-start | bytes 2359296 | tf_op jit(solution)/shard_map/reduce_scatter | solution.py:71
  187.3 2.4 copy-start.1
Sparse Core Ops, SparseCore 0:
  10.2 51.9 all-gather.2
  84.4 82.8 reduce-scatter.2
  170.6 16.7 all-gather.4
  194.2 124.9 all-reduce.1
  323.6 66.7 reduce-scatter.4
where the time goes:
time: 400 us; the launch traced here: 397 us
  waiting for transfers between devices  199 us (50%)
  blocking collectives  120 us (30%)
  other arithmetic  25.7 us (6%)
  matrix products  19.8 us (5%)
  between operations  13.9 us (3%)
  local copies, waits for them, and re-layouts  12.2 us (3%)
  loops' own time  6.57 us (2%)
    psum x1, blocking collectives, per_device(): weight_grad, bias_grad = lax.psum((weight_grad, bias_grad), ('row', 'col'))  120 us
    reduce_scatter x1, waiting for transfers between devices, per_device(): lax.psum_scatter(partial_value.astype(jnp.bfloat16), 'row', scatter_dimen...  83 us
    all_gather x1, waiting for transfers between devices, per_device(): column_block = lax.all_gather(features, 'col', axis=0, tiled=True)  52.1 us
    reduce_scatter x1, waiting for transfers between devices, per_device(): lax.psum_scatter(summed.astype(jnp.bfloat16), 'col', scatter_dimension=0,...  47.3 us
    scatter-add x4, other arithmetic, backward_slot(): return running.at[columns].add(contrib)  17.2 us
    all_gather x1, waiting for transfers between devices, per_device(): grad_block = lax.all_gather(hidden_grad, 'row', axis=0, tiled=True)  15.8 us
    gather x4, local copies, waits for them, and re-layouts, forward_slot(): jnp.take(x_tiles, columns, axis=0)  8.82 us
    dot_general x4, matrix products, forward_slot(): jnp.einsum('tij,tjf->tif', values, picked, preferred_element_type=jnp.flo...  8.51 us
  transfers between devices with their start and end apart: 5, of which 4 were waited for; matrix products, arithmetic and copies ran while one was open for 9% of the time, Pallas kernels for 0%

commit v1 on v0

v1 whole, which is shorter than its diff:
```python
import functools
import math

import jax
import jax.numpy as jnp
import numpy as np
from jax import lax
from jax.experimental import pallas as pl
from jax.experimental.pallas import tpu as pltpu
from jax.sharding import PartitionSpec as P

BF16 = jnp.bfloat16
F32 = jnp.float32
GROUP = 4
DEPTH = 4

VMEM = pl.BlockSpec(memory_space=pltpu.VMEM)
SMEM = pl.BlockSpec(memory_space=pltpu.SMEM)
HBM = pl.BlockSpec(memory_space=pl.ANY)


def ring_order(count):
    return list(range(0, count, 2)) + list(range(count - 1, 0, -2))


def params(mib):
    return pltpu.CompilerParams(vmem_limit_bytes=mib * 2**20)


def cost(flops, nbytes):
    return pl.CostEstimate(flops=int(flops), bytes_accessed=int(nbytes), transcendentals=0)


def lists_kernel(slots, far, cols, counts, place, pos_of, fwd, bwd, groups):
    row_tiles = pos_of.shape[0]
    col_tiles = place.shape[0]
    cap_f = fwd.shape[0] // 2
    cap_b = bwd.shape[0] // col_tiles

    def clear(k, _):
        groups[2 + k] = 0
        return 0

    lax.fori_loop(0, col_tiles, clear, 0)

    def tile_row(t, filled):
        pos = pos_of[t]

        def slot(s, filled):
            near_n, far_n = filled
            k = place[cols[t * slots + s]]
            head = (t * slots + s) * 65536 + pos * 256
            is_far = (k >= far).astype(jnp.int32)
            at = jnp.where(k >= far, cap_f + far_n, near_n)
            fwd[at] = head + k - is_far * far
            count = groups[2 + k]
            bwd[k * cap_b + count] = head
            groups[2 + k] = count + 1
            return near_n + 1 - is_far, far_n + is_far

        near_n, far_n = lax.fori_loop(0, counts[t], slot, filled)
        head = t * slots * 65536 + pos * 256
        near_top = (near_n + GROUP - 1) // GROUP * GROUP
        far_top = (far_n + GROUP - 1) // GROUP * GROUP

        def fill_near(i, _):
            fwd[i] = head + far
            return 0

        def fill_far(i, _):
            fwd[cap_f + i] = head + col_tiles - far
            return 0

        lax.fori_loop(near_n, near_top, fill_near, 0)
        lax.fori_loop(far_n, far_top, fill_far, 0)
        return near_top, far_top

    near_n, far_n = lax.fori_loop(0, row_tiles, tile_row, (0, 0))
    groups[0] = near_n // GROUP
    groups[1] = far_n // GROUP

    def fill_bwd(k, _):
        count = groups[2 + k]
        top = (count + GROUP - 1) // GROUP * GROUP

        def fill(i, _):
            bwd[k * cap_b + i] = row_tiles * 256
            return 0

        lax.fori_loop(count, top, fill, 0)
        groups[2 + k] = top // GROUP
        return 0

    lax.fori_loop(0, col_tiles, fill_bwd, 0)


def make_lists(tile_cols, tile_counts, place, pos_of, far):
    row_tiles, slots = tile_cols.shape
    col_tiles = place.shape[0]
    cap_f = row_tiles * (slots + GROUP)
    cap_b = row_tiles * slots + GROUP
    i32 = lambda n: jax.ShapeDtypeStruct((n,), jnp.int32)
    return pl.pallas_call(
        functools.partial(lists_kernel, slots, far),
        in_specs=[SMEM] * 4,
        out_specs=[SMEM] * 3,
        out_shape=[i32(2 * cap_f), i32(col_tiles * cap_b), i32(2 + col_tiles)],
        cost_estimate=cost(0, 2**22),
        name="lists",
    )(tile_cols.reshape(-1), tile_counts.reshape(-1), place, pos_of)


def tile_copy(entry, values, buffer, sems, at):
    return pltpu.make_async_copy(values.at[entry // 65536], buffer.at[at], sems.at[at])


def start_group(list_ref, base, g, values, buffer, sems):
    for u in range(GROUP):
        at = lax.rem(g, DEPTH) * GROUP + u
        tile_copy(list_ref[base + g * GROUP + u], values, buffer, sems, at).start()


def wait_group(list_ref, base, g, values, buffer, sems):
    for u in range(GROUP):
        at = lax.rem(g, DEPTH) * GROUP + u
        tile_copy(list_ref[base + g * GROUP + u], values, buffer, sems, at).wait()


def stream(list_ref, base, count, values, buffer, sems, use):
    def ahead(g, _):
        start_group(list_ref, base, g, values, buffer, sems)
        return 0

    lax.fori_loop(0, jnp.minimum(count, DEPTH - 1), ahead, 0)

    def step(g, _):
        @pl.when(g + DEPTH - 1 < count)
        def _():
            start_group(list_ref, base, g + DEPTH - 1, values, buffer, sems)

        wait_group(list_ref, base, g, values, buffer, sems)
        use(base + g * GROUP, lax.rem(g, DEPTH) * GROUP)
        return 0

    lax.fori_loop(0, count, step, 0)


def forward_near_kernel(n_blocks, fwd, groups, values, *refs):
    blocks, (total, source, buffer, sems, block_sems) = refs[:n_blocks], refs[n_blocks:]
    tiles_each = blocks[0].shape[0]
    copies = [
        pltpu.make_async_copy(b, source.at[pl.ds(i * tiles_each, tiles_each)], block_sems.at[i])
        for i, b in enumerate(blocks)
    ]
    for c in copies:
        c.start()
    source[n_blocks * tiles_each] = jnp.zeros(source.shape[1:], BF16)
    total[...] = jnp.zeros(total.shape, F32)
    for c in copies:
        c.wait()

    def use(first, at):
        pos = lax.rem(fwd[first] // 256, 256)
        added = None
        for u in range(GROUP):
            k = lax.rem(fwd[first + u], 256)
            part = jnp.dot(buffer[at + u], source[k], preferred_element_type=F32)
            added = part if added is None else added + part
        total[pos] += added

    stream(fwd, 0, groups[0], values, buffer, sems, use)


def forward_far_kernel(cap_f, fwd, groups, values, before, near, away, mine, other, total, source, buffer, sems, block_sems):
    half = near.shape[0]
    copies = [
        pltpu.make_async_copy(near, source.at[pl.ds(0, half)], block_sems.at[0]),
        pltpu.make_async_copy(away, source.at[pl.ds(half, half)], block_sems.at[1]),
        pltpu.make_async_copy(before, total, block_sems.at[2]),
    ]
    for c in copies:
        c.start()
    source[2 * half] = jnp.zeros(source.shape[1:], BF16)
    for c in copies:
        c.wait()

    def use(first, at):
        pos = lax.rem(fwd[first] // 256, 256)
        added = None
        for u in range(GROUP):
            k = lax.rem(fwd[first + u], 256)
            part = jnp.dot(buffer[at + u], source[k], preferred_element_type=F32)
            added = part if added is None else added + part
        total[pos] += added

    stream(fwd, cap_f, groups[1], values, buffer, sems, use)
    half_rows = mine.shape[0]
    mine[...] = total[:half_rows].astype(BF16)
    other[...] = total[half_rows:].astype(BF16)


def dense_kernel(own, came, weight, bias, cot_own, cot_other, out, grad_t, wgrad):
    tile = grad_t.shape[1]
    half = out.shape[0]
    tiles_half = half // tile
    w = weight[...]
    b = bias[...]
    wg = None
    bg = None
    for h in range(2):
        near = own[h * tiles_half : (h + 1) * tiles_half].reshape(half, -1).astype(F32)
        away = came[(1 - h) * tiles_half : (2 - h) * tiles_half].reshape(half, -1).astype(F32)
        hidden = (near + away).astype(BF16)
        preact = jnp.dot(hidden, w, preferred_element_type=F32) + b
        sig = 1.0 / (1.0 + jnp.exp(-preact))
        cot = (cot_own if h == 0 else cot_other)[...].astype(F32)
        if h == 0:
            out[...] = (preact * sig).astype(BF16)
        pgrad = (cot * (sig * (1.0 + preact * (1.0 - sig)))).astype(BF16)
        for i in range(tiles_half):
            rows = pgrad[i * tile : (i + 1) * tile]
            grad_t[h * tiles_half + i] = lax.dot_general(
                w, rows, (((1,), (1,)), ((), ())), preferred_element_type=F32
            ).astype(BF16)
        part = lax.dot_general(hidden, pgrad, (((0,), (0,)), ((), ())), preferred_element_type=F32)
        bias_part = jnp.sum(pgrad.astype(F32), axis=0, keepdims=True)
        wg = part if wg is None else wg + part
        bg = bias_part if bg is None else bg + bias_part
    rows = wg.shape[0] // 4
    for q in range(4):
        wgrad[q, :rows] = wg[q * rows : (q + 1) * rows]
        wgrad[q, rows:] = jnp.broadcast_to(bg, (wgrad.shape[1] - rows, bg.shape[1]))


def backward_kernel(ks, cap_b, bwd, groups, values, grad_mine, grad_came, out, grads, buffer, sems, block_sems):
    half = grad_mine.shape[0]
    copies = [
        pltpu.make_async_copy(grad_mine, grads.at[pl.ds(0, half)], block_sems.at[0]),
        pltpu.make_async_copy(grad_came, grads.at[pl.ds(half, half)], block_sems.at[1]),
    ]
    for c in copies:
        c.start()
    grads[2 * half] = jnp.zeros(grads.shape[1:], BF16)
    out[...] = jnp.zeros(out.shape, F32)
    for c in copies:
        c.wait()
    for i, k in enumerate(ks):

        def use(first, at, i=i):
            added = None
            for u in range(GROUP):
                pos = lax.rem(bwd[first + u] // 256, 256)
                part = jnp.dot(grads[pos], buffer[at + u], preferred_element_type=F32)
                added = part if added is None else added + part
            out[i] += added

        stream(bwd, k * cap_b, groups[2 + k], values, buffer, sems, use)


def finish_kernel(own, right, left, out):
    tiles, _, tile = own.shape
    for i in range(tiles):
        total = own[i] + right[i].astype(F32) + left[i].astype(F32)
        out[i * tile : (i + 1) * tile] = total.T.astype(BF16)


def per_device(n_col, features, tile_values, tile_cols, tile_counts, weight, bias, cotangent):
    node_dev, width = features.shape
    row_tiles, slots, tile, _ = tile_values.shape
    per_dev = node_dev // tile
    col_tiles = n_col * per_dev
    half = n_col // 2
    far = col_tiles - per_dev
    node_total = node_dev * lax.axis_size("row") * n_col
    grad_scale = 1.0 / math.sqrt(node_total)
    values = tile_values.reshape(row_tiles * slots, tile, tile)

    order = ring_order(n_col)
    right = [(order[i], order[(i + 1) % n_col]) for i in range(n_col)]
    left = [(b, a) for a, b in right]
    cores = [(0, 1), (1, 0), (2, 3), (3, 2)]
    across = [(0, 2), (2, 0), (1, 3), (3, 1)]
    row = lax.axis_index("row")
    col = lax.axis_index("col")
    my_y, my_core = row // 2, row % 2

    rank = np.zeros(n_col, np.int32)
    rank[order] = np.arange(n_col)
    steps = np.arange(n_col)
    arrival_of_step = np.where(steps == 0, 0, np.where(steps < half, 2 * steps, np.where(steps == half, n_col - 1, 2 * (n_col - steps) - 1)))
    table = np.zeros((n_col, col_tiles), np.int32)
    for d in range(n_col):
        for t in range(col_tiles):
            ahead = (rank[t // per_dev] - rank[d]) % n_col
            table[d, t] = arrival_of_step[ahead] * per_dev + t % per_dev
    place = lax.dynamic_index_in_dim(jnp.asarray(table), col, 0, keepdims=False)
    tiles = np.arange(row_tiles)
    tiles_r = row_tiles // 4
    pos_table = np.zeros((4, row_tiles), np.int32)
    for r in range(4):
        block = tiles // tiles_r
        pos_table[r] = ((block % 2 != r % 2) * 2 + (block // 2 != r // 2)) * tiles_r + tiles % tiles_r
    pos_of = lax.dynamic_index_in_dim(jnp.asarray(pos_table), row, 0, keepdims=False)

    fwd, bwd, groups = make_lists(tile_cols, tile_counts, place, pos_of, far)
    cap_f = fwd.shape[0] // 2
    cap_b = bwd.shape[0] // col_tiles

    mine = features.reshape(per_dev, tile, width)
    arrived = [mine]
    from_left = from_right = mine
    for _ in range(half - 1):
        from_left = lax.ppermute(from_left, "col", right)
        from_right = lax.ppermute(from_right, "col", left)
        arrived += [from_left, from_right]
    far_near = lax.ppermute(from_left[: per_dev // 2], "col", right)
    far_away = lax.ppermute(from_right[per_dev // 2 :], "col", left)
    cot_other = lax.ppermute(cotangent, "row", across)

    stream_scratch = [pltpu.VMEM((DEPTH * GROUP, tile, tile), BF16), pltpu.SemaphoreType.DMA((DEPTH * GROUP,))]
    dots = 2 * tile * tile * width
    total = pl.pallas_call(
        functools.partial(forward_near_kernel, len(arrived)),
        in_specs=[SMEM, SMEM, HBM] + [HBM] * len(arrived),
        out_specs=VMEM,
        out_shape=jax.ShapeDtypeStruct((row_tiles, tile, width), F32),
        scratch_shapes=[pltpu.VMEM((far + 1, tile, width), BF16)]
        + stream_scratch
        + [pltpu.SemaphoreType.DMA((len(arrived),))],
        compiler_params=params(40),
        cost_estimate=cost(64 * dots, 64 * tile * tile * 2),
        name="forward_near",
    )(fwd, groups, values, *arrived)
    half_shape = (row_tiles // 2, tile, width)
    hid_mine, hid_other = pl.pallas_call(
        functools.partial(forward_far_kernel, cap_f),
        in_specs=[SMEM, SMEM, HBM, HBM, HBM, HBM],
        out_specs=[VMEM, VMEM],
        out_shape=[jax.ShapeDtypeStruct(half_shape, BF16)] * 2,
        scratch_shapes=[pltpu.VMEM((row_tiles, tile, width), F32), pltpu.VMEM((per_dev + 1, tile, width), BF16)]
        + stream_scratch
        + [pltpu.SemaphoreType.DMA((3,))],
        compiler_params=params(40),
        cost_estimate=cost(16 * dots, 16 * tile * tile * 2),
        name="forward_far",
    )(fwd, groups, values, total, far_near, far_away)

    hid_came = lax.ppermute(hid_other, "row", cores)
    own = (hid_mine.astype(F32) + hid_came.astype(F32)).astype(BF16)
    came = lax.ppermute(own, "row", across)

    q_rows = width // 4 + 8
    layer_out, grad_mine, wgrad = pl.pallas_call(
        dense_kernel,
        in_specs=[VMEM] * 6,
        out_specs=[VMEM] * 3,
        out_shape=[
            jax.ShapeDtypeStruct((node_dev, width), BF16),
            jax.ShapeDtypeStruct((row_tiles // 2, width, tile), BF16),
            jax.ShapeDtypeStruct((4, q_rows, width), F32),
        ],
        compiler_params=params(40),
        cost_estimate=cost(3 * 2 * 2 * node_dev * width * width, 8 * node_dev * width),
        name="dense",
    )(own, came, weight, bias.reshape(1, -1), cotangent, cot_other)
    grad_came = lax.ppermute(grad_mine, "row", cores)

    wgrad = wgrad.reshape(2, 2, q_rows, width)
    part = lax.dynamic_index_in_dim(wgrad, my_core, 0, keepdims=False)
    part = part + lax.ppermute(lax.dynamic_index_in_dim(wgrad, 1 - my_core, 0, keepdims=False), "row", cores)
    part = lax.dynamic_index_in_dim(part, my_y, 0, keepdims=False)
    wsum, w_left, w_right = part, part, part
    for s in range(half):
        w_left = lax.ppermute(w_left, "col", right)
        wsum = wsum + w_left
        if s < half - 1:
            w_right = lax.ppermute(w_right, "col", left)
            wsum = wsum + w_right
    wsum = wsum * grad_scale
    w_y = lax.ppermute(wsum, "row", across)
    pair = jnp.where(my_y == 0, jnp.stack([wsum, w_y]), jnp.stack([w_y, wsum]))
    w_c = lax.ppermute(pair, "row", cores)
    quads = jnp.where(my_core == 0, jnp.stack([pair, w_c]), jnp.stack([w_c, pair]))
    quads = quads.reshape(4, q_rows, width)
    weight_grad = quads[:, : width // 4].reshape(width, width)
    bias_grad = quads[0, width // 4]

    def backward(ks, name):
        return pl.pallas_call(
            functools.partial(backward_kernel, ks, cap_b),
            in_specs=[SMEM, SMEM, HBM, HBM, HBM],
            out_specs=VMEM,
            out_shape=jax.ShapeDtypeStruct((len(ks), width, tile), F32),
            scratch_shapes=[pltpu.VMEM((row_tiles + 1, width, tile), BF16)]
            + stream_scratch
            + [pltpu.SemaphoreType.DMA((2,))],
            compiler_params=params(40),
            cost_estimate=cost(16 * dots, 16 * tile * tile * 2),
            name=name,
        )(bwd, groups, values, grad_mine, grad_came)

    def block(arrival):
        return [arrival * per_dev + i for i in range(per_dev)]

    far_part = backward(block(n_col - 1), "backward_far").astype(BF16)
    to_right = lax.ppermute(far_part[: per_dev // 2], "col", right)
    to_left = lax.ppermute(far_part[per_dev // 2 :], "col", left)
    for d in range(half - 1, 0, -1):
        both = backward(block(2 * d) + block(2 * d - 1), "backward")
        for_right, for_left = both[:per_dev], both[per_dev:]
        if d == half - 1:
            zeros = jnp.zeros((per_dev - per_dev // 2, width, tile), BF16)
            to_right = jnp.concatenate([to_right, zeros])
            to_left = jnp.concatenate([jnp.zeros((per_dev // 2, width, tile), BF16), to_left])
        to_right = lax.ppermute((for_right + to_right.astype(F32)).astype(BF16), "col", right)
        to_left = lax.ppermute((for_left + to_left.astype(F32)).astype(BF16), "col", left)
    own_part = backward(block(0), "backward_own")
    feature_grad = pl.pallas_call(
        finish_kernel,
        in_specs=[VMEM] * 3,
        out_specs=VMEM,
        out_shape=jax.ShapeDtypeStruct((node_dev, width), BF16),
        name="finish",
    )(own_part, to_right, to_left)
    return (layer_out, feature_grad, weight_grad, bias_grad)


def solution(mesh):
    placed = (
        P(("row", "col"), None),
        P("col", "row", None, None),
        P("col", "row"),
        P("col", "row"),
        P(),
        P(),
        P(("col", "row"), None),
    )
    return jax.shard_map(
        functools.partial(per_device, mesh.shape["col"]),
        mesh=mesh,
        in_specs=placed,
        out_specs=(P(("col", "row"), None), P(("row", "col"), None), P(), P()),
        check_vma=False,
    )
```

time: 400 us -> 134 us (0.34)
  waiting for transfers between devices: 199 us -> 46.3 us
  blocking collectives: 120 us -> 0 us
  starting transfers between devices: 0.2 us -> 43.8 us
  Pallas kernels: 0 us -> 33 us
  other arithmetic: 25.7 us -> 0.61 us
  matrix products: 19.8 us -> 0 us
  between operations: 13.9 us -> 0.92 us
  loops' own time: 6.57 us -> 0 us
    reduce_scatter x2 -> x0, waiting for transfers between devices: 130 us -> none  [the longest x1 83 us: per_device(): lax.psum_scatter(partial_value.astype(jnp.bfloat16), 'row', scatter_dimen...]
    psum x1 -> x0, blocking collectives: 120 us -> none  [per_device(): weight_grad, bias_grad = lax.psum((weight_grad, bias_grad), ('row', 'col'))]
    all_gather x2 -> x0, waiting for transfers between devices: 67.9 us -> none  [the longest x1 52.1 us: per_device(): column_block = lax.all_gather(features, 'col', axis=0, tiled=True)]
    ppermute x0 -> x30, waiting for transfers between devices: none -> 46.3 us  [the longest x1 18 us: per_device(): cot_other = lax.ppermute(cotangent, 'row', across)]
    ppermute x0 -> x30, starting transfers between devices: none -> 43.8 us  [the longest x3 8.2 us: per_device(): lax.ppermute((for_left + to_left.astype(F32)).astype(BF16), 'col', left)]
    pallas_call x0 -> x10, Pallas kernels: none -> 33 us  [the longest x5 17.8 us: backward(): pl.pallas_call(functools.partial(backward_kernel, ks, cap_b), in_specs=[S...]
    dot_general x11 -> x0, matrix products: 19.8 us -> none  [the longest x4 8.51 us: forward_slot(): jnp.einsum('tij,tjf->tif', values, picked, preferred_element_type=jnp.flo...]
    scatter-add x4 -> x0, other arithmetic: 17.2 us -> none  [backward_slot(): return running.at[columns].add(contrib)]
  transfers between devices with their start and end apart: 5 -> 30, of which waited for: 4 -> 10; matrix products, arithmetic and copies ran while one was open for 9% -> 4% of each run, Pallas kernels for 0% -> 19%
where the time goes in v1:
time: 134 us
  waiting for transfers between devices  46.3 us (35%)
  starting transfers between devices  43.8 us (33%)
  Pallas kernels  33 us (25%)
  local copies, waits for them, and re-layouts  9.47 us (7%)
    ppermute x1, waiting for transfers between devices, per_device(): cot_other = lax.ppermute(cotangent, 'row', across)  18 us
    pallas_call x5, Pallas kernels, backward(): pl.pallas_call(functools.partial(backward_kernel, ks, cap_b), in_specs=[S...  17.8 us
    ppermute x3, waiting for transfers between devices, per_device(): from_left = lax.ppermute(from_left, 'col', right)  11.9 us
    ppermute x3, starting transfers between devices, per_device(): lax.ppermute((for_left + to_left.astype(F32)).astype(BF16), 'col', left)  8.2 us
    ppermute x3, waiting for transfers between devices, per_device(): w_right = lax.ppermute(w_right, 'col', left)  8.19 us
    ppermute x3, starting transfers between devices, per_device(): lax.ppermute((for_right + to_right.astype(F32)).astype(BF16), 'col', right)  7.79 us
    ppermute x1, starting transfers between devices, per_device(): to_left = lax.ppermute(far_part[per_dev // 2:], 'col', left)  7.03 us
    ppermute x3, starting transfers between devices, per_device(): from_left = lax.ppermute(from_left, 'col', right)  6.4 us
  transfers between devices with their start and end apart: 30, of which 10 were waited for; matrix products, arithmetic and copies ran while one was open for 4% of the time, Pallas kernels for 19%

profile of v1, /device:TPU:0, one launch (start us, length us, event | category | flops | bytes accessed | tf_op | source)
XLA Modules:
  0.0 134.2 jit_solution(1644131908206407614)
XLA Ops:
  0.6 3.1 %collective-permute-start = (bf16[2,256,256]{2,1,0:T(8,128)(2,1)}, bf16[2,256,256]{2,1,0:T(8,128)(2,1)S(1)}, u32[]{:S(2)}, u32[]{:S(2)}) collective-permute-start(bf16[2,256,256]{2,1,0:T(8,128)(2,1)} %bitcast.24), channel_id=1, source_target_pairs={{0,2},{2,4},{4,6},{6,7},{7,5},{5,3},{3,1},{1,0},{8,10},{10,12},{12... | collective-permute-start | bytes 786440 | tf_op jit(solution)/shard_map/ppermute | solution.py:313
  3.7 6.4 %collective-permute-done.refs_1_ = bf16[2,256,256]{2,1,0:T(8,128)(2,1)S(1)} collective-permute-done((bf16[2,256,256]{2,1,0:T(8,128)(2,1)}, bf16[2,256,256]{2,1,0:T(8,128)(2,1)S(1)}, u32[]{:S(2)}, u32[]{:S(2)}) %collective-permute-start) | collective-permute-done | bytes 262176 | tf_op jit(solution)/shard_map/ppermute | solution.py:313
  10.1 1.8 %collective-permute-start.2 = (bf16[2,256,256]{2,1,0:T(8,128)(2,1)S(1)}, bf16[2,256,256]{2,1,0:T(8,128)(2,1)S(1)}, u32[]{:S(2)}, u32[]{:S(2)}) collective-permute-start(bf16[2,256,256]{2,1,0:T(8,128)(2,1)S(1)} %collective-permute-done.refs_1_), channel_id=1, source_target_pairs={{0,2},{2,4},{4,6},{6,7},{7,5},{5,3},{3,1},{1,0},{8,10},{10,12},{12... | collective-permute-start | bytes 786440 | tf_op jit(solution)/shard_map/ppermute | solution.py:313
  12.2 5.5 %collective-permute-done.2.refs_3_ = bf16[2,256,256]{2,1,0:T(8,128)(2,1)S(1)} collective-permute-done((bf16[2,256,256]{2,1,0:T(8,128)(2,1)S(1)}, bf16[2,256,256]{2,1,0:T(8,128)(2,1)S(1)}, u32[]{:S(2)}, u32[]{:S(2)}) %collective-permute-start.2) | collective-permute-done | bytes 262176 | tf_op jit(solution)/shard_map/ppermute | solution.py:313
  17.6 1.5 %collective-permute-start.4 = (bf16[2,256,256]{2,1,0:T(8,128)(2,1)S(1)}, bf16[2,256,256]{2,1,0:T(8,128)(2,1)S(1)}, u32[]{:S(2)}, u32[]{:S(2)}) collective-permute-start(bf16[2,256,256]{2,1,0:T(8,128)(2,1)S(1)} %collective-permute-done.2.refs_3_), channel_id=1, source_target_pairs={{0,2},{2,4},{4,6},{6,7},{7,5},{5,3},{3,1},{1,0},{8,10},{10,12},{12... | collective-permute-start | bytes 786440 | tf_op jit(solution)/shard_map/ppermute | solution.py:313
  19.7 1.3 reshape.93.cols
  20.9 1.2 fusion.8.pos_of
  22.1 1.2 fusion.7.place
  23.3 2.6 %lists.1 = (s32[320]{0:T(512)}, s32[2112]{0:T(1024)}, s32[18]{0:T(128)}) custom-call(s32[128]{0:T(128)} %reshape.93.cols, s32[8]{0:T(128)} %bitcast.44, s32[16]{0:T(128)} %fusion.7.place, s32[8]{0:T(128)} %fusion.8.pos_of), custom_call_target="tpu_custom_call" | custom-call | bytes 4194304 | tf_op jit(solution)/shard_map/lists/pallas_call | solution.py:103
  26.0 1.5 %collective-permute-start.6 = (bf16[1,256,256]{2,1,0:T(8,128)(2,1)S(1)}, bf16[1,256,256]{2,1,0:T(8,128)(2,1)S(1)}, u32[]{:S(2)}, u32[]{:S(2)}) collective-permute-start(bf16[1,256,256]{2,1,0:T(8,128)(2,1)S(1)} %slice.48), channel_id=1, source_target_pairs={{0,2},{2,4},{4,6},{6,7},{7,5},{5,3},{3,1},{1,0},{8,10},{10,12},{12... | collective-permute-start | bytes 393224 | tf_op jit(solution)/shard_map/ppermute | solution.py:316
  27.5 1.2 collective-permute-start.7
  28.7 0.9 copy-done.2
  29.6 0.6 copy-done.5
  30.2 0.7 copy-done.7
  30.9 5.6 %forward_near.1.before = f32[8,256,256]{2,1,0:T(8,128)S(1)} custom-call(s32[320]{0:T(512)S(1)} %copy-done.7, s32[18]{0:T(128)S(1)} %copy-done.5, bf16[128,256,256]{2,1,0:T(8,128)(2,1)} %bitcast.28, bf16[2,256,256]{2,1,0:T(8,128)(2,1)S(1)} %bitcast.26, bf16[2,256,256]{2,1,0:T(8,128)(2,1)S(1)} %collective-permute-done.refs_1_, ...), custom_call_target="tpu_custom_call" | custom-call | flops 2147483648 | bytes 8388608 | tf_op jit(solution)/shard_map/forward_near/pallas_call | solution.py:322
  36.5 3.5 %forward_far.1 = (bf16[4,256,256]{2,1,0:T(8,128)(2,1)S(1)}, bf16[4,256,256]{2,1,0:T(8,128)(2,1)S(1)}) custom-call(s32[320]{0:T(512)S(1)} %copy-done.7, s32[18]{0:T(128)S(1)} %copy-done.5, bf16[128,256,256]{2,1,0:T(8,128)(2,1)} %bitcast.29, f32[8,256,256]{2,1,0:T(8,128)S(1)} %forward_near.1.before, bf16[1,256,256]{2,1,0:T(8,128)(2,1)S(1)} %collective-permute-done.6.near, ...), custom_call_target="tpu_custom_call" | custom-call | flops 536870912 | bytes 2097152 | tf_op jit(solution)/shard_map/forward_far/pallas_call | solution.py:335
  40.1 1.9 %collective-permute-done.8 = bf16[4,256,256]{2,1,0:T(8,128)(2,1)S(1)} collective-permute-done((bf16[4,256,256]{2,1,0:T(8,128)(2,1)S(1)}, bf16[4,256,256]{2,1,0:T(8,128)(2,1)S(1)}, u32[]{:S(2)}, u32[]{:S(2)}) %collective-permute-start.8) | collective-permute-done | bytes 524320 | tf_op jit(solution)/shard_map/ppermute | solution.py:348
  42.2 2.1 %collective-permute-start.9 = (bf16[4,256,256]{2,1,0:T(8,128)(2,1)S(1)}, bf16[4,256,256]{2,1,0:T(8,128)(2,1)S(1)}, u32[]{:S(2)}, u32[]{:S(2)}) collective-permute-start(bf16[4,256,256]{2,1,0:T(8,128)(2,1)S(1)} %add_convert_fusion.own), channel_id=1, source_target_pairs={{0,16},{16,0},{8,24},{24,8},{1,17},{17,1},{9,25},{25,9},{2,18},{18... | collective-permute-start | bytes 1572872 | tf_op jit(solution)/shard_map/ppermute | solution.py:350
  44.4 18.0 %collective-permute-done.10.cot_other = bf16[512,256]{1,0:T(8,128)(2,1)S(1)} collective-permute-done((bf16[512,256]{1,0:T(8,128)(2,1)S(1)}, bf16[512,256]{1,0:T(8,128)(2,1)S(1)}, u32[]{:S(2)}, u32[]{:S(2)}) %collective-permute-start.10) | collective-permute-done | bytes 262176 | tf_op jit(solution)/shard_map/ppermute | solution.py:318
  62.3 1.5 %dense.1 = (bf16[512,256]{1,0:T(8,128)(2,1)}, bf16[4,256,256]{2,1,0:T(8,128)(2,1)S(1)}, f32[4,72,256]{2,1,0:T(8,128)S(1)}) custom-call(bf16[4,256,256]{2,1,0:T(8,128)(2,1)S(1)} %add_convert_fusion.own, bf16[4,256,256]{2,1,0:T(8,128)(2,1)S(1)} %collective-permute-done.9.came, bf16[256,256]{1,0:T(8,128)(2,1)S(1)} %copy-done.4, f32[1,256]{1,0:T(1,128)S(1)} %bitcast.27, ...), custom_call_target="tpu_custom_call" | custom-call | flops 402653184 | bytes 1048576 | tf_op jit(solution)/shard_map/dense/pallas_call | solution.py:353
  63.9 0.6 collective-permute-start.20
  64.5 1.3 collective-permute-done.11.grad_came
  65.8 3.8 %backward_far.1 = f32[2,256,256]{2,1,0:T(8,128)S(1)} custom-call(s32[2112]{0:T(1024)S(1)} %copy-done.1, s32[18]{0:T(128)S(1)} %copy-done.6, bf16[128,256,256]{2,1,0:T(8,128)(2,1)} %bitcast.30, bf16[4,256,256]{2,1,0:T(8,128)(2,1)S(1)} %get-tuple-element.18.grad_mine, bf16[4,256,256]{2,1,0:T(8,128)(2,1)S(1)} %collective-permute-done.11.grad_came), custom_call_target="tpu_custom_call" | custom-call | flops 536870912 | bytes 2097152 | tf_op jit(solution)/shard_map/backward_far/pallas_call | solution.py:389
  69.7 7.0 %collective-permute-start.16 = (bf16[1,256,256]{2,1,0:T(8,128)(2,1)S(1)}, bf16[1,256,256]{2,1,0:T(8,128)(2,1)S(1)}, u32[]{:S(2)}, u32[]{:S(2)}) collective-permute-start(bf16[1,256,256]{2,1,0:T(8,128)(2,1)S(1)} %get-tuple-element.28), channel_id=1, source_target_pairs={{2,0},{4,2},{6,4},{7,6},{5,7},{3,5},{1,3},{0,1},{10,8},{12,10},{14... | collective-permute-start | bytes 393224 | tf_op jit(solution)/shard_map/ppermute | solution.py:407
  76.8 0.9 collective-permute-start.21
  77.7 3.9 %backward.5 = f32[4,256,256]{2,1,0:T(8,128)S(1)} custom-call(s32[2112]{0:T(1024)S(1)} %copy-done.1, s32[18]{0:T(128)S(1)} %copy-done.6, bf16[128,256,256]{2,1,0:T(8,128)(2,1)} %bitcast.31, bf16[4,256,256]{2,1,0:T(8,128)(2,1)S(1)} %get-tuple-element.18.grad_mine, bf16[4,256,256]{2,1,0:T(8,128)(2,1)S(1)} %collective-permute-done.11.grad_came), custom_call_target="tpu_custom_call" | custom-call | flops 536870912 | bytes 2097152 | tf_op jit(solution)/shard_map/backward/pallas_call | solution.py:389
  81.7 2.0 %collective-permute-start.13 = (bf16[2,256,256]{2,1,0:T(8,128)(2,1)S(1)}, bf16[2,256,256]{2,1,0:T(8,128)(2,1)S(1)}, u32[]{:S(2)}, u32[]{:S(2)}) collective-permute-start(bf16[2,256,256]{2,1,0:T(8,128)(2,1)S(1)} %get-tuple-element.25), channel_id=1, source_target_pairs={{0,2},{2,4},{4,6},{6,7},{7,5},{5,3},{3,1},{1,0},{8,10},{10,12},{12... | collective-permute-start | bytes 786440 | tf_op jit(solution)/shard_map/ppermute | solution.py:415
  83.7 2.4 %collective-permute-start.17 = (bf16[2,256,256]{2,1,0:T(8,128)(2,1)S(1)}, bf16[2,256,256]{2,1,0:T(8,128)(2,1)S(1)}, u32[]{:S(2)}, u32[]{:S(2)}) collective-permute-start(bf16[2,256,256]{2,1,0:T(8,128)(2,1)S(1)} %get-tuple-element.24), channel_id=1, source_target_pairs={{2,0},{4,2},{6,4},{7,6},{5,7},{3,5},{1,3},{0,1},{10,8},{12,10},{14... | collective-permute-start | bytes 786440 | tf_op jit(solution)/shard_map/ppermute | solution.py:416
  86.1 2.0 %collective-permute-start.22 = (f32[72,256]{1,0:T(8,128)S(1)}, f32[72,256]{1,0:T(8,128)S(1)}, u32[]{:S(2)}, u32[]{:S(2)}) collective-permute-start(f32[72,256]{1,0:T(8,128)S(1)} %fusion.6), channel_id=1, source_target_pairs={{2,0},{4,2},{6,4},{7,6},{5,7},{3,5},{1,3},{0,1},{10,8},{12,10},{14... | collective-permute-start | bytes 221192 | tf_op jit(solution)/shard_map/ppermute | solution.py:377
  88.3 5.9 %collective-permute-done.22 = f32[72,256]{1,0:T(8,128)S(1)} collective-permute-done((f32[72,256]{1,0:T(8,128)S(1)}, f32[72,256]{1,0:T(8,128)S(1)}, u32[]{:S(2)}, u32[]{:S(2)}) %collective-permute-start.22) | collective-permute-done | bytes 73760 | tf_op jit(solution)/shard_map/ppermute | solution.py:377
  94.2 2.2 %collective-permute-start.25 = (f32[72,256]{1,0:T(8,128)S(1)}, f32[72,256]{1,0:T(8,128)S(1)}, u32[]{:S(2)}, u32[]{:S(2)}) collective-permute-start(f32[72,256]{1,0:T(8,128)S(1)} %collective-permute-done.23), channel_id=1, source_target_pairs={{0,2},{2,4},{4,6},{6,7},{7,5},{5,3},{3,1},{1,0},{8,10},{10,12},{12... | collective-permute-start | bytes 221192 | tf_op jit(solution)/shard_map/ppermute | solution.py:374
  96.4 2.3 %collective-permute-done.24 = f32[72,256]{1,0:T(8,128)S(1)} collective-permute-done((f32[72,256]{1,0:T(8,128)S(1)}, f32[72,256]{1,0:T(8,128)S(1)}, u32[]{:S(2)}, u32[]{:S(2)}) %collective-permute-start.24) | collective-permute-done | bytes 73760 | tf_op jit(solution)/shard_map/ppermute | solution.py:377
  98.8 2.0 %collective-permute-start.27 = (f32[72,256]{1,0:T(8,128)S(1)}, f32[72,256]{1,0:T(8,128)S(1)}, u32[]{:S(2)}, u32[]{:S(2)}) collective-permute-start(f32[72,256]{1,0:T(8,128)S(1)} %collective-permute-done.25), channel_id=1, source_target_pairs={{0,2},{2,4},{4,6},{6,7},{7,5},{5,3},{3,1},{1,0},{8,10},{10,12},{12... | collective-permute-start | bytes 221192 | tf_op jit(solution)/shard_map/ppermute | solution.py:374
  100.8 5.2 %backward.4 = f32[4,256,256]{2,1,0:T(8,128)S(1)} custom-call(s32[2112]{0:T(1024)S(1)} %copy-done.1, s32[18]{0:T(128)S(1)} %copy-done.6, bf16[128,256,256]{2,1,0:T(8,128)(2,1)} %bitcast.32, bf16[4,256,256]{2,1,0:T(8,128)(2,1)S(1)} %get-tuple-element.18.grad_mine, bf16[4,256,256]{2,1,0:T(8,128)(2,1)S(1)} %collective-permute-done.11.grad_came), custom_call_target="tpu_custom_call" | custom-call | flops 536870912 | bytes 2097152 | tf_op jit(solution)/shard_map/backward/pallas_call | solution.py:389
  106.2 3.0 %collective-permute-start.18 = (bf16[2,256,256]{2,1,0:T(8,128)(2,1)S(1)}, bf16[2,256,256]{2,1,0:T(8,128)(2,1)S(1)}, u32[]{:S(2)}, u32[]{:S(2)}) collective-permute-start(bf16[2,256,256]{2,1,0:T(8,128)(2,1)S(1)} %get-tuple-element.22), channel_id=1, source_target_pairs={{2,0},{4,2},{6,4},{7,6},{5,7},{3,5},{1,3},{0,1},{10,8},{12,10},{14... | collective-permute-start | bytes 786440 | tf_op jit(solution)/shard_map/ppermute | solution.py:416
  109.3 0.7 collective-permute-start.28
  110.0 3.7 %collective-permute-done.28 = f32[72,256]{1,0:T(8,128)S(1)} collective-permute-done((f32[72,256]{1,0:T(8,128)S(1)}, f32[72,256]{1,0:T(8,128)S(1)}, u32[]{:S(2)}, u32[]{:S(2)}) %collective-permute-start.28) | collective-permute-done | bytes 73760 | tf_op jit(solution)/shard_map/ppermute | solution.py:380
  113.8 1.0 backward.3
  114.9 1.3 collective-permute-done.18
  116.3 5.7 %collective-permute-start.15 = (bf16[2,256,256]{2,1,0:T(8,128)(2,1)S(1)}, bf16[2,256,256]{2,1,0:T(8,128)(2,1)S(1)}, u32[]{:S(2)}, u32[]{:S(2)}) collective-permute-start(bf16[2,256,256]{2,1,0:T(8,128)(2,1)S(1)} %get-tuple-element.21), channel_id=1, source_target_pairs={{0,2},{2,4},{4,6},{6,7},{7,5},{5,3},{3,1},{1,0},{8,10},{10,12},{12... | collective-permute-start | bytes 786440 | tf_op jit(solution)/shard_map/ppermute | solution.py:415
  122.0 2.8 %collective-permute-start.19 = (bf16[2,256,256]{2,1,0:T(8,128)(2,1)S(1)}, bf16[2,256,256]{2,1,0:T(8,128)(2,1)S(1)}, u32[]{:S(2)}, u32[]{:S(2)}) collective-permute-start(bf16[2,256,256]{2,1,0:T(8,128)(2,1)S(1)} %get-tuple-element.20), channel_id=1, source_target_pairs={{2,0},{4,2},{6,4},{7,6},{5,7},{3,5},{1,3},{0,1},{10,8},{12,10},{14... | collective-permute-start | bytes 786440 | tf_op jit(solution)/shard_map/ppermute | solution.py:416
  124.8 3.8 %backward_own.1.own = f32[2,256,256]{2,1,0:T(8,128)S(1)} custom-call(s32[2112]{0:T(1024)S(1)} %copy-done.1, s32[18]{0:T(128)S(1)} %copy-done.6, bf16[128,256,256]{2,1,0:T(8,128)(2,1)} %bitcast.34, bf16[4,256,256]{2,1,0:T(8,128)(2,1)S(1)} %get-tuple-element.18.grad_mine, bf16[4,256,256]{2,1,0:T(8,128)(2,1)S(1)} %collective-permute-done.11.grad_came), custom_call_target="tpu_custom_call" | custom-call | flops 536870912 | bytes 2097152 | tf_op jit(solution)/shard_map/backward_own/pallas_call | solution.py:389
  128.6 0.8 copy-done
  129.4 0.7 slice.58
  130.2 0.6 slice.59
  130.7 0.7 copy-done.9
  131.4 0.7 copy-done.10
  132.2 2.0 %finish.1 = bf16[512,256]{1,0:T(8,128)(2,1)} custom-call(f32[2,256,256]{2,1,0:T(8,128)} %copy-done, bf16[2,256,256]{2,1,0:T(8,128)(2,1)} %copy-done.9, bf16[2,256,256]{2,1,0:T(8,128)(2,1)} %copy-done.10), custom_call_target="tpu_custom_call" | custom-call | tf_op jit(solution)/shard_map/finish/pallas_call | solution.py:418
  (63 shorter events, 2.1 us)
Async XLA Ops:
  0.6 9.5 %collective-permute-start = (bf16[2,256,256]{2,1,0:T(8,128)(2,1)}, bf16[2,256,256]{2,1,0:T(8,128)(2,1)S(1)}, u32[]{:S(2)}, u32[]{:S(2)}) collective-permute-start(bf16[2,256,256]{2,1,0:T(8,128)(2,1)} %bitcast.24), channel_id=1, source_target_pairs={{0,2},{2,4},{4,6},{6,7},{7,5},{5,3},{3,1},{1,0},{8,10},{10,12},{12... | collective-permute-start | bytes 786440 | tf_op jit(solution)/shard_map/ppermute | solution.py:313
  3.7 8.3 %collective-permute-start.1 = (bf16[2,256,256]{2,1,0:T(8,128)(2,1)}, bf16[2,256,256]{2,1,0:T(8,128)(2,1)S(1)}, u32[]{:S(2)}, u32[]{:S(2)}) collective-permute-start(bf16[2,256,256]{2,1,0:T(8,128)(2,1)} %bitcast.25), channel_id=1, source_target_pairs={{2,0},{4,2},{6,4},{7,6},{5,7},{3,5},{1,3},{0,1},{10,8},{12,10},{14... | collective-permute-start | bytes 786440 | tf_op jit(solution)/shard_map/ppermute | solution.py:314
  10.1 7.5 %collective-permute-start.2 = (bf16[2,256,256]{2,1,0:T(8,128)(2,1)S(1)}, bf16[2,256,256]{2,1,0:T(8,128)(2,1)S(1)}, u32[]{:S(2)}, u32[]{:S(2)}) collective-permute-start(bf16[2,256,256]{2,1,0:T(8,128)(2,1)S(1)} %collective-permute-done.refs_1_), channel_id=1, source_target_pairs={{0,2},{2,4},{4,6},{6,7},{7,5},{5,3},{3,1},{1,0},{8,10},{10,12},{12... | collective-permute-start | bytes 786440 | tf_op jit(solution)/shard_map/ppermute | solution.py:313
  12.0 7.2 %collective-permute-start.3 = (bf16[2,256,256]{2,1,0:T(8,128)(2,1)S(1)}, bf16[2,256,256]{2,1,0:T(8,128)(2,1)S(1)}, u32[]{:S(2)}, u32[]{:S(2)}) collective-permute-start(bf16[2,256,256]{2,1,0:T(8,128)(2,1)S(1)} %collective-permute-done.1.refs_2_), channel_id=1, source_target_pairs={{2,0},{4,2},{6,4},{7,6},{5,7},{3,5},{1,3},{0,1},{10,8},{12,10},{14... | collective-permute-start | bytes 786440 | tf_op jit(solution)/shard_map/ppermute | solution.py:314
  17.6 8.3 %collective-permute-start.4 = (bf16[2,256,256]{2,1,0:T(8,128)(2,1)S(1)}, bf16[2,256,256]{2,1,0:T(8,128)(2,1)S(1)}, u32[]{:S(2)}, u32[]{:S(2)}) collective-permute-start(bf16[2,256,256]{2,1,0:T(8,128)(2,1)S(1)} %collective-permute-done.2.refs_3_), channel_id=1, source_target_pairs={{0,2},{2,4},{4,6},{6,7},{7,5},{5,3},{3,1},{1,0},{8,10},{10,12},{12... | collective-permute-start | bytes 786440 | tf_op jit(solution)/shard_map/ppermute | solution.py:313
  19.1 8.3 %collective-permute-start.5 = (bf16[2,256,256]{2,1,0:T(8,128)(2,1)S(1)}, bf16[2,256,256]{2,1,0:T(8,128)(2,1)S(1)}, u32[]{:S(2)}, u32[]{:S(2)}) collective-permute-start(bf16[2,256,256]{2,1,0:T(8,128)(2,1)S(1)} %collective-permute-done.3.refs_4_), channel_id=1, source_target_pairs={{2,0},{4,2},{6,4},{7,6},{5,7},{3,5},{1,3},{0,1},{10,8},{12,10},{14... | collective-permute-start | bytes 786440 | tf_op jit(solution)/shard_map/ppermute | solution.py:314
  26.0 10.6 %collective-permute-start.6 = (bf16[1,256,256]{2,1,0:T(8,128)(2,1)S(1)}, bf16[1,256,256]{2,1,0:T(8,128)(2,1)S(1)}, u32[]{:S(2)}, u32[]{:S(2)}) collective-permute-start(bf16[1,256,256]{2,1,0:T(8,128)(2,1)S(1)} %slice.48), channel_id=1, source_target_pairs={{0,2},{2,4},{4,6},{6,7},{7,5},{5,3},{3,1},{1,0},{8,10},{10,12},{12... | collective-permute-start | bytes 393224 | tf_op jit(solution)/shard_map/ppermute | solution.py:316
  27.5 9.1 %collective-permute-start.7 = (bf16[1,256,256]{2,1,0:T(8,128)(2,1)S(1)}, bf16[1,256,256]{2,1,0:T(8,128)(2,1)S(1)}, u32[]{:S(2)}, u32[]{:S(2)}) collective-permute-start(bf16[1,256,256]{2,1,0:T(8,128)(2,1)S(1)} %slice.49), channel_id=1, source_target_pairs={{2,0},{4,2},{6,4},{7,6},{5,7},{3,5},{1,3},{0,1},{10,8},{12,10},{14... | collective-permute-start | bytes 393224 | tf_op jit(solution)/shard_map/ppermute | solution.py:317
  28.7 0.9 copy-start.2
  29.6 0.6 copy-start.5
  30.2 0.7 copy-start.7
  30.9 13.4 %copy-start.3 = (bf16[512,256]{1,0:T(8,128)(2,1)S(1)}, bf16[512,256]{1,0:T(8,128)(2,1)}, u32[]{:S(2)}) copy-start(bf16[512,256]{1,0:T(8,128)(2,1)} %cot_own.1) | copy-start | bytes 786436
  30.9 31.4 %copy-start.4 = (bf16[256,256]{1,0:T(8,128)(2,1)S(1)}, bf16[256,256]{1,0:T(8,128)(2,1)}, u32[]{:S(2)}) copy-start(bf16[256,256]{1,0:T(8,128)(2,1)} %weight.1) | copy-start | bytes 393220
  30.9 31.4 %copy-start.8 = (f32[256]{0:T(256)S(1)}, f32[256]{0:T(256)}, u32[]{:S(2)}) copy-start(f32[256]{0:T(256)} %param.14) | copy-start | bytes 3076
  30.9 34.9 %copy-start.1 = (s32[2112]{0:T(1024)S(1)}, s32[2112]{0:T(1024)}, u32[]{:S(2)}) copy-start(s32[2112]{0:T(1024)} %get-tuple-element.17.bwd) | copy-start | bytes 25348
  30.9 34.9 %copy-start.6 = (s32[18]{0:T(128)S(1)}, s32[18]{0:T(128)}, u32[]{:S(2)}) copy-start(s32[18]{0:T(128)} %get-tuple-element.13.groups) | copy-start | bytes 220
  40.1 2.0 %collective-permute-start.8 = (bf16[4,256,256]{2,1,0:T(8,128)(2,1)S(1)}, bf16[4,256,256]{2,1,0:T(8,128)(2,1)S(1)}, u32[]{:S(2)}, u32[]{:S(2)}) collective-permute-start(bf16[4,256,256]{2,1,0:T(8,128)(2,1)S(1)} %get-tuple-element.15), channel_id=1, source_target_pairs={{0,8},{8,0},{16,24},{24,16},{1,9},{9,1},{17,25},{25,17},{2,10},{10... | collective-permute-start | bytes 1572872 | tf_op jit(solution)/shard_map/ppermute | solution.py:348
  42.2 20.2 %collective-permute-start.9 = (bf16[4,256,256]{2,1,0:T(8,128)(2,1)S(1)}, bf16[4,256,256]{2,1,0:T(8,128)(2,1)S(1)}, u32[]{:S(2)}, u32[]{:S(2)}) collective-permute-start(bf16[4,256,256]{2,1,0:T(8,128)(2,1)S(1)} %add_convert_fusion.own), channel_id=1, source_target_pairs={{0,16},{16,0},{8,24},{24,8},{1,17},{17,1},{9,25},{25,9},{2,18},{18... | collective-permute-start | bytes 1572872 | tf_op jit(solution)/shard_map/ppermute | solution.py:350
  44.3 18.1 %collective-permute-start.10 = (bf16[512,256]{1,0:T(8,128)(2,1)S(1)}, bf16[512,256]{1,0:T(8,128)(2,1)S(1)}, u32[]{:S(2)}, u32[]{:S(2)}) collective-permute-start(bf16[512,256]{1,0:T(8,128)(2,1)S(1)} %copy-done.3), channel_id=1, source_target_pairs={{0,16},{16,0},{8,24},{24,8},{1,17},{17,1},{9,25},{25,9},{2,18},{18... | collective-permute-start | bytes 786440 | tf_op jit(solution)/shard_map/ppermute | solution.py:318
  63.9 1.9 %collective-permute-start.11 = (bf16[4,256,256]{2,1,0:T(8,128)(2,1)S(1)}, bf16[4,256,256]{2,1,0:T(8,128)(2,1)S(1)}, u32[]{:S(2)}, u32[]{:S(2)}) collective-permute-start(bf16[4,256,256]{2,1,0:T(8,128)(2,1)S(1)} %get-tuple-element.18.grad_mine), channel_id=1, source_target_pairs={{0,8},{8,0},{16,24},{24,16},{1,9},{9,1},{17,25},{25,17},{2,10},{10... | collective-permute-start | bytes 1572872 | tf_op jit(solution)/shard_map/ppermute | solution.py:366
  63.9 12.8 %collective-permute-start.20 = (f32[2,72,256]{2,1,0:T(8,128)S(1)}, f32[2,72,256]{2,1,0:T(8,128)S(1)}, u32[]{:S(2)}, u32[]{:S(2)}) collective-permute-start(f32[2,72,256]{2,1,0:T(8,128)S(1)} %get-tuple-element.27), channel_id=1, source_target_pairs={{0,8},{8,0},{16,24},{24,16},{1,9},{9,1},{17,25},{25,17},{2,10},{10... | collective-permute-start | bytes 442376 | tf_op jit(solution)/shard_map/ppermute | solution.py:370
  69.7 11.9 %collective-permute-start.12 = (bf16[1,256,256]{2,1,0:T(8,128)(2,1)S(1)}, bf16[1,256,256]{2,1,0:T(8,128)(2,1)S(1)}, u32[]{:S(2)}, u32[]{:S(2)}) collective-permute-start(bf16[1,256,256]{2,1,0:T(8,128)(2,1)S(1)} %get-tuple-element.29), channel_id=1, source_target_pairs={{0,2},{2,4},{4,6},{6,7},{7,5},{5,3},{3,1},{1,0},{8,10},{10,12},{12... | collective-permute-start | bytes 393224 | tf_op jit(solution)/shard_map/ppermute | solution.py:406
  69.7 11.9 %collective-permute-start.16 = (bf16[1,256,256]{2,1,0:T(8,128)(2,1)S(1)}, bf16[1,256,256]{2,1,0:T(8,128)(2,1)S(1)}, u32[]{:S(2)}, u32[]{:S(2)}) collective-permute-start(bf16[1,256,256]{2,1,0:T(8,128)(2,1)S(1)} %get-tuple-element.28), channel_id=1, source_target_pairs={{2,0},{4,2},{6,4},{7,6},{5,7},{3,5},{1,3},{0,1},{10,8},{12,10},{14... | collective-permute-start | bytes 393224 | tf_op jit(solution)/shard_map/ppermute | solution.py:407
  76.8 11.3 %collective-permute-start.21 = (f32[72,256]{1,0:T(8,128)S(1)}, f32[72,256]{1,0:T(8,128)S(1)}, u32[]{:S(2)}, u32[]{:S(2)}) collective-permute-start(f32[72,256]{1,0:T(8,128)S(1)} %fusion.6), channel_id=1, source_target_pairs={{0,2},{2,4},{4,6},{6,7},{7,5},{5,3},{3,1},{1,0},{8,10},{10,12},{12... | collective-permute-start | bytes 221192 | tf_op jit(solution)/shard_map/ppermute | solution.py:374
  81.7 24.4 %collective-permute-start.13 = (bf16[2,256,256]{2,1,0:T(8,128)(2,1)S(1)}, bf16[2,256,256]{2,1,0:T(8,128)(2,1)S(1)}, u32[]{:S(2)}, u32[]{:S(2)}) collective-permute-start(bf16[2,256,256]{2,1,0:T(8,128)(2,1)S(1)} %get-tuple-element.25), channel_id=1, source_target_pairs={{0,2},{2,4},{4,6},{6,7},{7,5},{5,3},{3,1},{1,0},{8,10},{10,12},{12... | collective-permute-start | bytes 786440 | tf_op jit(solution)/shard_map/ppermute | solution.py:415
  83.7 22.3 %collective-permute-start.17 = (bf16[2,256,256]{2,1,0:T(8,128)(2,1)S(1)}, bf16[2,256,256]{2,1,0:T(8,128)(2,1)S(1)}, u32[]{:S(2)}, u32[]{:S(2)}) collective-permute-start(bf16[2,256,256]{2,1,0:T(8,128)(2,1)S(1)} %get-tuple-element.24), channel_id=1, source_target_pairs={{2,0},{4,2},{6,4},{7,6},{5,7},{3,5},{1,3},{0,1},{10,8},{12,10},{14... | collective-permute-start | bytes 786440 | tf_op jit(solution)/shard_map/ppermute | solution.py:416
  86.1 8.1 %collective-permute-start.22 = (f32[72,256]{1,0:T(8,128)S(1)}, f32[72,256]{1,0:T(8,128)S(1)}, u32[]{:S(2)}, u32[]{:S(2)}) collective-permute-start(f32[72,256]{1,0:T(8,128)S(1)} %fusion.6), channel_id=1, source_target_pairs={{2,0},{4,2},{6,4},{7,6},{5,7},{3,5},{1,3},{0,1},{10,8},{12,10},{14... | collective-permute-start | bytes 221192 | tf_op jit(solution)/shard_map/ppermute | solution.py:377
  88.0 6.1 %collective-permute-start.23 = (f32[72,256]{1,0:T(8,128)S(1)}, f32[72,256]{1,0:T(8,128)S(1)}, u32[]{:S(2)}, u32[]{:S(2)}) collective-permute-start(f32[72,256]{1,0:T(8,128)S(1)} %collective-permute-done.21), channel_id=1, source_target_pairs={{0,2},{2,4},{4,6},{6,7},{7,5},{5,3},{3,1},{1,0},{8,10},{10,12},{12... | collective-permute-start | bytes 221192 | tf_op jit(solution)/shard_map/ppermute | solution.py:374
  94.2 4.6 %collective-permute-start.24 = (f32[72,256]{1,0:T(8,128)S(1)}, f32[72,256]{1,0:T(8,128)S(1)}, u32[]{:S(2)}, u32[]{:S(2)}) collective-permute-start(f32[72,256]{1,0:T(8,128)S(1)} %collective-permute-done.22), channel_id=1, source_target_pairs={{2,0},{4,2},{6,4},{7,6},{5,7},{3,5},{1,3},{0,1},{10,8},{12,10},{14... | collective-permute-start | bytes 221192 | tf_op jit(solution)/shard_map/ppermute | solution.py:377
  94.2 4.6 %collective-permute-start.25 = (f32[72,256]{1,0:T(8,128)S(1)}, f32[72,256]{1,0:T(8,128)S(1)}, u32[]{:S(2)}, u32[]{:S(2)}) collective-permute-start(f32[72,256]{1,0:T(8,128)S(1)} %collective-permute-done.23), channel_id=1, source_target_pairs={{0,2},{2,4},{4,6},{6,7},{7,5},{5,3},{3,1},{1,0},{8,10},{10,12},{12... | collective-permute-start | bytes 221192 | tf_op jit(solution)/shard_map/ppermute | solution.py:374
  98.7 10.5 %collective-permute-start.26 = (f32[72,256]{1,0:T(8,128)S(1)}, f32[72,256]{1,0:T(8,128)S(1)}, u32[]{:S(2)}, u32[]{:S(2)}) collective-permute-start(f32[72,256]{1,0:T(8,128)S(1)} %collective-permute-done.24), channel_id=1, source_target_pairs={{2,0},{4,2},{6,4},{7,6},{5,7},{3,5},{1,3},{0,1},{10,8},{12,10},{14... | collective-permute-start | bytes 221192 | tf_op jit(solution)/shard_map/ppermute | solution.py:377
  98.8 10.4 %collective-permute-start.27 = (f32[72,256]{1,0:T(8,128)S(1)}, f32[72,256]{1,0:T(8,128)S(1)}, u32[]{:S(2)}, u32[]{:S(2)}) collective-permute-start(f32[72,256]{1,0:T(8,128)S(1)} %collective-permute-done.25), channel_id=1, source_target_pairs={{0,2},{2,4},{4,6},{6,7},{7,5},{5,3},{3,1},{1,0},{8,10},{10,12},{12... | collective-permute-start | bytes 221192 | tf_op jit(solution)/shard_map/ppermute | solution.py:374
  106.2 8.7 %collective-permute-start.14 = (bf16[2,256,256]{2,1,0:T(8,128)(2,1)S(1)}, bf16[2,256,256]{2,1,0:T(8,128)(2,1)S(1)}, u32[]{:S(2)}, u32[]{:S(2)}) collective-permute-start(bf16[2,256,256]{2,1,0:T(8,128)(2,1)S(1)} %get-tuple-element.23), channel_id=1, source_target_pairs={{0,2},{2,4},{4,6},{6,7},{7,5},{5,3},{3,1},{1,0},{8,10},{10,12},{12... | collective-permute-start | bytes 786440 | tf_op jit(solution)/shard_map/ppermute | solution.py:415
  106.2 9.9 %collective-permute-start.18 = (bf16[2,256,256]{2,1,0:T(8,128)(2,1)S(1)}, bf16[2,256,256]{2,1,0:T(8,128)(2,1)S(1)}, u32[]{:S(2)}, u32[]{:S(2)}) collective-permute-start(bf16[2,256,256]{2,1,0:T(8,128)(2,1)S(1)} %get-tuple-element.22), channel_id=1, source_target_pairs={{2,0},{4,2},{6,4},{7,6},{5,7},{3,5},{1,3},{0,1},{10,8},{12,10},{14... | collective-permute-start | bytes 786440 | tf_op jit(solution)/shard_map/ppermute | solution.py:416
  109.3 4.4 %collective-permute-start.28 = (f32[72,256]{1,0:T(8,128)S(1)}, f32[72,256]{1,0:T(8,128)S(1)}, u32[]{:S(2)}, u32[]{:S(2)}) collective-permute-start(f32[72,256]{1,0:T(8,128)S(1)} %add_multiply_fusion), channel_id=1, source_target_pairs={{0,16},{16,0},{8,24},{24,8},{1,17},{17,1},{9,25},{25,9},{2,18},{18... | collective-permute-start | bytes 221192 | tf_op jit(solution)/shard_map/ppermute | solution.py:380
  113.7 15.7 %collective-permute-start.29 = (f32[2,72,256]{2,1,0:T(8,128)S(1)}, f32[2,72,256]{2,1,0:T(8,128)S(1)}, u32[]{:S(2)}, u32[]{:S(2)}) collective-permute-start(f32[2,72,256]{2,1,0:T(8,128)S(1)} %maximum_select_fusion.2), channel_id=1, source_target_pairs={{0,8},{8,0},{16,24},{24,16},{1,9},{9,1},{17,25},{25,17},{2,10},{10... | collective-permute-start | bytes 442376 | tf_op jit(solution)/shard_map/ppermute | solution.py:382
  116.3 14.5 %collective-permute-start.15 = (bf16[2,256,256]{2,1,0:T(8,128)(2,1)S(1)}, bf16[2,256,256]{2,1,0:T(8,128)(2,1)S(1)}, u32[]{:S(2)}, u32[]{:S(2)}) collective-permute-start(bf16[2,256,256]{2,1,0:T(8,128)(2,1)S(1)} %get-tuple-element.21), channel_id=1, source_target_pairs={{0,2},{2,4},{4,6},{6,7},{7,5},{5,3},{3,1},{1,0},{8,10},{10,12},{12... | collective-permute-start | bytes 786440 | tf_op jit(solution)/shard_map/ppermute | solution.py:415
  122.0 8.8 %collective-permute-start.19 = (bf16[2,256,256]{2,1,0:T(8,128)(2,1)S(1)}, bf16[2,256,256]{2,1,0:T(8,128)(2,1)S(1)}, u32[]{:S(2)}, u32[]{:S(2)}) collective-permute-start(bf16[2,256,256]{2,1,0:T(8,128)(2,1)S(1)} %get-tuple-element.20), channel_id=1, source_target_pairs={{2,0},{4,2},{6,4},{7,6},{5,7},{3,5},{1,3},{0,1},{10,8},{12,10},{14... | collective-permute-start | bytes 786440 | tf_op jit(solution)/shard_map/ppermute | solution.py:416
  128.6 0.8 copy-start
  130.7 0.7 copy-start.9
  131.4 0.7 copy-start.10

commit v2 on v1

v2 whole, which is shorter than its diff:
```python
import functools
import math

import jax
import jax.numpy as jnp
import numpy as np
from jax import lax
from jax.experimental import pallas as pl
from jax.experimental.pallas import tpu as pltpu
from jax.sharding import PartitionSpec as P

BF16 = jnp.bfloat16
F32 = jnp.float32
GROUP = 4
FWD_GROUPS = (4, 4, 2)
DEPTH = 8

VMEM = pl.BlockSpec(memory_space=pltpu.VMEM)
SMEM = pl.BlockSpec(memory_space=pltpu.SMEM)
HBM = pl.BlockSpec(memory_space=pl.ANY)


def ring_order(count):
    return list(range(0, count, 2)) + list(range(count - 1, 0, -2))


def params(mib):
    return pltpu.CompilerParams(vmem_limit_bytes=mib * 2**20)


def cost(flops, nbytes):
    return pl.CostEstimate(flops=int(flops), bytes_accessed=int(nbytes), transcendentals=0)


def round_up(n, step):
    return (n + step - 1) // step * step


def lists_kernel(slots, cuts, cols, counts, place, pos_of, fwd, bwd, groups):
    row_tiles = pos_of.shape[0]
    col_tiles = place.shape[0]
    passes = len(cuts) - 1
    cap_f = fwd.shape[0] // passes
    cap_b = bwd.shape[0] // col_tiles

    def clear(k, _):
        groups[passes + k] = 0
        return 0

    lax.fori_loop(0, col_tiles, clear, 0)

    def tile_row(t, filled):
        pos = pos_of[t]

        def slot(s, filled):
            k = place[cols[t * slots + s]]
            head = (t * slots + s) * 65536 + pos * 256
            at = filled[0]
            first = 0
            for p in range(1, passes):
                at = jnp.where(k >= cuts[p], p * cap_f + filled[p], at)
                first = jnp.where(k >= cuts[p], cuts[p], first)
            fwd[at] = head + k - first
            count = groups[passes + k]
            bwd[k * cap_b + count] = head
            groups[passes + k] = count + 1
            return tuple(
                n + ((k >= cuts[p]) & (k < cuts[p + 1])).astype(jnp.int32) for p, n in enumerate(filled)
            )

        filled = lax.fori_loop(0, counts[t], slot, filled)
        head = t * slots * 65536 + pos * 256
        tops = []
        for p, n in enumerate(filled):
            top = round_up(n, FWD_GROUPS[p])

            def fill(i, _, p=p):
                fwd[p * cap_f + i] = head + cuts[p + 1] - cuts[p]
                return 0

            lax.fori_loop(n, top, fill, 0)
            tops.append(top)
        return tuple(tops)

    filled = lax.fori_loop(0, row_tiles, tile_row, (0,) * passes)
    for p in range(passes):
        groups[p] = filled[p] // FWD_GROUPS[p]

    def fill_bwd(k, _):
        count = groups[passes + k]
        top = round_up(count, GROUP)

        def fill(i, _):
            bwd[k * cap_b + i] = row_tiles * 256
            return 0

        lax.fori_loop(count, top, fill, 0)
        groups[passes + k] = top // GROUP
        return 0

    lax.fori_loop(0, col_tiles, fill_bwd, 0)


def make_lists(tile_cols, tile_counts, place, pos_of, cuts):
    row_tiles, slots = tile_cols.shape
    col_tiles = place.shape[0]
    passes = len(cuts) - 1
    cap_f = row_tiles * (slots + GROUP)
    cap_b = row_tiles * slots + GROUP
    i32 = lambda n: jax.ShapeDtypeStruct((n,), jnp.int32)
    return pl.pallas_call(
        functools.partial(lists_kernel, slots, cuts),
        in_specs=[SMEM] * 4,
        out_specs=[SMEM] * 3,
        out_shape=[i32(passes * cap_f), i32(col_tiles * cap_b), i32(passes + col_tiles)],
        compiler_params=params(8),
        cost_estimate=cost(0, 2**22),
        name="lists",
    )(tile_cols.reshape(-1), tile_counts.reshape(-1), place, pos_of)


def stream(list_ref, segments, size, values, buffer, sems, between, use):
    depth = buffer.shape[0] // size
    ends = []
    for _, n in segments:
        ends.append(n + (ends[-1] if ends else 0))
    total = ends[-1]

    def locate(g):
        segment, first = 0, segments[0][0] + g * size
        for i in range(1, len(segments)):
            past = g >= ends[i - 1]
            segment = jnp.where(past, i, segment)
            first = jnp.where(past, segments[i][0] + (g - ends[i - 1]) * size, first)
        return segment, first

    def copies(g):
        _, first = locate(g)
        at = lax.rem(g, depth) * size
        for u in range(size):
            yield pltpu.make_async_copy(values.at[list_ref[first + u] // 65536], buffer.at[at + u], sems.at[at + u])

    def ahead(g, _):
        for c in copies(g):
            c.start()
        return 0

    lax.fori_loop(0, jnp.minimum(total, depth - 1), ahead, 0)
    between()

    def step(g, _):
        @pl.when(g + depth - 1 < total)
        def _():
            ahead(g + depth - 1, 0)

        for c in copies(g):
            c.wait()
        segment, first = locate(g)
        use(segment, first, lax.rem(g, depth) * size)
        return 0

    lax.fori_loop(0, total, step, 0)


def forward_kernel(p, cap_f, n_blocks, n_before, last, fwd, groups, values, *refs):
    blocks, refs = refs[:n_blocks], refs[n_blocks:]
    before, refs = refs[:n_before], refs[n_before:]
    outs, (total, source, buffer, sems, block_sems) = refs[:-5], refs[-5:]
    size = FWD_GROUPS[p]
    copies = []
    at = 0
    for i, b in enumerate(blocks):
        copies.append(pltpu.make_async_copy(b, source.at[pl.ds(at, b.shape[0])], block_sems.at[i]))
        at += b.shape[0]

    def between():
        for c in copies:
            c.start()
        source[at] = jnp.zeros(source.shape[1:], BF16)
        total[...] = jnp.zeros(total.shape, F32)
        for c in copies:
            c.wait()

    def use(segment, first, at):
        pos = lax.rem(fwd[first] // 256, 256)
        added = None
        for u in range(size):
            k = lax.rem(fwd[first + u], 256)
            part = jnp.dot(buffer[at + u], source[k], preferred_element_type=F32)
            added = part if added is None else added + part
        total[pos] += added

    stream(fwd, [(p * cap_f, groups[p])], size, values, buffer, sems, between, use)
    row_tiles = total.shape[0]
    for i in range(row_tiles):
        done = total[i]
        for b in before:
            done = done + b[i]
        if last:
            mine, other = outs
            if i < row_tiles // 2:
                mine[i] = done.astype(BF16)
            else:
                other[i - row_tiles // 2] = done.astype(BF16)
        else:
            outs[0][i] = done


def dense_kernel(own, came, weight, bias, cot_own, cot_other, out, grad_t, wgrad):
    tile = grad_t.shape[1]
    half = out.shape[0]
    tiles_half = half // tile
    w = weight[...]
    b = bias[...]
    wg = None
    bg = None
    for h in range(2):
        near = own[h * tiles_half : (h + 1) * tiles_half].reshape(half, -1).astype(F32)
        away = came[(1 - h) * tiles_half : (2 - h) * tiles_half].reshape(half, -1).astype(F32)
        hidden = (near + away).astype(BF16)
        preact = jnp.dot(hidden, w, preferred_element_type=F32) + b
        sig = 1.0 / (1.0 + jnp.exp(-preact))
        cot = (cot_own if h == 0 else cot_other)[...].astype(F32)
        if h == 0:
            out[...] = (preact * sig).astype(BF16)
        pgrad = (cot * (sig * (1.0 + preact * (1.0 - sig)))).astype(BF16)
        for i in range(tiles_half):
            rows = pgrad[i * tile : (i + 1) * tile]
            grad_t[h * tiles_half + i] = lax.dot_general(
                w, rows, (((1,), (1,)), ((), ())), preferred_element_type=F32
            ).astype(BF16)
        part = lax.dot_general(hidden, pgrad, (((0,), (0,)), ((), ())), preferred_element_type=F32)
        bias_part = jnp.sum(pgrad.astype(F32), axis=0, keepdims=True)
        wg = part if wg is None else wg + part
        bg = bias_part if bg is None else bg + bias_part
    rows = wg.shape[0] // 2
    for q in range(2):
        wgrad[q, :rows] = wg[q * rows : (q + 1) * rows]
        wgrad[q, rows:] = jnp.broadcast_to(bg, (wgrad.shape[1] - rows, bg.shape[1]))


def backward_kernel(ks, passes, cap_b, bwd, groups, values, grad_mine, grad_came, out, grads, buffer, sems, block_sems):
    half = grad_mine.shape[0]
    copies = [
        pltpu.make_async_copy(grad_mine, grads.at[pl.ds(0, half)], block_sems.at[0]),
        pltpu.make_async_copy(grad_came, grads.at[pl.ds(half, half)], block_sems.at[1]),
    ]

    def between():
        for c in copies:
            c.start()
        grads[2 * half] = jnp.zeros(grads.shape[1:], BF16)
        out[...] = jnp.zeros(out.shape, F32)
        for c in copies:
            c.wait()

    def use(segment, first, at):
        added = None
        for u in range(GROUP):
            pos = lax.rem(bwd[first + u] // 256, 256)
            part = jnp.dot(grads[pos], buffer[at + u], preferred_element_type=F32)
            added = part if added is None else added + part
        out[segment] += added

    segments = [(k * cap_b, groups[passes + k]) for k in ks]
    stream(bwd, segments, GROUP, values, buffer, sems, between, use)


def finish_kernel(own, right, left, out):
    tiles, _, tile = own.shape
    for i in range(tiles):
        rows = pl.ds(i * tile, tile)
        total = own[i] + right[rows, :].astype(F32) + left[rows, :].astype(F32)
        out[rows, :] = total.T.astype(BF16)


def per_device(n_col, features, tile_values, tile_cols, tile_counts, weight, bias, cotangent):
    node_dev, width = features.shape
    row_tiles, slots, tile, _ = tile_values.shape
    per_dev = node_dev // tile
    col_tiles = n_col * per_dev
    half = n_col // 2
    far = col_tiles - per_dev
    node_total = node_dev * lax.axis_size("row") * n_col
    grad_scale = 1.0 / math.sqrt(node_total)
    values = tile_values.reshape(row_tiles * slots, tile, tile)

    order = ring_order(n_col)
    right = [(order[i], order[(i + 1) % n_col]) for i in range(n_col)]
    left = [(b, a) for a, b in right]
    cores = [(0, 1), (1, 0), (2, 3), (3, 2)]
    across = [(0, 2), (2, 0), (1, 3), (3, 1)]
    row = lax.axis_index("row")
    col = lax.axis_index("col")
    my_y, my_core = row // 2, row % 2

    rank = np.zeros(n_col, np.int32)
    rank[order] = np.arange(n_col)
    steps = np.arange(n_col)
    arrival_of_step = np.where(steps == 0, 0, np.where(steps < half, 2 * steps, np.where(steps == half, n_col - 1, 2 * (n_col - steps) - 1)))
    table = np.zeros((n_col, col_tiles), np.int32)
    for d in range(n_col):
        for t in range(col_tiles):
            ahead = (rank[t // per_dev] - rank[d]) % n_col
            table[d, t] = arrival_of_step[ahead] * per_dev + t % per_dev
    place = lax.dynamic_index_in_dim(jnp.asarray(table), col, 0, keepdims=False)
    tiles = np.arange(row_tiles)
    tiles_r = row_tiles // 4
    pos_table = np.zeros((4, row_tiles), np.int32)
    for r in range(4):
        block = tiles // tiles_r
        pos_table[r] = ((block % 2 != r % 2) * 2 + (block // 2 != r // 2)) * tiles_r + tiles % tiles_r
    pos_of = lax.dynamic_index_in_dim(jnp.asarray(pos_table), row, 0, keepdims=False)

    cuts = (0, far - 2 * per_dev, far, col_tiles)
    passes = len(cuts) - 1
    fwd, bwd, groups = make_lists(tile_cols, tile_counts, place, pos_of, cuts)
    cap_f = fwd.shape[0] // passes
    cap_b = bwd.shape[0] // col_tiles

    stream_scratch = [pltpu.VMEM((DEPTH * GROUP, tile, tile), BF16), pltpu.SemaphoreType.DMA((DEPTH * GROUP,))]
    dots = 2 * tile * tile * width
    total_shape = jax.ShapeDtypeStruct((row_tiles, tile, width), F32)
    half_shape = jax.ShapeDtypeStruct((row_tiles // 2, tile, width), BF16)

    def forward(p, blocks, before, last=False):
        n_tiles = sum(b.shape[0] for b in blocks)
        return pl.pallas_call(
            functools.partial(forward_kernel, p, cap_f, len(blocks), len(before), last),
            in_specs=[SMEM, SMEM, HBM] + [HBM] * len(blocks) + [VMEM] * len(before),
            out_specs=[VMEM] * (2 if last else 1),
            out_shape=[half_shape] * 2 if last else [total_shape],
            scratch_shapes=[pltpu.VMEM(total_shape.shape, F32), pltpu.VMEM((n_tiles + 1, tile, width), BF16)]
            + stream_scratch
            + [pltpu.SemaphoreType.DMA((len(blocks),))],
            compiler_params=params(40),
            cost_estimate=cost(4 * n_tiles * dots, 4 * n_tiles * tile * tile * 2),
            name=f"forward_{p}",
        )(fwd, groups, values, *blocks, *before)

    mine = features.reshape(per_dev, tile, width)
    arrived = [mine]
    from_left = from_right = mine
    cot_other = None
    for s in range(1, half):
        from_left = lax.ppermute(from_left, "col", right)
        from_right = lax.ppermute(from_right, "col", left)
        if s == 1:
            cot_other = lax.ppermute(cotangent, "row", across)
            from_left, from_right, cot_other, fwd, bwd, groups = lax.optimization_barrier(
                (from_left, from_right, cot_other, fwd, bwd, groups)
            )
        if s == half - 1:
            (total,) = forward(0, arrived, [])
            from_left, from_right, total = lax.optimization_barrier((from_left, from_right, total))
        arrived += [from_left, from_right]
    far_near = lax.ppermute(from_left[: per_dev // 2], "col", right)
    far_away = lax.ppermute(from_right[per_dev // 2 :], "col", left)
    (total,) = forward(1, arrived[-2:], [total])
    hid_mine, hid_other = forward(2, [far_near, far_away], [total], last=True)

    hid_came = lax.ppermute(hid_other, "row", cores)
    own = (hid_mine.astype(F32) + hid_came.astype(F32)).astype(BF16)
    came = lax.ppermute(own, "row", across)

    w_rows = width // 2 + 16
    layer_out, grad_mine, wgrad = pl.pallas_call(
        dense_kernel,
        in_specs=[VMEM] * 6,
        out_specs=[VMEM] * 3,
        out_shape=[
            jax.ShapeDtypeStruct((node_dev, width), BF16),
            jax.ShapeDtypeStruct((row_tiles // 2, width, tile), BF16),
            jax.ShapeDtypeStruct((2, w_rows, width), F32),
        ],
        compiler_params=params(40),
        cost_estimate=cost(3 * 2 * 2 * node_dev * width * width, 8 * node_dev * width),
        name="dense",
    )(own, came, weight, bias.reshape(1, -1), cotangent, cot_other)
    grad_came = lax.ppermute(grad_mine, "row", cores)

    w_came = lax.ppermute(lax.dynamic_index_in_dim(wgrad, 1 - my_core, 0, keepdims=False), "row", cores)
    w_own = (lax.dynamic_index_in_dim(wgrad, my_core, 0, keepdims=False) + w_came).astype(BF16)
    wsum = w_own.astype(F32)

    def backward(ks, name):
        return pl.pallas_call(
            functools.partial(backward_kernel, ks, passes, cap_b),
            in_specs=[SMEM, SMEM, HBM, HBM, HBM],
            out_specs=VMEM,
            out_shape=jax.ShapeDtypeStruct((len(ks), width, tile), F32),
            scratch_shapes=[pltpu.VMEM((row_tiles + 1, width, tile), BF16)]
            + stream_scratch
            + [pltpu.SemaphoreType.DMA((2,))],
            compiler_params=params(40),
            cost_estimate=cost(16 * dots, 16 * tile * tile * 2),
            name=name,
        )(bwd, groups, values, grad_mine, grad_came)

    def block(arrival):
        return [arrival * per_dev + i for i in range(per_dev)]

    far_part = backward(block(n_col - 1), "backward_far").astype(BF16).reshape(node_dev, width)
    cut = per_dev // 2 * tile
    rest = node_dev - cut
    to_right = lax.ppermute(jnp.concatenate([far_part[:cut], w_own]), "col", right)
    to_left = lax.ppermute(jnp.concatenate([far_part[cut:], w_own]), "col", left)
    for d in range(half - 1, 0, -1):
        both = backward(block(2 * d) + block(2 * d - 1), "backward").reshape(2, node_dev, width)
        for_right, for_left = both[0], both[1]
        w_right, w_left = to_right[-w_rows:], to_left[-w_rows:]
        wsum = wsum + w_right.astype(F32) + w_left.astype(F32)
        if d == half - 1:
            add_right = (for_right[:cut] + to_right[:cut].astype(F32)).astype(BF16)
            to_right = jnp.concatenate([add_right, for_right[cut:].astype(BF16), w_right])
            add_left = (for_left[cut:] + to_left[:rest].astype(F32)).astype(BF16)
            to_left = jnp.concatenate([for_left[:cut].astype(BF16), add_left, w_left])
        else:
            add_right = (for_right + to_right[:node_dev].astype(F32)).astype(BF16)
            to_right = lax.dynamic_update_slice(to_right, add_right, (0, 0))
            add_left = (for_left + to_left[:node_dev].astype(F32)).astype(BF16)
            to_left = lax.dynamic_update_slice(to_left, add_left, (0, 0)) if d > 1 else add_left
        to_right = lax.ppermute(to_right, "col", right)
        to_left = lax.ppermute(to_left, "col", left)
    own_part = backward(block(0), "backward_own")
    wsum = (wsum + to_right[-w_rows:].astype(F32)) * grad_scale
    w_half = wsum[: width // 2]
    w_other = lax.ppermute(w_half, "row", cores)
    weight_grad = jnp.where(
        my_core == 0, jnp.concatenate([w_half, w_other]), jnp.concatenate([w_other, w_half])
    )
    bias_grad = wsum[width // 2]
    feature_grad = pl.pallas_call(
        finish_kernel,
        in_specs=[VMEM] * 3,
        out_specs=VMEM,
        out_shape=jax.ShapeDtypeStruct((node_dev, width), BF16),
        compiler_params=params(8),
        name="finish",
    )(own_part, to_right, to_left)
    return (layer_out, feature_grad, weight_grad, bias_grad)


def solution(mesh):
    placed = (
        P(("row", "col"), None),
        P("col", "row", None, None),
        P("col", "row"),
        P("col", "row"),
        P(),
        P(),
        P(("col", "row"), None),
    )
    return jax.shard_map(
        functools.partial(per_device, mesh.shape["col"]),
        mesh=mesh,
        in_specs=placed,
        out_specs=(P(("col", "row"), None), P(("row", "col"), None), P(), P()),
        check_vma=False,
    )
```

time: 134 us -> 111 us (0.83)
  starting transfers between devices: 43.8 us -> 24.9 us
  local copies, waits for them, and re-layouts: 9.47 us -> 4.66 us
  waiting for transfers between devices: 46.3 us -> 44.4 us
    ppermute x17 -> x9, starting transfers between devices: 31.2 us -> 11.5 us  [the longest x3 4.78 us: per_device(): to_right = lax.ppermute(to_right, 'col', right)]
    ppermute x1, waiting for transfers between devices: 18 us -> 0.01 us  [per_device(): cot_other = lax.ppermute(cotangent, 'row', across)]
    ppermute x1, waiting for transfers between devices: 0.01 us -> 13.6 us  [per_device(): came = lax.ppermute(own, 'row', across)]
    ppermute x17 -> x9, waiting for transfers between devices: 13.2 us -> 21.2 us  [the longest x3 20.7 us: per_device(): to_right = lax.ppermute(to_right, 'col', right)]
    ppermute x3, waiting for transfers between devices: 11.9 us -> 6.15 us  [per_device(): from_left = lax.ppermute(from_left, 'col', right)]
    unnamed x22 -> x13, local copies, waits for them, and re-layouts: 4.48 us -> 1.69 us
    pallas_call x8 -> x9, Pallas kernels: 29.4 us -> 31.9 us  [the longest x5 16.5 us: backward(): pl.pallas_call(functools.partial(backward_kernel, ks, passes, cap_b), in_...]
    ppermute x1, starting transfers between devices: 0.09 us -> 1.97 us  [per_device(): cot_other = lax.ppermute(cotangent, 'row', across)]
  transfers between devices with their start and end apart: 30 -> 22, of which waited for: 10 -> 9; matrix products, arithmetic and copies ran while one was open for 4% -> 3% of each run, Pallas kernels for 19% -> 25%
where the time goes in v2:
time: 111 us
  waiting for transfers between devices  44.4 us (40%)
  Pallas kernels  34.2 us (31%)
  starting transfers between devices  24.9 us (22%)
  local copies, waits for them, and re-layouts  4.66 us (4%)
  other arithmetic  1.45 us (1%)
    ppermute x3, waiting for transfers between devices, per_device(): to_right = lax.ppermute(to_right, 'col', right)  20.7 us
    pallas_call x5, Pallas kernels, backward(): pl.pallas_call(functools.partial(backward_kernel, ks, passes, cap_b), in_...  16.5 us
    ppermute x1, waiting for transfers between devices, per_device(): came = lax.ppermute(own, 'row', across)  13.6 us
    pallas_call x3, Pallas kernels, forward(): pl.pallas_call(functools.partial(forward_kernel, p, cap_f, len(blocks), l...  12.2 us
    ppermute x3, waiting for transfers between devices, per_device(): from_left = lax.ppermute(from_left, 'col', right)  6.15 us
    ppermute x3, starting transfers between devices, per_device(): from_left = lax.ppermute(from_left, 'col', right)  5.29 us
    ppermute x3, starting transfers between devices, per_device(): to_right = lax.ppermute(to_right, 'col', right)  4.78 us
    pallas_call x1, Pallas kernels, make_lists(): pl.pallas_call(functools.partial(lists_kernel, slots, cuts), in_specs=[SM...  3.17 us
  transfers between devices with their start and end apart: 22, of which 9 were waited for; matrix products, arithmetic and copies ran while one was open for 3% of the time, Pallas kernels for 25%

profile of v2, /device:TPU:0, one launch (start us, length us, event | category | flops | bytes accessed | tf_op | source)
XLA Modules:
  0.0 110.6 jit_solution(8734000787293442851)
XLA Ops:
  0.6 3.1 %collective-permute-start = (bf16[2,256,256]{2,1,0:T(8,128)(2,1)}, bf16[2,256,256]{2,1,0:T(8,128)(2,1)S(1)}, u32[]{:S(2)}, u32[]{:S(2)}) collective-permute-start(bf16[2,256,256]{2,1,0:T(8,128)(2,1)} %bitcast.51), channel_id=1, source_target_pairs={{0,2},{2,4},{4,6},{6,7},{7,5},{5,3},{3,1},{1,0},{8,10},{10,12},{12... | collective-permute-start | bytes 786440 | tf_op jit(solution)/shard_map/ppermute | solution.py:346
  3.7 2.0 %collective-permute-start.2 = (bf16[512,256]{1,0:T(8,128)(2,1)}, bf16[512,256]{1,0:T(8,128)(2,1)S(1)}, u32[]{:S(2)}, u32[]{:S(2)}) collective-permute-start(bf16[512,256]{1,0:T(8,128)(2,1)} %cot_own.1), channel_id=1, source_target_pairs={{0,16},{16,0},{8,24},{24,8},{1,17},{17,1},{9,25},{25,9},{2,18},{18... | collective-permute-start | bytes 786440 | tf_op jit(solution)/shard_map/ppermute | solution.py:349
  5.7 0.8 reshape.48.cols
  6.4 0.7 fusion.9.place
  7.1 0.7 fusion.10.pos_of
  7.8 0.7 copy-done.4
  8.5 3.2 %lists.1 = (s32[480]{0:T(512)S(1)}, s32[2112]{0:T(1024)S(1)}, s32[19]{0:T(128)S(1)}) custom-call(s32[128]{0:T(128)S(1)} %reshape.48.cols, s32[8]{0:T(128)S(1)} %bitcast.55, s32[16]{0:T(128)S(1)} %fusion.9.place, s32[8]{0:T(128)S(1)} %fusion.10.pos_of), custom_call_target="tpu_custom_call" | custom-call | bytes 4194304 | tf_op jit(solution)/shard_map/lists/pallas_call | solution.py:111
  11.7 1.7 %collective-permute-start.3 = (bf16[2,256,256]{2,1,0:T(8,128)(2,1)S(1)}, bf16[2,256,256]{2,1,0:T(8,128)(2,1)S(1)}, u32[]{:S(2)}, u32[]{:S(2)}) collective-permute-start(bf16[2,256,256]{2,1,0:T(8,128)(2,1)S(1)} %collective-permute-done.refs_1_), channel_id=1, source_target_pairs={{0,2},{2,4},{4,6},{6,7},{7,5},{5,3},{3,1},{1,0},{8,10},{10,12},{12... | collective-permute-start | bytes 786440 | tf_op jit(solution)/shard_map/ppermute | solution.py:346
  13.4 0.3 collective-permute-start.5
  13.8 6.1 %collective-permute-done.3.refs_3_ = bf16[2,256,256]{2,1,0:T(8,128)(2,1)S(1)} collective-permute-done((bf16[2,256,256]{2,1,0:T(8,128)(2,1)S(1)}, bf16[2,256,256]{2,1,0:T(8,128)(2,1)S(1)}, u32[]{:S(2)}, u32[]{:S(2)}) %collective-permute-start.3) | collective-permute-done | bytes 262176 | tf_op jit(solution)/shard_map/ppermute | solution.py:346
  19.9 0.5 collective-permute-start.4
  20.4 1.6 %collective-permute-start.6 = (bf16[2,256,256]{2,1,0:T(8,128)(2,1)S(1)}, bf16[2,256,256]{2,1,0:T(8,128)(2,1)S(1)}, u32[]{:S(2)}, u32[]{:S(2)}) collective-permute-start(bf16[2,256,256]{2,1,0:T(8,128)(2,1)S(1)} %collective-permute-done.5.refs_4_), channel_id=1, source_target_pairs={{2,0},{4,2},{6,4},{7,6},{5,7},{3,5},{1,3},{0,1},{10,8},{12,10},{14... | collective-permute-start | bytes 786440 | tf_op jit(solution)/shard_map/ppermute | solution.py:347
  21.9 0.9 copy-done
  22.9 4.5 %forward_0.1.refs_2_ = f32[8,256,256]{2,1,0:T(8,128)S(1)} custom-call(s32[480]{0:T(512)S(1)} %get-tuple-element.24.fwd, s32[19]{0:T(128)S(1)} %get-tuple-element.25.groups, bf16[128,256,256]{2,1,0:T(8,128)(2,1)} %bitcast.56, bf16[2,256,256]{2,1,0:T(8,128)(2,1)S(1)} %bitcast.53, bf16[2,256,256]{2,1,0:T(8,128)(2,1)S(1)} %collective-permute-done.refs_1_, ...), custom_call_target="tpu_custom_call" | custom-call | flops 1342177280 | bytes 5242880 | tf_op jit(solution)/shard_map/forward_0/pallas_call | solution.py:328
  27.5 1.2 %collective-permute-start.7 = (bf16[1,256,256]{2,1,0:T(8,128)(2,1)S(1)}, bf16[1,256,256]{2,1,0:T(8,128)(2,1)S(1)}, u32[]{:S(2)}, u32[]{:S(2)}) collective-permute-start(bf16[1,256,256]{2,1,0:T(8,128)(2,1)S(1)} %slice.109), channel_id=1, source_target_pairs={{0,2},{2,4},{4,6},{6,7},{7,5},{5,3},{3,1},{1,0},{8,10},{10,12},{12... | collective-permute-start | bytes 393224 | tf_op jit(solution)/shard_map/ppermute | solution.py:357
  28.7 1.9 %collective-permute-start.8 = (bf16[1,256,256]{2,1,0:T(8,128)(2,1)S(1)}, bf16[1,256,256]{2,1,0:T(8,128)(2,1)S(1)}, u32[]{:S(2)}, u32[]{:S(2)}) collective-permute-start(bf16[1,256,256]{2,1,0:T(8,128)(2,1)S(1)} %slice.110), channel_id=1, source_target_pairs={{2,0},{4,2},{6,4},{7,6},{5,7},{3,5},{1,3},{0,1},{10,8},{12,10},{14... | collective-permute-start | bytes 393224 | tf_op jit(solution)/shard_map/ppermute | solution.py:358
  30.6 4.9 %forward_1.1.refs_2_ = f32[8,256,256]{2,1,0:T(8,128)S(1)} custom-call(s32[480]{0:T(512)S(1)} %get-tuple-element.24.fwd, s32[19]{0:T(128)S(1)} %get-tuple-element.25.groups, bf16[128,256,256]{2,1,0:T(8,128)(2,1)} %bitcast.57, bf16[2,256,256]{2,1,0:T(8,128)(2,1)S(1)} %collective-permute-done.4.refs_0_, ...), custom_call_target="tpu_custom_call" | custom-call | flops 536870912 | bytes 2097152 | tf_op jit(solution)/shard_map/forward_1/pallas_call | solution.py:328
  35.6 2.7 %forward_2.1 = (bf16[4,256,256]{2,1,0:T(8,128)(2,1)S(1)}, bf16[4,256,256]{2,1,0:T(8,128)(2,1)S(1)}) custom-call(s32[480]{0:T(512)S(1)} %get-tuple-element.24.fwd, s32[19]{0:T(128)S(1)} %get-tuple-element.25.groups, bf16[128,256,256]{2,1,0:T(8,128)(2,1)} %bitcast.58, bf16[1,256,256]{2,1,0:T(8,128)(2,1)S(1)} %collective-permute-done.7.refs_0_, ...), custom_call_target="tpu_custom_call" | custom-call | flops 268435456 | bytes 1048576 | tf_op jit(solution)/shard_map/forward_2/pallas_call | solution.py:328
  38.3 0.1 collective-permute-start.9
  38.4 1.9 %collective-permute-done.9 = bf16[4,256,256]{2,1,0:T(8,128)(2,1)S(1)} collective-permute-done((bf16[4,256,256]{2,1,0:T(8,128)(2,1)S(1)}, bf16[4,256,256]{2,1,0:T(8,128)(2,1)S(1)}, u32[]{:S(2)}, u32[]{:S(2)}) %collective-permute-start.9) | collective-permute-done | bytes 524320 | tf_op jit(solution)/shard_map/ppermute | solution.py:362
  40.3 0.1 add_convert_fusion.own
  40.4 0.4 collective-permute-start.10
  40.9 13.6 %collective-permute-done.10.came = bf16[4,256,256]{2,1,0:T(8,128)(2,1)S(1)} collective-permute-done((bf16[4,256,256]{2,1,0:T(8,128)(2,1)S(1)}, bf16[4,256,256]{2,1,0:T(8,128)(2,1)S(1)}, u32[]{:S(2)}, u32[]{:S(2)}) %collective-permute-start.10) | collective-permute-done | bytes 524320 | tf_op jit(solution)/shard_map/ppermute | solution.py:364
  54.5 1.5 %dense.1 = (bf16[512,256]{1,0:T(8,128)(2,1)}, bf16[4,256,256]{2,1,0:T(8,128)(2,1)S(1)}, f32[2,144,256]{2,1,0:T(8,128)S(1)}) custom-call(bf16[4,256,256]{2,1,0:T(8,128)(2,1)S(1)} %add_convert_fusion.own, bf16[4,256,256]{2,1,0:T(8,128)(2,1)S(1)} %collective-permute-done.10.came, bf16[256,256]{1,0:T(8,128)(2,1)S(1)} %copy-done.2, f32[1,256]{1,0:T(1,128)S(1)} %bitcast.54, ...), custom_call_target="tpu_custom_call" | custom-call | flops 402653184 | bytes 1048576 | tf_op jit(solution)/shard_map/dense/pallas_call | solution.py:367
  56.0 0.6 collective-permute-start.12
  56.6 1.5 %collective-permute-done.12 = f32[144,256]{1,0:T(8,128)S(1)} collective-permute-done((f32[144,256]{1,0:T(8,128)S(1)}, f32[144,256]{1,0:T(8,128)S(1)}, u32[]{:S(2)}, u32[]{:S(2)}) %collective-permute-start.12) | collective-permute-done | bytes 147488 | tf_op jit(solution)/shard_map/ppermute | solution.py:382
  58.2 2.9 %backward_far.1 = f32[2,256,256]{2,1,0:T(8,128)S(1)} custom-call(s32[2112]{0:T(1024)S(1)} %get-tuple-element.35.bwd, s32[19]{0:T(128)S(1)} %get-tuple-element.25.groups, bf16[128,256,256]{2,1,0:T(8,128)(2,1)} %bitcast.59, bf16[4,256,256]{2,1,0:T(8,128)(2,1)S(1)} %get-tuple-element.36.grad_mine, bf16[4,256,256]{2,1,0:T(8,128)(2,1)S(1)} %collective-permute-done.11.grad_came), custom_call_target="tpu_custom_call" | custom-call | flops 536870912 | bytes 2097152 | tf_op jit(solution)/shard_map/backward_far/pallas_call | solution.py:387
  61.1 1.4 %collective-permute-start.13 = (bf16[400,256]{1,0:T(8,128)(2,1)S(1)}, bf16[400,256]{1,0:T(8,128)(2,1)S(1)}, u32[]{:S(2)}, u32[]{:S(2)}) collective-permute-start(bf16[400,256]{1,0:T(8,128)(2,1)S(1)} %get-tuple-element.49), channel_id=1, source_target_pairs={{0,2},{2,4},{4,6},{6,7},{7,5},{5,3},{3,1},{1,0},{8,10},{10,12},{12... | collective-permute-start | bytes 614408 | tf_op jit(solution)/shard_map/ppermute | solution.py:406
  62.6 4.1 %backward.3 = f32[4,256,256]{2,1,0:T(8,128)S(1)} custom-call(s32[2112]{0:T(1024)S(1)} %get-tuple-element.35.bwd, s32[19]{0:T(128)S(1)} %get-tuple-element.25.groups, bf16[128,256,256]{2,1,0:T(8,128)(2,1)} %bitcast.60, bf16[4,256,256]{2,1,0:T(8,128)(2,1)S(1)} %get-tuple-element.36.grad_mine, bf16[4,256,256]{2,1,0:T(8,128)(2,1)S(1)} %collective-permute-done.11.grad_came), custom_call_target="tpu_custom_call" | custom-call | flops 536870912 | bytes 2097152 | tf_op jit(solution)/shard_map/backward/pallas_call | solution.py:387
  66.8 2.8 %collective-permute-start.17 = (bf16[400,256]{1,0:T(8,128)(2,1)S(1)}, bf16[400,256]{1,0:T(8,128)(2,1)S(1)}, u32[]{:S(2)}, u32[]{:S(2)}) collective-permute-start(bf16[400,256]{1,0:T(8,128)(2,1)S(1)} %get-tuple-element.48), channel_id=1, source_target_pairs={{2,0},{4,2},{6,4},{7,6},{5,7},{3,5},{1,3},{0,1},{10,8},{12,10},{14... | collective-permute-start | bytes 614408 | tf_op jit(solution)/shard_map/ppermute | solution.py:407
  69.6 3.5 %backward.4 = f32[4,256,256]{2,1,0:T(8,128)S(1)} custom-call(s32[2112]{0:T(1024)S(1)} %get-tuple-element.35.bwd, s32[19]{0:T(128)S(1)} %get-tuple-element.25.groups, bf16[128,256,256]{2,1,0:T(8,128)(2,1)} %bitcast.61, bf16[4,256,256]{2,1,0:T(8,128)(2,1)S(1)} %get-tuple-element.36.grad_mine, bf16[4,256,256]{2,1,0:T(8,128)(2,1)S(1)} %collective-permute-done.11.grad_came), custom_call_target="tpu_custom_call" | custom-call | flops 536870912 | bytes 2097152 | tf_op jit(solution)/shard_map/backward/pallas_call | solution.py:387
  73.1 3.3 %backward.5 = f32[4,256,256]{2,1,0:T(8,128)S(1)} custom-call(s32[2112]{0:T(1024)S(1)} %get-tuple-element.35.bwd, s32[19]{0:T(128)S(1)} %get-tuple-element.25.groups, bf16[128,256,256]{2,1,0:T(8,128)(2,1)} %bitcast.62, bf16[4,256,256]{2,1,0:T(8,128)(2,1)S(1)} %get-tuple-element.36.grad_mine, bf16[4,256,256]{2,1,0:T(8,128)(2,1)S(1)} %collective-permute-done.11.grad_came), custom_call_target="tpu_custom_call" | custom-call | flops 536870912 | bytes 2097152 | tf_op jit(solution)/shard_map/backward/pallas_call | solution.py:387
  76.6 0.1 fusion.11
  76.8 2.1 %collective-permute-start.18 = (bf16[656,256]{1,0:T(8,128)(2,1)S(1)}, bf16[656,256]{1,0:T(8,128)(2,1)S(1)}, u32[]{:S(2)}, u32[]{:S(2)}) collective-permute-start(bf16[656,256]{1,0:T(8,128)(2,1)S(1)} %pad_maximum_fusion.1), channel_id=1, source_target_pairs={{2,0},{4,2},{6,4},{7,6},{5,7},{3,5},{1,3},{0,1},{10,8},{12,10},{14... | collective-permute-start | bytes 1007624 | tf_op jit(solution)/shard_map/ppermute | solution.py:424
  78.8 5.3 %collective-permute-done.14 = bf16[656,256]{1,0:T(8,128)(2,1)S(1)} collective-permute-done((bf16[656,256]{1,0:T(8,128)(2,1)S(1)}, bf16[656,256]{1,0:T(8,128)(2,1)S(1)}, u32[]{:S(2)}, u32[]{:S(2)}) %collective-permute-start.14) | collective-permute-done | bytes 335904 | tf_op jit(solution)/shard_map/ppermute | solution.py:423
  84.3 2.2 %collective-permute-start.15 = (bf16[656,256]{1,0:T(8,128)(2,1)S(1)}, bf16[656,256]{1,0:T(8,128)(2,1)S(1)}, u32[]{:S(2)}, u32[]{:S(2)}) collective-permute-start(bf16[656,256]{1,0:T(8,128)(2,1)S(1)} %constant_dynamic-update-slice_fusion.2), channel_id=1, source_target_pairs={{0,2},{2,4},{4,6},{6,7},{7,5},{5,3},{3,1},{1,0},{8,10},{10,12},{12... | collective-permute-start | bytes 1007624 | tf_op jit(solution)/shard_map/ppermute | solution.py:423
  86.5 0.1 fusion.12
  86.5 0.3 collective-permute-done.18
  87.0 7.5 %collective-permute-done.15 = bf16[656,256]{1,0:T(8,128)(2,1)S(1)} collective-permute-done((bf16[656,256]{1,0:T(8,128)(2,1)S(1)}, bf16[656,256]{1,0:T(8,128)(2,1)S(1)}, u32[]{:S(2)}, u32[]{:S(2)}) %collective-permute-start.15) | collective-permute-done | bytes 335904 | tf_op jit(solution)/shard_map/ppermute | solution.py:423
  94.6 2.5 %collective-permute-start.16 = (bf16[656,256]{1,0:T(8,128)(2,1)S(1)}, bf16[656,256]{1,0:T(8,128)(2,1)S(1)}, u32[]{:S(2)}, u32[]{:S(2)}) collective-permute-start(bf16[656,256]{1,0:T(8,128)(2,1)S(1)} %constant_dynamic-update-slice_fusion.1), channel_id=1, source_target_pairs={{0,2},{2,4},{4,6},{6,7},{7,5},{5,3},{3,1},{1,0},{8,10},{10,12},{12... | collective-permute-start | bytes 1007624 | tf_op jit(solution)/shard_map/ppermute | solution.py:423
  97.2 0.2 collective-permute-done.19
  97.5 7.8 %collective-permute-done.16.right = bf16[656,256]{1,0:T(8,128)(2,1)S(1)} collective-permute-done((bf16[656,256]{1,0:T(8,128)(2,1)S(1)}, bf16[656,256]{1,0:T(8,128)(2,1)S(1)}, u32[]{:S(2)}, u32[]{:S(2)}) %collective-permute-start.16) | collective-permute-done | bytes 335904 | tf_op jit(solution)/shard_map/ppermute | solution.py:423
  105.3 0.1 add_multiply_fusion
  105.4 0.3 collective-permute-start.21
  105.7 2.7 %backward_own.1.own = f32[2,256,256]{2,1,0:T(8,128)S(1)} custom-call(s32[2112]{0:T(1024)S(1)} %get-tuple-element.35.bwd, s32[19]{0:T(128)S(1)} %get-tuple-element.25.groups, bf16[128,256,256]{2,1,0:T(8,128)(2,1)} %bitcast.63, bf16[4,256,256]{2,1,0:T(8,128)(2,1)S(1)} %get-tuple-element.36.grad_mine, bf16[4,256,256]{2,1,0:T(8,128)(2,1)S(1)} %collective-permute-done.11.grad_came), custom_call_target="tpu_custom_call" | custom-call | flops 536870912 | bytes 2097152 | tf_op jit(solution)/shard_map/backward_own/pallas_call | solution.py:387
  108.5 0.6 slice.164
  109.1 0.9 finish.1
  109.9 0.7 maximum_select_fusion
  (48 shorter events, 0.9 us)
Async XLA Ops:
  0.6 11.0 %collective-permute-start = (bf16[2,256,256]{2,1,0:T(8,128)(2,1)}, bf16[2,256,256]{2,1,0:T(8,128)(2,1)S(1)}, u32[]{:S(2)}, u32[]{:S(2)}) collective-permute-start(bf16[2,256,256]{2,1,0:T(8,128)(2,1)} %bitcast.51), channel_id=1, source_target_pairs={{0,2},{2,4},{4,6},{6,7},{7,5},{5,3},{3,1},{1,0},{8,10},{10,12},{12... | collective-permute-start | bytes 786440 | tf_op jit(solution)/shard_map/ppermute | solution.py:346
  3.7 8.0 %collective-permute-start.1 = (bf16[2,256,256]{2,1,0:T(8,128)(2,1)}, bf16[2,256,256]{2,1,0:T(8,128)(2,1)S(1)}, u32[]{:S(2)}, u32[]{:S(2)}) collective-permute-start(bf16[2,256,256]{2,1,0:T(8,128)(2,1)} %bitcast.52), channel_id=1, source_target_pairs={{2,0},{4,2},{6,4},{7,6},{5,7},{3,5},{1,3},{0,1},{10,8},{12,10},{14... | collective-permute-start | bytes 786440 | tf_op jit(solution)/shard_map/ppermute | solution.py:347
  3.7 8.0 %collective-permute-start.2 = (bf16[512,256]{1,0:T(8,128)(2,1)}, bf16[512,256]{1,0:T(8,128)(2,1)S(1)}, u32[]{:S(2)}, u32[]{:S(2)}) collective-permute-start(bf16[512,256]{1,0:T(8,128)(2,1)} %cot_own.1), channel_id=1, source_target_pairs={{0,16},{16,0},{8,24},{24,8},{1,17},{17,1},{9,25},{25,9},{2,18},{18... | collective-permute-start | bytes 786440 | tf_op jit(solution)/shard_map/ppermute | solution.py:349
  7.8 0.7 copy-start.4
  11.7 8.2 %collective-permute-start.3 = (bf16[2,256,256]{2,1,0:T(8,128)(2,1)S(1)}, bf16[2,256,256]{2,1,0:T(8,128)(2,1)S(1)}, u32[]{:S(2)}, u32[]{:S(2)}) collective-permute-start(bf16[2,256,256]{2,1,0:T(8,128)(2,1)S(1)} %collective-permute-done.refs_1_), channel_id=1, source_target_pairs={{0,2},{2,4},{4,6},{6,7},{7,5},{5,3},{3,1},{1,0},{8,10},{10,12},{12... | collective-permute-start | bytes 786440 | tf_op jit(solution)/shard_map/ppermute | solution.py:346
  13.4 7.0 %collective-permute-start.5 = (bf16[2,256,256]{2,1,0:T(8,128)(2,1)S(1)}, bf16[2,256,256]{2,1,0:T(8,128)(2,1)S(1)}, u32[]{:S(2)}, u32[]{:S(2)}) collective-permute-start(bf16[2,256,256]{2,1,0:T(8,128)(2,1)S(1)} %collective-permute-done.1.refs_2_), channel_id=1, source_target_pairs={{2,0},{4,2},{6,4},{7,6},{5,7},{3,5},{1,3},{0,1},{10,8},{12,10},{14... | collective-permute-start | bytes 786440 | tf_op jit(solution)/shard_map/ppermute | solution.py:347
  19.9 7.5 %collective-permute-start.4 = (bf16[2,256,256]{2,1,0:T(8,128)(2,1)S(1)}, bf16[2,256,256]{2,1,0:T(8,128)(2,1)S(1)}, u32[]{:S(2)}, u32[]{:S(2)}) collective-permute-start(bf16[2,256,256]{2,1,0:T(8,128)(2,1)S(1)} %collective-permute-done.3.refs_3_), channel_id=1, source_target_pairs={{0,2},{2,4},{4,6},{6,7},{7,5},{5,3},{3,1},{1,0},{8,10},{10,12},{12... | collective-permute-start | bytes 786440 | tf_op jit(solution)/shard_map/ppermute | solution.py:346
  20.4 7.0 %collective-permute-start.6 = (bf16[2,256,256]{2,1,0:T(8,128)(2,1)S(1)}, bf16[2,256,256]{2,1,0:T(8,128)(2,1)S(1)}, u32[]{:S(2)}, u32[]{:S(2)}) collective-permute-start(bf16[2,256,256]{2,1,0:T(8,128)(2,1)S(1)} %collective-permute-done.5.refs_4_), channel_id=1, source_target_pairs={{2,0},{4,2},{6,4},{7,6},{5,7},{3,5},{1,3},{0,1},{10,8},{12,10},{14... | collective-permute-start | bytes 786440 | tf_op jit(solution)/shard_map/ppermute | solution.py:347
  21.9 0.9 copy-start
  27.5 8.1 %collective-permute-start.7 = (bf16[1,256,256]{2,1,0:T(8,128)(2,1)S(1)}, bf16[1,256,256]{2,1,0:T(8,128)(2,1)S(1)}, u32[]{:S(2)}, u32[]{:S(2)}) collective-permute-start(bf16[1,256,256]{2,1,0:T(8,128)(2,1)S(1)} %slice.109), channel_id=1, source_target_pairs={{0,2},{2,4},{4,6},{6,7},{7,5},{5,3},{3,1},{1,0},{8,10},{10,12},{12... | collective-permute-start | bytes 393224 | tf_op jit(solution)/shard_map/ppermute | solution.py:357
  28.7 6.9 %collective-permute-start.8 = (bf16[1,256,256]{2,1,0:T(8,128)(2,1)S(1)}, bf16[1,256,256]{2,1,0:T(8,128)(2,1)S(1)}, u32[]{:S(2)}, u32[]{:S(2)}) collective-permute-start(bf16[1,256,256]{2,1,0:T(8,128)(2,1)S(1)} %slice.110), channel_id=1, source_target_pairs={{2,0},{4,2},{6,4},{7,6},{5,7},{3,5},{1,3},{0,1},{10,8},{12,10},{14... | collective-permute-start | bytes 393224 | tf_op jit(solution)/shard_map/ppermute | solution.py:358
  35.5 18.9 %copy-start.1 = (bf16[512,256]{1,0:T(8,128)(2,1)S(1)}, bf16[512,256]{1,0:T(8,128)(2,1)}, u32[]{:S(2)}) copy-start(bf16[512,256]{1,0:T(8,128)(2,1)} %cot_own.1) | copy-start | bytes 786436
  35.6 18.9 %copy-start.2 = (bf16[256,256]{1,0:T(8,128)(2,1)S(1)}, bf16[256,256]{1,0:T(8,128)(2,1)}, u32[]{:S(2)}) copy-start(bf16[256,256]{1,0:T(8,128)(2,1)} %weight.1) | copy-start | bytes 393220
  35.6 18.9 %copy-start.3 = (f32[256]{0:T(256)S(1)}, f32[256]{0:T(256)}, u32[]{:S(2)}) copy-start(f32[256]{0:T(256)} %param.14) | copy-start | bytes 3076
  38.3 2.0 %collective-permute-start.9 = (bf16[4,256,256]{2,1,0:T(8,128)(2,1)S(1)}, bf16[4,256,256]{2,1,0:T(8,128)(2,1)S(1)}, u32[]{:S(2)}, u32[]{:S(2)}) collective-permute-start(bf16[4,256,256]{2,1,0:T(8,128)(2,1)S(1)} %get-tuple-element.32), channel_id=1, source_target_pairs={{0,8},{8,0},{16,24},{24,16},{1,9},{9,1},{17,25},{25,17},{2,10},{10... | collective-permute-start | bytes 1572872 | tf_op jit(solution)/shard_map/ppermute | solution.py:362
  40.4 14.0 %collective-permute-start.10 = (bf16[4,256,256]{2,1,0:T(8,128)(2,1)S(1)}, bf16[4,256,256]{2,1,0:T(8,128)(2,1)S(1)}, u32[]{:S(2)}, u32[]{:S(2)}) collective-permute-start(bf16[4,256,256]{2,1,0:T(8,128)(2,1)S(1)} %add_convert_fusion.own), channel_id=1, source_target_pairs={{0,16},{16,0},{8,24},{24,8},{1,17},{17,1},{9,25},{25,9},{2,18},{18... | collective-permute-start | bytes 1572872 | tf_op jit(solution)/shard_map/ppermute | solution.py:364
  56.0 2.1 %collective-permute-start.11 = (bf16[4,256,256]{2,1,0:T(8,128)(2,1)S(1)}, bf16[4,256,256]{2,1,0:T(8,128)(2,1)S(1)}, u32[]{:S(2)}, u32[]{:S(2)}) collective-permute-start(bf16[4,256,256]{2,1,0:T(8,128)(2,1)S(1)} %get-tuple-element.36.grad_mine), channel_id=1, source_target_pairs={{0,8},{8,0},{16,24},{24,16},{1,9},{9,1},{17,25},{25,17},{2,10},{10... | collective-permute-start | bytes 1572872 | tf_op jit(solution)/shard_map/ppermute | solution.py:380
  56.0 2.1 %collective-permute-start.12 = (f32[144,256]{1,0:T(8,128)S(1)}, f32[144,256]{1,0:T(8,128)S(1)}, u32[]{:S(2)}, u32[]{:S(2)}) collective-permute-start(f32[144,256]{1,0:T(8,128)S(1)} %dynamic-slice_bitcast_fusion), channel_id=1, source_target_pairs={{0,8},{8,0},{16,24},{24,16},{1,9},{9,1},{17,25},{25,17},{2,10},{10... | collective-permute-start | bytes 442376 | tf_op jit(solution)/shard_map/ppermute | solution.py:382
  61.1 15.3 %collective-permute-start.13 = (bf16[400,256]{1,0:T(8,128)(2,1)S(1)}, bf16[400,256]{1,0:T(8,128)(2,1)S(1)}, u32[]{:S(2)}, u32[]{:S(2)}) collective-permute-start(bf16[400,256]{1,0:T(8,128)(2,1)S(1)} %get-tuple-element.49), channel_id=1, source_target_pairs={{0,2},{2,4},{4,6},{6,7},{7,5},{5,3},{3,1},{1,0},{8,10},{10,12},{12... | collective-permute-start | bytes 614408 | tf_op jit(solution)/shard_map/ppermute | solution.py:406
  66.8 9.7 %collective-permute-start.17 = (bf16[400,256]{1,0:T(8,128)(2,1)S(1)}, bf16[400,256]{1,0:T(8,128)(2,1)S(1)}, u32[]{:S(2)}, u32[]{:S(2)}) collective-permute-start(bf16[400,256]{1,0:T(8,128)(2,1)S(1)} %get-tuple-element.48), channel_id=1, source_target_pairs={{2,0},{4,2},{6,4},{7,6},{5,7},{3,5},{1,3},{0,1},{10,8},{12,10},{14... | collective-permute-start | bytes 614408 | tf_op jit(solution)/shard_map/ppermute | solution.py:407
  76.6 7.6 %collective-permute-start.14 = (bf16[656,256]{1,0:T(8,128)(2,1)S(1)}, bf16[656,256]{1,0:T(8,128)(2,1)S(1)}, u32[]{:S(2)}, u32[]{:S(2)}) collective-permute-start(bf16[656,256]{1,0:T(8,128)(2,1)S(1)} %pad_maximum_fusion), channel_id=1, source_target_pairs={{0,2},{2,4},{4,6},{6,7},{7,5},{5,3},{3,1},{1,0},{8,10},{10,12},{12... | collective-permute-start | bytes 1007624 | tf_op jit(solution)/shard_map/ppermute | solution.py:423
  76.8 10.1 %collective-permute-start.18 = (bf16[656,256]{1,0:T(8,128)(2,1)S(1)}, bf16[656,256]{1,0:T(8,128)(2,1)S(1)}, u32[]{:S(2)}, u32[]{:S(2)}) collective-permute-start(bf16[656,256]{1,0:T(8,128)(2,1)S(1)} %pad_maximum_fusion.1), channel_id=1, source_target_pairs={{2,0},{4,2},{6,4},{7,6},{5,7},{3,5},{1,3},{0,1},{10,8},{12,10},{14... | collective-permute-start | bytes 1007624 | tf_op jit(solution)/shard_map/ppermute | solution.py:424
  84.3 10.3 %collective-permute-start.15 = (bf16[656,256]{1,0:T(8,128)(2,1)S(1)}, bf16[656,256]{1,0:T(8,128)(2,1)S(1)}, u32[]{:S(2)}, u32[]{:S(2)}) collective-permute-start(bf16[656,256]{1,0:T(8,128)(2,1)S(1)} %constant_dynamic-update-slice_fusion.2), channel_id=1, source_target_pairs={{0,2},{2,4},{4,6},{6,7},{7,5},{5,3},{3,1},{1,0},{8,10},{10,12},{12... | collective-permute-start | bytes 1007624 | tf_op jit(solution)/shard_map/ppermute | solution.py:423
  86.9 10.5 %collective-permute-start.19 = (bf16[656,256]{1,0:T(8,128)(2,1)S(1)}, bf16[656,256]{1,0:T(8,128)(2,1)S(1)}, u32[]{:S(2)}, u32[]{:S(2)}) collective-permute-start(bf16[656,256]{1,0:T(8,128)(2,1)S(1)} %constant_dynamic-update-slice_fusion), channel_id=1, source_target_pairs={{2,0},{4,2},{6,4},{7,6},{5,7},{3,5},{1,3},{0,1},{10,8},{12,10},{14... | collective-permute-start | bytes 1007624 | tf_op jit(solution)/shard_map/ppermute | solution.py:424
  94.6 10.7 %collective-permute-start.16 = (bf16[656,256]{1,0:T(8,128)(2,1)S(1)}, bf16[656,256]{1,0:T(8,128)(2,1)S(1)}, u32[]{:S(2)}, u32[]{:S(2)}) collective-permute-start(bf16[656,256]{1,0:T(8,128)(2,1)S(1)} %constant_dynamic-update-slice_fusion.1), channel_id=1, source_target_pairs={{0,2},{2,4},{4,6},{6,7},{7,5},{5,3},{3,1},{1,0},{8,10},{10,12},{12... | collective-permute-start | bytes 1007624 | tf_op jit(solution)/shard_map/ppermute | solution.py:423
  97.5 11.6 %collective-permute-start.20 = (bf16[512,256]{1,0:T(8,128)(2,1)S(1)}, bf16[512,256]{1,0:T(8,128)(2,1)S(1)}, u32[]{:S(2)}, u32[]{:S(2)}) collective-permute-start(bf16[512,256]{1,0:T(8,128)(2,1)S(1)} %fusion.1), channel_id=1, source_target_pairs={{2,0},{4,2},{6,4},{7,6},{5,7},{3,5},{1,3},{0,1},{10,8},{12,10},{14... | collective-permute-start | bytes 786440 | tf_op jit(solution)/shard_map/ppermute | solution.py:424
  105.4 4.5 %collective-permute-start.21 = (f32[128,256]{1,0:T(8,128)S(1)}, f32[128,256]{1,0:T(8,128)S(1)}, u32[]{:S(2)}, u32[]{:S(2)}) collective-permute-start(f32[128,256]{1,0:T(8,128)S(1)} %slice.163), channel_id=1, source_target_pairs={{0,8},{8,0},{16,24},{24,16},{1,9},{9,1},{17,25},{25,17},{2,10},{10... | collective-permute-start | bytes 393224 | tf_op jit(solution)/shard_map/ppermute | solution.py:428

commit v3 on v0

v3 whole, which is shorter than its diff:
```python
import functools
import math

import jax
import jax.numpy as jnp
import numpy as np
from jax import lax
from jax.experimental import pallas as pl
from jax.experimental.pallas import tpu as pltpu
from jax.sharding import PartitionSpec as P

BF16 = jnp.bfloat16
F32 = jnp.float32
UNIT = 8
DEPTH = 5

VMEM = pl.BlockSpec(memory_space=pltpu.VMEM)
SMEM = pl.BlockSpec(memory_space=pltpu.SMEM)
HBM = pl.BlockSpec(memory_space=pltpu.HBM)
ANY = pl.BlockSpec(memory_space=pl.ANY)


def ring_order(count):
    return list(range(0, count, 2)) + list(range(count - 1, 0, -2))


def params(mib):
    return pltpu.CompilerParams(vmem_limit_bytes=mib * 2**20)


def cost(flops, nbytes):
    return pl.CostEstimate(flops=int(flops), bytes_accessed=int(nbytes), transcendentals=0)


def lists_kernel(n_buckets, cap, col_tiles, place_base, cols, counts, tables, lists):
    row_tiles, slots = cols.shape
    ends = n_buckets * cap
    first_place = place_base + lax.axis_index("col") * col_tiles
    first_pos = lax.axis_index("row") * row_tiles
    for b in range(n_buckets):
        lists[ends + b] = 0

    def tile_row(t, _):
        head = t * slots * 65536 + tables[first_pos + t] * 256

        def slot(s, _):
            place = tables[first_place + cols[t, s]]
            bucket = place // 256
            n = lists[ends + bucket]
            lists[bucket * cap + n] = head + s * 65536 + lax.rem(place, 256)
            lists[ends + bucket] = n + 1
            return 0

        lax.fori_loop(0, counts[t], slot, 0)
        return 0

    lax.fori_loop(0, row_tiles, tile_row, 0)
    for b in range(n_buckets):
        n = lists[ends + b]
        units = (n + UNIT - 1) // UNIT

        def fill(i, _, b=b):
            lists[b * cap + i] = row_tiles * 256
            return 0

        lax.fori_loop(n, units * UNIT, fill, 0)
        lists[ends + b] = units


def stream(lists, buckets, cap, n_buckets, values, buffer, sems, between, use):
    ends = []
    for b in buckets:
        n = lists[n_buckets * cap + b]
        ends.append(n + (ends[-1] if ends else 0))
    total = ends[-1]

    def locate(g):
        first = buckets[0] * cap + g * UNIT
        for i in range(1, len(buckets)):
            first = jnp.where(g >= ends[i - 1], buckets[i] * cap + (g - ends[i - 1]) * UNIT, first)
        return first

    def copies(g):
        first = locate(g)
        at = lax.rem(g, DEPTH) * UNIT
        for u in range(UNIT):
            yield pltpu.make_async_copy(values.at[lists[first + u] // 65536], buffer.at[at + u], sems.at[at + u])

    def ahead(g, _):
        for c in copies(g):
            c.start()
        return 0

    lax.fori_loop(0, jnp.minimum(total, DEPTH - 1), ahead, 0)
    between()

    def step(g, _):
        @pl.when(g + DEPTH - 1 < total)
        def _():
            ahead(g + DEPTH - 1, 0)

        for c in copies(g):
            c.wait()
        use(locate(g), lax.rem(g, DEPTH) * UNIT)
        return 0

    lax.fori_loop(0, total, step, 0)


def destination(entry):
    return lax.rem(entry // 256, 256)


def source(entry):
    return lax.rem(entry, 256)


def forward_kernel(buckets, cap, n_buckets, n_blocks, n_before, last, lists, values, *refs):
    blocks, refs = refs[:n_blocks], refs[n_blocks:]
    before, refs = refs[:n_before], refs[n_before:]
    (buffer, sems, block_sems, sources), refs = refs[-4:], refs[:-4]
    total = refs[-1]
    copies = []
    starts = []
    at = 0
    for i, b in enumerate(blocks):
        copies.append(pltpu.make_async_copy(b, sources.at[pl.ds(at, b.shape[0])], block_sems.at[i]))
        starts.append(at)
        at += b.shape[0]

    def between():
        for c in copies:
            c.start()
        if n_before:
            total[...] = before[0][...]
        else:
            total[...] = jnp.zeros(total.shape, F32)
        for c in copies:
            c.wait()

    def use(first, at):
        parts = []
        for u in range(UNIT):
            parts.append(jnp.dot(buffer[at + u], sources[source(lists[first + u])], preferred_element_type=F32))
        for u in range(UNIT):
            total[destination(lists[first + u])] += parts[u]

    stream(lists, buckets, cap, n_buckets, values, buffer, sems, between, use)
    if last:
        mine, other, _ = refs
        half = mine.shape[0]
        mine[...] = total[:half].astype(BF16)
        other[...] = total[half : 2 * half].astype(BF16)


def dense_kernel(second, near, away, weight, bias, cot, *refs):
    if second:
        before, grad_t, wgrad = refs
    else:
        out, grad_t, wgrad = refs
    tiles, tile, width = near.shape
    w = weight[...]
    hidden = near[...].reshape(tiles * tile, width).astype(F32) + away[...].reshape(tiles * tile, width).astype(F32)
    hidden = hidden.astype(BF16)
    preact = jnp.dot(hidden, w, preferred_element_type=F32) + bias[...]
    sig = 1.0 / (1.0 + jnp.exp(-preact))
    if not second:
        out[...] = (preact * sig).astype(BF16)
    pgrad = (cot[...].astype(F32) * (sig * (1.0 + preact * (1.0 - sig)))).astype(BF16)
    for i in range(tiles):
        grad_t[i] = lax.dot_general(
            w, pgrad[i * tile : (i + 1) * tile], (((1,), (1,)), ((), ())), preferred_element_type=F32
        ).astype(BF16)
    wg = lax.dot_general(hidden, pgrad, (((0,), (0,)), ((), ())), preferred_element_type=F32)
    bg = jnp.sum(pgrad.astype(F32), axis=0, keepdims=True)
    if second:
        wg = wg + before[:width]
        bg = bg + before[width : width + 1]
        rows = width // 4
        for q in range(4):
            wgrad[q, :rows] = wg[q * rows : (q + 1) * rows]
            wgrad[q, rows:] = jnp.broadcast_to(bg, (wgrad.shape[1] - rows, width))
    else:
        wgrad[:width] = wg
        wgrad[width:] = jnp.broadcast_to(bg, (wgrad.shape[0] - width, width))


def backward_kernel(bucket, cap, n_buckets, lists, values, *refs):
    parts, (out, grads, buffer, sems, part_sems) = refs[:-5], refs[-5:]
    copies = []
    at = 0
    for i, g in enumerate(parts):
        copies.append(pltpu.make_async_copy(g, grads.at[pl.ds(at, g.shape[0])], part_sems.at[i]))
        at += g.shape[0]

    def between():
        for c in copies:
            c.start()
        grads[at] = jnp.zeros(grads.shape[1:], BF16)
        out[...] = jnp.zeros(out.shape, F32)
        for c in copies:
            c.wait()

    def use(first, at):
        parts = []
        for u in range(UNIT):
            parts.append(jnp.dot(grads[destination(lists[first + u])], buffer[at + u], preferred_element_type=F32))
        for u in range(UNIT):
            out[source(lists[first + u])] += parts[u]

    stream(lists, [bucket], cap, n_buckets, values, buffer, sems, between, use)


def finish_kernel(own, right, left, out):
    tiles, _, tile = own.shape
    for i in range(tiles):
        rows = pl.ds(i * tile, tile)
        total = own[i] + right[rows, :].astype(F32) + left[rows, :].astype(F32)
        out[rows, :] = total.T.astype(BF16)


def quarters_kernel(own, y, core, both, out):
    row = lax.axis_index("row")
    me = lax.rem(row, 2) * 2 + row // 2
    rows = own.shape[0]
    for i, part in enumerate((own, y, core, both)):
        high = lax.rem(me // 2 + i // 2, 2)
        low = lax.rem(me + i % 2, 2)
        out[pl.ds(pl.multiple_of((high * 2 + low) * rows, rows), rows), :] = part[...]


def per_device(n_col, features, tile_values, tile_cols, tile_counts, weight, bias, cotangent):
    node_dev, width = features.shape
    row_tiles, slots, tile, _ = tile_values.shape
    per_dev = node_dev // tile
    col_tiles = n_col * per_dev
    half = n_col // 2
    node_total = node_dev * lax.axis_size("row") * n_col
    grad_scale = 1.0 / math.sqrt(node_total)
    values = tile_values.reshape(row_tiles * slots, tile, tile)

    order = ring_order(n_col)
    right = [(order[i], order[(i + 1) % n_col]) for i in range(n_col)]
    left = [(b, a) for a, b in right]
    cores = [(0, 1), (1, 0), (2, 3), (3, 2)]
    across = [(0, 2), (2, 0), (1, 3), (3, 1)]
    corners = [(0, 3), (3, 0), (1, 2), (2, 1)]
    row = lax.axis_index("row")
    my_y, my_core = row // 2, row % 2

    n_buckets = half + 1
    rank = np.zeros(n_col, np.int64)
    rank[order] = np.arange(n_col)
    place = np.zeros((n_col, col_tiles), np.int32)
    for d in range(n_col):
        for t in range(col_tiles):
            ahead = (rank[t // per_dev] - rank[d]) % n_col
            bucket = min(ahead, n_col - ahead)
            side = 1 if 0 < ahead < half else 0
            place[d, t] = bucket * 256 + side * per_dev + t % per_dev
    tiles = np.arange(row_tiles)
    block = tiles // (row_tiles // 4)
    pos = [
        ((block % 2 != r % 2) * 2 + (block // 2 != r // 2)) * (row_tiles // 4) + tiles % (row_tiles // 4)
        for r in range(4)
    ]
    tables = np.concatenate([np.concatenate(pos), place.reshape(-1)]).astype(np.int32)
    cap = row_tiles * slots + UNIT
    lists = pl.pallas_call(
        functools.partial(lists_kernel, n_buckets, cap, col_tiles, 4 * row_tiles),
        in_specs=[SMEM] * 3,
        out_specs=SMEM,
        out_shape=jax.ShapeDtypeStruct((n_buckets * cap + n_buckets,), jnp.int32),
        compiler_params=params(8),
        cost_estimate=cost(0, 2**12),
        name="lists",
    )(tile_cols, tile_counts.reshape(-1), jnp.asarray(tables))

    dots = 2 * tile * tile * width
    small = cost(dots, tile * tile * 2)
    stream_scratch = [pltpu.VMEM((DEPTH * UNIT, tile, tile), BF16), pltpu.SemaphoreType.DMA((DEPTH * UNIT,))]
    total_shape = jax.ShapeDtypeStruct((row_tiles + 1, tile, width), F32)
    half_shape = jax.ShapeDtypeStruct((row_tiles // 2, tile, width), BF16)

    def forward(bucket, blocks, before, last=False):
        n_tiles = sum(b.shape[0] for b in blocks)
        out = pl.pallas_call(
            functools.partial(forward_kernel, [bucket], cap, n_buckets, len(blocks), len(before), last),
            in_specs=[SMEM, HBM] + [ANY if bucket else HBM] * len(blocks) + [VMEM] * len(before),
            out_specs=[VMEM] * (2 if last else 1),
            out_shape=[half_shape] * 2 if last else [total_shape],
            scratch_shapes=([pltpu.VMEM(total_shape.shape, F32)] if last else [])
            + stream_scratch
            + [pltpu.SemaphoreType.DMA((len(blocks),)), pltpu.VMEM((n_tiles, tile, width), BF16)],
            compiler_params=params(40),
            cost_estimate=small,
            name=f"forward_{bucket}",
        )(lists, values, *blocks, *before)
        return out if last else out[0]

    mine = features.reshape(per_dev, tile, width)
    from_left = from_right = mine
    total = None
    cot_other = None
    for s in range(1, half):
        now = [from_left, from_right] if s > 1 else [mine]
        from_left = lax.ppermute(from_left, "col", right)
        from_right = lax.ppermute(from_right, "col", left)
        if s == 1:
            cot_other = lax.ppermute(cotangent, "row", across)
            from_left, from_right, cot_other, lists = lax.optimization_barrier(
                (from_left, from_right, cot_other, lists)
            )
        else:
            if s == 2:
                total = forward(0, [mine], [])
            total = forward(s - 1, now, [total])
            from_left, from_right, total = lax.optimization_barrier((from_left, from_right, total))
    far_near = lax.ppermute(from_left[: per_dev // 2], "col", right)
    far_away = lax.ppermute(from_right[per_dev // 2 :], "col", left)
    total = forward(half - 1, [from_left, from_right], [total])
    hid_mine, hid_other = forward(half, [far_near, far_away], [total], last=True)

    hid_came = lax.ppermute(hid_other, "row", cores)
    own = (hid_mine.astype(F32) + hid_came.astype(F32)).astype(BF16)
    mid = row_tiles // 4
    own, own_away = own[:mid], own[mid:]
    came = lax.ppermute(own_away, "row", across)
    came_away = lax.ppermute(own, "row", across)

    w_rows = width // 4 + 16
    grad_shape = jax.ShapeDtypeStruct((mid, width, tile), BF16)
    dense_cost = cost(3 * 2 * node_dev * width * width // 4, node_dev * width)
    bias_row = bias.reshape(1, -1)
    layer_out, grad_1, wgrad = pl.pallas_call(
        functools.partial(dense_kernel, False),
        in_specs=[VMEM] * 5,
        out_specs=[VMEM] * 3,
        out_shape=[
            jax.ShapeDtypeStruct((node_dev, width), BF16),
            grad_shape,
            jax.ShapeDtypeStruct((width + 8, width), F32),
        ],
        compiler_params=params(24),
        cost_estimate=dense_cost,
        name="dense_own",
    )(own, came, weight, bias_row, cotangent)
    grad_3 = lax.ppermute(grad_1, "row", cores)
    came_away, layer_out, grad_1, grad_3, wgrad = lax.optimization_barrier(
        (came_away, layer_out, grad_1, grad_3, wgrad)
    )
    grad_2, wgrad = pl.pallas_call(
        functools.partial(dense_kernel, True),
        in_specs=[VMEM] * 6,
        out_specs=[VMEM] * 2,
        out_shape=[grad_shape, jax.ShapeDtypeStruct((4, w_rows, width), F32)],
        compiler_params=params(24),
        cost_estimate=dense_cost,
        name="dense_away",
    )(own_away, came_away, weight, bias_row, cot_other, wgrad)
    grad_4 = lax.ppermute(grad_2, "row", cores)

    wgrad = wgrad.reshape(2, 2, w_rows, width)

    def quarter(core):
        return lax.dynamic_slice(wgrad, (core, my_y, 0, 0), (1, 1, w_rows, width))[0, 0]

    w_sum = quarter(my_core) + lax.ppermute(quarter(1 - my_core), "row", cores)

    def backward(bucket, n_tiles, after=()):
        its_lists, *_ = lax.optimization_barrier((lists, *after))
        return pl.pallas_call(
            functools.partial(backward_kernel, bucket, cap, n_buckets),
            in_specs=[SMEM, HBM] + [ANY] * 4,
            out_specs=VMEM,
            out_shape=jax.ShapeDtypeStruct((n_tiles, width, tile), F32),
            scratch_shapes=[pltpu.VMEM((row_tiles + 1, width, tile), BF16)]
            + stream_scratch
            + [pltpu.SemaphoreType.DMA((4,))],
            compiler_params=params(40),
            cost_estimate=small,
            name=f"backward_{bucket}",
        )(its_lists, values, grad_1, grad_2, grad_3, grad_4)

    def add(local, came):
        return (local + came.astype(F32)).astype(BF16)

    far_part = backward(half, per_dev).astype(BF16)
    cut = per_dev // 2
    sent = lax.optimization_barrier((far_part[:cut], far_part[cut:]))
    stages = [1 << i for i in range((n_col - 1).bit_length())]
    for d in range(half - 1, -1, -1):
        to_right = lax.ppermute(sent[0], "col", right)
        to_left = lax.ppermute(sent[1], "col", left)
        step = half - 1 - d
        quarters = ()
        if step < len(stages):
            w_now, *_ = lax.optimization_barrier((w_sum.astype(BF16), *sent))
            w_came = lax.ppermute(w_now, "col", [(i, i ^ stages[step]) for i in range(n_col)])
            w_sum = w_now.astype(F32) + w_came.astype(F32)
        elif step == len(stages):
            w_now, *_ = lax.optimization_barrier((w_sum * grad_scale, *sent))
            w_own = w_now[: width // 4]
            quarters = [w_own] + [lax.ppermute(w_own, "row", perm) for perm in (across, cores, corners)]
            weight_grad = pl.pallas_call(
                quarters_kernel,
                in_specs=[VMEM] * 4,
                out_specs=VMEM,
                out_shape=jax.ShapeDtypeStruct((width, width), F32),
                compiler_params=params(8),
                cost_estimate=cost(0, 2**12),
                name="quarters",
            )(*quarters)
            bias_grad = w_now[width // 4]
            w_sum = (weight_grad, bias_grad)
        part = backward(d, 2 * per_dev if d else per_dev, sent)
        part, to_right, to_left, w_sum = lax.optimization_barrier((part, to_right, to_left, w_sum))
        if d == 0:
            break
        for_left, for_right = part[:per_dev], part[per_dev:]
        if step == 0:
            sent = (
                jnp.concatenate([add(for_right[:cut], to_right), for_right[cut:].astype(BF16)]),
                jnp.concatenate([for_left[:cut].astype(BF16), add(for_left[cut:], to_left)]),
            )
        else:
            sent = (add(for_right, to_right), add(for_left, to_left))
        sent = lax.optimization_barrier(sent)
    weight_grad, bias_grad = w_sum
    feature_grad = pl.pallas_call(
        finish_kernel,
        in_specs=[VMEM] * 3,
        out_specs=VMEM,
        out_shape=jax.ShapeDtypeStruct((node_dev, width), BF16),
        compiler_params=params(8),
        name="finish",
    )(part, to_right.reshape(node_dev, width), to_left.reshape(node_dev, width))
    return (layer_out, feature_grad, weight_grad, bias_grad)


def solution(mesh):
    placed = (
        P(("row", "col"), None),
        P("col", "row", None, None),
        P("col", "row"),
        P("col", "row"),
        P(),
        P(),
        P(("col", "row"), None),
    )
    return jax.shard_map(
        functools.partial(per_device, mesh.shape["col"]),
        mesh=mesh,
        in_specs=placed,
        out_specs=(P(("col", "row"), None), P(("row", "col"), None), P(), P()),
        check_vma=False,
    )
```

time: 400 us -> 97.9 us (0.24)
  waiting for transfers between devices: 199 us -> 28.5 us
  blocking collectives: 120 us -> 0 us
  Pallas kernels: 0 us -> 34.7 us
  starting transfers between devices: 0.2 us -> 28.5 us
  other arithmetic: 25.7 us -> 0.67 us
  matrix products: 19.8 us -> 0 us
  between operations: 13.9 us -> 0.96 us
  local copies, waits for them, and re-layouts: 12.2 us -> 3.67 us
  loops' own time: 6.57 us -> 0 us
    reduce_scatter x2 -> x0, waiting for transfers between devices: 130 us -> none  [the longest x1 83 us: per_device(): lax.psum_scatter(partial_value.astype(jnp.bfloat16), 'row', scatter_dimen...]
    psum x1 -> x0, blocking collectives: 120 us -> none  [per_device(): weight_grad, bias_grad = lax.psum((weight_grad, bias_grad), ('row', 'col'))]
    all_gather x2 -> x0, waiting for transfers between devices: 67.9 us -> none  [the longest x1 52.1 us: per_device(): column_block = lax.all_gather(features, 'col', axis=0, tiled=True)]
    pallas_call x0 -> x15, Pallas kernels: none -> 34.7 us  [the longest x5 14.7 us: forward(): pl.pallas_call(functools.partial(forward_kernel, [bucket], cap, n_buckets...]
    ppermute x0 -> x29, starting transfers between devices: none -> 28.5 us  [the longest x3 6.93 us: per_device(): from_left = lax.ppermute(from_left, 'col', right)]
    ppermute x0 -> x29, waiting for transfers between devices: none -> 28.5 us  [the longest x1 7.11 us: per_device(): came = lax.ppermute(own_away, 'row', across)]
    dot_general x11 -> x0, matrix products: 19.8 us -> none  [the longest x4 8.51 us: forward_slot(): jnp.einsum('tij,tjf->tif', values, picked, preferred_element_type=jnp.flo...]
    scatter-add x4 -> x0, other arithmetic: 17.2 us -> none  [backward_slot(): return running.at[columns].add(contrib)]
  transfers between devices with their start and end apart: 5 -> 29, of which waited for: 4 -> 17; matrix products, arithmetic and copies ran while one was open for 9% -> 1% of each run, Pallas kernels for 0% -> 28%
where the time goes in v3:
time: 97.9 us; the launch traced here: 96.9 us
  Pallas kernels  34.7 us (35%)
  starting transfers between devices  28.5 us (29%)
  waiting for transfers between devices  28.5 us (29%)
  local copies, waits for them, and re-layouts  3.67 us (4%)
    pallas_call x5, Pallas kernels, forward(): pl.pallas_call(functools.partial(forward_kernel, [bucket], cap, n_buckets...  14.7 us
    pallas_call x5, Pallas kernels, backward(): pl.pallas_call(functools.partial(backward_kernel, bucket, cap, n_buckets)...  14.7 us
    ppermute x1, waiting for transfers between devices, per_device(): came = lax.ppermute(own_away, 'row', across)  7.11 us
    ppermute x3, starting transfers between devices, per_device(): from_left = lax.ppermute(from_left, 'col', right)  6.93 us
    ppermute x4, waiting for transfers between devices, per_device(): to_right = lax.ppermute(sent[0], 'col', right)  4.96 us
    ppermute x4, starting transfers between devices, per_device(): to_right = lax.ppermute(sent[0], 'col', right)  4.95 us
    ppermute x1, waiting for transfers between devices, per_device(): came_away = lax.ppermute(own, 'row', across)  3.79 us
    ppermute x3, starting transfers between devices, per_device(): lax.ppermute(w_now, 'col', [(i, i ^ stages[step]) for i in range(n_col)])  3.38 us
  transfers between devices with their start and end apart: 29, of which 17 were waited for; matrix products, arithmetic and copies ran while one was open for 1% of the time, Pallas kernels for 28%

profile of v3, /device:TPU:0, one launch (start us, length us, event | category | flops | bytes accessed | tf_op | source)
XLA Modules:
  0.0 96.9 jit_solution(5203187554533288036)
XLA Ops:
  0.6 3.1 %collective-permute-start = (bf16[2,256,256]{2,1,0:T(8,128)(2,1)}, bf16[2,256,256]{2,1,0:T(8,128)(2,1)S(1)}, u32[]{:S(2)}, u32[]{:S(2)}) collective-permute-start(bf16[2,256,256]{2,1,0:T(8,128)(2,1)} %bitcast.14), channel_id=1, source_target_pairs={{0,2},{2,4},{4,6},{6,7},{7,5},{5,3},{3,1},{1,0},{8,10},{10,12},{12... | collective-permute-start | bytes 786440 | tf_op jit(solution)/shard_map/ppermute | solution.py:307
  3.7 2.0 %collective-permute-start.2 = (bf16[512,256]{1,0:T(8,128)(2,1)}, bf16[512,256]{1,0:T(8,128)(2,1)S(1)}, u32[]{:S(2)}, u32[]{:S(2)}) collective-permute-start(bf16[512,256]{1,0:T(8,128)(2,1)} %cot.1), channel_id=1, source_target_pairs={{0,16},{16,0},{8,24},{24,8},{1,17},{17,1},{9,25},{25,9},{2,18},{18... | collective-permute-start | bytes 786440 | tf_op jit(solution)/shard_map/ppermute | solution.py:310
  5.7 0.7 copy-done.3
  6.4 0.7 copy-done.5
  7.7 1.9 %lists.1 = s32[685]{0:T(1024)S(1)} custom-call(s32[8,16]{1,0:T(8,128)S(1)} %copy-done.3, s32[8]{0:T(128)S(1)} %bitcast.23, s32[160]{0:T(256)S(1)} %copy-done.5), custom_call_target="tpu_custom_call" | custom-call | bytes 4096 | tf_op jit(solution)/shard_map/lists/pallas_call | solution.py:269
  10.1 1.5 %collective-permute-done.1.refs_1_ = bf16[2,256,256]{2,1,0:T(8,128)(2,1)S(1)} collective-permute-done((bf16[2,256,256]{2,1,0:T(8,128)(2,1)}, bf16[2,256,256]{2,1,0:T(8,128)(2,1)S(1)}, u32[]{:S(2)}, u32[]{:S(2)}) %collective-permute-start.1) | collective-permute-done | bytes 262176 | tf_op jit(solution)/shard_map/ppermute | solution.py:308
  11.7 1.7 %collective-permute-start.3 = (bf16[2,256,256]{2,1,0:T(8,128)(2,1)S(1)}, bf16[2,256,256]{2,1,0:T(8,128)(2,1)S(1)}, u32[]{:S(2)}, u32[]{:S(2)}) collective-permute-start(bf16[2,256,256]{2,1,0:T(8,128)(2,1)S(1)} %collective-permute-done.refs_0_), channel_id=1, source_target_pairs={{0,2},{2,4},{4,6},{6,7},{7,5},{5,3},{3,1},{1,0},{8,10},{10,12},{12... | collective-permute-start | bytes 786440 | tf_op jit(solution)/shard_map/ppermute | solution.py:307
  13.7 0.9 copy-done.1
  14.7 3.1 %forward_0.1.refs_2_ = f32[9,256,256]{2,1,0:T(8,128)S(1)} custom-call(s32[685]{0:T(1024)S(1)} %lists.1, bf16[128,256,256]{2,1,0:T(8,128)(2,1)} %bitcast.24, bf16[2,256,256]{2,1,0:T(8,128)(2,1)S(1)} %bitcast.16), custom_call_target="tpu_custom_call" | custom-call | flops 33554432 | bytes 131072 | tf_op jit(solution)/shard_map/forward_0/pallas_call | solution.py:287
  17.8 2.8 %forward_1.1.refs_2_ = f32[9,256,256]{2,1,0:T(8,128)S(1)} custom-call(s32[685]{0:T(1024)S(1)} %lists.1, bf16[128,256,256]{2,1,0:T(8,128)(2,1)} %bitcast.25, bf16[2,256,256]{2,1,0:T(8,128)(2,1)S(1)} %collective-permute-done.refs_0_, bf16[2,256,256]{2,1,0:T(8,128)(2,1)S(1)} %collective-permute-done.1.refs_1_, f32[9,256,256]{2,1,0:T(8,128)S(1)} %forward_0.1.refs_2_), custom_call_target="tpu_custom_call" | custom-call | flops 33554432 | bytes 131072 | tf_op jit(solution)/shard_map/forward_1/pallas_call | solution.py:287
  20.6 2.1 %collective-permute-start.5 = (bf16[2,256,256]{2,1,0:T(8,128)(2,1)S(1)}, bf16[2,256,256]{2,1,0:T(8,128)(2,1)S(1)}, u32[]{:S(2)}, u32[]{:S(2)}) collective-permute-start(bf16[2,256,256]{2,1,0:T(8,128)(2,1)S(1)} %collective-permute-done.3.refs_0_), channel_id=1, source_target_pairs={{0,2},{2,4},{4,6},{6,7},{7,5},{5,3},{3,1},{1,0},{8,10},{10,12},{12... | collective-permute-start | bytes 786440 | tf_op jit(solution)/shard_map/ppermute | solution.py:307
  23.1 2.9 %forward_2.1.refs_2_ = f32[9,256,256]{2,1,0:T(8,128)S(1)} custom-call(s32[685]{0:T(1024)S(1)} %lists.1, bf16[128,256,256]{2,1,0:T(8,128)(2,1)} %bitcast.26, bf16[2,256,256]{2,1,0:T(8,128)(2,1)S(1)} %collective-permute-done.3.refs_0_, bf16[2,256,256]{2,1,0:T(8,128)(2,1)S(1)} %collective-permute-done.4.refs_1_, f32[9,256,256]{2,1,0:T(8,128)S(1)} %forward_1.1.refs_2_), custom_call_target="tpu_custom_call" | custom-call | flops 33554432 | bytes 131072 | tf_op jit(solution)/shard_map/forward_2/pallas_call | solution.py:287
  26.1 1.4 %collective-permute-done.5.refs_0_ = bf16[2,256,256]{2,1,0:T(8,128)(2,1)S(1)} collective-permute-done((bf16[2,256,256]{2,1,0:T(8,128)(2,1)S(1)}, bf16[2,256,256]{2,1,0:T(8,128)(2,1)S(1)}, u32[]{:S(2)}, u32[]{:S(2)}) %collective-permute-start.5) | collective-permute-done | bytes 262176 | tf_op jit(solution)/shard_map/ppermute | solution.py:307
  27.4 1.6 %collective-permute-done.6.refs_1_ = bf16[2,256,256]{2,1,0:T(8,128)(2,1)S(1)} collective-permute-done((bf16[2,256,256]{2,1,0:T(8,128)(2,1)S(1)}, bf16[2,256,256]{2,1,0:T(8,128)(2,1)S(1)}, u32[]{:S(2)}, u32[]{:S(2)}) %collective-permute-start.6) | collective-permute-done | bytes 262176 | tf_op jit(solution)/shard_map/ppermute | solution.py:308
  29.1 1.2 %collective-permute-start.7 = (bf16[1,256,256]{2,1,0:T(8,128)(2,1)S(1)}, bf16[1,256,256]{2,1,0:T(8,128)(2,1)S(1)}, u32[]{:S(2)}, u32[]{:S(2)}) collective-permute-start(bf16[1,256,256]{2,1,0:T(8,128)(2,1)S(1)} %slice.56), channel_id=1, source_target_pairs={{0,2},{2,4},{4,6},{6,7},{7,5},{5,3},{3,1},{1,0},{8,10},{10,12},{12... | collective-permute-start | bytes 393224 | tf_op jit(solution)/shard_map/ppermute | solution.py:319
  30.3 0.9 collective-permute-start.8
  31.2 2.8 %forward_3.1.refs_2_ = f32[9,256,256]{2,1,0:T(8,128)S(1)} custom-call(s32[685]{0:T(1024)S(1)} %lists.1, bf16[128,256,256]{2,1,0:T(8,128)(2,1)} %bitcast.27, bf16[2,256,256]{2,1,0:T(8,128)(2,1)S(1)} %collective-permute-done.5.refs_0_, bf16[2,256,256]{2,1,0:T(8,128)(2,1)S(1)} %collective-permute-done.6.refs_1_, f32[9,256,256]{2,1,0:T(8,128)S(1)} %forward_2.1.refs_2_), custom_call_target="tpu_custom_call" | custom-call | flops 33554432 | bytes 131072 | tf_op jit(solution)/shard_map/forward_3/pallas_call | solution.py:287
  34.1 1.2 %collective-permute-done.8.refs_1_ = bf16[1,256,256]{2,1,0:T(8,128)(2,1)S(1)} collective-permute-done((bf16[1,256,256]{2,1,0:T(8,128)(2,1)S(1)}, bf16[1,256,256]{2,1,0:T(8,128)(2,1)S(1)}, u32[]{:S(2)}, u32[]{:S(2)}) %collective-permute-start.8) | collective-permute-done | bytes 131104 | tf_op jit(solution)/shard_map/ppermute | solution.py:320
  35.3 3.1 %forward_4.1 = (bf16[4,256,256]{2,1,0:T(8,128)(2,1)S(1)}, bf16[4,256,256]{2,1,0:T(8,128)(2,1)S(1)}) custom-call(s32[685]{0:T(1024)S(1)} %lists.1, bf16[128,256,256]{2,1,0:T(8,128)(2,1)} %bitcast.28, bf16[1,256,256]{2,1,0:T(8,128)(2,1)S(1)} %collective-permute-done.7.refs_0_, bf16[1,256,256]{2,1,0:T(8,128)(2,1)S(1)} %collective-permute-done.8.refs_1_, ...), custom_call_target="tpu_custom_call" | custom-call | flops 33554432 | bytes 131072 | tf_op jit(solution)/shard_map/forward_4/pallas_call | solution.py:287
  38.6 1.9 %collective-permute-done.9 = bf16[4,256,256]{2,1,0:T(8,128)(2,1)S(1)} collective-permute-done((bf16[4,256,256]{2,1,0:T(8,128)(2,1)S(1)}, bf16[4,256,256]{2,1,0:T(8,128)(2,1)S(1)}, u32[]{:S(2)}, u32[]{:S(2)}) %collective-permute-start.9) | collective-permute-done | bytes 524320 | tf_op jit(solution)/shard_map/ppermute | solution.py:324
  40.7 1.9 %collective-permute-start.11 = (bf16[2,256,256]{2,1,0:T(8,128)(2,1)S(1)}, bf16[2,256,256]{2,1,0:T(8,128)(2,1)S(1)}, u32[]{:S(2)}, u32[]{:S(2)}) collective-permute-start(bf16[2,256,256]{2,1,0:T(8,128)(2,1)S(1)} %get-tuple-element.122.near), channel_id=1, source_target_pairs={{0,16},{16,0},{8,24},{24,8},{1,17},{17,1},{9,25},{25,9},{2,18},{18... | collective-permute-start | bytes 786440 | tf_op jit(solution)/shard_map/ppermute | solution.py:328
  42.7 7.1 %collective-permute-done.11.away = bf16[2,256,256]{2,1,0:T(8,128)(2,1)S(1)} collective-permute-done((bf16[2,256,256]{2,1,0:T(8,128)(2,1)S(1)}, bf16[2,256,256]{2,1,0:T(8,128)(2,1)S(1)}, u32[]{:S(2)}, u32[]{:S(2)}) %collective-permute-start.11) | collective-permute-done | bytes 262176 | tf_op jit(solution)/shard_map/ppermute | solution.py:328
  49.9 1.2 %dense_own.1 = (bf16[512,256]{1,0:T(8,128)(2,1)}, bf16[2,256,256]{2,1,0:T(8,128)(2,1)S(1)}, f32[264,256]{1,0:T(8,128)S(1)}) custom-call(bf16[2,256,256]{2,1,0:T(8,128)(2,1)S(1)} %get-tuple-element.123.near, bf16[2,256,256]{2,1,0:T(8,128)(2,1)S(1)} %collective-permute-done.11.away, bf16[256,256]{1,0:T(8,128)(2,1)S(1)} %copy-done, f32[1,256]{1,0:T(1,128)S(1)} %bitcast.21, ...), custom_call_target="tpu_custom_call" | custom-call | flops 50331648 | bytes 131072 | tf_op jit(solution)/shard_map/dense_own/pallas_call | solution.py:335
  51.0 3.8 %collective-permute-done.10.away = bf16[2,256,256]{2,1,0:T(8,128)(2,1)S(1)} collective-permute-done((bf16[2,256,256]{2,1,0:T(8,128)(2,1)S(1)}, bf16[2,256,256]{2,1,0:T(8,128)(2,1)S(1)}, u32[]{:S(2)}, u32[]{:S(2)}) %collective-permute-start.10) | collective-permute-done | bytes 262176 | tf_op jit(solution)/shard_map/ppermute | solution.py:329
  56.1 0.8 collective-permute-done.16
  57.2 3.1 %backward_4.1 = f32[2,256,256]{2,1,0:T(8,128)S(1)} custom-call(s32[685]{0:T(1024)S(1)} %lists.1, bf16[128,256,256]{2,1,0:T(8,128)(2,1)} %bitcast.29, bf16[2,256,256]{2,1,0:T(8,128)(2,1)S(1)} %get-tuple-element.74.refs_0_, bf16[2,256,256]{2,1,0:T(8,128)(2,1)S(1)} %get-tuple-element.78.refs_1_, bf16[2,256,256]{2,1,0:T(8,128)(2,1)S(1)} %collective-permute-done.12.refs_2_, ...), custom_call_target="tpu_custom_call" | custom-call | flops 33554432 | bytes 131072 | tf_op jit(solution)/shard_map/backward_4/pallas_call | solution.py:372
  60.6 2.1 %collective-permute-start.14 = (bf16[1,256,256]{2,1,0:T(8,128)(2,1)S(1)}, bf16[1,256,256]{2,1,0:T(8,128)(2,1)S(1)}, u32[]{:S(2)}, u32[]{:S(2)}) collective-permute-start(bf16[1,256,256]{2,1,0:T(8,128)(2,1)S(1)} %get-tuple-element.80), channel_id=1, source_target_pairs={{0,2},{2,4},{4,6},{6,7},{7,5},{5,3},{3,1},{1,0},{8,10},{10,12},{12... | collective-permute-start | bytes 393224 | tf_op jit(solution)/shard_map/ppermute | solution.py:393
  62.7 2.8 %backward_3.1 = f32[4,256,256]{2,1,0:T(8,128)S(1)} custom-call(s32[685]{0:T(1024)S(1)} %lists.1, bf16[128,256,256]{2,1,0:T(8,128)(2,1)} %bitcast.30, bf16[2,256,256]{2,1,0:T(8,128)(2,1)S(1)} %get-tuple-element.74.refs_0_, bf16[2,256,256]{2,1,0:T(8,128)(2,1)S(1)} %get-tuple-element.78.refs_1_, bf16[2,256,256]{2,1,0:T(8,128)(2,1)S(1)} %collective-permute-done.12.refs_2_, ...), custom_call_target="tpu_custom_call" | custom-call | flops 33554432 | bytes 131072 | tf_op jit(solution)/shard_map/backward_3/pallas_call | solution.py:372
  65.5 1.6 %collective-permute-done.14 = bf16[1,256,256]{2,1,0:T(8,128)(2,1)S(1)} collective-permute-done((bf16[1,256,256]{2,1,0:T(8,128)(2,1)S(1)}, bf16[1,256,256]{2,1,0:T(8,128)(2,1)S(1)}, u32[]{:S(2)}, u32[]{:S(2)}) %collective-permute-start.14) | collective-permute-done | bytes 131104 | tf_op jit(solution)/shard_map/ppermute | solution.py:393
  67.1 1.1 %collective-permute-done.15 = bf16[1,256,256]{2,1,0:T(8,128)(2,1)S(1)} collective-permute-done((bf16[1,256,256]{2,1,0:T(8,128)(2,1)S(1)}, bf16[1,256,256]{2,1,0:T(8,128)(2,1)S(1)}, u32[]{:S(2)}, u32[]{:S(2)}) %collective-permute-start.15) | collective-permute-done | bytes 131104 | tf_op jit(solution)/shard_map/ppermute | solution.py:394
  68.3 1.4 %collective-permute-start.20 = (bf16[80,256]{1,0:T(8,128)(2,1)S(1)}, bf16[80,256]{1,0:T(8,128)(2,1)S(1)}, u32[]{:S(2)}, u32[]{:S(2)}) collective-permute-start(bf16[80,256]{1,0:T(8,128)(2,1)S(1)} %convert_add_fusion.2), channel_id=1, source_target_pairs={{0,2},{1,3},{2,0},{3,1},{4,6},{5,7},{6,4},{7,5},{8,10},{9,11},{10,... | collective-permute-start | bytes 122888 | tf_op jit(solution)/shard_map/ppermute | solution.py:399
  69.7 0.7 collective-permute-start.18
  70.4 1.3 %collective-permute-start.19 = (bf16[2,256,256]{2,1,0:T(8,128)(2,1)S(1)}, bf16[2,256,256]{2,1,0:T(8,128)(2,1)S(1)}, u32[]{:S(2)}, u32[]{:S(2)}) collective-permute-start(bf16[2,256,256]{2,1,0:T(8,128)(2,1)S(1)} %get-tuple-element.89), channel_id=1, source_target_pairs={{2,0},{4,2},{6,4},{7,6},{5,7},{3,5},{1,3},{0,1},{10,8},{12,10},{14... | collective-permute-start | bytes 786440 | tf_op jit(solution)/shard_map/ppermute | solution.py:394
  71.8 2.9 %backward_2.1 = f32[4,256,256]{2,1,0:T(8,128)S(1)} custom-call(s32[685]{0:T(1024)S(1)} %lists.1, bf16[128,256,256]{2,1,0:T(8,128)(2,1)} %bitcast.31, bf16[2,256,256]{2,1,0:T(8,128)(2,1)S(1)} %get-tuple-element.74.refs_0_, bf16[2,256,256]{2,1,0:T(8,128)(2,1)S(1)} %get-tuple-element.78.refs_1_, bf16[2,256,256]{2,1,0:T(8,128)(2,1)S(1)} %collective-permute-done.12.refs_2_, ...), custom_call_target="tpu_custom_call" | custom-call | flops 33554432 | bytes 131072 | tf_op jit(solution)/shard_map/backward_2/pallas_call | solution.py:372
  74.7 1.9 %collective-permute-done.18 = bf16[2,256,256]{2,1,0:T(8,128)(2,1)S(1)} collective-permute-done((bf16[2,256,256]{2,1,0:T(8,128)(2,1)S(1)}, bf16[2,256,256]{2,1,0:T(8,128)(2,1)S(1)}, u32[]{:S(2)}, u32[]{:S(2)}) %collective-permute-start.18) | collective-permute-done | bytes 262176 | tf_op jit(solution)/shard_map/ppermute | solution.py:393
  76.6 1.2 %collective-permute-done.19 = bf16[2,256,256]{2,1,0:T(8,128)(2,1)S(1)} collective-permute-done((bf16[2,256,256]{2,1,0:T(8,128)(2,1)S(1)}, bf16[2,256,256]{2,1,0:T(8,128)(2,1)S(1)}, u32[]{:S(2)}, u32[]{:S(2)}) %collective-permute-start.19) | collective-permute-done | bytes 262176 | tf_op jit(solution)/shard_map/ppermute | solution.py:394
  77.9 1.7 %collective-permute-start.23 = (bf16[80,256]{1,0:T(8,128)(2,1)S(1)}, bf16[80,256]{1,0:T(8,128)(2,1)S(1)}, u32[]{:S(2)}, u32[]{:S(2)}) collective-permute-start(bf16[80,256]{1,0:T(8,128)(2,1)S(1)} %convert_add_fusion.1), channel_id=1, source_target_pairs={{0,4},{1,5},{2,6},{3,7},{4,0},{5,1},{6,2},{7,3},{8,12},{9,13},{10,... | collective-permute-start | bytes 122888 | tf_op jit(solution)/shard_map/ppermute | solution.py:399
  79.6 0.9 collective-permute-start.21
  80.5 1.1 %collective-permute-start.22 = (bf16[2,256,256]{2,1,0:T(8,128)(2,1)S(1)}, bf16[2,256,256]{2,1,0:T(8,128)(2,1)S(1)}, u32[]{:S(2)}, u32[]{:S(2)}) collective-permute-start(bf16[2,256,256]{2,1,0:T(8,128)(2,1)S(1)} %get-tuple-element.97), channel_id=1, source_target_pairs={{2,0},{4,2},{6,4},{7,6},{5,7},{3,5},{1,3},{0,1},{10,8},{12,10},{14... | collective-permute-start | bytes 786440 | tf_op jit(solution)/shard_map/ppermute | solution.py:394
  81.6 2.8 %backward_1.1 = f32[4,256,256]{2,1,0:T(8,128)S(1)} custom-call(s32[685]{0:T(1024)S(1)} %lists.1, bf16[128,256,256]{2,1,0:T(8,128)(2,1)} %bitcast.32, bf16[2,256,256]{2,1,0:T(8,128)(2,1)S(1)} %get-tuple-element.74.refs_0_, bf16[2,256,256]{2,1,0:T(8,128)(2,1)S(1)} %get-tuple-element.78.refs_1_, bf16[2,256,256]{2,1,0:T(8,128)(2,1)S(1)} %collective-permute-done.12.refs_2_, ...), custom_call_target="tpu_custom_call" | custom-call | flops 33554432 | bytes 131072 | tf_op jit(solution)/shard_map/backward_1/pallas_call | solution.py:372
  84.5 1.5 %collective-permute-done.21 = bf16[2,256,256]{2,1,0:T(8,128)(2,1)S(1)} collective-permute-done((bf16[2,256,256]{2,1,0:T(8,128)(2,1)S(1)}, bf16[2,256,256]{2,1,0:T(8,128)(2,1)S(1)}, u32[]{:S(2)}, u32[]{:S(2)}) %collective-permute-start.21) | collective-permute-done | bytes 262176 | tf_op jit(solution)/shard_map/ppermute | solution.py:393
  86.0 0.9 collective-permute-done.22
  87.0 1.3 %collective-permute-start.24 = (bf16[2,256,256]{2,1,0:T(8,128)(2,1)S(1)}, bf16[2,256,256]{2,1,0:T(8,128)(2,1)S(1)}, u32[]{:S(2)}, u32[]{:S(2)}) collective-permute-start(bf16[2,256,256]{2,1,0:T(8,128)(2,1)S(1)} %get-tuple-element.104), channel_id=1, source_target_pairs={{0,2},{2,4},{4,6},{6,7},{7,5},{5,3},{3,1},{1,0},{8,10},{10,12},{12... | collective-permute-start | bytes 786440 | tf_op jit(solution)/shard_map/ppermute | solution.py:393
  88.3 0.8 collective-permute-start.25
  89.1 2.2 %collective-permute-start.26 = (f32[64,256]{1,0:T(8,128)S(1)}, f32[64,256]{1,0:T(8,128)S(1)}, u32[]{:S(2)}, u32[]{:S(2)}) collective-permute-start(f32[64,256]{1,0:T(8,128)S(1)} %slice.70.own), channel_id=1, source_target_pairs={{0,16},{16,0},{8,24},{24,8},{1,17},{17,1},{9,25},{25,9},{2,18},{18... | collective-permute-start | bytes 196616 | tf_op jit(solution)/shard_map/ppermute | solution.py:404
  92.1 3.1 %backward_0.1.own = f32[2,256,256]{2,1,0:T(8,128)S(1)} custom-call(s32[685]{0:T(1024)S(1)} %lists.1, bf16[128,256,256]{2,1,0:T(8,128)(2,1)} %bitcast.33, bf16[2,256,256]{2,1,0:T(8,128)(2,1)S(1)} %get-tuple-element.74.refs_0_, bf16[2,256,256]{2,1,0:T(8,128)(2,1)S(1)} %get-tuple-element.78.refs_1_, bf16[2,256,256]{2,1,0:T(8,128)(2,1)S(1)} %collective-permute-done.12.refs_2_, ...), custom_call_target="tpu_custom_call" | custom-call | flops 33554432 | bytes 131072 | tf_op jit(solution)/shard_map/backward_0/pallas_call | solution.py:372
  95.3 0.7 quarters.1
  96.1 0.9 finish.1
  (59 shorter events, 5.7 us)
Async XLA Ops:
  0.6 9.5 %collective-permute-start = (bf16[2,256,256]{2,1,0:T(8,128)(2,1)}, bf16[2,256,256]{2,1,0:T(8,128)(2,1)S(1)}, u32[]{:S(2)}, u32[]{:S(2)}) collective-permute-start(bf16[2,256,256]{2,1,0:T(8,128)(2,1)} %bitcast.14), channel_id=1, source_target_pairs={{0,2},{2,4},{4,6},{6,7},{7,5},{5,3},{3,1},{1,0},{8,10},{10,12},{12... | collective-permute-start | bytes 786440 | tf_op jit(solution)/shard_map/ppermute | solution.py:307
  3.7 8.0 %collective-permute-start.1 = (bf16[2,256,256]{2,1,0:T(8,128)(2,1)}, bf16[2,256,256]{2,1,0:T(8,128)(2,1)S(1)}, u32[]{:S(2)}, u32[]{:S(2)}) collective-permute-start(bf16[2,256,256]{2,1,0:T(8,128)(2,1)} %bitcast.15), channel_id=1, source_target_pairs={{2,0},{4,2},{6,4},{7,6},{5,7},{3,5},{1,3},{0,1},{10,8},{12,10},{14... | collective-permute-start | bytes 786440 | tf_op jit(solution)/shard_map/ppermute | solution.py:308
  3.7 8.0 %collective-permute-start.2 = (bf16[512,256]{1,0:T(8,128)(2,1)}, bf16[512,256]{1,0:T(8,128)(2,1)S(1)}, u32[]{:S(2)}, u32[]{:S(2)}) collective-permute-start(bf16[512,256]{1,0:T(8,128)(2,1)} %cot.1), channel_id=1, source_target_pairs={{0,16},{16,0},{8,24},{24,8},{1,17},{17,1},{9,25},{25,9},{2,18},{18... | collective-permute-start | bytes 786440 | tf_op jit(solution)/shard_map/ppermute | solution.py:310
  5.7 0.7 copy-start.3
  6.4 0.7 copy-start.5
  7.0 0.7 copy-start.6
  11.7 8.9 %collective-permute-start.3 = (bf16[2,256,256]{2,1,0:T(8,128)(2,1)S(1)}, bf16[2,256,256]{2,1,0:T(8,128)(2,1)S(1)}, u32[]{:S(2)}, u32[]{:S(2)}) collective-permute-start(bf16[2,256,256]{2,1,0:T(8,128)(2,1)S(1)} %collective-permute-done.refs_0_), channel_id=1, source_target_pairs={{0,2},{2,4},{4,6},{6,7},{7,5},{5,3},{3,1},{1,0},{8,10},{10,12},{12... | collective-permute-start | bytes 786440 | tf_op jit(solution)/shard_map/ppermute | solution.py:307
  13.4 7.1 %collective-permute-start.4 = (bf16[2,256,256]{2,1,0:T(8,128)(2,1)S(1)}, bf16[2,256,256]{2,1,0:T(8,128)(2,1)S(1)}, u32[]{:S(2)}, u32[]{:S(2)}) collective-permute-start(bf16[2,256,256]{2,1,0:T(8,128)(2,1)S(1)} %collective-permute-done.1.refs_1_), channel_id=1, source_target_pairs={{2,0},{4,2},{6,4},{7,6},{5,7},{3,5},{1,3},{0,1},{10,8},{12,10},{14... | collective-permute-start | bytes 786440 | tf_op jit(solution)/shard_map/ppermute | solution.py:308
  13.7 0.9 copy-start.1
  20.6 6.8 %collective-permute-start.5 = (bf16[2,256,256]{2,1,0:T(8,128)(2,1)S(1)}, bf16[2,256,256]{2,1,0:T(8,128)(2,1)S(1)}, u32[]{:S(2)}, u32[]{:S(2)}) collective-permute-start(bf16[2,256,256]{2,1,0:T(8,128)(2,1)S(1)} %collective-permute-done.3.refs_0_), channel_id=1, source_target_pairs={{0,2},{2,4},{4,6},{6,7},{7,5},{5,3},{3,1},{1,0},{8,10},{10,12},{12... | collective-permute-start | bytes 786440 | tf_op jit(solution)/shard_map/ppermute | solution.py:307
  22.7 6.4 %collective-permute-start.6 = (bf16[2,256,256]{2,1,0:T(8,128)(2,1)S(1)}, bf16[2,256,256]{2,1,0:T(8,128)(2,1)S(1)}, u32[]{:S(2)}, u32[]{:S(2)}) collective-permute-start(bf16[2,256,256]{2,1,0:T(8,128)(2,1)S(1)} %collective-permute-done.4.refs_1_), channel_id=1, source_target_pairs={{2,0},{4,2},{6,4},{7,6},{5,7},{3,5},{1,3},{0,1},{10,8},{12,10},{14... | collective-permute-start | bytes 786440 | tf_op jit(solution)/shard_map/ppermute | solution.py:308
  29.1 5.0 %collective-permute-start.7 = (bf16[1,256,256]{2,1,0:T(8,128)(2,1)S(1)}, bf16[1,256,256]{2,1,0:T(8,128)(2,1)S(1)}, u32[]{:S(2)}, u32[]{:S(2)}) collective-permute-start(bf16[1,256,256]{2,1,0:T(8,128)(2,1)S(1)} %slice.56), channel_id=1, source_target_pairs={{0,2},{2,4},{4,6},{6,7},{7,5},{5,3},{3,1},{1,0},{8,10},{10,12},{12... | collective-permute-start | bytes 393224 | tf_op jit(solution)/shard_map/ppermute | solution.py:319
  30.3 5.0 %collective-permute-start.8 = (bf16[1,256,256]{2,1,0:T(8,128)(2,1)S(1)}, bf16[1,256,256]{2,1,0:T(8,128)(2,1)S(1)}, u32[]{:S(2)}, u32[]{:S(2)}) collective-permute-start(bf16[1,256,256]{2,1,0:T(8,128)(2,1)S(1)} %slice.57), channel_id=1, source_target_pairs={{2,0},{4,2},{6,4},{7,6},{5,7},{3,5},{1,3},{0,1},{10,8},{12,10},{14... | collective-permute-start | bytes 393224 | tf_op jit(solution)/shard_map/ppermute | solution.py:320
  38.5 11.4 %copy-start = (bf16[256,256]{1,0:T(8,128)(2,1)S(1)}, bf16[256,256]{1,0:T(8,128)(2,1)}, u32[]{:S(2)}) copy-start(bf16[256,256]{1,0:T(8,128)(2,1)} %weight.3) | copy-start | bytes 393220
  38.5 11.4 %copy-start.2 = (bf16[512,256]{1,0:T(8,128)(2,1)S(1)}, bf16[512,256]{1,0:T(8,128)(2,1)}, u32[]{:S(2)}) copy-start(bf16[512,256]{1,0:T(8,128)(2,1)} %cot.1) | copy-start | bytes 786436
  38.5 11.4 %copy-start.4 = (f32[256]{0:T(256)S(1)}, f32[256]{0:T(256)}, u32[]{:S(2)}) copy-start(f32[256]{0:T(256)} %param.13) | copy-start | bytes 3076
  38.5 2.0 %collective-permute-start.9 = (bf16[4,256,256]{2,1,0:T(8,128)(2,1)S(1)}, bf16[4,256,256]{2,1,0:T(8,128)(2,1)S(1)}, u32[]{:S(2)}, u32[]{:S(2)}) collective-permute-start(bf16[4,256,256]{2,1,0:T(8,128)(2,1)S(1)} %get-tuple-element.69), channel_id=1, source_target_pairs={{0,8},{8,0},{16,24},{24,16},{1,9},{9,1},{17,25},{25,17},{2,10},{10... | collective-permute-start | bytes 1572872 | tf_op jit(solution)/shard_map/ppermute | solution.py:324
  40.7 9.2 %collective-permute-start.11 = (bf16[2,256,256]{2,1,0:T(8,128)(2,1)S(1)}, bf16[2,256,256]{2,1,0:T(8,128)(2,1)S(1)}, u32[]{:S(2)}, u32[]{:S(2)}) collective-permute-start(bf16[2,256,256]{2,1,0:T(8,128)(2,1)S(1)} %get-tuple-element.122.near), channel_id=1, source_target_pairs={{0,16},{16,0},{8,24},{24,8},{1,17},{17,1},{9,25},{25,9},{2,18},{18... | collective-permute-start | bytes 786440 | tf_op jit(solution)/shard_map/ppermute | solution.py:328
  42.6 12.2 %collective-permute-start.10 = (bf16[2,256,256]{2,1,0:T(8,128)(2,1)S(1)}, bf16[2,256,256]{2,1,0:T(8,128)(2,1)S(1)}, u32[]{:S(2)}, u32[]{:S(2)}) collective-permute-start(bf16[2,256,256]{2,1,0:T(8,128)(2,1)S(1)} %get-tuple-element.123.near), channel_id=1, source_target_pairs={{0,16},{16,0},{8,24},{24,8},{1,17},{17,1},{9,25},{25,9},{2,18},{18... | collective-permute-start | bytes 786440 | tf_op jit(solution)/shard_map/ppermute | solution.py:329
  51.0 3.8 %collective-permute-start.12 = (bf16[2,256,256]{2,1,0:T(8,128)(2,1)S(1)}, bf16[2,256,256]{2,1,0:T(8,128)(2,1)S(1)}, u32[]{:S(2)}, u32[]{:S(2)}) collective-permute-start(bf16[2,256,256]{2,1,0:T(8,128)(2,1)S(1)} %get-tuple-element.74.refs_0_), channel_id=1, source_target_pairs={{0,8},{8,0},{16,24},{24,16},{1,9},{9,1},{17,25},{25,17},{2,10},{10... | collective-permute-start | bytes 786440 | tf_op jit(solution)/shard_map/ppermute | solution.py:348
  55.5 1.3 %collective-permute-start.16 = (f32[80,256]{1,0:T(8,128)S(1)}, f32[80,256]{1,0:T(8,128)S(1)}, u32[]{:S(2)}, u32[]{:S(2)}) collective-permute-start(f32[80,256]{1,0:T(8,128)S(1)} %dynamic-slice_bitcast_fusion), channel_id=1, source_target_pairs={{0,8},{8,0},{16,24},{24,16},{1,9},{9,1},{17,25},{25,17},{2,10},{10... | collective-permute-start | bytes 245768 | tf_op jit(solution)/shard_map/ppermute | solution.py:368
  55.6 1.7 %collective-permute-start.13 = (bf16[2,256,256]{2,1,0:T(8,128)(2,1)S(1)}, bf16[2,256,256]{2,1,0:T(8,128)(2,1)S(1)}, u32[]{:S(2)}, u32[]{:S(2)}) collective-permute-start(bf16[2,256,256]{2,1,0:T(8,128)(2,1)S(1)} %get-tuple-element.78.refs_1_), channel_id=1, source_target_pairs={{0,8},{8,0},{16,24},{24,16},{1,9},{9,1},{17,25},{25,17},{2,10},{10... | collective-permute-start | bytes 786440 | tf_op jit(solution)/shard_map/ppermute | solution.py:361
  60.4 5.1 %collective-permute-start.17 = (bf16[80,256]{1,0:T(8,128)(2,1)S(1)}, bf16[80,256]{1,0:T(8,128)(2,1)S(1)}, u32[]{:S(2)}, u32[]{:S(2)}) collective-permute-start(bf16[80,256]{1,0:T(8,128)(2,1)S(1)} %fusion), channel_id=1, source_target_pairs={{0,1},{1,0},{2,3},{3,2},{4,5},{5,4},{6,7},{7,6},{8,9},{9,8},{10,11... | collective-permute-start | bytes 122888 | tf_op jit(solution)/shard_map/ppermute | solution.py:399
  60.6 6.4 %collective-permute-start.14 = (bf16[1,256,256]{2,1,0:T(8,128)(2,1)S(1)}, bf16[1,256,256]{2,1,0:T(8,128)(2,1)S(1)}, u32[]{:S(2)}, u32[]{:S(2)}) collective-permute-start(bf16[1,256,256]{2,1,0:T(8,128)(2,1)S(1)} %get-tuple-element.80), channel_id=1, source_target_pairs={{0,2},{2,4},{4,6},{6,7},{7,5},{5,3},{3,1},{1,0},{8,10},{10,12},{12... | collective-permute-start | bytes 393224 | tf_op jit(solution)/shard_map/ppermute | solution.py:393
  62.7 5.5 %collective-permute-start.15 = (bf16[1,256,256]{2,1,0:T(8,128)(2,1)S(1)}, bf16[1,256,256]{2,1,0:T(8,128)(2,1)S(1)}, u32[]{:S(2)}, u32[]{:S(2)}) collective-permute-start(bf16[1,256,256]{2,1,0:T(8,128)(2,1)S(1)} %get-tuple-element.81), channel_id=1, source_target_pairs={{2,0},{4,2},{6,4},{7,6},{5,7},{3,5},{1,3},{0,1},{10,8},{12,10},{14... | collective-permute-start | bytes 393224 | tf_op jit(solution)/shard_map/ppermute | solution.py:394
  68.3 6.3 %collective-permute-start.20 = (bf16[80,256]{1,0:T(8,128)(2,1)S(1)}, bf16[80,256]{1,0:T(8,128)(2,1)S(1)}, u32[]{:S(2)}, u32[]{:S(2)}) collective-permute-start(bf16[80,256]{1,0:T(8,128)(2,1)S(1)} %convert_add_fusion.2), channel_id=1, source_target_pairs={{0,2},{1,3},{2,0},{3,1},{4,6},{5,7},{6,4},{7,5},{8,10},{9,11},{10,... | collective-permute-start | bytes 122888 | tf_op jit(solution)/shard_map/ppermute | solution.py:399
  69.7 6.9 %collective-permute-start.18 = (bf16[2,256,256]{2,1,0:T(8,128)(2,1)S(1)}, bf16[2,256,256]{2,1,0:T(8,128)(2,1)S(1)}, u32[]{:S(2)}, u32[]{:S(2)}) collective-permute-start(bf16[2,256,256]{2,1,0:T(8,128)(2,1)S(1)} %get-tuple-element.88), channel_id=1, source_target_pairs={{0,2},{2,4},{4,6},{6,7},{7,5},{5,3},{3,1},{1,0},{8,10},{10,12},{12... | collective-permute-start | bytes 786440 | tf_op jit(solution)/shard_map/ppermute | solution.py:393
  70.4 7.3 %collective-permute-start.19 = (bf16[2,256,256]{2,1,0:T(8,128)(2,1)S(1)}, bf16[2,256,256]{2,1,0:T(8,128)(2,1)S(1)}, u32[]{:S(2)}, u32[]{:S(2)}) collective-permute-start(bf16[2,256,256]{2,1,0:T(8,128)(2,1)S(1)} %get-tuple-element.89), channel_id=1, source_target_pairs={{2,0},{4,2},{6,4},{7,6},{5,7},{3,5},{1,3},{0,1},{10,8},{12,10},{14... | collective-permute-start | bytes 786440 | tf_op jit(solution)/shard_map/ppermute | solution.py:394
  77.9 6.6 %collective-permute-start.23 = (bf16[80,256]{1,0:T(8,128)(2,1)S(1)}, bf16[80,256]{1,0:T(8,128)(2,1)S(1)}, u32[]{:S(2)}, u32[]{:S(2)}) collective-permute-start(bf16[80,256]{1,0:T(8,128)(2,1)S(1)} %convert_add_fusion.1), channel_id=1, source_target_pairs={{0,4},{1,5},{2,6},{3,7},{4,0},{5,1},{6,2},{7,3},{8,12},{9,13},{10,... | collective-permute-start | bytes 122888 | tf_op jit(solution)/shard_map/ppermute | solution.py:399
  79.6 6.4 %collective-permute-start.21 = (bf16[2,256,256]{2,1,0:T(8,128)(2,1)S(1)}, bf16[2,256,256]{2,1,0:T(8,128)(2,1)S(1)}, u32[]{:S(2)}, u32[]{:S(2)}) collective-permute-start(bf16[2,256,256]{2,1,0:T(8,128)(2,1)S(1)} %get-tuple-element.96), channel_id=1, source_target_pairs={{0,2},{2,4},{4,6},{6,7},{7,5},{5,3},{3,1},{1,0},{8,10},{10,12},{12... | collective-permute-start | bytes 786440 | tf_op jit(solution)/shard_map/ppermute | solution.py:393
  80.5 6.4 %collective-permute-start.22 = (bf16[2,256,256]{2,1,0:T(8,128)(2,1)S(1)}, bf16[2,256,256]{2,1,0:T(8,128)(2,1)S(1)}, u32[]{:S(2)}, u32[]{:S(2)}) collective-permute-start(bf16[2,256,256]{2,1,0:T(8,128)(2,1)S(1)} %get-tuple-element.97), channel_id=1, source_target_pairs={{2,0},{4,2},{6,4},{7,6},{5,7},{3,5},{1,3},{0,1},{10,8},{12,10},{14... | collective-permute-start | bytes 786440 | tf_op jit(solution)/shard_map/ppermute | solution.py:394
  87.0 9.0 %collective-permute-start.24 = (bf16[2,256,256]{2,1,0:T(8,128)(2,1)S(1)}, bf16[2,256,256]{2,1,0:T(8,128)(2,1)S(1)}, u32[]{:S(2)}, u32[]{:S(2)}) collective-permute-start(bf16[2,256,256]{2,1,0:T(8,128)(2,1)S(1)} %get-tuple-element.104), channel_id=1, source_target_pairs={{0,2},{2,4},{4,6},{6,7},{7,5},{5,3},{3,1},{1,0},{8,10},{10,12},{12... | collective-permute-start | bytes 786440 | tf_op jit(solution)/shard_map/ppermute | solution.py:393
  88.3 7.8 %collective-permute-start.25 = (bf16[2,256,256]{2,1,0:T(8,128)(2,1)S(1)}, bf16[2,256,256]{2,1,0:T(8,128)(2,1)S(1)}, u32[]{:S(2)}, u32[]{:S(2)}) collective-permute-start(bf16[2,256,256]{2,1,0:T(8,128)(2,1)S(1)} %get-tuple-element.105), channel_id=1, source_target_pairs={{2,0},{4,2},{6,4},{7,6},{5,7},{3,5},{1,3},{0,1},{10,8},{12,10},{14... | collective-permute-start | bytes 786440 | tf_op jit(solution)/shard_map/ppermute | solution.py:394
  89.1 6.1 %collective-permute-start.26 = (f32[64,256]{1,0:T(8,128)S(1)}, f32[64,256]{1,0:T(8,128)S(1)}, u32[]{:S(2)}, u32[]{:S(2)}) collective-permute-start(f32[64,256]{1,0:T(8,128)S(1)} %slice.70.own), channel_id=1, source_target_pairs={{0,16},{16,0},{8,24},{24,8},{1,17},{17,1},{9,25},{25,9},{2,18},{18... | collective-permute-start | bytes 196616 | tf_op jit(solution)/shard_map/ppermute | solution.py:404
  91.4 3.9 %collective-permute-start.27 = (f32[64,256]{1,0:T(8,128)S(1)}, f32[64,256]{1,0:T(8,128)S(1)}, u32[]{:S(2)}, u32[]{:S(2)}) collective-permute-start(f32[64,256]{1,0:T(8,128)S(1)} %slice.70.own), channel_id=1, source_target_pairs={{0,8},{8,0},{16,24},{24,16},{1,9},{9,1},{17,25},{25,17},{2,10},{10... | collective-permute-start | bytes 196616 | tf_op jit(solution)/shard_map/ppermute | solution.py:404
  91.4 3.9 %collective-permute-start.28 = (f32[64,256]{1,0:T(8,128)S(1)}, f32[64,256]{1,0:T(8,128)S(1)}, u32[]{:S(2)}, u32[]{:S(2)}) collective-permute-start(f32[64,256]{1,0:T(8,128)S(1)} %slice.70.own), channel_id=1, source_target_pairs={{0,24},{24,0},{8,16},{16,8},{1,25},{25,1},{9,17},{17,9},{2,26},{26... | collective-permute-start | bytes 196616 | tf_op jit(solution)/shard_map/ppermute | solution.py:404

commit v4 on v3

--- a/solution.py
+++ b/solution.py
@@ -13,6 +13,7 @@
 F32 = jnp.float32
 UNIT = 8
 DEPTH = 5
+AHEAD = 2
 
 VMEM = pl.BlockSpec(memory_space=pltpu.VMEM)
 SMEM = pl.BlockSpec(memory_space=pltpu.SMEM)
@@ -32,7 +33,8 @@
     return pl.CostEstimate(flops=int(flops), bytes_accessed=int(nbytes), transcendentals=0)
 
 
-def lists_kernel(n_buckets, cap, col_tiles, place_base, cols, counts, tables, lists):
+def lists_kernel(n_buckets, cap, col_tiles, place_base, cols, counts, tables, block, lists, kept):
+    kept[...] = block[...]
     row_tiles, slots = cols.shape
     ends = n_buckets * cap
     first_place = place_base + lax.axis_index("col") * col_tiles
@@ -67,7 +69,12 @@
         lists[ends + b] = units
 
 
-def stream(lists, buckets, cap, n_buckets, values, buffer, sems, between, use):
+def unit_copies(lists, first, at, values, buffer, sems):
+    for u in range(UNIT):
+        yield pltpu.make_async_copy(values.at[lists[first + u] // 65536], buffer.at[at + u], sems.at[at + u])
+
+
+def stream(lists, buckets, cap, n_buckets, values, buffer, sems, between, use, skip=0):
     ends = []
     for b in buckets:
         n = lists[n_buckets * cap + b]
@@ -81,17 +88,14 @@
         return first
 
     def copies(g):
-        first = locate(g)
-        at = lax.rem(g, DEPTH) * UNIT
-        for u in range(UNIT):
-            yield pltpu.make_async_copy(values.at[lists[first + u] // 65536], buffer.at[at + u], sems.at[at + u])
+        return unit_copies(lists, locate(g), lax.rem(g, DEPTH) * UNIT, values, buffer, sems)
 
     def ahead(g, _):
         for c in copies(g):
             c.start()
         return 0
 
-    lax.fori_loop(0, jnp.minimum(total, DEPTH - 1), ahead, 0)
+    lax.fori_loop(skip, jnp.minimum(total, skip + DEPTH - 1), ahead, 0)
     between()
 
     def step(g, _):
@@ -101,10 +105,10 @@
 
         for c in copies(g):
             c.wait()
-        use(locate(g), lax.rem(g, DEPTH) * UNIT)
+        use(locate(g), lax.rem(g, DEPTH) * UNIT, buffer)
         return 0
 
-    lax.fori_loop(0, total, step, 0)
+    lax.fori_loop(skip, total, step, 0)
 
 
 def destination(entry):
@@ -115,18 +119,31 @@
     return lax.rem(entry, 256)
 
 
-def forward_kernel(buckets, cap, n_buckets, n_blocks, n_before, last, lists, values, *refs):
+def forward_kernel(buckets, cap, n_buckets, n_blocks, n_before, role, lists, values, *refs):
     blocks, refs = refs[:n_blocks], refs[n_blocks:]
     before, refs = refs[:n_before], refs[n_before:]
+    if role == "last":
+        early, refs = refs[0], refs[1:]
     (buffer, sems, block_sems, sources), refs = refs[-4:], refs[:-4]
     total = refs[-1]
+    offsets = []
     copies = []
-    starts = []
     at = 0
     for i, b in enumerate(blocks):
         copies.append(pltpu.make_async_copy(b, sources.at[pl.ds(at, b.shape[0])], block_sems.at[i]))
-        starts.append(at)
+        offsets.append(at)
         at += b.shape[0]
+    far = n_buckets - 1
+    far_units = lists[n_buckets * cap + far]
+
+    if role == "next":
+        _, early, early_sems, total = refs[0], refs[1], refs[2], refs[0]
+        for g in range(AHEAD):
+
+            @pl.when(g < far_units)
+            def _(g=g):
+                for c in unit_copies(lists, far * cap + g * UNIT, g * UNIT, values, early, early_sems):
+                    c.start()
 
     def between():
         for c in copies:
@@ -138,19 +155,40 @@
         for c in copies:
             c.wait()
 
-    def use(first, at):
+    def use(first, at, tiles):
+        shift = jnp.where(first >= buckets[-1] * cap, offsets[len(buckets) - 1], 0)
         parts = []
         for u in range(UNIT):
-            parts.append(jnp.dot(buffer[at + u], sources[source(lists[first + u])], preferred_element_type=F32))
+            k = source(lists[first + u]) + shift
+            parts.append(jnp.dot(tiles[at + u], sources[k], preferred_element_type=F32))
         for u in range(UNIT):
             total[destination(lists[first + u])] += parts[u]
 
-    stream(lists, buckets, cap, n_buckets, values, buffer, sems, between, use)
-    if last:
-        mine, other, _ = refs
-        half = mine.shape[0]
-        mine[...] = total[:half].astype(BF16)
-        other[...] = total[half : 2 * half].astype(BF16)
+    if role == "last":
+
+        def start():
+            between()
+
+            def step(g, _):
+                use(far * cap + g * UNIT, g * UNIT, early)
+                return 0
+
+            lax.fori_loop(0, jnp.minimum(far_units, AHEAD), step, 0)
+
+        stream(lists, buckets, cap, n_buckets, values, buffer, sems, start, use, skip=AHEAD)
+        quarter = refs[0].shape[0]
+        for i, out in enumerate(refs[:4]):
+            out[...] = total[i * quarter : (i + 1) * quarter].astype(BF16)
+    else:
+        stream(lists, buckets, cap, n_buckets, values, buffer, sems, between, use)
+
+    if role == "next":
+        for g in range(AHEAD):
+
+            @pl.when(g < far_units)
+            def _(g=g):
+                for c in unit_copies(lists, far * cap + g * UNIT, g * UNIT, values, early, early_sems):
+                    c.wait()
 
 
 def dense_kernel(second, near, away, weight, bias, cot, *refs):
@@ -185,13 +223,21 @@
         wgrad[width:] = jnp.broadcast_to(bg, (wgrad.shape[0] - width, width))
 
 
-def backward_kernel(bucket, cap, n_buckets, lists, values, *refs):
+def backward_kernel(bucket, cap, n_buckets, n_early, lists, values, *refs):
+    early, refs = refs[:n_early], refs[n_early:]
     parts, (out, grads, buffer, sems, part_sems) = refs[:-5], refs[-5:]
     copies = []
     at = 0
     for i, g in enumerate(parts):
         copies.append(pltpu.make_async_copy(g, grads.at[pl.ds(at, g.shape[0])], part_sems.at[i]))
         at += g.shape[0]
+
+    def use(first, at, tiles):
+        parts = []
+        for u in range(UNIT):
+            parts.append(jnp.dot(grads[destination(lists[first + u])], tiles[at + u], preferred_element_type=F32))
+        for u in range(UNIT):
+            out[source(lists[first + u])] += parts[u]
 
     def between():
         for c in copies:
@@ -200,15 +246,16 @@
         out[...] = jnp.zeros(out.shape, F32)
         for c in copies:
             c.wait()
-
-    def use(first, at):
-        parts = []
-        for u in range(UNIT):
-            parts.append(jnp.dot(grads[destination(lists[first + u])], buffer[at + u], preferred_element_type=F32))
-        for u in range(UNIT):
-            out[source(lists[first + u])] += parts[u]
-
-    stream(lists, [bucket], cap, n_buckets, values, buffer, sems, between, use)
+        if n_early:
+
+            def step(g, _):
+                use(bucket * cap + g * UNIT, g * UNIT, early[0])
+                return 0
+
+            lax.fori_loop(0, jnp.minimum(lists[n_buckets * cap + bucket], AHEAD), step, 0)
+
+    skip = AHEAD if n_early else 0
+    stream(lists, [bucket], cap, n_buckets, values, buffer, sems, between, use, skip)
 
 
 def finish_kernel(own, right, left, out):
@@ -266,66 +313,83 @@
     ]
     tables = np.concatenate([np.concatenate(pos), place.reshape(-1)]).astype(np.int32)
     cap = row_tiles * slots + UNIT
-    lists = pl.pallas_call(
+    mine = features.reshape(per_dev, tile, width)
+    lists, kept = pl.pallas_call(
         functools.partial(lists_kernel, n_buckets, cap, col_tiles, 4 * row_tiles),
-        in_specs=[SMEM] * 3,
-        out_specs=SMEM,
-        out_shape=jax.ShapeDtypeStruct((n_buckets * cap + n_buckets,), jnp.int32),
+        in_specs=[SMEM] * 3 + [VMEM],
+        out_specs=[SMEM, VMEM],
+        out_shape=[
+            jax.ShapeDtypeStruct((n_buckets * cap + n_buckets,), jnp.int32),
+            jax.ShapeDtypeStruct((per_dev, tile, width), BF16),
+        ],
         compiler_params=params(8),
         cost_estimate=cost(0, 2**12),
         name="lists",
-    )(tile_cols, tile_counts.reshape(-1), jnp.asarray(tables))
+    )(tile_cols, tile_counts.reshape(-1), jnp.asarray(tables), mine)
 
     dots = 2 * tile * tile * width
     small = cost(dots, tile * tile * 2)
     stream_scratch = [pltpu.VMEM((DEPTH * UNIT, tile, tile), BF16), pltpu.SemaphoreType.DMA((DEPTH * UNIT,))]
     total_shape = jax.ShapeDtypeStruct((row_tiles + 1, tile, width), F32)
-    half_shape = jax.ShapeDtypeStruct((row_tiles // 2, tile, width), BF16)
-
-    def forward(bucket, blocks, before, last=False):
+    quarter_shape = jax.ShapeDtypeStruct((row_tiles // 4, tile, width), BF16)
+
+    early_shape = jax.ShapeDtypeStruct((AHEAD * UNIT, tile, tile), BF16)
+
+    def forward(buckets, blocks, before, role="", early=()):
         n_tiles = sum(b.shape[0] for b in blocks)
-        out = pl.pallas_call(
-            functools.partial(forward_kernel, [bucket], cap, n_buckets, len(blocks), len(before), last),
-            in_specs=[SMEM, HBM] + [ANY if bucket else HBM] * len(blocks) + [VMEM] * len(before),
-            out_specs=[VMEM] * (2 if last else 1),
-            out_shape=[half_shape] * 2 if last else [total_shape],
-            scratch_shapes=([pltpu.VMEM(total_shape.shape, F32)] if last else [])
-            + stream_scratch
-            + [pltpu.SemaphoreType.DMA((len(blocks),)), pltpu.VMEM((n_tiles, tile, width), BF16)],
+        scratch = stream_scratch + [
+            pltpu.SemaphoreType.DMA((len(blocks),)),
+            pltpu.VMEM((n_tiles, tile, width), BF16),
+        ]
+        out_shape = [total_shape]
+        if role == "next":
+            out_shape = [total_shape, early_shape]
+            scratch = [pltpu.SemaphoreType.DMA((AHEAD * UNIT,))] + scratch
+        elif role == "last":
+            out_shape = [quarter_shape] * 4
+            scratch = [pltpu.VMEM(total_shape.shape, F32)] + scratch
+        return pl.pallas_call(
+            functools.partial(forward_kernel, buckets, cap, n_buckets, len(blocks), len(before), role),
+            in_specs=[SMEM, HBM] + [ANY] * len(blocks) + [VMEM] * (len(before) + len(early)),
+            out_specs=[VMEM] * len(out_shape),
+            out_shape=out_shape,
+            scratch_shapes=scratch,
             compiler_params=params(40),
             cost_estimate=small,
-            name=f"forward_{bucket}",
-        )(lists, values, *blocks, *before)
-        return out if last else out[0]
-
-    mine = features.reshape(per_dev, tile, width)
+            name=f"forward_{buckets[-1]}",
+        )(lists, values, *blocks, *before, *early)
+
     from_left = from_right = mine
-    total = None
     cot_other = None
     for s in range(1, half):
-        now = [from_left, from_right] if s > 1 else [mine]
+        now = [from_left, from_right]
         from_left = lax.ppermute(from_left, "col", right)
         from_right = lax.ppermute(from_right, "col", left)
         if s == 1:
             cot_other = lax.ppermute(cotangent, "row", across)
-            from_left, from_right, cot_other, lists = lax.optimization_barrier(
-                (from_left, from_right, cot_other, lists)
+            from_left, from_right, cot_other, lists, kept = lax.optimization_barrier(
+                (from_left, from_right, cot_other, lists, kept)
             )
         else:
             if s == 2:
-                total = forward(0, [mine], [])
-            total = forward(s - 1, now, [total])
+                (total,) = forward([0, 1], [kept, *now], [])
+            else:
+                (total,) = forward([s - 1], now, [total])
             from_left, from_right, total = lax.optimization_barrier((from_left, from_right, total))
     far_near = lax.ppermute(from_left[: per_dev // 2], "col", right)
     far_away = lax.ppermute(from_right[per_dev // 2 :], "col", left)
-    total = forward(half - 1, [from_left, from_right], [total])
-    hid_mine, hid_other = forward(half, [far_near, far_away], [total], last=True)
-
-    hid_came = lax.ppermute(hid_other, "row", cores)
-    own = (hid_mine.astype(F32) + hid_came.astype(F32)).astype(BF16)
+    total, early = forward([half - 1], [from_left, from_right], [total], "next")
+    own_1, own_2, other_1, other_2 = forward([half], [far_near, far_away], [total], "last", [early])
+
+    def add(local, came):
+        return (local.astype(F32) + came.astype(F32)).astype(BF16)
+
     mid = row_tiles // 4
-    own, own_away = own[:mid], own[mid:]
+    came_2 = lax.ppermute(other_2, "row", cores)
+    came_1 = lax.ppermute(other_1, "row", cores)
+    own_away = add(own_2, came_2)
     came = lax.ppermute(own_away, "row", across)
+    own = add(own_1, came_1)
     came_away = lax.ppermute(own, "row", across)
 
     w_rows = width // 4 + 16
@@ -367,11 +431,11 @@
 
     w_sum = quarter(my_core) + lax.ppermute(quarter(1 - my_core), "row", cores)
 
-    def backward(bucket, n_tiles, after=()):
+    def backward(bucket, n_tiles, after=(), early=()):
         its_lists, *_ = lax.optimization_barrier((lists, *after))
         return pl.pallas_call(
-            functools.partial(backward_kernel, bucket, cap, n_buckets),
-            in_specs=[SMEM, HBM] + [ANY] * 4,
+            functools.partial(backward_kernel, bucket, cap, n_buckets, len(early)),
+            in_specs=[SMEM, HBM] + [VMEM] * len(early) + [ANY] * 4,
             out_specs=VMEM,
             out_shape=jax.ShapeDtypeStruct((n_tiles, width, tile), F32),
             scratch_shapes=[pltpu.VMEM((row_tiles + 1, width, tile), BF16)]
@@ -380,12 +444,9 @@
             compiler_params=params(40),
             cost_estimate=small,
             name=f"backward_{bucket}",
-        )(its_lists, values, grad_1, grad_2, grad_3, grad_4)
-
-    def add(local, came):
-        return (local + came.astype(F32)).astype(BF16)
-
-    far_part = backward(half, per_dev).astype(BF16)
+        )(its_lists, values, *early, grad_1, grad_2, grad_3, grad_4)
+
+    far_part = backward(half, per_dev, early=[early]).astype(BF16)
     cut = per_dev // 2
     sent = lax.optimization_barrier((far_part[:cut], far_part[cut:]))
     stages = [1 << i for i in range((n_col - 1).bit_length())]
@@ -393,12 +454,7 @@
         to_right = lax.ppermute(sent[0], "col", right)
         to_left = lax.ppermute(sent[1], "col", left)
         step = half - 1 - d
-        quarters = ()
-        if step < len(stages):
-            w_now, *_ = lax.optimization_barrier((w_sum.astype(BF16), *sent))
-            w_came = lax.ppermute(w_now, "col", [(i, i ^ stages[step]) for i in range(n_col)])
-            w_sum = w_now.astype(F32) + w_came.astype(F32)
-        elif step == len(stages):
+        if step == len(stages):
             w_now, *_ = lax.optimization_barrier((w_sum * grad_scale, *sent))
             w_own = w_now[: width // 4]
             quarters = [w_own] + [lax.ppermute(w_own, "row", perm) for perm in (across, cores, corners)]
@@ -412,11 +468,14 @@
                 name="quarters",
             )(*quarters)
             bias_grad = w_now[width // 4]
-            w_sum = (weight_grad, bias_grad)
         part = backward(d, 2 * per_dev if d else per_dev, sent)
-        part, to_right, to_left, w_sum = lax.optimization_barrier((part, to_right, to_left, w_sum))
+        if step < len(stages):
+            w_now, part, *_ = lax.optimization_barrier((w_sum.astype(BF16), part, *sent))
+            w_came = lax.ppermute(w_now, "col", [(i, i ^ stages[step]) for i in range(n_col)])
+            w_sum = w_now.astype(F32) + w_came.astype(F32)
         if d == 0:
             break
+        part, to_right, to_left = lax.optimization_barrier((part, to_right, to_left))
         for_left, for_right = part[:per_dev], part[per_dev:]
         if step == 0:
             sent = (
@@ -426,7 +485,9 @@
         else:
             sent = (add(for_right, to_right), add(for_left, to_left))
         sent = lax.optimization_barrier(sent)
-    weight_grad, bias_grad = w_sum
+    part, to_right, to_left, weight_grad, bias_grad = lax.optimization_barrier(
+        (part, to_right, to_left, weight_grad, bias_grad)
+    )
     feature_grad = pl.pallas_call(
         finish_kernel,
         in_specs=[VMEM] * 3,

time: 97.9 us -> 91.7 us (0.937)
  waiting for transfers between devices: 28.5 us -> 22.2 us
  starting transfers between devices: 28.5 us -> 30.2 us
  Pallas kernels: 34.7 us -> 33.2 us
    ppermute x4, waiting for transfers between devices: 4.96 us -> 1.53 us  [per_device(): to_right = lax.ppermute(sent[0], 'col', right)]
    ppermute x4, waiting for transfers between devices: 3.14 us -> 0.87 us  [per_device(): to_left = lax.ppermute(sent[1], 'col', left)]
    pallas_call x10 -> x9, Pallas kernels: 29.4 us -> 27.3 us  [the longest x5 14.3 us: backward(): pl.pallas_call(functools.partial(backward_kernel, bucket, cap, n_buckets,...]
    ppermute x4, starting transfers between devices: 4.95 us -> 6.96 us  [per_device(): to_right = lax.ppermute(sent[0], 'col', right)]
    ppermute x4, starting transfers between devices: 3.24 us -> 1.6 us  [per_device(): to_left = lax.ppermute(sent[1], 'col', left)]
    ppermute x3, starting transfers between devices: 3.38 us -> 4.96 us  [per_device(): lax.ppermute(w_now, 'col', [(i, i ^ stages[step]) for i in range(n_col)])]
  transfers between devices with their start and end apart: 29 -> 30, of which waited for: 17 -> 16; matrix products, arithmetic and copies ran while one was open for 1% -> 1% of each run, Pallas kernels for 28% -> 33%
where the time goes in v4:
time: 91.7 us; the launch traced here: 90.8 us
  Pallas kernels  33.2 us (36%)
  starting transfers between devices  30.2 us (33%)
  waiting for transfers between devices  22.2 us (24%)
  local copies, waits for them, and re-layouts  3.62 us (4%)
  between operations  0.93 us (1%)
    pallas_call x5, Pallas kernels, backward(): pl.pallas_call(functools.partial(backward_kernel, bucket, cap, n_buckets,...  14.3 us
    pallas_call x4, Pallas kernels, forward(): pl.pallas_call(functools.partial(forward_kernel, buckets, cap, n_buckets,...  13 us
    ppermute x1, waiting for transfers between devices, per_device(): came = lax.ppermute(own_away, 'row', across)  6.98 us
    ppermute x4, starting transfers between devices, per_device(): to_right = lax.ppermute(sent[0], 'col', right)  6.96 us
    ppermute x3, starting transfers between devices, per_device(): from_left = lax.ppermute(from_left, 'col', right)  6.39 us
    ppermute x3, starting transfers between devices, per_device(): lax.ppermute(w_now, 'col', [(i, i ^ stages[step]) for i in range(n_col)])  4.96 us
    ppermute x1, waiting for transfers between devices, per_device(): came_away = lax.ppermute(own, 'row', across)  3.64 us
    ppermute x3, waiting for transfers between devices, per_device(): from_right = lax.ppermute(from_right, 'col', left)  3.34 us
  transfers between devices with their start and end apart: 30, of which 16 were waited for; matrix products, arithmetic and copies ran while one was open for 1% of the time, Pallas kernels for 33%

profile of v4, /device:TPU:0, one launch (start us, length us, event | category | flops | bytes accessed | tf_op | source)
XLA Modules:
  0.0 90.8 jit_solution(10434090487040426696)
XLA Ops:
  0.6 3.1 %collective-permute-start = (bf16[2,256,256]{2,1,0:T(8,128)(2,1)}, bf16[2,256,256]{2,1,0:T(8,128)(2,1)S(1)}, u32[]{:S(2)}, u32[]{:S(2)}) collective-permute-start(bf16[2,256,256]{2,1,0:T(8,128)(2,1)} %bitcast.16), channel_id=1, source_target_pairs={{0,2},{2,4},{4,6},{6,7},{7,5},{5,3},{3,1},{1,0},{8,10},{10,12},{12... | collective-permute-start | bytes 786440 | tf_op jit(solution)/shard_map/ppermute | solution.py:366
  3.7 2.0 %collective-permute-start.2 = (bf16[512,256]{1,0:T(8,128)(2,1)}, bf16[512,256]{1,0:T(8,128)(2,1)S(1)}, u32[]{:S(2)}, u32[]{:S(2)}) collective-permute-start(bf16[512,256]{1,0:T(8,128)(2,1)} %cot.1), channel_id=1, source_target_pairs={{0,16},{16,0},{8,24},{24,8},{1,17},{17,1},{9,25},{25,9},{2,18},{18... | collective-permute-start | bytes 786440 | tf_op jit(solution)/shard_map/ppermute | solution.py:369
  5.7 0.9 %copy-done.1 = bf16[512,256]{1,0:T(8,128)(2,1)S(1)} copy-done((bf16[512,256]{1,0:T(8,128)(2,1)S(1)}, bf16[512,256]{1,0:T(8,128)(2,1)}, u32[]{:S(2)}) %copy-start.1) | copy-done | bytes 262168
  6.6 0.7 copy-done.3
  7.3 0.7 copy-done.5
  8.0 0.7 copy-done.6
  8.6 2.5 %lists.1 = (s32[685]{0:T(1024)S(1)}, bf16[2,256,256]{2,1,0:T(8,128)(2,1)S(1)}) custom-call(s32[8,16]{1,0:T(8,128)S(1)} %copy-done.3, s32[8]{0:T(128)S(1)} %bitcast.23, s32[160]{0:T(256)S(1)} %copy-done.5, bf16[2,256,256]{2,1,0:T(8,128)(2,1)S(1)} %bitcast.18), custom_call_target="tpu_custom_call" | custom-call | bytes 4096 | tf_op jit(solution)/shard_map/lists/pallas_call | solution.py:317
  11.2 0.5 collective-permute-done.1.refs_2_
  11.7 1.7 %collective-permute-start.3 = (bf16[2,256,256]{2,1,0:T(8,128)(2,1)S(1)}, bf16[2,256,256]{2,1,0:T(8,128)(2,1)S(1)}, u32[]{:S(2)}, u32[]{:S(2)}) collective-permute-start(bf16[2,256,256]{2,1,0:T(8,128)(2,1)S(1)} %collective-permute-done.refs_1_), channel_id=1, source_target_pairs={{0,2},{2,4},{4,6},{6,7},{7,5},{5,3},{3,1},{1,0},{8,10},{10,12},{12... | collective-permute-start | bytes 786440 | tf_op jit(solution)/shard_map/ppermute | solution.py:366
  13.7 3.9 %forward_1.1.refs_2_ = f32[9,256,256]{2,1,0:T(8,128)S(1)} custom-call(s32[685]{0:T(1024)S(1)} %get-tuple-element.120.lists, bf16[128,256,256]{2,1,0:T(8,128)(2,1)} %bitcast.24, bf16[2,256,256]{2,1,0:T(8,128)(2,1)S(1)} %get-tuple-element.71.refs_0_, bf16[2,256,256]{2,1,0:T(8,128)(2,1)S(1)} %collective-permute-done.refs_1_, ...), custom_call_target="tpu_custom_call" | custom-call | flops 33554432 | bytes 131072 | tf_op jit(solution)/shard_map/forward_1/pallas_call | solution.py:351
  17.6 0.9 %collective-permute-done.3.refs_0_ = bf16[2,256,256]{2,1,0:T(8,128)(2,1)S(1)} collective-permute-done((bf16[2,256,256]{2,1,0:T(8,128)(2,1)S(1)}, bf16[2,256,256]{2,1,0:T(8,128)(2,1)S(1)}, u32[]{:S(2)}, u32[]{:S(2)}) %collective-permute-start.3) | collective-permute-done | bytes 262176 | tf_op jit(solution)/shard_map/ppermute | solution.py:366
  18.5 1.3 %collective-permute-done.4.refs_1_ = bf16[2,256,256]{2,1,0:T(8,128)(2,1)S(1)} collective-permute-done((bf16[2,256,256]{2,1,0:T(8,128)(2,1)S(1)}, bf16[2,256,256]{2,1,0:T(8,128)(2,1)S(1)}, u32[]{:S(2)}, u32[]{:S(2)}) %collective-permute-start.4) | collective-permute-done | bytes 262176 | tf_op jit(solution)/shard_map/ppermute | solution.py:367
  19.8 1.6 %collective-permute-start.5 = (bf16[2,256,256]{2,1,0:T(8,128)(2,1)S(1)}, bf16[2,256,256]{2,1,0:T(8,128)(2,1)S(1)}, u32[]{:S(2)}, u32[]{:S(2)}) collective-permute-start(bf16[2,256,256]{2,1,0:T(8,128)(2,1)S(1)} %collective-permute-done.3.refs_0_), channel_id=1, source_target_pairs={{0,2},{2,4},{4,6},{6,7},{7,5},{5,3},{3,1},{1,0},{8,10},{10,12},{12... | collective-permute-start | bytes 786440 | tf_op jit(solution)/shard_map/ppermute | solution.py:366
  21.9 3.3 %forward_2.1.refs_2_ = f32[9,256,256]{2,1,0:T(8,128)S(1)} custom-call(s32[685]{0:T(1024)S(1)} %get-tuple-element.120.lists, bf16[128,256,256]{2,1,0:T(8,128)(2,1)} %bitcast.25, bf16[2,256,256]{2,1,0:T(8,128)(2,1)S(1)} %collective-permute-done.3.refs_0_, bf16[2,256,256]{2,1,0:T(8,128)(2,1)S(1)} %collective-permute-done.4.refs_1_, ...), custom_call_target="tpu_custom_call" | custom-call | flops 33554432 | bytes 131072 | tf_op jit(solution)/shard_map/forward_2/pallas_call | solution.py:351
  25.2 1.1 %collective-permute-done.5.refs_0_ = bf16[2,256,256]{2,1,0:T(8,128)(2,1)S(1)} collective-permute-done((bf16[2,256,256]{2,1,0:T(8,128)(2,1)S(1)}, bf16[2,256,256]{2,1,0:T(8,128)(2,1)S(1)}, u32[]{:S(2)}, u32[]{:S(2)}) %collective-permute-start.5) | collective-permute-done | bytes 262176 | tf_op jit(solution)/shard_map/ppermute | solution.py:366
  26.2 1.6 %collective-permute-done.6.refs_1_ = bf16[2,256,256]{2,1,0:T(8,128)(2,1)S(1)} collective-permute-done((bf16[2,256,256]{2,1,0:T(8,128)(2,1)S(1)}, bf16[2,256,256]{2,1,0:T(8,128)(2,1)S(1)}, u32[]{:S(2)}, u32[]{:S(2)}) %collective-permute-start.6) | collective-permute-done | bytes 262176 | tf_op jit(solution)/shard_map/ppermute | solution.py:367
  27.8 1.9 %collective-permute-start.7 = (bf16[1,256,256]{2,1,0:T(8,128)(2,1)S(1)}, bf16[1,256,256]{2,1,0:T(8,128)(2,1)S(1)}, u32[]{:S(2)}, u32[]{:S(2)}) collective-permute-start(bf16[1,256,256]{2,1,0:T(8,128)(2,1)S(1)} %slice.50), channel_id=1, source_target_pairs={{0,2},{2,4},{4,6},{6,7},{7,5},{5,3},{3,1},{1,0},{8,10},{10,12},{12... | collective-permute-start | bytes 393224 | tf_op jit(solution)/shard_map/ppermute | solution.py:379
  29.9 3.8 %forward_3.1 = (f32[9,256,256]{2,1,0:T(8,128)S(1)}, bf16[16,256,256]{2,1,0:T(8,128)(2,1)S(1)}) custom-call(s32[685]{0:T(1024)S(1)} %get-tuple-element.120.lists, bf16[128,256,256]{2,1,0:T(8,128)(2,1)} %bitcast.26, bf16[2,256,256]{2,1,0:T(8,128)(2,1)S(1)} %collective-permute-done.5.refs_0_, bf16[2,256,256]{2,1,0:T(8,128)(2,1)S(1)} %collective-permute-done.6.refs_1_, ...), custom_call_target="tpu_custom_call" | custom-call | flops 33554432 | bytes 131072 | tf_op jit(solution)/shard_map/forward_3/pallas_call | solution.py:351
  33.7 1.0 %collective-permute-done.8.refs_1_ = bf16[1,256,256]{2,1,0:T(8,128)(2,1)S(1)} collective-permute-done((bf16[1,256,256]{2,1,0:T(8,128)(2,1)S(1)}, bf16[1,256,256]{2,1,0:T(8,128)(2,1)S(1)}, u32[]{:S(2)}, u32[]{:S(2)}) %collective-permute-start.8) | collective-permute-done | bytes 131104 | tf_op jit(solution)/shard_map/ppermute | solution.py:380
  34.8 2.1 %forward_4.1 = (bf16[2,256,256]{2,1,0:T(8,128)(2,1)S(1)}, bf16[2,256,256]{2,1,0:T(8,128)(2,1)S(1)}, bf16[2,256,256]{2,1,0:T(8,128)(2,1)S(1)}, bf16[2,256,256]{2,1,0:T(8,128)(2,1)S(1)}) custom-call(s32[685]{0:T(1024)S(1)} %get-tuple-element.120.lists, bf16[128,256,256]{2,1,0:T(8,128)(2,1)} %bitcast.27, ...), custom_call_target="tpu_custom_call" | custom-call | flops 33554432 | bytes 131072 | tf_op jit(solution)/shard_map/forward_4/pallas_call | solution.py:351
  36.9 0.5 collective-permute-start.9
  37.4 1.0 %collective-permute-done.11 = bf16[2,256,256]{2,1,0:T(8,128)(2,1)S(1)} collective-permute-done((bf16[2,256,256]{2,1,0:T(8,128)(2,1)S(1)}, bf16[2,256,256]{2,1,0:T(8,128)(2,1)S(1)}, u32[]{:S(2)}, u32[]{:S(2)}) %collective-permute-start.11) | collective-permute-done | bytes 262176 | tf_op jit(solution)/shard_map/ppermute | solution.py:388
  38.5 1.0 %collective-permute-start.12 = (bf16[2,256,256]{2,1,0:T(8,128)(2,1)S(1)}, bf16[2,256,256]{2,1,0:T(8,128)(2,1)S(1)}, u32[]{:S(2)}, u32[]{:S(2)}) collective-permute-start(bf16[2,256,256]{2,1,0:T(8,128)(2,1)S(1)} %add_convert_fusion.4.near), channel_id=1, source_target_pairs={{0,16},{16,0},{8,24},{24,8},{1,17},{17,1},{9,25},{25,9},{2,18},{18... | collective-permute-start | bytes 786440 | tf_op jit(solution)/shard_map/ppermute | solution.py:391
  39.6 1.1 %collective-permute-start.10 = (bf16[2,256,256]{2,1,0:T(8,128)(2,1)S(1)}, bf16[2,256,256]{2,1,0:T(8,128)(2,1)S(1)}, u32[]{:S(2)}, u32[]{:S(2)}) collective-permute-start(bf16[2,256,256]{2,1,0:T(8,128)(2,1)S(1)} %add_convert_fusion.5.near), channel_id=1, source_target_pairs={{0,16},{16,0},{8,24},{24,8},{1,17},{17,1},{9,25},{25,9},{2,18},{18... | collective-permute-start | bytes 786440 | tf_op jit(solution)/shard_map/ppermute | solution.py:393
  40.7 7.0 %collective-permute-done.12.away = bf16[2,256,256]{2,1,0:T(8,128)(2,1)S(1)} collective-permute-done((bf16[2,256,256]{2,1,0:T(8,128)(2,1)S(1)}, bf16[2,256,256]{2,1,0:T(8,128)(2,1)S(1)}, u32[]{:S(2)}, u32[]{:S(2)}) %collective-permute-start.12) | collective-permute-done | bytes 262176 | tf_op jit(solution)/shard_map/ppermute | solution.py:391
  47.7 1.2 %dense_own.1 = (bf16[512,256]{1,0:T(8,128)(2,1)}, bf16[2,256,256]{2,1,0:T(8,128)(2,1)S(1)}, f32[264,256]{1,0:T(8,128)S(1)}) custom-call(bf16[2,256,256]{2,1,0:T(8,128)(2,1)S(1)} %add_convert_fusion.5.near, bf16[2,256,256]{2,1,0:T(8,128)(2,1)S(1)} %collective-permute-done.12.away, bf16[256,256]{1,0:T(8,128)(2,1)S(1)} %copy-done, f32[1,256]{1,0:T(1,128)S(1)} %bitcast.21, ...), custom_call_target="tpu_custom_call" | custom-call | flops 50331648 | bytes 131072 | tf_op jit(solution)/shard_map/dense_own/pallas_call | solution.py:399
  48.9 3.6 %collective-permute-done.10.away = bf16[2,256,256]{2,1,0:T(8,128)(2,1)S(1)} collective-permute-done((bf16[2,256,256]{2,1,0:T(8,128)(2,1)S(1)}, bf16[2,256,256]{2,1,0:T(8,128)(2,1)S(1)}, u32[]{:S(2)}, u32[]{:S(2)}) %collective-permute-start.10) | collective-permute-done | bytes 262176 | tf_op jit(solution)/shard_map/ppermute | solution.py:393
  52.5 0.7 dense_away.1
  53.8 1.0 %collective-permute-done.15.refs_4_.refs_3_ = bf16[2,256,256]{2,1,0:T(8,128)(2,1)S(1)} collective-permute-done((bf16[2,256,256]{2,1,0:T(8,128)(2,1)S(1)}, bf16[2,256,256]{2,1,0:T(8,128)(2,1)S(1)}, u32[]{:S(2)}, u32[]{:S(2)}) %collective-permute-start.15) | collective-permute-done | bytes 262176 | tf_op jit(solution)/shard_map/ppermute | solution.py:425
  54.8 1.6 %backward_4.1 = f32[2,256,256]{2,1,0:T(8,128)S(1)} custom-call(s32[685]{0:T(1024)S(1)} %get-tuple-element.120.lists, bf16[128,256,256]{2,1,0:T(8,128)(2,1)} %bitcast.28, bf16[16,256,256]{2,1,0:T(8,128)(2,1)S(1)} %get-tuple-element.79.refs_3_.refs_0_, bf16[2,256,256]{2,1,0:T(8,128)(2,1)S(1)} %get-tuple-element.92.refs_1_.refs_0_, ...), custom_call_target="tpu_custom_call" | custom-call | flops 33554432 | bytes 131072 | tf_op jit(solution)/shard_map/backward_4/pallas_call | solution.py:436
  56.5 1.8 %collective-permute-start.17 = (bf16[1,256,256]{2,1,0:T(8,128)(2,1)S(1)}, bf16[1,256,256]{2,1,0:T(8,128)(2,1)S(1)}, u32[]{:S(2)}, u32[]{:S(2)}) collective-permute-start(bf16[1,256,256]{2,1,0:T(8,128)(2,1)S(1)} %get-tuple-element.95), channel_id=1, source_target_pairs={{0,2},{2,4},{4,6},{6,7},{7,5},{5,3},{3,1},{1,0},{8,10},{10,12},{12... | collective-permute-start | bytes 393224 | tf_op jit(solution)/shard_map/ppermute | solution.py:454
  58.6 3.3 %backward_3.1 = f32[4,256,256]{2,1,0:T(8,128)S(1)} custom-call(s32[685]{0:T(1024)S(1)} %get-tuple-element.120.lists, bf16[128,256,256]{2,1,0:T(8,128)(2,1)} %bitcast.29, bf16[2,256,256]{2,1,0:T(8,128)(2,1)S(1)} %get-tuple-element.92.refs_1_.refs_0_, bf16[2,256,256]{2,1,0:T(8,128)(2,1)S(1)} %get-tuple-element.93.refs_2_.refs_1_, ...), custom_call_target="tpu_custom_call" | custom-call | flops 33554432 | bytes 131072 | tf_op jit(solution)/shard_map/backward_3/pallas_call | solution.py:436
  61.9 1.3 %collective-permute-start.16 = (bf16[80,256]{1,0:T(8,128)(2,1)S(1)}, bf16[80,256]{1,0:T(8,128)(2,1)S(1)}, u32[]{:S(2)}, u32[]{:S(2)}) collective-permute-start(bf16[80,256]{1,0:T(8,128)(2,1)S(1)} %fusion), channel_id=1, source_target_pairs={{0,1},{1,0},{2,3},{3,2},{4,5},{5,4},{6,7},{7,6},{8,9},{9,8},{10,11... | collective-permute-start | bytes 122888 | tf_op jit(solution)/shard_map/ppermute | solution.py:474
  63.8 1.3 %collective-permute-start.20 = (bf16[2,256,256]{2,1,0:T(8,128)(2,1)S(1)}, bf16[2,256,256]{2,1,0:T(8,128)(2,1)S(1)}, u32[]{:S(2)}, u32[]{:S(2)}) collective-permute-start(bf16[2,256,256]{2,1,0:T(8,128)(2,1)S(1)} %get-tuple-element.103), channel_id=1, source_target_pairs={{0,2},{2,4},{4,6},{6,7},{7,5},{5,3},{3,1},{1,0},{8,10},{10,12},{12... | collective-permute-start | bytes 786440 | tf_op jit(solution)/shard_map/ppermute | solution.py:454
  65.0 0.8 collective-permute-start.21
  66.2 3.3 %backward_2.1 = f32[4,256,256]{2,1,0:T(8,128)S(1)} custom-call(s32[685]{0:T(1024)S(1)} %get-tuple-element.120.lists, bf16[128,256,256]{2,1,0:T(8,128)(2,1)} %bitcast.30, bf16[2,256,256]{2,1,0:T(8,128)(2,1)S(1)} %get-tuple-element.92.refs_1_.refs_0_, bf16[2,256,256]{2,1,0:T(8,128)(2,1)S(1)} %get-tuple-element.93.refs_2_.refs_1_, ...), custom_call_target="tpu_custom_call" | custom-call | flops 33554432 | bytes 131072 | tf_op jit(solution)/shard_map/backward_2/pallas_call | solution.py:436
  69.5 0.5 collective-permute-start.19
  70.1 1.5 %collective-permute-done.20 = bf16[2,256,256]{2,1,0:T(8,128)(2,1)S(1)} collective-permute-done((bf16[2,256,256]{2,1,0:T(8,128)(2,1)S(1)}, bf16[2,256,256]{2,1,0:T(8,128)(2,1)S(1)}, u32[]{:S(2)}, u32[]{:S(2)}) %collective-permute-start.20) | collective-permute-done | bytes 262176 | tf_op jit(solution)/shard_map/ppermute | solution.py:454
  72.0 1.6 %collective-permute-start.22 = (bf16[2,256,256]{2,1,0:T(8,128)(2,1)S(1)}, bf16[2,256,256]{2,1,0:T(8,128)(2,1)S(1)}, u32[]{:S(2)}, u32[]{:S(2)}) collective-permute-start(bf16[2,256,256]{2,1,0:T(8,128)(2,1)S(1)} %get-tuple-element.111), channel_id=1, source_target_pairs={{0,2},{2,4},{4,6},{6,7},{7,5},{5,3},{3,1},{1,0},{8,10},{10,12},{12... | collective-permute-start | bytes 786440 | tf_op jit(solution)/shard_map/ppermute | solution.py:454
  73.6 0.5 collective-permute-start.23
  74.1 3.3 %backward_1.1 = f32[4,256,256]{2,1,0:T(8,128)S(1)} custom-call(s32[685]{0:T(1024)S(1)} %get-tuple-element.120.lists, bf16[128,256,256]{2,1,0:T(8,128)(2,1)} %bitcast.31, bf16[2,256,256]{2,1,0:T(8,128)(2,1)S(1)} %get-tuple-element.92.refs_1_.refs_0_, bf16[2,256,256]{2,1,0:T(8,128)(2,1)S(1)} %get-tuple-element.93.refs_2_.refs_1_, ...), custom_call_target="tpu_custom_call" | custom-call | flops 33554432 | bytes 131072 | tf_op jit(solution)/shard_map/backward_1/pallas_call | solution.py:436
  77.5 3.2 %collective-permute-start.26 = (bf16[80,256]{1,0:T(8,128)(2,1)S(1)}, bf16[80,256]{1,0:T(8,128)(2,1)S(1)}, u32[]{:S(2)}, u32[]{:S(2)}) collective-permute-start(bf16[80,256]{1,0:T(8,128)(2,1)S(1)} %add_convert_fusion.8), channel_id=1, source_target_pairs={{0,4},{1,5},{2,6},{3,7},{4,0},{5,1},{6,2},{7,3},{8,12},{9,13},{10,... | collective-permute-start | bytes 122888 | tf_op jit(solution)/shard_map/ppermute | solution.py:474
  80.9 2.3 %collective-permute-start.24 = (bf16[2,256,256]{2,1,0:T(8,128)(2,1)S(1)}, bf16[2,256,256]{2,1,0:T(8,128)(2,1)S(1)}, u32[]{:S(2)}, u32[]{:S(2)}) collective-permute-start(bf16[2,256,256]{2,1,0:T(8,128)(2,1)S(1)} %get-tuple-element.118), channel_id=1, source_target_pairs={{0,2},{2,4},{4,6},{6,7},{7,5},{5,3},{3,1},{1,0},{8,10},{10,12},{12... | collective-permute-start | bytes 786440 | tf_op jit(solution)/shard_map/ppermute | solution.py:454
  83.6 1.9 %collective-permute-start.27 = (f32[64,256]{1,0:T(8,128)S(1)}, f32[64,256]{1,0:T(8,128)S(1)}, u32[]{:S(2)}, u32[]{:S(2)}) collective-permute-start(f32[64,256]{1,0:T(8,128)S(1)} %slice.62.own), channel_id=1, source_target_pairs={{0,16},{16,0},{8,24},{24,8},{1,17},{17,1},{9,25},{25,9},{2,18},{18... | collective-permute-start | bytes 196616 | tf_op jit(solution)/shard_map/ppermute | solution.py:460
  85.8 0.6 slice.63
  86.3 2.8 %backward_0.1.own = f32[2,256,256]{2,1,0:T(8,128)S(1)} custom-call(s32[685]{0:T(1024)S(1)} %get-tuple-element.120.lists, bf16[128,256,256]{2,1,0:T(8,128)(2,1)} %bitcast.32, bf16[2,256,256]{2,1,0:T(8,128)(2,1)S(1)} %get-tuple-element.92.refs_1_.refs_0_, bf16[2,256,256]{2,1,0:T(8,128)(2,1)S(1)} %get-tuple-element.93.refs_2_.refs_1_, ...), custom_call_target="tpu_custom_call" | custom-call | flops 33554432 | bytes 131072 | tf_op jit(solution)/shard_map/backward_0/pallas_call | solution.py:436
  89.2 0.7 quarters.1
  89.9 0.9 finish.1
  (59 shorter events, 4.5 us)
Async XLA Ops:
  0.6 10.6 %collective-permute-start = (bf16[2,256,256]{2,1,0:T(8,128)(2,1)}, bf16[2,256,256]{2,1,0:T(8,128)(2,1)S(1)}, u32[]{:S(2)}, u32[]{:S(2)}) collective-permute-start(bf16[2,256,256]{2,1,0:T(8,128)(2,1)} %bitcast.16), channel_id=1, source_target_pairs={{0,2},{2,4},{4,6},{6,7},{7,5},{5,3},{3,1},{1,0},{8,10},{10,12},{12... | collective-permute-start | bytes 786440 | tf_op jit(solution)/shard_map/ppermute | solution.py:366
  3.7 8.0 %collective-permute-start.1 = (bf16[2,256,256]{2,1,0:T(8,128)(2,1)}, bf16[2,256,256]{2,1,0:T(8,128)(2,1)S(1)}, u32[]{:S(2)}, u32[]{:S(2)}) collective-permute-start(bf16[2,256,256]{2,1,0:T(8,128)(2,1)} %bitcast.17), channel_id=1, source_target_pairs={{2,0},{4,2},{6,4},{7,6},{5,7},{3,5},{1,3},{0,1},{10,8},{12,10},{14... | collective-permute-start | bytes 786440 | tf_op jit(solution)/shard_map/ppermute | solution.py:367
  3.7 8.0 %collective-permute-start.2 = (bf16[512,256]{1,0:T(8,128)(2,1)}, bf16[512,256]{1,0:T(8,128)(2,1)S(1)}, u32[]{:S(2)}, u32[]{:S(2)}) collective-permute-start(bf16[512,256]{1,0:T(8,128)(2,1)} %cot.1), channel_id=1, source_target_pairs={{0,16},{16,0},{8,24},{24,8},{1,17},{17,1},{9,25},{25,9},{2,18},{18... | collective-permute-start | bytes 786440 | tf_op jit(solution)/shard_map/ppermute | solution.py:369
  5.7 0.9 %copy-start.1 = (bf16[512,256]{1,0:T(8,128)(2,1)S(1)}, bf16[512,256]{1,0:T(8,128)(2,1)}, u32[]{:S(2)}) copy-start(bf16[512,256]{1,0:T(8,128)(2,1)} %param.8) | copy-start | bytes 786436
  6.6 0.7 copy-start.3
  7.3 0.7 copy-start.5
  8.0 0.7 copy-start.6
  11.7 6.9 %collective-permute-start.3 = (bf16[2,256,256]{2,1,0:T(8,128)(2,1)S(1)}, bf16[2,256,256]{2,1,0:T(8,128)(2,1)S(1)}, u32[]{:S(2)}, u32[]{:S(2)}) collective-permute-start(bf16[2,256,256]{2,1,0:T(8,128)(2,1)S(1)} %collective-permute-done.refs_1_), channel_id=1, source_target_pairs={{0,2},{2,4},{4,6},{6,7},{7,5},{5,3},{3,1},{1,0},{8,10},{10,12},{12... | collective-permute-start | bytes 786440 | tf_op jit(solution)/shard_map/ppermute | solution.py:366
  13.4 6.4 %collective-permute-start.4 = (bf16[2,256,256]{2,1,0:T(8,128)(2,1)S(1)}, bf16[2,256,256]{2,1,0:T(8,128)(2,1)S(1)}, u32[]{:S(2)}, u32[]{:S(2)}) collective-permute-start(bf16[2,256,256]{2,1,0:T(8,128)(2,1)S(1)} %collective-permute-done.1.refs_2_), channel_id=1, source_target_pairs={{2,0},{4,2},{6,4},{7,6},{5,7},{3,5},{1,3},{0,1},{10,8},{12,10},{14... | collective-permute-start | bytes 786440 | tf_op jit(solution)/shard_map/ppermute | solution.py:367
  19.8 6.4 %collective-permute-start.5 = (bf16[2,256,256]{2,1,0:T(8,128)(2,1)S(1)}, bf16[2,256,256]{2,1,0:T(8,128)(2,1)S(1)}, u32[]{:S(2)}, u32[]{:S(2)}) collective-permute-start(bf16[2,256,256]{2,1,0:T(8,128)(2,1)S(1)} %collective-permute-done.3.refs_0_), channel_id=1, source_target_pairs={{0,2},{2,4},{4,6},{6,7},{7,5},{5,3},{3,1},{1,0},{8,10},{10,12},{12... | collective-permute-start | bytes 786440 | tf_op jit(solution)/shard_map/ppermute | solution.py:366
  21.4 6.4 %collective-permute-start.6 = (bf16[2,256,256]{2,1,0:T(8,128)(2,1)S(1)}, bf16[2,256,256]{2,1,0:T(8,128)(2,1)S(1)}, u32[]{:S(2)}, u32[]{:S(2)}) collective-permute-start(bf16[2,256,256]{2,1,0:T(8,128)(2,1)S(1)} %collective-permute-done.4.refs_1_), channel_id=1, source_target_pairs={{2,0},{4,2},{6,4},{7,6},{5,7},{3,5},{1,3},{0,1},{10,8},{12,10},{14... | collective-permute-start | bytes 786440 | tf_op jit(solution)/shard_map/ppermute | solution.py:367
  27.8 5.9 %collective-permute-start.7 = (bf16[1,256,256]{2,1,0:T(8,128)(2,1)S(1)}, bf16[1,256,256]{2,1,0:T(8,128)(2,1)S(1)}, u32[]{:S(2)}, u32[]{:S(2)}) collective-permute-start(bf16[1,256,256]{2,1,0:T(8,128)(2,1)S(1)} %slice.50), channel_id=1, source_target_pairs={{0,2},{2,4},{4,6},{6,7},{7,5},{5,3},{3,1},{1,0},{8,10},{10,12},{12... | collective-permute-start | bytes 393224 | tf_op jit(solution)/shard_map/ppermute | solution.py:379
  29.8 5.0 %collective-permute-start.8 = (bf16[1,256,256]{2,1,0:T(8,128)(2,1)S(1)}, bf16[1,256,256]{2,1,0:T(8,128)(2,1)S(1)}, u32[]{:S(2)}, u32[]{:S(2)}) collective-permute-start(bf16[1,256,256]{2,1,0:T(8,128)(2,1)S(1)} %slice.51), channel_id=1, source_target_pairs={{2,0},{4,2},{6,4},{7,6},{5,7},{3,5},{1,3},{0,1},{10,8},{12,10},{14... | collective-permute-start | bytes 393224 | tf_op jit(solution)/shard_map/ppermute | solution.py:380
  34.8 13.0 %copy-start = (bf16[256,256]{1,0:T(8,128)(2,1)S(1)}, bf16[256,256]{1,0:T(8,128)(2,1)}, u32[]{:S(2)}) copy-start(bf16[256,256]{1,0:T(8,128)(2,1)} %weight.3) | copy-start | bytes 393220
  34.8 13.0 %copy-start.2 = (bf16[512,256]{1,0:T(8,128)(2,1)S(1)}, bf16[512,256]{1,0:T(8,128)(2,1)}, u32[]{:S(2)}) copy-start(bf16[512,256]{1,0:T(8,128)(2,1)} %cot.1) | copy-start | bytes 786436
  34.8 13.0 %copy-start.4 = (f32[256]{0:T(256)S(1)}, f32[256]{0:T(256)}, u32[]{:S(2)}) copy-start(f32[256]{0:T(256)} %param.13) | copy-start | bytes 3076
  36.8 1.6 %collective-permute-start.11 = (bf16[2,256,256]{2,1,0:T(8,128)(2,1)S(1)}, bf16[2,256,256]{2,1,0:T(8,128)(2,1)S(1)}, u32[]{:S(2)}, u32[]{:S(2)}) collective-permute-start(bf16[2,256,256]{2,1,0:T(8,128)(2,1)S(1)} %get-tuple-element.83), channel_id=1, source_target_pairs={{0,8},{8,0},{16,24},{24,16},{1,9},{9,1},{17,25},{25,17},{2,10},{10... | collective-permute-start | bytes 786440 | tf_op jit(solution)/shard_map/ppermute | solution.py:388
  36.9 2.6 %collective-permute-start.9 = (bf16[2,256,256]{2,1,0:T(8,128)(2,1)S(1)}, bf16[2,256,256]{2,1,0:T(8,128)(2,1)S(1)}, u32[]{:S(2)}, u32[]{:S(2)}) collective-permute-start(bf16[2,256,256]{2,1,0:T(8,128)(2,1)S(1)} %get-tuple-element.81), channel_id=1, source_target_pairs={{0,8},{8,0},{16,24},{24,16},{1,9},{9,1},{17,25},{25,17},{2,10},{10... | collective-permute-start | bytes 786440 | tf_op jit(solution)/shard_map/ppermute | solution.py:389
  38.5 9.2 %collective-permute-start.12 = (bf16[2,256,256]{2,1,0:T(8,128)(2,1)S(1)}, bf16[2,256,256]{2,1,0:T(8,128)(2,1)S(1)}, u32[]{:S(2)}, u32[]{:S(2)}) collective-permute-start(bf16[2,256,256]{2,1,0:T(8,128)(2,1)S(1)} %add_convert_fusion.4.near), channel_id=1, source_target_pairs={{0,16},{16,0},{8,24},{24,8},{1,17},{17,1},{9,25},{25,9},{2,18},{18... | collective-permute-start | bytes 786440 | tf_op jit(solution)/shard_map/ppermute | solution.py:391
  39.6 12.9 %collective-permute-start.10 = (bf16[2,256,256]{2,1,0:T(8,128)(2,1)S(1)}, bf16[2,256,256]{2,1,0:T(8,128)(2,1)S(1)}, u32[]{:S(2)}, u32[]{:S(2)}) collective-permute-start(bf16[2,256,256]{2,1,0:T(8,128)(2,1)S(1)} %add_convert_fusion.5.near), channel_id=1, source_target_pairs={{0,16},{16,0},{8,24},{24,8},{1,17},{17,1},{9,25},{25,9},{2,18},{18... | collective-permute-start | bytes 786440 | tf_op jit(solution)/shard_map/ppermute | solution.py:393
  48.9 3.6 %collective-permute-start.13 = (bf16[2,256,256]{2,1,0:T(8,128)(2,1)S(1)}, bf16[2,256,256]{2,1,0:T(8,128)(2,1)S(1)}, u32[]{:S(2)}, u32[]{:S(2)}) collective-permute-start(bf16[2,256,256]{2,1,0:T(8,128)(2,1)S(1)} %get-tuple-element.92.refs_1_.refs_0_), channel_id=1, source_target_pairs={{0,8},{8,0},{16,24},{24,16},{1,9},{9,1},{17,25},{25,17},{2,10},{10... | collective-permute-start | bytes 786440 | tf_op jit(solution)/shard_map/ppermute | solution.py:412
  53.2 1.6 %collective-permute-start.15 = (bf16[2,256,256]{2,1,0:T(8,128)(2,1)S(1)}, bf16[2,256,256]{2,1,0:T(8,128)(2,1)S(1)}, u32[]{:S(2)}, u32[]{:S(2)}) collective-permute-start(bf16[2,256,256]{2,1,0:T(8,128)(2,1)S(1)} %get-tuple-element.93.refs_2_.refs_1_), channel_id=1, source_target_pairs={{0,8},{8,0},{16,24},{24,16},{1,9},{9,1},{17,25},{25,17},{2,10},{10... | collective-permute-start | bytes 786440 | tf_op jit(solution)/shard_map/ppermute | solution.py:425
  53.3 5.2 %collective-permute-start.14 = (f32[80,256]{1,0:T(8,128)S(1)}, f32[80,256]{1,0:T(8,128)S(1)}, u32[]{:S(2)}, u32[]{:S(2)}) collective-permute-start(f32[80,256]{1,0:T(8,128)S(1)} %dynamic-slice_bitcast_fusion), channel_id=1, source_target_pairs={{0,8},{8,0},{16,24},{24,16},{1,9},{9,1},{17,25},{25,17},{2,10},{10... | collective-permute-start | bytes 245768 | tf_op jit(solution)/shard_map/ppermute | solution.py:432
  56.5 6.7 %collective-permute-start.17 = (bf16[1,256,256]{2,1,0:T(8,128)(2,1)S(1)}, bf16[1,256,256]{2,1,0:T(8,128)(2,1)S(1)}, u32[]{:S(2)}, u32[]{:S(2)}) collective-permute-start(bf16[1,256,256]{2,1,0:T(8,128)(2,1)S(1)} %get-tuple-element.95), channel_id=1, source_target_pairs={{0,2},{2,4},{4,6},{6,7},{7,5},{5,3},{3,1},{1,0},{8,10},{10,12},{12... | collective-permute-start | bytes 393224 | tf_op jit(solution)/shard_map/ppermute | solution.py:454
  58.3 5.3 %collective-permute-start.18 = (bf16[1,256,256]{2,1,0:T(8,128)(2,1)S(1)}, bf16[1,256,256]{2,1,0:T(8,128)(2,1)S(1)}, u32[]{:S(2)}, u32[]{:S(2)}) collective-permute-start(bf16[1,256,256]{2,1,0:T(8,128)(2,1)S(1)} %get-tuple-element.96), channel_id=1, source_target_pairs={{2,0},{4,2},{6,4},{7,6},{5,7},{3,5},{1,3},{0,1},{10,8},{12,10},{14... | collective-permute-start | bytes 393224 | tf_op jit(solution)/shard_map/ppermute | solution.py:455
  61.9 4.3 %collective-permute-start.16 = (bf16[80,256]{1,0:T(8,128)(2,1)S(1)}, bf16[80,256]{1,0:T(8,128)(2,1)S(1)}, u32[]{:S(2)}, u32[]{:S(2)}) collective-permute-start(bf16[80,256]{1,0:T(8,128)(2,1)S(1)} %fusion), channel_id=1, source_target_pairs={{0,1},{1,0},{2,3},{3,2},{4,5},{5,4},{6,7},{7,6},{8,9},{9,8},{10,11... | collective-permute-start | bytes 122888 | tf_op jit(solution)/shard_map/ppermute | solution.py:474
  63.8 7.8 %collective-permute-start.20 = (bf16[2,256,256]{2,1,0:T(8,128)(2,1)S(1)}, bf16[2,256,256]{2,1,0:T(8,128)(2,1)S(1)}, u32[]{:S(2)}, u32[]{:S(2)}) collective-permute-start(bf16[2,256,256]{2,1,0:T(8,128)(2,1)S(1)} %get-tuple-element.103), channel_id=1, source_target_pairs={{0,2},{2,4},{4,6},{6,7},{7,5},{5,3},{3,1},{1,0},{8,10},{10,12},{12... | collective-permute-start | bytes 786440 | tf_op jit(solution)/shard_map/ppermute | solution.py:454
  65.0 6.9 %collective-permute-start.21 = (bf16[2,256,256]{2,1,0:T(8,128)(2,1)S(1)}, bf16[2,256,256]{2,1,0:T(8,128)(2,1)S(1)}, u32[]{:S(2)}, u32[]{:S(2)}) collective-permute-start(bf16[2,256,256]{2,1,0:T(8,128)(2,1)S(1)} %get-tuple-element.104), channel_id=1, source_target_pairs={{2,0},{4,2},{6,4},{7,6},{5,7},{3,5},{1,3},{0,1},{10,8},{12,10},{14... | collective-permute-start | bytes 786440 | tf_op jit(solution)/shard_map/ppermute | solution.py:455
  69.5 4.6 %collective-permute-start.19 = (bf16[80,256]{1,0:T(8,128)(2,1)S(1)}, bf16[80,256]{1,0:T(8,128)(2,1)S(1)}, u32[]{:S(2)}, u32[]{:S(2)}) collective-permute-start(bf16[80,256]{1,0:T(8,128)(2,1)S(1)} %add_convert_fusion.9), channel_id=1, source_target_pairs={{0,2},{1,3},{2,0},{3,1},{4,6},{5,7},{6,4},{7,5},{8,10},{9,11},{10,... | collective-permute-start | bytes 122888 | tf_op jit(solution)/shard_map/ppermute | solution.py:474
  72.0 8.6 %collective-permute-start.22 = (bf16[2,256,256]{2,1,0:T(8,128)(2,1)S(1)}, bf16[2,256,256]{2,1,0:T(8,128)(2,1)S(1)}, u32[]{:S(2)}, u32[]{:S(2)}) collective-permute-start(bf16[2,256,256]{2,1,0:T(8,128)(2,1)S(1)} %get-tuple-element.111), channel_id=1, source_target_pairs={{0,2},{2,4},{4,6},{6,7},{7,5},{5,3},{3,1},{1,0},{8,10},{10,12},{12... | collective-permute-start | bytes 786440 | tf_op jit(solution)/shard_map/ppermute | solution.py:454
  73.6 7.2 %collective-permute-start.23 = (bf16[2,256,256]{2,1,0:T(8,128)(2,1)S(1)}, bf16[2,256,256]{2,1,0:T(8,128)(2,1)S(1)}, u32[]{:S(2)}, u32[]{:S(2)}) collective-permute-start(bf16[2,256,256]{2,1,0:T(8,128)(2,1)S(1)} %get-tuple-element.112), channel_id=1, source_target_pairs={{2,0},{4,2},{6,4},{7,6},{5,7},{3,5},{1,3},{0,1},{10,8},{12,10},{14... | collective-permute-start | bytes 786440 | tf_op jit(solution)/shard_map/ppermute | solution.py:455
  77.5 6.1 %collective-permute-start.26 = (bf16[80,256]{1,0:T(8,128)(2,1)S(1)}, bf16[80,256]{1,0:T(8,128)(2,1)S(1)}, u32[]{:S(2)}, u32[]{:S(2)}) collective-permute-start(bf16[80,256]{1,0:T(8,128)(2,1)S(1)} %add_convert_fusion.8), channel_id=1, source_target_pairs={{0,4},{1,5},{2,6},{3,7},{4,0},{5,1},{6,2},{7,3},{8,12},{9,13},{10,... | collective-permute-start | bytes 122888 | tf_op jit(solution)/shard_map/ppermute | solution.py:474
  80.9 9.0 %collective-permute-start.24 = (bf16[2,256,256]{2,1,0:T(8,128)(2,1)S(1)}, bf16[2,256,256]{2,1,0:T(8,128)(2,1)S(1)}, u32[]{:S(2)}, u32[]{:S(2)}) collective-permute-start(bf16[2,256,256]{2,1,0:T(8,128)(2,1)S(1)} %get-tuple-element.118), channel_id=1, source_target_pairs={{0,2},{2,4},{4,6},{6,7},{7,5},{5,3},{3,1},{1,0},{8,10},{10,12},{12... | collective-permute-start | bytes 786440 | tf_op jit(solution)/shard_map/ppermute | solution.py:454
  83.2 6.7 %collective-permute-start.25 = (bf16[2,256,256]{2,1,0:T(8,128)(2,1)S(1)}, bf16[2,256,256]{2,1,0:T(8,128)(2,1)S(1)}, u32[]{:S(2)}, u32[]{:S(2)}) collective-permute-start(bf16[2,256,256]{2,1,0:T(8,128)(2,1)S(1)} %get-tuple-element.119), channel_id=1, source_target_pairs={{2,0},{4,2},{6,4},{7,6},{5,7},{3,5},{1,3},{0,1},{10,8},{12,10},{14... | collective-permute-start | bytes 786440 | tf_op jit(solution)/shard_map/ppermute | solution.py:455
  83.6 5.6 %collective-permute-start.27 = (f32[64,256]{1,0:T(8,128)S(1)}, f32[64,256]{1,0:T(8,128)S(1)}, u32[]{:S(2)}, u32[]{:S(2)}) collective-permute-start(f32[64,256]{1,0:T(8,128)S(1)} %slice.62.own), channel_id=1, source_target_pairs={{0,16},{16,0},{8,24},{24,8},{1,17},{17,1},{9,25},{25,9},{2,18},{18... | collective-permute-start | bytes 196616 | tf_op jit(solution)/shard_map/ppermute | solution.py:460
  85.4 3.7 %collective-permute-start.28 = (f32[64,256]{1,0:T(8,128)S(1)}, f32[64,256]{1,0:T(8,128)S(1)}, u32[]{:S(2)}, u32[]{:S(2)}) collective-permute-start(f32[64,256]{1,0:T(8,128)S(1)} %slice.62.own), channel_id=1, source_target_pairs={{0,8},{8,0},{16,24},{24,16},{1,9},{9,1},{17,25},{25,17},{2,10},{10... | collective-permute-start | bytes 196616 | tf_op jit(solution)/shard_map/ppermute | solution.py:460
  85.4 3.7 %collective-permute-start.29 = (f32[64,256]{1,0:T(8,128)S(1)}, f32[64,256]{1,0:T(8,128)S(1)}, u32[]{:S(2)}, u32[]{:S(2)}) collective-permute-start(f32[64,256]{1,0:T(8,128)S(1)} %slice.62.own), channel_id=1, source_target_pairs={{0,24},{24,0},{8,16},{16,8},{1,25},{25,1},{9,17},{17,9},{2,26},{26... | collective-permute-start | bytes 196616 | tf_op jit(solution)/shard_map/ppermute | solution.py:460

commit v5 on v4

--- a/solution.py
+++ b/solution.py
@@ -223,7 +223,8 @@
         wgrad[width:] = jnp.broadcast_to(bg, (wgrad.shape[0] - width, width))
 
 
-def backward_kernel(bucket, cap, n_buckets, n_early, lists, values, *refs):
+def backward_kernel(buckets, shift, sides, cap, n_buckets, n_early, lists, values, *refs):
+    swap = lax.rem(lax.axis_index("row"), 2) * sides
     early, refs = refs[:n_early], refs[n_early:]
     parts, (out, grads, buffer, sems, part_sems) = refs[:-5], refs[-5:]
     copies = []
@@ -236,8 +237,12 @@
         parts = []
         for u in range(UNIT):
             parts.append(jnp.dot(grads[destination(lists[first + u])], tiles[at + u], preferred_element_type=F32))
+        begin = jnp.where(first // cap == buckets[-1], shift, 0)
         for u in range(UNIT):
-            out[source(lists[first + u])] += parts[u]
+            k = source(lists[first + u])
+            if sides:
+                k = jnp.where(begin == 0, lax.rem(k + swap, 2 * sides), k)
+            out[k + begin] += parts[u]
 
     def between():
         for c in copies:
@@ -249,13 +254,13 @@
         if n_early:
 
             def step(g, _):
-                use(bucket * cap + g * UNIT, g * UNIT, early[0])
+                use(buckets[0] * cap + g * UNIT, g * UNIT, early[0])
                 return 0
 
-            lax.fori_loop(0, jnp.minimum(lists[n_buckets * cap + bucket], AHEAD), step, 0)
+            lax.fori_loop(0, jnp.minimum(lists[n_buckets * cap + buckets[0]], AHEAD), step, 0)
 
     skip = AHEAD if n_early else 0
-    stream(lists, [bucket], cap, n_buckets, values, buffer, sems, between, use, skip)
+    stream(lists, buckets, cap, n_buckets, values, buffer, sems, between, use, skip)
 
 
 def finish_kernel(own, right, left, out):
@@ -367,15 +372,16 @@
         from_right = lax.ppermute(from_right, "col", left)
         if s == 1:
             cot_other = lax.ppermute(cotangent, "row", across)
-            from_left, from_right, cot_other, lists, kept = lax.optimization_barrier(
-                (from_left, from_right, cot_other, lists, kept)
-            )
+            from_left, lists, kept = lax.optimization_barrier((from_left, lists, kept))
         else:
             if s == 2:
                 (total,) = forward([0, 1], [kept, *now], [])
             else:
                 (total,) = forward([s - 1], now, [total])
-            from_left, from_right, total = lax.optimization_barrier((from_left, from_right, total))
+            if s == 2:
+                from_left, total, cot_other = lax.optimization_barrier((from_left, total, cot_other))
+            else:
+                from_left, total = lax.optimization_barrier((from_left, total))
     far_near = lax.ppermute(from_left[: per_dev // 2], "col", right)
     far_away = lax.ppermute(from_right[per_dev // 2 :], "col", left)
     total, early = forward([half - 1], [from_left, from_right], [total], "next")
@@ -431,10 +437,18 @@
 
     w_sum = quarter(my_core) + lax.ppermute(quarter(1 - my_core), "row", cores)
 
-    def backward(bucket, n_tiles, after=(), early=()):
+    def backward(buckets, n_tiles, after=(), early=()):
         its_lists, *_ = lax.optimization_barrier((lists, *after))
         return pl.pallas_call(
-            functools.partial(backward_kernel, bucket, cap, n_buckets, len(early)),
+            functools.partial(
+                backward_kernel,
+                buckets,
+                n_tiles - per_dev if len(buckets) > 1 else 0,
+                0 if early else per_dev,
+                cap,
+                n_buckets,
+                len(early),
+            ),
             in_specs=[SMEM, HBM] + [VMEM] * len(early) + [ANY] * 4,
             out_specs=VMEM,
             out_shape=jax.ShapeDtypeStruct((n_tiles, width, tile), F32),
@@ -443,16 +457,19 @@
             + [pltpu.SemaphoreType.DMA((4,))],
             compiler_params=params(40),
             cost_estimate=small,
-            name=f"backward_{bucket}",
+            name=f"backward_{buckets[0]}",
         )(its_lists, values, *early, grad_1, grad_2, grad_3, grad_4)
 
-    far_part = backward(half, per_dev, early=[early]).astype(BF16)
+    far_part = backward([half], per_dev, early=[early]).astype(BF16)
     cut = per_dev // 2
+    axes = ("row", "col")
+    first = [(r * n_col + a, r * n_col + b) for r in range(4) for a, b in (left if r % 2 else right)]
+    second = [(b, a) for a, b in first]
     sent = lax.optimization_barrier((far_part[:cut], far_part[cut:]))
     stages = [1 << i for i in range((n_col - 1).bit_length())]
     for d in range(half - 1, -1, -1):
-        to_right = lax.ppermute(sent[0], "col", right)
-        to_left = lax.ppermute(sent[1], "col", left)
+        to_right = lax.ppermute(sent[0], axes, first)
+        to_left = lax.ppermute(sent[1], axes, second)
         step = half - 1 - d
         if step == len(stages):
             w_now, *_ = lax.optimization_barrier((w_sum * grad_scale, *sent))
@@ -468,7 +485,11 @@
                 name="quarters",
             )(*quarters)
             bias_grad = w_now[width // 4]
-        part = backward(d, 2 * per_dev if d else per_dev, sent)
+        if step == 0:
+            part = backward([d, 0], 3 * per_dev, sent)
+            part, own_part = part[: 2 * per_dev], part[2 * per_dev :]
+        elif d:
+            part = backward([d], 2 * per_dev, sent)
         if step < len(stages):
             w_now, part, *_ = lax.optimization_barrier((w_sum.astype(BF16), part, *sent))
             w_came = lax.ppermute(w_now, "col", [(i, i ^ stages[step]) for i in range(n_col)])
@@ -484,9 +505,8 @@
             )
         else:
             sent = (add(for_right, to_right), add(for_left, to_left))
-        sent = lax.optimization_barrier(sent)
-    part, to_right, to_left, weight_grad, bias_grad = lax.optimization_barrier(
-        (part, to_right, to_left, weight_grad, bias_grad)
+    to_right, to_left, weight_grad, bias_grad = lax.optimization_barrier(
+        (to_right, to_left, weight_grad, bias_grad)
     )
     feature_grad = pl.pallas_call(
         finish_kernel,
@@ -495,7 +515,7 @@
         out_shape=jax.ShapeDtypeStruct((node_dev, width), BF16),
         compiler_params=params(8),
         name="finish",
-    )(part, to_right.reshape(node_dev, width), to_left.reshape(node_dev, width))
+    )(own_part, to_right.reshape(node_dev, width), to_left.reshape(node_dev, width))
     return (layer_out, feature_grad, weight_grad, bias_grad)
 
 

time: 91.7 us -> 91.9 us (level)
  starting transfers between devices: 30.2 us -> 34.1 us
  Pallas kernels: 33.2 us -> 29.4 us
    ppermute x3, waiting for transfers between devices: 3.34 us -> 0.01 us  [per_device(): from_right = lax.ppermute(from_right, 'col', left)]
    ppermute x3, waiting for transfers between devices: 1.98 us -> 5.28 us  [per_device(): from_left = lax.ppermute(from_left, 'col', right)]
    pallas_call x5 -> x4, Pallas kernels: 14.3 us -> 11.8 us  [backward(): pl.pallas_call(functools.partial(backward_kernel, buckets, n_tiles - per_...]
    ppermute x3, starting transfers between devices: 4.96 us -> 7.01 us  [per_device(): lax.ppermute(w_now, 'col', [(i, i ^ stages[step]) for i in range(n_col)])]
    ppermute x3, waiting for transfers between devices: 0.04 us -> 2.05 us  [per_device(): lax.ppermute(w_own, 'row', perm)]
    ppermute x8, starting transfers between devices: 8.56 us -> 10.5 us  [the longest x4 6.42 us: per_device(): to_right = lax.ppermute(sent[0], axes, first)]
    ppermute x1, starting transfers between devices: 0.19 us -> 1.79 us  [per_device(): far_away = lax.ppermute(from_right[per_dev // 2:], 'col', left)]
    ppermute x1, starting transfers between devices: 1.94 us -> 0.34 us  [per_device(): far_near = lax.ppermute(from_left[:per_dev // 2], 'col', right)]
  transfers between devices with their start and end apart: 30 -> 30, of which waited for: 16 -> 11; matrix products, arithmetic and copies ran while one was open for 1% -> 2% of each run, Pallas kernels for 33% -> 28%
where the time goes in v5:
time: 91.9 us; the launch traced here: 91.1 us
  starting transfers between devices  34.1 us (37%)
  Pallas kernels  29.4 us (32%)
  waiting for transfers between devices  22.2 us (24%)
  local copies, waits for them, and re-layouts  3.75 us (4%)
  between operations  0.97 us (1%)
    pallas_call x4, Pallas kernels, forward(): pl.pallas_call(functools.partial(forward_kernel, buckets, cap, n_buckets,...  12.3 us
    pallas_call x4, Pallas kernels, backward(): pl.pallas_call(functools.partial(backward_kernel, buckets, n_tiles - per_...  11.8 us
    ppermute x3, starting transfers between devices, per_device(): lax.ppermute(w_now, 'col', [(i, i ^ stages[step]) for i in range(n_col)])  7.01 us
    ppermute x1, waiting for transfers between devices, per_device(): came = lax.ppermute(own_away, 'row', across)  6.98 us
    ppermute x4, starting transfers between devices, per_device(): to_right = lax.ppermute(sent[0], axes, first)  6.42 us
    ppermute x3, waiting for transfers between devices, per_device(): from_left = lax.ppermute(from_left, 'col', right)  5.28 us
    ppermute x3, starting transfers between devices, per_device(): from_left = lax.ppermute(from_left, 'col', right)  5.26 us
    ppermute x4, starting transfers between devices, per_device(): to_left = lax.ppermute(sent[1], axes, second)  4.12 us
  transfers between devices with their start and end apart: 30, of which 11 were waited for; matrix products, arithmetic and copies ran while one was open for 2% of the time, Pallas kernels for 28%

profile of v5, /device:TPU:0, one launch (start us, length us, event | category | flops | bytes accessed | tf_op | source)
XLA Modules:
  0.0 91.1 jit_solution(14251607864381557955)
XLA Ops:
  0.6 3.1 %collective-permute-start = (bf16[2,256,256]{2,1,0:T(8,128)(2,1)}, bf16[2,256,256]{2,1,0:T(8,128)(2,1)S(1)}, u32[]{:S(2)}, u32[]{:S(2)}) collective-permute-start(bf16[2,256,256]{2,1,0:T(8,128)(2,1)} %bitcast.16), channel_id=1, source_target_pairs={{0,2},{2,4},{4,6},{6,7},{7,5},{5,3},{3,1},{1,0},{8,10},{10,12},{12... | collective-permute-start | bytes 786440 | tf_op jit(solution)/shard_map/ppermute | solution.py:371
  3.7 2.0 %collective-permute-start.3 = (bf16[512,256]{1,0:T(8,128)(2,1)}, bf16[512,256]{1,0:T(8,128)(2,1)S(1)}, u32[]{:S(2)}, u32[]{:S(2)}) collective-permute-start(bf16[512,256]{1,0:T(8,128)(2,1)} %cot.1), channel_id=1, source_target_pairs={{0,16},{16,0},{8,24},{24,8},{1,17},{17,1},{9,25},{25,9},{2,18},{18... | collective-permute-start | bytes 786440 | tf_op jit(solution)/shard_map/ppermute | solution.py:374
  5.7 0.9 %copy-done.1 = bf16[512,256]{1,0:T(8,128)(2,1)S(1)} copy-done((bf16[512,256]{1,0:T(8,128)(2,1)S(1)}, bf16[512,256]{1,0:T(8,128)(2,1)}, u32[]{:S(2)}) %copy-start.1) | copy-done | bytes 262168
  6.6 0.7 copy-done.3
  7.3 0.7 copy-done.5
  8.0 0.7 copy-done.6
  8.6 1.9 %lists.1 = (s32[685]{0:T(1024)S(1)}, bf16[2,256,256]{2,1,0:T(8,128)(2,1)S(1)}) custom-call(s32[8,16]{1,0:T(8,128)S(1)} %copy-done.3, s32[8]{0:T(128)S(1)} %bitcast.23, s32[160]{0:T(256)S(1)} %copy-done.5, bf16[2,256,256]{2,1,0:T(8,128)(2,1)S(1)} %bitcast.18), custom_call_target="tpu_custom_call" | custom-call | bytes 4096 | tf_op jit(solution)/shard_map/lists/pallas_call | solution.py:322
  10.6 1.6 %collective-permute-start.1 = (bf16[2,256,256]{2,1,0:T(8,128)(2,1)S(1)}, bf16[2,256,256]{2,1,0:T(8,128)(2,1)S(1)}, u32[]{:S(2)}, u32[]{:S(2)}) collective-permute-start(bf16[2,256,256]{2,1,0:T(8,128)(2,1)S(1)} %collective-permute-done.refs_1_), channel_id=1, source_target_pairs={{0,2},{2,4},{4,6},{6,7},{7,5},{5,3},{3,1},{1,0},{8,10},{10,12},{12... | collective-permute-start | bytes 786440 | tf_op jit(solution)/shard_map/ppermute | solution.py:371
  12.1 0.5 collective-permute-start.5
  12.6 3.6 %forward_1.1.refs_2_ = f32[9,256,256]{2,1,0:T(8,128)S(1)} custom-call(s32[685]{0:T(1024)S(1)} %get-tuple-element.95.lists, bf16[128,256,256]{2,1,0:T(8,128)(2,1)} %bitcast.24, bf16[2,256,256]{2,1,0:T(8,128)(2,1)S(1)} %get-tuple-element.59.refs_0_, bf16[2,256,256]{2,1,0:T(8,128)(2,1)S(1)} %collective-permute-done.refs_1_, ...), custom_call_target="tpu_custom_call" | custom-call | flops 33554432 | bytes 131072 | tf_op jit(solution)/shard_map/forward_1/pallas_call | solution.py:356
  16.2 2.6 %collective-permute-done.1.refs_0_ = bf16[2,256,256]{2,1,0:T(8,128)(2,1)S(1)} collective-permute-done((bf16[2,256,256]{2,1,0:T(8,128)(2,1)S(1)}, bf16[2,256,256]{2,1,0:T(8,128)(2,1)S(1)}, u32[]{:S(2)}, u32[]{:S(2)}) %collective-permute-start.1) | collective-permute-done | bytes 262176 | tf_op jit(solution)/shard_map/ppermute | solution.py:371
  18.9 0.6 collective-permute-start.4
  19.5 1.4 %collective-permute-start.7 = (bf16[2,256,256]{2,1,0:T(8,128)(2,1)S(1)}, bf16[2,256,256]{2,1,0:T(8,128)(2,1)S(1)}, u32[]{:S(2)}, u32[]{:S(2)}) collective-permute-start(bf16[2,256,256]{2,1,0:T(8,128)(2,1)S(1)} %collective-permute-done.5.refs_1_), channel_id=1, source_target_pairs={{2,0},{4,2},{6,4},{7,6},{5,7},{3,5},{1,3},{0,1},{10,8},{12,10},{14... | collective-permute-start | bytes 786440 | tf_op jit(solution)/shard_map/ppermute | solution.py:372
  20.9 2.8 %forward_2.1.refs_2_ = f32[9,256,256]{2,1,0:T(8,128)S(1)} custom-call(s32[685]{0:T(1024)S(1)} %get-tuple-element.95.lists, bf16[128,256,256]{2,1,0:T(8,128)(2,1)} %bitcast.25, bf16[2,256,256]{2,1,0:T(8,128)(2,1)S(1)} %collective-permute-done.1.refs_0_, bf16[2,256,256]{2,1,0:T(8,128)(2,1)S(1)} %collective-permute-done.5.refs_1_, ...), custom_call_target="tpu_custom_call" | custom-call | flops 33554432 | bytes 131072 | tf_op jit(solution)/shard_map/forward_2/pallas_call | solution.py:356
  23.7 2.6 %collective-permute-done.4.refs_0_ = bf16[2,256,256]{2,1,0:T(8,128)(2,1)S(1)} collective-permute-done((bf16[2,256,256]{2,1,0:T(8,128)(2,1)S(1)}, bf16[2,256,256]{2,1,0:T(8,128)(2,1)S(1)}, u32[]{:S(2)}, u32[]{:S(2)}) %collective-permute-start.4) | collective-permute-done | bytes 262176 | tf_op jit(solution)/shard_map/ppermute | solution.py:371
  26.7 1.8 %collective-permute-start.8 = (bf16[1,256,256]{2,1,0:T(8,128)(2,1)S(1)}, bf16[1,256,256]{2,1,0:T(8,128)(2,1)S(1)}, u32[]{:S(2)}, u32[]{:S(2)}) collective-permute-start(bf16[1,256,256]{2,1,0:T(8,128)(2,1)S(1)} %slice.72), channel_id=1, source_target_pairs={{2,0},{4,2},{6,4},{7,6},{5,7},{3,5},{1,3},{0,1},{10,8},{12,10},{14... | collective-permute-start | bytes 393224 | tf_op jit(solution)/shard_map/ppermute | solution.py:386
  28.5 3.9 %forward_3.1 = (f32[9,256,256]{2,1,0:T(8,128)S(1)}, bf16[16,256,256]{2,1,0:T(8,128)(2,1)S(1)}) custom-call(s32[685]{0:T(1024)S(1)} %get-tuple-element.95.lists, bf16[128,256,256]{2,1,0:T(8,128)(2,1)} %bitcast.26, bf16[2,256,256]{2,1,0:T(8,128)(2,1)S(1)} %collective-permute-done.4.refs_0_, bf16[2,256,256]{2,1,0:T(8,128)(2,1)S(1)} %collective-permute-done.7.refs_1_, ...), custom_call_target="tpu_custom_call" | custom-call | flops 33554432 | bytes 131072 | tf_op jit(solution)/shard_map/forward_3/pallas_call | solution.py:356
  32.5 2.1 %forward_4.1 = (bf16[2,256,256]{2,1,0:T(8,128)(2,1)S(1)}, bf16[2,256,256]{2,1,0:T(8,128)(2,1)S(1)}, bf16[2,256,256]{2,1,0:T(8,128)(2,1)S(1)}, bf16[2,256,256]{2,1,0:T(8,128)(2,1)S(1)}) custom-call(s32[685]{0:T(1024)S(1)} %get-tuple-element.95.lists, bf16[128,256,256]{2,1,0:T(8,128)(2,1)} %bitcast.27, ...), custom_call_target="tpu_custom_call" | custom-call | flops 33554432 | bytes 131072 | tf_op jit(solution)/shard_map/forward_4/pallas_call | solution.py:356
  34.6 0.5 collective-permute-start.9
  35.1 1.0 %collective-permute-done.11 = bf16[2,256,256]{2,1,0:T(8,128)(2,1)S(1)} collective-permute-done((bf16[2,256,256]{2,1,0:T(8,128)(2,1)S(1)}, bf16[2,256,256]{2,1,0:T(8,128)(2,1)S(1)}, u32[]{:S(2)}, u32[]{:S(2)}) %collective-permute-start.11) | collective-permute-done | bytes 262176 | tf_op jit(solution)/shard_map/ppermute | solution.py:394
  36.6 1.9 %collective-permute-start.10 = (bf16[2,256,256]{2,1,0:T(8,128)(2,1)S(1)}, bf16[2,256,256]{2,1,0:T(8,128)(2,1)S(1)}, u32[]{:S(2)}, u32[]{:S(2)}) collective-permute-start(bf16[2,256,256]{2,1,0:T(8,128)(2,1)S(1)} %add_convert_fusion.5.near), channel_id=1, source_target_pairs={{0,16},{16,0},{8,24},{24,8},{1,17},{17,1},{9,25},{25,9},{2,18},{18... | collective-permute-start | bytes 786440 | tf_op jit(solution)/shard_map/ppermute | solution.py:399
  38.4 7.0 %collective-permute-done.12.away = bf16[2,256,256]{2,1,0:T(8,128)(2,1)S(1)} collective-permute-done((bf16[2,256,256]{2,1,0:T(8,128)(2,1)S(1)}, bf16[2,256,256]{2,1,0:T(8,128)(2,1)S(1)}, u32[]{:S(2)}, u32[]{:S(2)}) %collective-permute-start.12) | collective-permute-done | bytes 262176 | tf_op jit(solution)/shard_map/ppermute | solution.py:397
  45.4 1.2 %dense_own.1 = (bf16[512,256]{1,0:T(8,128)(2,1)}, bf16[2,256,256]{2,1,0:T(8,128)(2,1)S(1)}, f32[264,256]{1,0:T(8,128)S(1)}) custom-call(bf16[2,256,256]{2,1,0:T(8,128)(2,1)S(1)} %add_convert_fusion.5.near, bf16[2,256,256]{2,1,0:T(8,128)(2,1)S(1)} %collective-permute-done.12.away, bf16[256,256]{1,0:T(8,128)(2,1)S(1)} %copy-done, f32[1,256]{1,0:T(1,128)S(1)} %bitcast.21, ...), custom_call_target="tpu_custom_call" | custom-call | flops 50331648 | bytes 131072 | tf_op jit(solution)/shard_map/dense_own/pallas_call | solution.py:405
  46.6 3.6 %collective-permute-done.10.away = bf16[2,256,256]{2,1,0:T(8,128)(2,1)S(1)} collective-permute-done((bf16[2,256,256]{2,1,0:T(8,128)(2,1)S(1)}, bf16[2,256,256]{2,1,0:T(8,128)(2,1)S(1)}, u32[]{:S(2)}, u32[]{:S(2)}) %collective-permute-start.10) | collective-permute-done | bytes 262176 | tf_op jit(solution)/shard_map/ppermute | solution.py:399
  50.2 0.7 dense_away.1
  51.0 0.4 collective-permute-start.15
  51.5 1.0 %collective-permute-done.14.refs_4_.refs_3_ = bf16[2,256,256]{2,1,0:T(8,128)(2,1)S(1)} collective-permute-done((bf16[2,256,256]{2,1,0:T(8,128)(2,1)S(1)}, bf16[2,256,256]{2,1,0:T(8,128)(2,1)S(1)}, u32[]{:S(2)}, u32[]{:S(2)}) %collective-permute-start.14) | collective-permute-done | bytes 262176 | tf_op jit(solution)/shard_map/ppermute | solution.py:431
  52.5 1.6 %backward_4.1 = f32[2,256,256]{2,1,0:T(8,128)S(1)} custom-call(s32[685]{0:T(1024)S(1)} %get-tuple-element.95.lists, bf16[128,256,256]{2,1,0:T(8,128)(2,1)} %bitcast.28, bf16[16,256,256]{2,1,0:T(8,128)(2,1)S(1)} %get-tuple-element.65.refs_3_.refs_0_, bf16[2,256,256]{2,1,0:T(8,128)(2,1)S(1)} %get-tuple-element.74.refs_1_.refs_0_, ...), custom_call_target="tpu_custom_call" | custom-call | flops 33554432 | bytes 131072 | tf_op jit(solution)/shard_map/backward_4/pallas_call | solution.py:442
  54.2 1.0 %collective-permute-start.17 = (bf16[1,256,256]{2,1,0:T(8,128)(2,1)S(1)}, bf16[1,256,256]{2,1,0:T(8,128)(2,1)S(1)}, u32[]{:S(2)}, u32[]{:S(2)}) collective-permute-start(bf16[1,256,256]{2,1,0:T(8,128)(2,1)S(1)} %get-tuple-element.80), channel_id=1, source_target_pairs={{0,2},{2,4},{4,6},{6,7},{7,5},{5,3},{3,1},{1,0},{10,8},{12,10},{14... | collective-permute-start | bytes 393224 | tf_op jit(solution)/shard_map/ppermute | solution.py:471
  55.2 1.1 %collective-permute-start.18 = (bf16[1,256,256]{2,1,0:T(8,128)(2,1)S(1)}, bf16[1,256,256]{2,1,0:T(8,128)(2,1)S(1)}, u32[]{:S(2)}, u32[]{:S(2)}) collective-permute-start(bf16[1,256,256]{2,1,0:T(8,128)(2,1)S(1)} %get-tuple-element.81), channel_id=1, source_target_pairs={{2,0},{4,2},{6,4},{7,6},{5,7},{3,5},{1,3},{0,1},{8,10},{10,12},{12... | collective-permute-start | bytes 393224 | tf_op jit(solution)/shard_map/ppermute | solution.py:472
  56.4 3.6 %backward_3.1 = f32[6,256,256]{2,1,0:T(8,128)S(1)} custom-call(s32[685]{0:T(1024)S(1)} %get-tuple-element.95.lists, bf16[128,256,256]{2,1,0:T(8,128)(2,1)} %bitcast.29, bf16[2,256,256]{2,1,0:T(8,128)(2,1)S(1)} %get-tuple-element.74.refs_1_.refs_0_, bf16[2,256,256]{2,1,0:T(8,128)(2,1)S(1)} %get-tuple-element.78.refs_2_.refs_1_, ...), custom_call_target="tpu_custom_call" | custom-call | flops 33554432 | bytes 131072 | tf_op jit(solution)/shard_map/backward_3/pallas_call | solution.py:442
  60.1 4.1 %collective-permute-start.16 = (bf16[80,256]{1,0:T(8,128)(2,1)S(1)}, bf16[80,256]{1,0:T(8,128)(2,1)S(1)}, u32[]{:S(2)}, u32[]{:S(2)}) collective-permute-start(bf16[80,256]{1,0:T(8,128)(2,1)S(1)} %fusion), channel_id=1, source_target_pairs={{0,1},{1,0},{2,3},{3,2},{4,5},{5,4},{6,7},{7,6},{8,9},{9,8},{10,11... | collective-permute-start | bytes 122888 | tf_op jit(solution)/shard_map/ppermute | solution.py:495
  64.5 2.0 %collective-permute-start.20 = (bf16[2,256,256]{2,1,0:T(8,128)(2,1)S(1)}, bf16[2,256,256]{2,1,0:T(8,128)(2,1)S(1)}, u32[]{:S(2)}, u32[]{:S(2)}) collective-permute-start(bf16[2,256,256]{2,1,0:T(8,128)(2,1)S(1)} %pad_maximum_fusion), channel_id=1, source_target_pairs={{0,2},{2,4},{4,6},{6,7},{7,5},{5,3},{3,1},{1,0},{10,8},{12,10},{14... | collective-permute-start | bytes 786440 | tf_op jit(solution)/shard_map/ppermute | solution.py:471
  66.6 3.1 %backward_2.1 = f32[4,256,256]{2,1,0:T(8,128)S(1)} custom-call(s32[685]{0:T(1024)S(1)} %get-tuple-element.95.lists, bf16[128,256,256]{2,1,0:T(8,128)(2,1)} %bitcast.30, bf16[2,256,256]{2,1,0:T(8,128)(2,1)S(1)} %get-tuple-element.74.refs_1_.refs_0_, bf16[2,256,256]{2,1,0:T(8,128)(2,1)S(1)} %get-tuple-element.78.refs_2_.refs_1_, ...), custom_call_target="tpu_custom_call" | custom-call | flops 33554432 | bytes 131072 | tf_op jit(solution)/shard_map/backward_2/pallas_call | solution.py:442
  69.7 1.9 %collective-permute-start.19 = (bf16[80,256]{1,0:T(8,128)(2,1)S(1)}, bf16[80,256]{1,0:T(8,128)(2,1)S(1)}, u32[]{:S(2)}, u32[]{:S(2)}) collective-permute-start(bf16[80,256]{1,0:T(8,128)(2,1)S(1)} %add_convert_fusion.9), channel_id=1, source_target_pairs={{0,2},{1,3},{2,0},{3,1},{4,6},{5,7},{6,4},{7,5},{8,10},{9,11},{10,... | collective-permute-start | bytes 122888 | tf_op jit(solution)/shard_map/ppermute | solution.py:495
  71.7 0.8 collective-permute-done.21
  72.6 0.9 %collective-permute-start.22 = (bf16[2,256,256]{2,1,0:T(8,128)(2,1)S(1)}, bf16[2,256,256]{2,1,0:T(8,128)(2,1)S(1)}, u32[]{:S(2)}, u32[]{:S(2)}) collective-permute-start(bf16[2,256,256]{2,1,0:T(8,128)(2,1)S(1)} %get-tuple-element.109), channel_id=1, source_target_pairs={{0,2},{2,4},{4,6},{6,7},{7,5},{5,3},{3,1},{1,0},{10,8},{12,10},{14... | collective-permute-start | bytes 786440 | tf_op jit(solution)/shard_map/ppermute | solution.py:471
  73.6 1.7 %collective-permute-start.23 = (bf16[2,256,256]{2,1,0:T(8,128)(2,1)S(1)}, bf16[2,256,256]{2,1,0:T(8,128)(2,1)S(1)}, u32[]{:S(2)}, u32[]{:S(2)}) collective-permute-start(bf16[2,256,256]{2,1,0:T(8,128)(2,1)S(1)} %get-tuple-element.108), channel_id=1, source_target_pairs={{2,0},{4,2},{6,4},{7,6},{5,7},{3,5},{1,3},{0,1},{8,10},{10,12},{12... | collective-permute-start | bytes 786440 | tf_op jit(solution)/shard_map/ppermute | solution.py:472
  75.2 3.5 %backward_1.1 = f32[4,256,256]{2,1,0:T(8,128)S(1)} custom-call(s32[685]{0:T(1024)S(1)} %get-tuple-element.95.lists, bf16[128,256,256]{2,1,0:T(8,128)(2,1)} %bitcast.31, bf16[2,256,256]{2,1,0:T(8,128)(2,1)S(1)} %get-tuple-element.74.refs_1_.refs_0_, bf16[2,256,256]{2,1,0:T(8,128)(2,1)S(1)} %get-tuple-element.78.refs_2_.refs_1_, ...), custom_call_target="tpu_custom_call" | custom-call | flops 33554432 | bytes 131072 | tf_op jit(solution)/shard_map/backward_1/pallas_call | solution.py:442
  78.7 1.0 %collective-permute-start.26 = (bf16[80,256]{1,0:T(8,128)(2,1)S(1)}, bf16[80,256]{1,0:T(8,128)(2,1)S(1)}, u32[]{:S(2)}, u32[]{:S(2)}) collective-permute-start(bf16[80,256]{1,0:T(8,128)(2,1)S(1)} %add_convert_fusion.8), channel_id=1, source_target_pairs={{0,4},{1,5},{2,6},{3,7},{4,0},{5,1},{6,2},{7,3},{8,12},{9,13},{10,... | collective-permute-start | bytes 122888 | tf_op jit(solution)/shard_map/ppermute | solution.py:495
  80.1 2.4 %collective-permute-start.24 = (bf16[2,256,256]{2,1,0:T(8,128)(2,1)S(1)}, bf16[2,256,256]{2,1,0:T(8,128)(2,1)S(1)}, u32[]{:S(2)}, u32[]{:S(2)}) collective-permute-start(bf16[2,256,256]{2,1,0:T(8,128)(2,1)S(1)} %get-tuple-element.107), channel_id=1, source_target_pairs={{0,2},{2,4},{4,6},{6,7},{7,5},{5,3},{3,1},{1,0},{10,8},{12,10},{14... | collective-permute-start | bytes 786440 | tf_op jit(solution)/shard_map/ppermute | solution.py:471
  82.5 1.3 %collective-permute-start.25 = (bf16[2,256,256]{2,1,0:T(8,128)(2,1)S(1)}, bf16[2,256,256]{2,1,0:T(8,128)(2,1)S(1)}, u32[]{:S(2)}, u32[]{:S(2)}) collective-permute-start(bf16[2,256,256]{2,1,0:T(8,128)(2,1)S(1)} %get-tuple-element.106), channel_id=1, source_target_pairs={{2,0},{4,2},{6,4},{7,6},{5,7},{3,5},{1,3},{0,1},{8,10},{10,12},{12... | collective-permute-start | bytes 786440 | tf_op jit(solution)/shard_map/ppermute | solution.py:472
  83.7 0.9 collective-permute-done.26
  84.8 2.0 %collective-permute-start.29 = (f32[64,256]{1,0:T(8,128)S(1)}, f32[64,256]{1,0:T(8,128)S(1)}, u32[]{:S(2)}, u32[]{:S(2)}) collective-permute-start(f32[64,256]{1,0:T(8,128)S(1)} %slice.70.own), channel_id=1, source_target_pairs={{0,24},{24,0},{8,16},{16,8},{1,25},{25,1},{9,17},{17,9},{2,26},{26... | collective-permute-start | bytes 196616 | tf_op jit(solution)/shard_map/ppermute | solution.py:477
  86.9 0.6 slice.71
  87.5 2.0 %collective-permute-done.27.y = f32[64,256]{1,0:T(8,128)S(1)} collective-permute-done((f32[64,256]{1,0:T(8,128)S(1)}, f32[64,256]{1,0:T(8,128)S(1)}, u32[]{:S(2)}, u32[]{:S(2)}) %collective-permute-start.27) | collective-permute-done | bytes 65568 | tf_op jit(solution)/shard_map/ppermute | solution.py:477
  89.5 0.7 quarters.1
  90.3 0.9 finish.1
  (61 shorter events, 2.2 us)
Async XLA Ops:
  0.6 9.9 %collective-permute-start = (bf16[2,256,256]{2,1,0:T(8,128)(2,1)}, bf16[2,256,256]{2,1,0:T(8,128)(2,1)S(1)}, u32[]{:S(2)}, u32[]{:S(2)}) collective-permute-start(bf16[2,256,256]{2,1,0:T(8,128)(2,1)} %bitcast.16), channel_id=1, source_target_pairs={{0,2},{2,4},{4,6},{6,7},{7,5},{5,3},{3,1},{1,0},{8,10},{10,12},{12... | collective-permute-start | bytes 786440 | tf_op jit(solution)/shard_map/ppermute | solution.py:371
  3.7 8.4 %collective-permute-start.2 = (bf16[2,256,256]{2,1,0:T(8,128)(2,1)}, bf16[2,256,256]{2,1,0:T(8,128)(2,1)S(1)}, u32[]{:S(2)}, u32[]{:S(2)}) collective-permute-start(bf16[2,256,256]{2,1,0:T(8,128)(2,1)} %bitcast.17), channel_id=1, source_target_pairs={{2,0},{4,2},{6,4},{7,6},{5,7},{3,5},{1,3},{0,1},{10,8},{12,10},{14... | collective-permute-start | bytes 786440 | tf_op jit(solution)/shard_map/ppermute | solution.py:372
  3.7 12.5 %collective-permute-start.3 = (bf16[512,256]{1,0:T(8,128)(2,1)}, bf16[512,256]{1,0:T(8,128)(2,1)S(1)}, u32[]{:S(2)}, u32[]{:S(2)}) collective-permute-start(bf16[512,256]{1,0:T(8,128)(2,1)} %cot.1), channel_id=1, source_target_pairs={{0,16},{16,0},{8,24},{24,8},{1,17},{17,1},{9,25},{25,9},{2,18},{18... | collective-permute-start | bytes 786440 | tf_op jit(solution)/shard_map/ppermute | solution.py:374
  5.7 0.9 %copy-start.1 = (bf16[512,256]{1,0:T(8,128)(2,1)S(1)}, bf16[512,256]{1,0:T(8,128)(2,1)}, u32[]{:S(2)}) copy-start(bf16[512,256]{1,0:T(8,128)(2,1)} %param.8) | copy-start | bytes 786436
  6.6 0.7 copy-start.3
  7.3 0.7 copy-start.5
  8.0 0.7 copy-start.6
  10.6 8.3 %collective-permute-start.1 = (bf16[2,256,256]{2,1,0:T(8,128)(2,1)S(1)}, bf16[2,256,256]{2,1,0:T(8,128)(2,1)S(1)}, u32[]{:S(2)}, u32[]{:S(2)}) collective-permute-start(bf16[2,256,256]{2,1,0:T(8,128)(2,1)S(1)} %collective-permute-done.refs_1_), channel_id=1, source_target_pairs={{0,2},{2,4},{4,6},{6,7},{7,5},{5,3},{3,1},{1,0},{8,10},{10,12},{12... | collective-permute-start | bytes 786440 | tf_op jit(solution)/shard_map/ppermute | solution.py:371
  12.1 7.4 %collective-permute-start.5 = (bf16[2,256,256]{2,1,0:T(8,128)(2,1)S(1)}, bf16[2,256,256]{2,1,0:T(8,128)(2,1)S(1)}, u32[]{:S(2)}, u32[]{:S(2)}) collective-permute-start(bf16[2,256,256]{2,1,0:T(8,128)(2,1)S(1)} %collective-permute-done.2.refs_2_), channel_id=1, source_target_pairs={{2,0},{4,2},{6,4},{7,6},{5,7},{3,5},{1,3},{0,1},{10,8},{12,10},{14... | collective-permute-start | bytes 786440 | tf_op jit(solution)/shard_map/ppermute | solution.py:372
  18.9 7.4 %collective-permute-start.4 = (bf16[2,256,256]{2,1,0:T(8,128)(2,1)S(1)}, bf16[2,256,256]{2,1,0:T(8,128)(2,1)S(1)}, u32[]{:S(2)}, u32[]{:S(2)}) collective-permute-start(bf16[2,256,256]{2,1,0:T(8,128)(2,1)S(1)} %collective-permute-done.1.refs_0_), channel_id=1, source_target_pairs={{0,2},{2,4},{4,6},{6,7},{7,5},{5,3},{3,1},{1,0},{8,10},{10,12},{12... | collective-permute-start | bytes 786440 | tf_op jit(solution)/shard_map/ppermute | solution.py:371
  19.5 7.1 %collective-permute-start.7 = (bf16[2,256,256]{2,1,0:T(8,128)(2,1)S(1)}, bf16[2,256,256]{2,1,0:T(8,128)(2,1)S(1)}, u32[]{:S(2)}, u32[]{:S(2)}) collective-permute-start(bf16[2,256,256]{2,1,0:T(8,128)(2,1)S(1)} %collective-permute-done.5.refs_1_), channel_id=1, source_target_pairs={{2,0},{4,2},{6,4},{7,6},{5,7},{3,5},{1,3},{0,1},{10,8},{12,10},{14... | collective-permute-start | bytes 786440 | tf_op jit(solution)/shard_map/ppermute | solution.py:372
  26.3 6.1 %collective-permute-start.6 = (bf16[1,256,256]{2,1,0:T(8,128)(2,1)S(1)}, bf16[1,256,256]{2,1,0:T(8,128)(2,1)S(1)}, u32[]{:S(2)}, u32[]{:S(2)}) collective-permute-start(bf16[1,256,256]{2,1,0:T(8,128)(2,1)S(1)} %slice.56), channel_id=1, source_target_pairs={{0,2},{2,4},{4,6},{6,7},{7,5},{5,3},{3,1},{1,0},{8,10},{10,12},{12... | collective-permute-start | bytes 393224 | tf_op jit(solution)/shard_map/ppermute | solution.py:385
  26.7 5.8 %collective-permute-start.8 = (bf16[1,256,256]{2,1,0:T(8,128)(2,1)S(1)}, bf16[1,256,256]{2,1,0:T(8,128)(2,1)S(1)}, u32[]{:S(2)}, u32[]{:S(2)}) collective-permute-start(bf16[1,256,256]{2,1,0:T(8,128)(2,1)S(1)} %slice.72), channel_id=1, source_target_pairs={{2,0},{4,2},{6,4},{7,6},{5,7},{3,5},{1,3},{0,1},{10,8},{12,10},{14... | collective-permute-start | bytes 393224 | tf_op jit(solution)/shard_map/ppermute | solution.py:386
  32.4 13.0 %copy-start = (bf16[256,256]{1,0:T(8,128)(2,1)S(1)}, bf16[256,256]{1,0:T(8,128)(2,1)}, u32[]{:S(2)}) copy-start(bf16[256,256]{1,0:T(8,128)(2,1)} %weight.3) | copy-start | bytes 393220
  32.5 13.0 %copy-start.2 = (bf16[512,256]{1,0:T(8,128)(2,1)S(1)}, bf16[512,256]{1,0:T(8,128)(2,1)}, u32[]{:S(2)}) copy-start(bf16[512,256]{1,0:T(8,128)(2,1)} %cot.1) | copy-start | bytes 786436
  32.5 13.0 %copy-start.4 = (f32[256]{0:T(256)S(1)}, f32[256]{0:T(256)}, u32[]{:S(2)}) copy-start(f32[256]{0:T(256)} %param.13) | copy-start | bytes 3076
  34.5 1.6 %collective-permute-start.11 = (bf16[2,256,256]{2,1,0:T(8,128)(2,1)S(1)}, bf16[2,256,256]{2,1,0:T(8,128)(2,1)S(1)}, u32[]{:S(2)}, u32[]{:S(2)}) collective-permute-start(bf16[2,256,256]{2,1,0:T(8,128)(2,1)S(1)} %get-tuple-element.69), channel_id=1, source_target_pairs={{0,8},{8,0},{16,24},{24,16},{1,9},{9,1},{17,25},{25,17},{2,10},{10... | collective-permute-start | bytes 786440 | tf_op jit(solution)/shard_map/ppermute | solution.py:394
  34.6 1.9 %collective-permute-start.9 = (bf16[2,256,256]{2,1,0:T(8,128)(2,1)S(1)}, bf16[2,256,256]{2,1,0:T(8,128)(2,1)S(1)}, u32[]{:S(2)}, u32[]{:S(2)}) collective-permute-start(bf16[2,256,256]{2,1,0:T(8,128)(2,1)S(1)} %get-tuple-element.67), channel_id=1, source_target_pairs={{0,8},{8,0},{16,24},{24,16},{1,9},{9,1},{17,25},{25,17},{2,10},{10... | collective-permute-start | bytes 786440 | tf_op jit(solution)/shard_map/ppermute | solution.py:395
  36.2 9.2 %collective-permute-start.12 = (bf16[2,256,256]{2,1,0:T(8,128)(2,1)S(1)}, bf16[2,256,256]{2,1,0:T(8,128)(2,1)S(1)}, u32[]{:S(2)}, u32[]{:S(2)}) collective-permute-start(bf16[2,256,256]{2,1,0:T(8,128)(2,1)S(1)} %add_convert_fusion.4.near), channel_id=1, source_target_pairs={{0,16},{16,0},{8,24},{24,8},{1,17},{17,1},{9,25},{25,9},{2,18},{18... | collective-permute-start | bytes 786440 | tf_op jit(solution)/shard_map/ppermute | solution.py:397
  36.6 13.7 %collective-permute-start.10 = (bf16[2,256,256]{2,1,0:T(8,128)(2,1)S(1)}, bf16[2,256,256]{2,1,0:T(8,128)(2,1)S(1)}, u32[]{:S(2)}, u32[]{:S(2)}) collective-permute-start(bf16[2,256,256]{2,1,0:T(8,128)(2,1)S(1)} %add_convert_fusion.5.near), channel_id=1, source_target_pairs={{0,16},{16,0},{8,24},{24,8},{1,17},{17,1},{9,25},{25,9},{2,18},{18... | collective-permute-start | bytes 786440 | tf_op jit(solution)/shard_map/ppermute | solution.py:399
  46.6 3.6 %collective-permute-start.13 = (bf16[2,256,256]{2,1,0:T(8,128)(2,1)S(1)}, bf16[2,256,256]{2,1,0:T(8,128)(2,1)S(1)}, u32[]{:S(2)}, u32[]{:S(2)}) collective-permute-start(bf16[2,256,256]{2,1,0:T(8,128)(2,1)S(1)} %get-tuple-element.74.refs_1_.refs_0_), channel_id=1, source_target_pairs={{0,8},{8,0},{16,24},{24,16},{1,9},{9,1},{17,25},{25,17},{2,10},{10... | collective-permute-start | bytes 786440 | tf_op jit(solution)/shard_map/ppermute | solution.py:418
  50.9 1.6 %collective-permute-start.14 = (bf16[2,256,256]{2,1,0:T(8,128)(2,1)S(1)}, bf16[2,256,256]{2,1,0:T(8,128)(2,1)S(1)}, u32[]{:S(2)}, u32[]{:S(2)}) collective-permute-start(bf16[2,256,256]{2,1,0:T(8,128)(2,1)S(1)} %get-tuple-element.78.refs_2_.refs_1_), channel_id=1, source_target_pairs={{0,8},{8,0},{16,24},{24,16},{1,9},{9,1},{17,25},{25,17},{2,10},{10... | collective-permute-start | bytes 786440 | tf_op jit(solution)/shard_map/ppermute | solution.py:431
  51.0 5.3 %collective-permute-start.15 = (f32[80,256]{1,0:T(8,128)S(1)}, f32[80,256]{1,0:T(8,128)S(1)}, u32[]{:S(2)}, u32[]{:S(2)}) collective-permute-start(f32[80,256]{1,0:T(8,128)S(1)} %dynamic-slice_bitcast_fusion), channel_id=1, source_target_pairs={{0,8},{8,0},{16,24},{24,16},{1,9},{9,1},{17,25},{25,17},{2,10},{10... | collective-permute-start | bytes 245768 | tf_op jit(solution)/shard_map/ppermute | solution.py:438
  54.2 10.0 %collective-permute-start.17 = (bf16[1,256,256]{2,1,0:T(8,128)(2,1)S(1)}, bf16[1,256,256]{2,1,0:T(8,128)(2,1)S(1)}, u32[]{:S(2)}, u32[]{:S(2)}) collective-permute-start(bf16[1,256,256]{2,1,0:T(8,128)(2,1)S(1)} %get-tuple-element.80), channel_id=1, source_target_pairs={{0,2},{2,4},{4,6},{6,7},{7,5},{5,3},{3,1},{1,0},{10,8},{12,10},{14... | collective-permute-start | bytes 393224 | tf_op jit(solution)/shard_map/ppermute | solution.py:471
  55.2 9.0 %collective-permute-start.18 = (bf16[1,256,256]{2,1,0:T(8,128)(2,1)S(1)}, bf16[1,256,256]{2,1,0:T(8,128)(2,1)S(1)}, u32[]{:S(2)}, u32[]{:S(2)}) collective-permute-start(bf16[1,256,256]{2,1,0:T(8,128)(2,1)S(1)} %get-tuple-element.81), channel_id=1, source_target_pairs={{2,0},{4,2},{6,4},{7,6},{5,7},{3,5},{1,3},{0,1},{8,10},{10,12},{12... | collective-permute-start | bytes 393224 | tf_op jit(solution)/shard_map/ppermute | solution.py:472
  60.1 6.5 %collective-permute-start.16 = (bf16[80,256]{1,0:T(8,128)(2,1)S(1)}, bf16[80,256]{1,0:T(8,128)(2,1)S(1)}, u32[]{:S(2)}, u32[]{:S(2)}) collective-permute-start(bf16[80,256]{1,0:T(8,128)(2,1)S(1)} %fusion), channel_id=1, source_target_pairs={{0,1},{1,0},{2,3},{3,2},{4,5},{5,4},{6,7},{7,6},{8,9},{9,8},{10,11... | collective-permute-start | bytes 122888 | tf_op jit(solution)/shard_map/ppermute | solution.py:495
  64.4 8.1 %collective-permute-start.21 = (bf16[2,256,256]{2,1,0:T(8,128)(2,1)S(1)}, bf16[2,256,256]{2,1,0:T(8,128)(2,1)S(1)}, u32[]{:S(2)}, u32[]{:S(2)}) collective-permute-start(bf16[2,256,256]{2,1,0:T(8,128)(2,1)S(1)} %pad_maximum_fusion.1), channel_id=1, source_target_pairs={{2,0},{4,2},{6,4},{7,6},{5,7},{3,5},{1,3},{0,1},{8,10},{10,12},{12... | collective-permute-start | bytes 786440 | tf_op jit(solution)/shard_map/ppermute | solution.py:472
  64.5 8.0 %collective-permute-start.20 = (bf16[2,256,256]{2,1,0:T(8,128)(2,1)S(1)}, bf16[2,256,256]{2,1,0:T(8,128)(2,1)S(1)}, u32[]{:S(2)}, u32[]{:S(2)}) collective-permute-start(bf16[2,256,256]{2,1,0:T(8,128)(2,1)S(1)} %pad_maximum_fusion), channel_id=1, source_target_pairs={{0,2},{2,4},{4,6},{6,7},{7,5},{5,3},{3,1},{1,0},{10,8},{12,10},{14... | collective-permute-start | bytes 786440 | tf_op jit(solution)/shard_map/ppermute | solution.py:471
  69.7 5.5 %collective-permute-start.19 = (bf16[80,256]{1,0:T(8,128)(2,1)S(1)}, bf16[80,256]{1,0:T(8,128)(2,1)S(1)}, u32[]{:S(2)}, u32[]{:S(2)}) collective-permute-start(bf16[80,256]{1,0:T(8,128)(2,1)S(1)} %add_convert_fusion.9), channel_id=1, source_target_pairs={{0,2},{1,3},{2,0},{3,1},{4,6},{5,7},{6,4},{7,5},{8,10},{9,11},{10,... | collective-permute-start | bytes 122888 | tf_op jit(solution)/shard_map/ppermute | solution.py:495
  72.6 7.1 %collective-permute-start.22 = (bf16[2,256,256]{2,1,0:T(8,128)(2,1)S(1)}, bf16[2,256,256]{2,1,0:T(8,128)(2,1)S(1)}, u32[]{:S(2)}, u32[]{:S(2)}) collective-permute-start(bf16[2,256,256]{2,1,0:T(8,128)(2,1)S(1)} %get-tuple-element.109), channel_id=1, source_target_pairs={{0,2},{2,4},{4,6},{6,7},{7,5},{5,3},{3,1},{1,0},{10,8},{12,10},{14... | collective-permute-start | bytes 786440 | tf_op jit(solution)/shard_map/ppermute | solution.py:471
  73.6 6.4 %collective-permute-start.23 = (bf16[2,256,256]{2,1,0:T(8,128)(2,1)S(1)}, bf16[2,256,256]{2,1,0:T(8,128)(2,1)S(1)}, u32[]{:S(2)}, u32[]{:S(2)}) collective-permute-start(bf16[2,256,256]{2,1,0:T(8,128)(2,1)S(1)} %get-tuple-element.108), channel_id=1, source_target_pairs={{2,0},{4,2},{6,4},{7,6},{5,7},{3,5},{1,3},{0,1},{8,10},{10,12},{12... | collective-permute-start | bytes 786440 | tf_op jit(solution)/shard_map/ppermute | solution.py:472
  78.7 5.9 %collective-permute-start.26 = (bf16[80,256]{1,0:T(8,128)(2,1)S(1)}, bf16[80,256]{1,0:T(8,128)(2,1)S(1)}, u32[]{:S(2)}, u32[]{:S(2)}) collective-permute-start(bf16[80,256]{1,0:T(8,128)(2,1)S(1)} %add_convert_fusion.8), channel_id=1, source_target_pairs={{0,4},{1,5},{2,6},{3,7},{4,0},{5,1},{6,2},{7,3},{8,12},{9,13},{10,... | collective-permute-start | bytes 122888 | tf_op jit(solution)/shard_map/ppermute | solution.py:495
  80.1 10.2 %collective-permute-start.24 = (bf16[2,256,256]{2,1,0:T(8,128)(2,1)S(1)}, bf16[2,256,256]{2,1,0:T(8,128)(2,1)S(1)}, u32[]{:S(2)}, u32[]{:S(2)}) collective-permute-start(bf16[2,256,256]{2,1,0:T(8,128)(2,1)S(1)} %get-tuple-element.107), channel_id=1, source_target_pairs={{0,2},{2,4},{4,6},{6,7},{7,5},{5,3},{3,1},{1,0},{10,8},{12,10},{14... | collective-permute-start | bytes 786440 | tf_op jit(solution)/shard_map/ppermute | solution.py:471
  82.5 7.8 %collective-permute-start.25 = (bf16[2,256,256]{2,1,0:T(8,128)(2,1)S(1)}, bf16[2,256,256]{2,1,0:T(8,128)(2,1)S(1)}, u32[]{:S(2)}, u32[]{:S(2)}) collective-permute-start(bf16[2,256,256]{2,1,0:T(8,128)(2,1)S(1)} %get-tuple-element.106), channel_id=1, source_target_pairs={{2,0},{4,2},{6,4},{7,6},{5,7},{3,5},{1,3},{0,1},{8,10},{10,12},{12... | collective-permute-start | bytes 786440 | tf_op jit(solution)/shard_map/ppermute | solution.py:472
  84.7 4.9 %collective-permute-start.27 = (f32[64,256]{1,0:T(8,128)S(1)}, f32[64,256]{1,0:T(8,128)S(1)}, u32[]{:S(2)}, u32[]{:S(2)}) collective-permute-start(f32[64,256]{1,0:T(8,128)S(1)} %slice.70.own), channel_id=1, source_target_pairs={{0,16},{16,0},{8,24},{24,8},{1,17},{17,1},{9,25},{25,9},{2,18},{18... | collective-permute-start | bytes 196616 | tf_op jit(solution)/shard_map/ppermute | solution.py:477
  84.7 4.8 %collective-permute-start.28 = (f32[64,256]{1,0:T(8,128)S(1)}, f32[64,256]{1,0:T(8,128)S(1)}, u32[]{:S(2)}, u32[]{:S(2)}) collective-permute-start(f32[64,256]{1,0:T(8,128)S(1)} %slice.70.own), channel_id=1, source_target_pairs={{0,8},{8,0},{16,24},{24,16},{1,9},{9,1},{17,25},{25,17},{2,10},{10... | collective-permute-start | bytes 196616 | tf_op jit(solution)/shard_map/ppermute | solution.py:477
  84.8 4.7 %collective-permute-start.29 = (f32[64,256]{1,0:T(8,128)S(1)}, f32[64,256]{1,0:T(8,128)S(1)}, u32[]{:S(2)}, u32[]{:S(2)}) collective-permute-start(f32[64,256]{1,0:T(8,128)S(1)} %slice.70.own), channel_id=1, source_target_pairs={{0,24},{24,0},{8,16},{16,8},{1,25},{25,1},{9,17},{17,9},{2,26},{26... | collective-permute-start | bytes 196616 | tf_op jit(solution)/shard_map/ppermute | solution.py:477

commit v6 on v5

--- a/solution.py
+++ b/solution.py
@@ -491,7 +491,7 @@
         elif d:
             part = backward([d], 2 * per_dev, sent)
         if step < len(stages):
-            w_now, part, *_ = lax.optimization_barrier((w_sum.astype(BF16), part, *sent))
+            w_now, *_ = lax.optimization_barrier((w_sum.astype(BF16), *sent))
             w_came = lax.ppermute(w_now, "col", [(i, i ^ stages[step]) for i in range(n_col)])
             w_sum = w_now.astype(F32) + w_came.astype(F32)
         if d == 0:

time: 91.9 us -> 90.2 us (0.982)
  starting transfers between devices: 34.1 us -> 31 us
  Pallas kernels: 29.4 us -> 32.4 us
  waiting for transfers between devices: 22.2 us -> 20 us
    ppermute x3, waiting for transfers between devices: 5.28 us -> 2.67 us  [per_device(): from_left = lax.ppermute(from_left, 'col', right)]
    ppermute x4, starting transfers between devices: 4.12 us -> 1.67 us  [per_device(): to_left = lax.ppermute(sent[1], axes, second)]
    pallas_call x4, Pallas kernels: 11.8 us -> 13.4 us  [backward(): pl.pallas_call(functools.partial(backward_kernel, buckets, n_tiles - per_...]
    ppermute x1, starting transfers between devices: 0.1 us -> 1.39 us  [per_device(): came = lax.ppermute(own_away, 'row', across)]
    ppermute x3, starting transfers between devices: 7.01 us -> 5.91 us  [per_device(): lax.ppermute(w_now, 'col', [(i, i ^ stages[step]) for i in range(n_col)])]
    ppermute x1, starting transfers between devices: 1.85 us -> 0.77 us  [per_device(): came_away = lax.ppermute(own, 'row', across)]
  transfers between devices with their start and end apart: 30 -> 30, of which waited for: 11 -> 9; matrix products, arithmetic and copies ran while one was open for 2% -> 2% of each run, Pallas kernels for 28% -> 33%
where the time goes in v6:
time: 90.2 us; the launch traced here: 88.8 us
  Pallas kernels  32.4 us (36%)
  starting transfers between devices  31 us (34%)
  waiting for transfers between devices  20 us (22%)
  local copies, waits for them, and re-layouts  3.74 us (4%)
  between operations  0.96 us (1%)
    pallas_call x4, Pallas kernels, backward(): pl.pallas_call(functools.partial(backward_kernel, buckets, n_tiles - per_...  13.4 us
    pallas_call x4, Pallas kernels, forward(): pl.pallas_call(functools.partial(forward_kernel, buckets, cap, n_buckets,...  13.2 us
    ppermute x1, waiting for transfers between devices, per_device(): came = lax.ppermute(own_away, 'row', across)  6.98 us
    ppermute x4, starting transfers between devices, per_device(): to_right = lax.ppermute(sent[0], axes, first)  6.7 us
    ppermute x3, starting transfers between devices, per_device(): lax.ppermute(w_now, 'col', [(i, i ^ stages[step]) for i in range(n_col)])  5.91 us
    ppermute x3, starting transfers between devices, per_device(): from_left = lax.ppermute(from_left, 'col', right)  5.29 us
    ppermute x1, waiting for transfers between devices, per_device(): came_away = lax.ppermute(own, 'row', across)  3.64 us
    unnamed x14, local copies, waits for them, and re-layouts  2.98 us
  transfers between devices with their start and end apart: 30, of which 9 were waited for; matrix products, arithmetic and copies ran while one was open for 2% of the time, Pallas kernels for 33%

profile of v6, /device:TPU:0, one launch (start us, length us, event | category | flops | bytes accessed | tf_op | source)
XLA Modules:
  0.0 88.8 jit_solution(3064748742238236161)
XLA Ops:
  0.6 3.1 %collective-permute-start = (bf16[2,256,256]{2,1,0:T(8,128)(2,1)}, bf16[2,256,256]{2,1,0:T(8,128)(2,1)S(1)}, u32[]{:S(2)}, u32[]{:S(2)}) collective-permute-start(bf16[2,256,256]{2,1,0:T(8,128)(2,1)} %bitcast.16), channel_id=1, source_target_pairs={{0,2},{2,4},{4,6},{6,7},{7,5},{5,3},{3,1},{1,0},{8,10},{10,12},{12... | collective-permute-start | bytes 786440 | tf_op jit(solution)/shard_map/ppermute | solution.py:371
  3.7 2.0 %collective-permute-start.3 = (bf16[512,256]{1,0:T(8,128)(2,1)}, bf16[512,256]{1,0:T(8,128)(2,1)S(1)}, u32[]{:S(2)}, u32[]{:S(2)}) collective-permute-start(bf16[512,256]{1,0:T(8,128)(2,1)} %cot.1), channel_id=1, source_target_pairs={{0,16},{16,0},{8,24},{24,8},{1,17},{17,1},{9,25},{25,9},{2,18},{18... | collective-permute-start | bytes 786440 | tf_op jit(solution)/shard_map/ppermute | solution.py:374
  5.7 0.9 %copy-done.1 = bf16[512,256]{1,0:T(8,128)(2,1)S(1)} copy-done((bf16[512,256]{1,0:T(8,128)(2,1)S(1)}, bf16[512,256]{1,0:T(8,128)(2,1)}, u32[]{:S(2)}) %copy-start.1) | copy-done | bytes 262168
  6.6 0.7 copy-done.3
  7.3 0.7 copy-done.5
  8.0 0.7 copy-done.6
  8.6 2.4 %lists.1 = (s32[685]{0:T(1024)S(1)}, bf16[2,256,256]{2,1,0:T(8,128)(2,1)S(1)}) custom-call(s32[8,16]{1,0:T(8,128)S(1)} %copy-done.3, s32[8]{0:T(128)S(1)} %bitcast.23, s32[160]{0:T(256)S(1)} %copy-done.5, bf16[2,256,256]{2,1,0:T(8,128)(2,1)S(1)} %bitcast.18), custom_call_target="tpu_custom_call" | custom-call | bytes 4096 | tf_op jit(solution)/shard_map/lists/pallas_call | solution.py:322
  11.1 1.4 %collective-permute-start.1 = (bf16[2,256,256]{2,1,0:T(8,128)(2,1)S(1)}, bf16[2,256,256]{2,1,0:T(8,128)(2,1)S(1)}, u32[]{:S(2)}, u32[]{:S(2)}) collective-permute-start(bf16[2,256,256]{2,1,0:T(8,128)(2,1)S(1)} %collective-permute-done.refs_1_), channel_id=1, source_target_pairs={{0,2},{2,4},{4,6},{6,7},{7,5},{5,3},{3,1},{1,0},{8,10},{10,12},{12... | collective-permute-start | bytes 786440 | tf_op jit(solution)/shard_map/ppermute | solution.py:371
  12.5 0.7 collective-permute-start.5
  13.2 3.8 %forward_1.1.refs_2_ = f32[9,256,256]{2,1,0:T(8,128)S(1)} custom-call(s32[685]{0:T(1024)S(1)} %get-tuple-element.87.lists, bf16[128,256,256]{2,1,0:T(8,128)(2,1)} %bitcast.24, bf16[2,256,256]{2,1,0:T(8,128)(2,1)S(1)} %get-tuple-element.56.refs_0_, bf16[2,256,256]{2,1,0:T(8,128)(2,1)S(1)} %collective-permute-done.refs_1_, ...), custom_call_target="tpu_custom_call" | custom-call | flops 33554432 | bytes 131072 | tf_op jit(solution)/shard_map/forward_1/pallas_call | solution.py:356
  17.0 1.5 %collective-permute-done.1.refs_0_ = bf16[2,256,256]{2,1,0:T(8,128)(2,1)S(1)} collective-permute-done((bf16[2,256,256]{2,1,0:T(8,128)(2,1)S(1)}, bf16[2,256,256]{2,1,0:T(8,128)(2,1)S(1)}, u32[]{:S(2)}, u32[]{:S(2)}) %collective-permute-start.1) | collective-permute-done | bytes 262176 | tf_op jit(solution)/shard_map/ppermute | solution.py:371
  18.6 0.8 collective-permute-start.4
  19.4 1.2 %collective-permute-start.7 = (bf16[2,256,256]{2,1,0:T(8,128)(2,1)S(1)}, bf16[2,256,256]{2,1,0:T(8,128)(2,1)S(1)}, u32[]{:S(2)}, u32[]{:S(2)}) collective-permute-start(bf16[2,256,256]{2,1,0:T(8,128)(2,1)S(1)} %collective-permute-done.5.refs_1_), channel_id=1, source_target_pairs={{2,0},{4,2},{6,4},{7,6},{5,7},{3,5},{1,3},{0,1},{10,8},{12,10},{14... | collective-permute-start | bytes 786440 | tf_op jit(solution)/shard_map/ppermute | solution.py:372
  20.6 3.3 %forward_2.1.refs_2_ = f32[9,256,256]{2,1,0:T(8,128)S(1)} custom-call(s32[685]{0:T(1024)S(1)} %get-tuple-element.87.lists, bf16[128,256,256]{2,1,0:T(8,128)(2,1)} %bitcast.25, bf16[2,256,256]{2,1,0:T(8,128)(2,1)S(1)} %collective-permute-done.1.refs_0_, bf16[2,256,256]{2,1,0:T(8,128)(2,1)S(1)} %collective-permute-done.5.refs_1_, ...), custom_call_target="tpu_custom_call" | custom-call | flops 33554432 | bytes 131072 | tf_op jit(solution)/shard_map/forward_2/pallas_call | solution.py:356
  23.9 1.2 %collective-permute-done.4.refs_0_ = bf16[2,256,256]{2,1,0:T(8,128)(2,1)S(1)} collective-permute-done((bf16[2,256,256]{2,1,0:T(8,128)(2,1)S(1)}, bf16[2,256,256]{2,1,0:T(8,128)(2,1)S(1)}, u32[]{:S(2)}, u32[]{:S(2)}) %collective-permute-start.4) | collective-permute-done | bytes 262176 | tf_op jit(solution)/shard_map/ppermute | solution.py:371
  25.0 1.2 %collective-permute-start.6 = (bf16[1,256,256]{2,1,0:T(8,128)(2,1)S(1)}, bf16[1,256,256]{2,1,0:T(8,128)(2,1)S(1)}, u32[]{:S(2)}, u32[]{:S(2)}) collective-permute-start(bf16[1,256,256]{2,1,0:T(8,128)(2,1)S(1)} %slice.56), channel_id=1, source_target_pairs={{0,2},{2,4},{4,6},{6,7},{7,5},{5,3},{3,1},{1,0},{8,10},{10,12},{12... | collective-permute-start | bytes 393224 | tf_op jit(solution)/shard_map/ppermute | solution.py:385
  26.2 0.9 %collective-permute-start.8 = (bf16[1,256,256]{2,1,0:T(8,128)(2,1)S(1)}, bf16[1,256,256]{2,1,0:T(8,128)(2,1)S(1)}, u32[]{:S(2)}, u32[]{:S(2)}) collective-permute-start(bf16[1,256,256]{2,1,0:T(8,128)(2,1)S(1)} %slice.72), channel_id=1, source_target_pairs={{2,0},{4,2},{6,4},{7,6},{5,7},{3,5},{1,3},{0,1},{10,8},{12,10},{14... | collective-permute-start | bytes 393224 | tf_op jit(solution)/shard_map/ppermute | solution.py:386
  27.2 4.0 %forward_3.1 = (f32[9,256,256]{2,1,0:T(8,128)S(1)}, bf16[16,256,256]{2,1,0:T(8,128)(2,1)S(1)}) custom-call(s32[685]{0:T(1024)S(1)} %get-tuple-element.87.lists, bf16[128,256,256]{2,1,0:T(8,128)(2,1)} %bitcast.26, bf16[2,256,256]{2,1,0:T(8,128)(2,1)S(1)} %collective-permute-done.4.refs_0_, bf16[2,256,256]{2,1,0:T(8,128)(2,1)S(1)} %collective-permute-done.7.refs_1_, ...), custom_call_target="tpu_custom_call" | custom-call | flops 33554432 | bytes 131072 | tf_op jit(solution)/shard_map/forward_3/pallas_call | solution.py:356
  31.3 2.1 %forward_4.1 = (bf16[2,256,256]{2,1,0:T(8,128)(2,1)S(1)}, bf16[2,256,256]{2,1,0:T(8,128)(2,1)S(1)}, bf16[2,256,256]{2,1,0:T(8,128)(2,1)S(1)}, bf16[2,256,256]{2,1,0:T(8,128)(2,1)S(1)}) custom-call(s32[685]{0:T(1024)S(1)} %get-tuple-element.87.lists, bf16[128,256,256]{2,1,0:T(8,128)(2,1)} %bitcast.27, ...), custom_call_target="tpu_custom_call" | custom-call | flops 33554432 | bytes 131072 | tf_op jit(solution)/shard_map/forward_4/pallas_call | solution.py:356
  33.4 0.5 collective-permute-start.9
  33.9 1.0 %collective-permute-done.11 = bf16[2,256,256]{2,1,0:T(8,128)(2,1)S(1)} collective-permute-done((bf16[2,256,256]{2,1,0:T(8,128)(2,1)S(1)}, bf16[2,256,256]{2,1,0:T(8,128)(2,1)S(1)}, u32[]{:S(2)}, u32[]{:S(2)}) %collective-permute-start.11) | collective-permute-done | bytes 262176 | tf_op jit(solution)/shard_map/ppermute | solution.py:394
  35.0 1.4 %collective-permute-start.12 = (bf16[2,256,256]{2,1,0:T(8,128)(2,1)S(1)}, bf16[2,256,256]{2,1,0:T(8,128)(2,1)S(1)}, u32[]{:S(2)}, u32[]{:S(2)}) collective-permute-start(bf16[2,256,256]{2,1,0:T(8,128)(2,1)S(1)} %add_convert_fusion.4.near), channel_id=1, source_target_pairs={{0,16},{16,0},{8,24},{24,8},{1,17},{17,1},{9,25},{25,9},{2,18},{18... | collective-permute-start | bytes 786440 | tf_op jit(solution)/shard_map/ppermute | solution.py:397
  36.5 0.8 collective-permute-start.10
  37.2 7.0 %collective-permute-done.12.away = bf16[2,256,256]{2,1,0:T(8,128)(2,1)S(1)} collective-permute-done((bf16[2,256,256]{2,1,0:T(8,128)(2,1)S(1)}, bf16[2,256,256]{2,1,0:T(8,128)(2,1)S(1)}, u32[]{:S(2)}, u32[]{:S(2)}) %collective-permute-start.12) | collective-permute-done | bytes 262176 | tf_op jit(solution)/shard_map/ppermute | solution.py:397
  44.2 1.2 %dense_own.1 = (bf16[512,256]{1,0:T(8,128)(2,1)}, bf16[2,256,256]{2,1,0:T(8,128)(2,1)S(1)}, f32[264,256]{1,0:T(8,128)S(1)}) custom-call(bf16[2,256,256]{2,1,0:T(8,128)(2,1)S(1)} %add_convert_fusion.5.near, bf16[2,256,256]{2,1,0:T(8,128)(2,1)S(1)} %collective-permute-done.12.away, bf16[256,256]{1,0:T(8,128)(2,1)S(1)} %copy-done, f32[1,256]{1,0:T(1,128)S(1)} %bitcast.21, ...), custom_call_target="tpu_custom_call" | custom-call | flops 50331648 | bytes 131072 | tf_op jit(solution)/shard_map/dense_own/pallas_call | solution.py:405
  45.4 3.6 %collective-permute-done.10.away = bf16[2,256,256]{2,1,0:T(8,128)(2,1)S(1)} collective-permute-done((bf16[2,256,256]{2,1,0:T(8,128)(2,1)S(1)}, bf16[2,256,256]{2,1,0:T(8,128)(2,1)S(1)}, u32[]{:S(2)}, u32[]{:S(2)}) %collective-permute-start.10) | collective-permute-done | bytes 262176 | tf_op jit(solution)/shard_map/ppermute | solution.py:399
  49.0 0.7 dense_away.1
  50.3 1.0 %collective-permute-done.14.refs_4_.refs_3_ = bf16[2,256,256]{2,1,0:T(8,128)(2,1)S(1)} collective-permute-done((bf16[2,256,256]{2,1,0:T(8,128)(2,1)S(1)}, bf16[2,256,256]{2,1,0:T(8,128)(2,1)S(1)}, u32[]{:S(2)}, u32[]{:S(2)}) %collective-permute-start.14) | collective-permute-done | bytes 262176 | tf_op jit(solution)/shard_map/ppermute | solution.py:431
  51.3 1.6 %backward_4.1 = f32[2,256,256]{2,1,0:T(8,128)S(1)} custom-call(s32[685]{0:T(1024)S(1)} %get-tuple-element.87.lists, bf16[128,256,256]{2,1,0:T(8,128)(2,1)} %bitcast.28, bf16[16,256,256]{2,1,0:T(8,128)(2,1)S(1)} %get-tuple-element.62.refs_3_.refs_0_, bf16[2,256,256]{2,1,0:T(8,128)(2,1)S(1)} %get-tuple-element.71.refs_1_.refs_0_, ...), custom_call_target="tpu_custom_call" | custom-call | flops 33554432 | bytes 131072 | tf_op jit(solution)/shard_map/backward_4/pallas_call | solution.py:442
  53.0 1.7 %collective-permute-start.15 = (bf16[1,256,256]{2,1,0:T(8,128)(2,1)S(1)}, bf16[1,256,256]{2,1,0:T(8,128)(2,1)S(1)}, u32[]{:S(2)}, u32[]{:S(2)}) collective-permute-start(bf16[1,256,256]{2,1,0:T(8,128)(2,1)S(1)} %get-tuple-element.77), channel_id=1, source_target_pairs={{0,2},{2,4},{4,6},{6,7},{7,5},{5,3},{3,1},{1,0},{10,8},{12,10},{14... | collective-permute-start | bytes 393224 | tf_op jit(solution)/shard_map/ppermute | solution.py:471
  55.1 1.7 %collective-permute-start.24 = (bf16[80,256]{1,0:T(8,128)(2,1)S(1)}, bf16[80,256]{1,0:T(8,128)(2,1)S(1)}, u32[]{:S(2)}, u32[]{:S(2)}) collective-permute-start(bf16[80,256]{1,0:T(8,128)(2,1)S(1)} %fusion), channel_id=1, source_target_pairs={{0,1},{1,0},{2,3},{3,2},{4,5},{5,4},{6,7},{7,6},{8,9},{9,8},{10,11... | collective-permute-start | bytes 122888 | tf_op jit(solution)/shard_map/ppermute | solution.py:495
  56.8 3.9 %backward_3.1 = f32[6,256,256]{2,1,0:T(8,128)S(1)} custom-call(s32[685]{0:T(1024)S(1)} %get-tuple-element.87.lists, bf16[128,256,256]{2,1,0:T(8,128)(2,1)} %bitcast.29, bf16[2,256,256]{2,1,0:T(8,128)(2,1)S(1)} %get-tuple-element.71.refs_1_.refs_0_, bf16[2,256,256]{2,1,0:T(8,128)(2,1)S(1)} %get-tuple-element.75.refs_2_.refs_1_, ...), custom_call_target="tpu_custom_call" | custom-call | flops 33554432 | bytes 131072 | tf_op jit(solution)/shard_map/backward_3/pallas_call | solution.py:442
  61.4 1.8 %collective-permute-start.17 = (bf16[2,256,256]{2,1,0:T(8,128)(2,1)S(1)}, bf16[2,256,256]{2,1,0:T(8,128)(2,1)S(1)}, u32[]{:S(2)}, u32[]{:S(2)}) collective-permute-start(bf16[2,256,256]{2,1,0:T(8,128)(2,1)S(1)} %pad_maximum_fusion), channel_id=1, source_target_pairs={{0,2},{2,4},{4,6},{6,7},{7,5},{5,3},{3,1},{1,0},{10,8},{12,10},{14... | collective-permute-start | bytes 786440 | tf_op jit(solution)/shard_map/ppermute | solution.py:471
  63.2 1.4 %collective-permute-start.25 = (bf16[80,256]{1,0:T(8,128)(2,1)S(1)}, bf16[80,256]{1,0:T(8,128)(2,1)S(1)}, u32[]{:S(2)}, u32[]{:S(2)}) collective-permute-start(bf16[80,256]{1,0:T(8,128)(2,1)S(1)} %add_convert_fusion.9), channel_id=1, source_target_pairs={{0,2},{1,3},{2,0},{3,1},{4,6},{5,7},{6,4},{7,5},{8,10},{9,11},{10,... | collective-permute-start | bytes 122888 | tf_op jit(solution)/shard_map/ppermute | solution.py:495
  64.6 3.9 %backward_2.1 = f32[4,256,256]{2,1,0:T(8,128)S(1)} custom-call(s32[685]{0:T(1024)S(1)} %get-tuple-element.87.lists, bf16[128,256,256]{2,1,0:T(8,128)(2,1)} %bitcast.30, bf16[2,256,256]{2,1,0:T(8,128)(2,1)S(1)} %get-tuple-element.71.refs_1_.refs_0_, bf16[2,256,256]{2,1,0:T(8,128)(2,1)S(1)} %get-tuple-element.75.refs_2_.refs_1_, ...), custom_call_target="tpu_custom_call" | custom-call | flops 33554432 | bytes 131072 | tf_op jit(solution)/shard_map/backward_2/pallas_call | solution.py:442
  68.6 1.6 %collective-permute-done.18 = bf16[2,256,256]{2,1,0:T(8,128)(2,1)S(1)} collective-permute-done((bf16[2,256,256]{2,1,0:T(8,128)(2,1)S(1)}, bf16[2,256,256]{2,1,0:T(8,128)(2,1)S(1)}, u32[]{:S(2)}, u32[]{:S(2)}) %collective-permute-start.18) | collective-permute-done | bytes 262176 | tf_op jit(solution)/shard_map/ppermute | solution.py:472
  70.4 1.4 %collective-permute-start.19 = (bf16[2,256,256]{2,1,0:T(8,128)(2,1)S(1)}, bf16[2,256,256]{2,1,0:T(8,128)(2,1)S(1)}, u32[]{:S(2)}, u32[]{:S(2)}) collective-permute-start(bf16[2,256,256]{2,1,0:T(8,128)(2,1)S(1)} %get-tuple-element.103), channel_id=1, source_target_pairs={{0,2},{2,4},{4,6},{6,7},{7,5},{5,3},{3,1},{1,0},{10,8},{12,10},{14... | collective-permute-start | bytes 786440 | tf_op jit(solution)/shard_map/ppermute | solution.py:471
  71.8 0.7 collective-permute-start.20
  72.5 2.8 %collective-permute-start.26 = (bf16[80,256]{1,0:T(8,128)(2,1)S(1)}, bf16[80,256]{1,0:T(8,128)(2,1)S(1)}, u32[]{:S(2)}, u32[]{:S(2)}) collective-permute-start(bf16[80,256]{1,0:T(8,128)(2,1)S(1)} %add_convert_fusion.8), channel_id=1, source_target_pairs={{0,4},{1,5},{2,6},{3,7},{4,0},{5,1},{6,2},{7,3},{8,12},{9,13},{10,... | collective-permute-start | bytes 122888 | tf_op jit(solution)/shard_map/ppermute | solution.py:495
  75.3 3.9 %backward_1.1 = f32[4,256,256]{2,1,0:T(8,128)S(1)} custom-call(s32[685]{0:T(1024)S(1)} %get-tuple-element.87.lists, bf16[128,256,256]{2,1,0:T(8,128)(2,1)} %bitcast.31, bf16[2,256,256]{2,1,0:T(8,128)(2,1)S(1)} %get-tuple-element.71.refs_1_.refs_0_, bf16[2,256,256]{2,1,0:T(8,128)(2,1)S(1)} %get-tuple-element.75.refs_2_.refs_1_, ...), custom_call_target="tpu_custom_call" | custom-call | flops 33554432 | bytes 131072 | tf_op jit(solution)/shard_map/backward_1/pallas_call | solution.py:442
  79.4 1.8 %collective-permute-start.21 = (bf16[2,256,256]{2,1,0:T(8,128)(2,1)S(1)}, bf16[2,256,256]{2,1,0:T(8,128)(2,1)S(1)}, u32[]{:S(2)}, u32[]{:S(2)}) collective-permute-start(bf16[2,256,256]{2,1,0:T(8,128)(2,1)S(1)} %get-tuple-element.101), channel_id=1, source_target_pairs={{0,2},{2,4},{4,6},{6,7},{7,5},{5,3},{3,1},{1,0},{10,8},{12,10},{14... | collective-permute-start | bytes 786440 | tf_op jit(solution)/shard_map/ppermute | solution.py:471
  81.5 0.5 collective-permute-start.27
  82.0 1.7 %collective-permute-start.29 = (f32[64,256]{1,0:T(8,128)S(1)}, f32[64,256]{1,0:T(8,128)S(1)}, u32[]{:S(2)}, u32[]{:S(2)}) collective-permute-start(f32[64,256]{1,0:T(8,128)S(1)} %slice.70.own), channel_id=1, source_target_pairs={{0,24},{24,0},{8,16},{16,8},{1,25},{25,1},{9,17},{17,9},{2,26},{26... | collective-permute-start | bytes 196616 | tf_op jit(solution)/shard_map/ppermute | solution.py:477
  83.7 0.6 slice.71
  84.3 2.0 %collective-permute-done.27.y = f32[64,256]{1,0:T(8,128)S(1)} collective-permute-done((f32[64,256]{1,0:T(8,128)S(1)}, f32[64,256]{1,0:T(8,128)S(1)}, u32[]{:S(2)}, u32[]{:S(2)}) %collective-permute-start.27) | collective-permute-done | bytes 65568 | tf_op jit(solution)/shard_map/ppermute | solution.py:477
  86.4 0.7 quarters.1
  87.1 0.8 collective-permute-done.21
  87.9 0.9 finish.1
  (61 shorter events, 2.6 us)
Async XLA Ops:
  0.6 10.5 %collective-permute-start = (bf16[2,256,256]{2,1,0:T(8,128)(2,1)}, bf16[2,256,256]{2,1,0:T(8,128)(2,1)S(1)}, u32[]{:S(2)}, u32[]{:S(2)}) collective-permute-start(bf16[2,256,256]{2,1,0:T(8,128)(2,1)} %bitcast.16), channel_id=1, source_target_pairs={{0,2},{2,4},{4,6},{6,7},{7,5},{5,3},{3,1},{1,0},{8,10},{10,12},{12... | collective-permute-start | bytes 786440 | tf_op jit(solution)/shard_map/ppermute | solution.py:371
  3.7 8.8 %collective-permute-start.2 = (bf16[2,256,256]{2,1,0:T(8,128)(2,1)}, bf16[2,256,256]{2,1,0:T(8,128)(2,1)S(1)}, u32[]{:S(2)}, u32[]{:S(2)}) collective-permute-start(bf16[2,256,256]{2,1,0:T(8,128)(2,1)} %bitcast.17), channel_id=1, source_target_pairs={{2,0},{4,2},{6,4},{7,6},{5,7},{3,5},{1,3},{0,1},{10,8},{12,10},{14... | collective-permute-start | bytes 786440 | tf_op jit(solution)/shard_map/ppermute | solution.py:372
  3.7 13.3 %collective-permute-start.3 = (bf16[512,256]{1,0:T(8,128)(2,1)}, bf16[512,256]{1,0:T(8,128)(2,1)S(1)}, u32[]{:S(2)}, u32[]{:S(2)}) collective-permute-start(bf16[512,256]{1,0:T(8,128)(2,1)} %cot.1), channel_id=1, source_target_pairs={{0,16},{16,0},{8,24},{24,8},{1,17},{17,1},{9,25},{25,9},{2,18},{18... | collective-permute-start | bytes 786440 | tf_op jit(solution)/shard_map/ppermute | solution.py:374
  5.7 0.9 %copy-start.1 = (bf16[512,256]{1,0:T(8,128)(2,1)S(1)}, bf16[512,256]{1,0:T(8,128)(2,1)}, u32[]{:S(2)}) copy-start(bf16[512,256]{1,0:T(8,128)(2,1)} %param.8) | copy-start | bytes 786436
  6.6 0.7 copy-start.3
  7.3 0.7 copy-start.5
  8.0 0.7 copy-start.6
  11.1 7.4 %collective-permute-start.1 = (bf16[2,256,256]{2,1,0:T(8,128)(2,1)S(1)}, bf16[2,256,256]{2,1,0:T(8,128)(2,1)S(1)}, u32[]{:S(2)}, u32[]{:S(2)}) collective-permute-start(bf16[2,256,256]{2,1,0:T(8,128)(2,1)S(1)} %collective-permute-done.refs_1_), channel_id=1, source_target_pairs={{0,2},{2,4},{4,6},{6,7},{7,5},{5,3},{3,1},{1,0},{8,10},{10,12},{12... | collective-permute-start | bytes 786440 | tf_op jit(solution)/shard_map/ppermute | solution.py:371
  12.5 6.9 %collective-permute-start.5 = (bf16[2,256,256]{2,1,0:T(8,128)(2,1)S(1)}, bf16[2,256,256]{2,1,0:T(8,128)(2,1)S(1)}, u32[]{:S(2)}, u32[]{:S(2)}) collective-permute-start(bf16[2,256,256]{2,1,0:T(8,128)(2,1)S(1)} %collective-permute-done.2.refs_2_), channel_id=1, source_target_pairs={{2,0},{4,2},{6,4},{7,6},{5,7},{3,5},{1,3},{0,1},{10,8},{12,10},{14... | collective-permute-start | bytes 786440 | tf_op jit(solution)/shard_map/ppermute | solution.py:372
  18.6 6.5 %collective-permute-start.4 = (bf16[2,256,256]{2,1,0:T(8,128)(2,1)S(1)}, bf16[2,256,256]{2,1,0:T(8,128)(2,1)S(1)}, u32[]{:S(2)}, u32[]{:S(2)}) collective-permute-start(bf16[2,256,256]{2,1,0:T(8,128)(2,1)S(1)} %collective-permute-done.1.refs_0_), channel_id=1, source_target_pairs={{0,2},{2,4},{4,6},{6,7},{7,5},{5,3},{3,1},{1,0},{8,10},{10,12},{12... | collective-permute-start | bytes 786440 | tf_op jit(solution)/shard_map/ppermute | solution.py:371
  19.4 6.8 %collective-permute-start.7 = (bf16[2,256,256]{2,1,0:T(8,128)(2,1)S(1)}, bf16[2,256,256]{2,1,0:T(8,128)(2,1)S(1)}, u32[]{:S(2)}, u32[]{:S(2)}) collective-permute-start(bf16[2,256,256]{2,1,0:T(8,128)(2,1)S(1)} %collective-permute-done.5.refs_1_), channel_id=1, source_target_pairs={{2,0},{4,2},{6,4},{7,6},{5,7},{3,5},{1,3},{0,1},{10,8},{12,10},{14... | collective-permute-start | bytes 786440 | tf_op jit(solution)/shard_map/ppermute | solution.py:372
  25.0 6.2 %collective-permute-start.6 = (bf16[1,256,256]{2,1,0:T(8,128)(2,1)S(1)}, bf16[1,256,256]{2,1,0:T(8,128)(2,1)S(1)}, u32[]{:S(2)}, u32[]{:S(2)}) collective-permute-start(bf16[1,256,256]{2,1,0:T(8,128)(2,1)S(1)} %slice.56), channel_id=1, source_target_pairs={{0,2},{2,4},{4,6},{6,7},{7,5},{5,3},{3,1},{1,0},{8,10},{10,12},{12... | collective-permute-start | bytes 393224 | tf_op jit(solution)/shard_map/ppermute | solution.py:385
  26.2 5.0 %collective-permute-start.8 = (bf16[1,256,256]{2,1,0:T(8,128)(2,1)S(1)}, bf16[1,256,256]{2,1,0:T(8,128)(2,1)S(1)}, u32[]{:S(2)}, u32[]{:S(2)}) collective-permute-start(bf16[1,256,256]{2,1,0:T(8,128)(2,1)S(1)} %slice.72), channel_id=1, source_target_pairs={{2,0},{4,2},{6,4},{7,6},{5,7},{3,5},{1,3},{0,1},{10,8},{12,10},{14... | collective-permute-start | bytes 393224 | tf_op jit(solution)/shard_map/ppermute | solution.py:386
  31.3 13.0 %copy-start = (bf16[256,256]{1,0:T(8,128)(2,1)S(1)}, bf16[256,256]{1,0:T(8,128)(2,1)}, u32[]{:S(2)}) copy-start(bf16[256,256]{1,0:T(8,128)(2,1)} %weight.3) | copy-start | bytes 393220
  31.3 13.0 %copy-start.2 = (bf16[512,256]{1,0:T(8,128)(2,1)S(1)}, bf16[512,256]{1,0:T(8,128)(2,1)}, u32[]{:S(2)}) copy-start(bf16[512,256]{1,0:T(8,128)(2,1)} %cot.1) | copy-start | bytes 786436
  31.3 13.0 %copy-start.4 = (f32[256]{0:T(256)S(1)}, f32[256]{0:T(256)}, u32[]{:S(2)}) copy-start(f32[256]{0:T(256)} %param.13) | copy-start | bytes 3076
  33.3 1.6 %collective-permute-start.11 = (bf16[2,256,256]{2,1,0:T(8,128)(2,1)S(1)}, bf16[2,256,256]{2,1,0:T(8,128)(2,1)S(1)}, u32[]{:S(2)}, u32[]{:S(2)}) collective-permute-start(bf16[2,256,256]{2,1,0:T(8,128)(2,1)S(1)} %get-tuple-element.66), channel_id=1, source_target_pairs={{0,8},{8,0},{16,24},{24,16},{1,9},{9,1},{17,25},{25,17},{2,10},{10... | collective-permute-start | bytes 786440 | tf_op jit(solution)/shard_map/ppermute | solution.py:394
  33.4 3.0 %collective-permute-start.9 = (bf16[2,256,256]{2,1,0:T(8,128)(2,1)S(1)}, bf16[2,256,256]{2,1,0:T(8,128)(2,1)S(1)}, u32[]{:S(2)}, u32[]{:S(2)}) collective-permute-start(bf16[2,256,256]{2,1,0:T(8,128)(2,1)S(1)} %get-tuple-element.64), channel_id=1, source_target_pairs={{0,8},{8,0},{16,24},{24,16},{1,9},{9,1},{17,25},{25,17},{2,10},{10... | collective-permute-start | bytes 786440 | tf_op jit(solution)/shard_map/ppermute | solution.py:395
  35.0 9.2 %collective-permute-start.12 = (bf16[2,256,256]{2,1,0:T(8,128)(2,1)S(1)}, bf16[2,256,256]{2,1,0:T(8,128)(2,1)S(1)}, u32[]{:S(2)}, u32[]{:S(2)}) collective-permute-start(bf16[2,256,256]{2,1,0:T(8,128)(2,1)S(1)} %add_convert_fusion.4.near), channel_id=1, source_target_pairs={{0,16},{16,0},{8,24},{24,8},{1,17},{17,1},{9,25},{25,9},{2,18},{18... | collective-permute-start | bytes 786440 | tf_op jit(solution)/shard_map/ppermute | solution.py:397
  36.5 12.6 %collective-permute-start.10 = (bf16[2,256,256]{2,1,0:T(8,128)(2,1)S(1)}, bf16[2,256,256]{2,1,0:T(8,128)(2,1)S(1)}, u32[]{:S(2)}, u32[]{:S(2)}) collective-permute-start(bf16[2,256,256]{2,1,0:T(8,128)(2,1)S(1)} %add_convert_fusion.5.near), channel_id=1, source_target_pairs={{0,16},{16,0},{8,24},{24,8},{1,17},{17,1},{9,25},{25,9},{2,18},{18... | collective-permute-start | bytes 786440 | tf_op jit(solution)/shard_map/ppermute | solution.py:399
  45.4 3.6 %collective-permute-start.13 = (bf16[2,256,256]{2,1,0:T(8,128)(2,1)S(1)}, bf16[2,256,256]{2,1,0:T(8,128)(2,1)S(1)}, u32[]{:S(2)}, u32[]{:S(2)}) collective-permute-start(bf16[2,256,256]{2,1,0:T(8,128)(2,1)S(1)} %get-tuple-element.71.refs_1_.refs_0_), channel_id=1, source_target_pairs={{0,8},{8,0},{16,24},{24,16},{1,9},{9,1},{17,25},{25,17},{2,10},{10... | collective-permute-start | bytes 786440 | tf_op jit(solution)/shard_map/ppermute | solution.py:418
  49.7 1.6 %collective-permute-start.14 = (bf16[2,256,256]{2,1,0:T(8,128)(2,1)S(1)}, bf16[2,256,256]{2,1,0:T(8,128)(2,1)S(1)}, u32[]{:S(2)}, u32[]{:S(2)}) collective-permute-start(bf16[2,256,256]{2,1,0:T(8,128)(2,1)S(1)} %get-tuple-element.75.refs_2_.refs_1_), channel_id=1, source_target_pairs={{0,8},{8,0},{16,24},{24,16},{1,9},{9,1},{17,25},{25,17},{2,10},{10... | collective-permute-start | bytes 786440 | tf_op jit(solution)/shard_map/ppermute | solution.py:431
  49.8 5.2 %collective-permute-start.23 = (f32[80,256]{1,0:T(8,128)S(1)}, f32[80,256]{1,0:T(8,128)S(1)}, u32[]{:S(2)}, u32[]{:S(2)}) collective-permute-start(f32[80,256]{1,0:T(8,128)S(1)} %dynamic-slice_bitcast_fusion), channel_id=1, source_target_pairs={{0,8},{8,0},{16,24},{24,16},{1,9},{9,1},{17,25},{25,17},{2,10},{10... | collective-permute-start | bytes 245768 | tf_op jit(solution)/shard_map/ppermute | solution.py:438
  53.0 7.8 %collective-permute-start.15 = (bf16[1,256,256]{2,1,0:T(8,128)(2,1)S(1)}, bf16[1,256,256]{2,1,0:T(8,128)(2,1)S(1)}, u32[]{:S(2)}, u32[]{:S(2)}) collective-permute-start(bf16[1,256,256]{2,1,0:T(8,128)(2,1)S(1)} %get-tuple-element.77), channel_id=1, source_target_pairs={{0,2},{2,4},{4,6},{6,7},{7,5},{5,3},{3,1},{1,0},{10,8},{12,10},{14... | collective-permute-start | bytes 393224 | tf_op jit(solution)/shard_map/ppermute | solution.py:471
  54.7 6.2 %collective-permute-start.16 = (bf16[1,256,256]{2,1,0:T(8,128)(2,1)S(1)}, bf16[1,256,256]{2,1,0:T(8,128)(2,1)S(1)}, u32[]{:S(2)}, u32[]{:S(2)}) collective-permute-start(bf16[1,256,256]{2,1,0:T(8,128)(2,1)S(1)} %get-tuple-element.78), channel_id=1, source_target_pairs={{2,0},{4,2},{6,4},{7,6},{5,7},{3,5},{1,3},{0,1},{8,10},{10,12},{12... | collective-permute-start | bytes 393224 | tf_op jit(solution)/shard_map/ppermute | solution.py:472
  55.1 8.1 %collective-permute-start.24 = (bf16[80,256]{1,0:T(8,128)(2,1)S(1)}, bf16[80,256]{1,0:T(8,128)(2,1)S(1)}, u32[]{:S(2)}, u32[]{:S(2)}) collective-permute-start(bf16[80,256]{1,0:T(8,128)(2,1)S(1)} %fusion), channel_id=1, source_target_pairs={{0,1},{1,0},{2,3},{3,2},{4,5},{5,4},{6,7},{7,6},{8,9},{9,8},{10,11... | collective-permute-start | bytes 122888 | tf_op jit(solution)/shard_map/ppermute | solution.py:495
  61.1 9.2 %collective-permute-start.18 = (bf16[2,256,256]{2,1,0:T(8,128)(2,1)S(1)}, bf16[2,256,256]{2,1,0:T(8,128)(2,1)S(1)}, u32[]{:S(2)}, u32[]{:S(2)}) collective-permute-start(bf16[2,256,256]{2,1,0:T(8,128)(2,1)S(1)} %pad_maximum_fusion.1), channel_id=1, source_target_pairs={{2,0},{4,2},{6,4},{7,6},{5,7},{3,5},{1,3},{0,1},{8,10},{10,12},{12... | collective-permute-start | bytes 786440 | tf_op jit(solution)/shard_map/ppermute | solution.py:472
  61.4 8.8 %collective-permute-start.17 = (bf16[2,256,256]{2,1,0:T(8,128)(2,1)S(1)}, bf16[2,256,256]{2,1,0:T(8,128)(2,1)S(1)}, u32[]{:S(2)}, u32[]{:S(2)}) collective-permute-start(bf16[2,256,256]{2,1,0:T(8,128)(2,1)S(1)} %pad_maximum_fusion), channel_id=1, source_target_pairs={{0,2},{2,4},{4,6},{6,7},{7,5},{5,3},{3,1},{1,0},{10,8},{12,10},{14... | collective-permute-start | bytes 786440 | tf_op jit(solution)/shard_map/ppermute | solution.py:471
  63.2 9.2 %collective-permute-start.25 = (bf16[80,256]{1,0:T(8,128)(2,1)S(1)}, bf16[80,256]{1,0:T(8,128)(2,1)S(1)}, u32[]{:S(2)}, u32[]{:S(2)}) collective-permute-start(bf16[80,256]{1,0:T(8,128)(2,1)S(1)} %add_convert_fusion.9), channel_id=1, source_target_pairs={{0,2},{1,3},{2,0},{3,1},{4,6},{5,7},{6,4},{7,5},{8,10},{9,11},{10,... | collective-permute-start | bytes 122888 | tf_op jit(solution)/shard_map/ppermute | solution.py:495
  70.4 8.9 %collective-permute-start.19 = (bf16[2,256,256]{2,1,0:T(8,128)(2,1)S(1)}, bf16[2,256,256]{2,1,0:T(8,128)(2,1)S(1)}, u32[]{:S(2)}, u32[]{:S(2)}) collective-permute-start(bf16[2,256,256]{2,1,0:T(8,128)(2,1)S(1)} %get-tuple-element.103), channel_id=1, source_target_pairs={{0,2},{2,4},{4,6},{6,7},{7,5},{5,3},{3,1},{1,0},{10,8},{12,10},{14... | collective-permute-start | bytes 786440 | tf_op jit(solution)/shard_map/ppermute | solution.py:471
  71.8 7.5 %collective-permute-start.20 = (bf16[2,256,256]{2,1,0:T(8,128)(2,1)S(1)}, bf16[2,256,256]{2,1,0:T(8,128)(2,1)S(1)}, u32[]{:S(2)}, u32[]{:S(2)}) collective-permute-start(bf16[2,256,256]{2,1,0:T(8,128)(2,1)S(1)} %get-tuple-element.102), channel_id=1, source_target_pairs={{2,0},{4,2},{6,4},{7,6},{5,7},{3,5},{1,3},{0,1},{8,10},{10,12},{12... | collective-permute-start | bytes 786440 | tf_op jit(solution)/shard_map/ppermute | solution.py:472
  72.5 9.0 %collective-permute-start.26 = (bf16[80,256]{1,0:T(8,128)(2,1)S(1)}, bf16[80,256]{1,0:T(8,128)(2,1)S(1)}, u32[]{:S(2)}, u32[]{:S(2)}) collective-permute-start(bf16[80,256]{1,0:T(8,128)(2,1)S(1)} %add_convert_fusion.8), channel_id=1, source_target_pairs={{0,4},{1,5},{2,6},{3,7},{4,0},{5,1},{6,2},{7,3},{8,12},{9,13},{10,... | collective-permute-start | bytes 122888 | tf_op jit(solution)/shard_map/ppermute | solution.py:495
  79.4 8.6 %collective-permute-start.21 = (bf16[2,256,256]{2,1,0:T(8,128)(2,1)S(1)}, bf16[2,256,256]{2,1,0:T(8,128)(2,1)S(1)}, u32[]{:S(2)}, u32[]{:S(2)}) collective-permute-start(bf16[2,256,256]{2,1,0:T(8,128)(2,1)S(1)} %get-tuple-element.101), channel_id=1, source_target_pairs={{0,2},{2,4},{4,6},{6,7},{7,5},{5,3},{3,1},{1,0},{10,8},{12,10},{14... | collective-permute-start | bytes 786440 | tf_op jit(solution)/shard_map/ppermute | solution.py:471
  81.1 6.8 %collective-permute-start.22 = (bf16[2,256,256]{2,1,0:T(8,128)(2,1)S(1)}, bf16[2,256,256]{2,1,0:T(8,128)(2,1)S(1)}, u32[]{:S(2)}, u32[]{:S(2)}) collective-permute-start(bf16[2,256,256]{2,1,0:T(8,128)(2,1)S(1)} %get-tuple-element.100), channel_id=1, source_target_pairs={{2,0},{4,2},{6,4},{7,6},{5,7},{3,5},{1,3},{0,1},{8,10},{10,12},{12... | collective-permute-start | bytes 786440 | tf_op jit(solution)/shard_map/ppermute | solution.py:472
  81.5 4.9 %collective-permute-start.27 = (f32[64,256]{1,0:T(8,128)S(1)}, f32[64,256]{1,0:T(8,128)S(1)}, u32[]{:S(2)}, u32[]{:S(2)}) collective-permute-start(f32[64,256]{1,0:T(8,128)S(1)} %slice.70.own), channel_id=1, source_target_pairs={{0,16},{16,0},{8,24},{24,8},{1,17},{17,1},{9,25},{25,9},{2,18},{18... | collective-permute-start | bytes 196616 | tf_op jit(solution)/shard_map/ppermute | solution.py:477
  81.9 4.4 %collective-permute-start.28 = (f32[64,256]{1,0:T(8,128)S(1)}, f32[64,256]{1,0:T(8,128)S(1)}, u32[]{:S(2)}, u32[]{:S(2)}) collective-permute-start(f32[64,256]{1,0:T(8,128)S(1)} %slice.70.own), channel_id=1, source_target_pairs={{0,8},{8,0},{16,24},{24,16},{1,9},{9,1},{17,25},{25,17},{2,10},{10... | collective-permute-start | bytes 196616 | tf_op jit(solution)/shard_map/ppermute | solution.py:477
  82.0 4.4 %collective-permute-start.29 = (f32[64,256]{1,0:T(8,128)S(1)}, f32[64,256]{1,0:T(8,128)S(1)}, u32[]{:S(2)}, u32[]{:S(2)}) collective-permute-start(f32[64,256]{1,0:T(8,128)S(1)} %slice.70.own), channel_id=1, source_target_pairs={{0,24},{24,0},{8,16},{16,8},{1,25},{25,1},{9,17},{17,9},{2,26},{26... | collective-permute-start | bytes 196616 | tf_op jit(solution)/shard_map/ppermute | solution.py:477

commit v7 on v6

--- a/solution.py
+++ b/solution.py
@@ -3,7 +3,6 @@
 
 import jax
 import jax.numpy as jnp
-import numpy as np
 from jax import lax
 from jax.experimental import pallas as pl
 from jax.experimental.pallas import tpu as pltpu
@@ -33,23 +32,44 @@
     return pl.CostEstimate(flops=int(flops), bytes_accessed=int(nbytes), transcendentals=0)
 
 
-def lists_kernel(n_buckets, cap, col_tiles, place_base, cols, counts, tables, block, lists, kept):
+def ring_rank(device, count):
+    return jnp.where(lax.rem(device, 2) == 0, device // 2, count - 1 - device // 2)
+
+
+def lists_kernel(n_buckets, cap, cols, counts, block, lists, kept, places):
     kept[...] = block[...]
     row_tiles, slots = cols.shape
     ends = n_buckets * cap
-    first_place = place_base + lax.axis_index("col") * col_tiles
-    first_pos = lax.axis_index("row") * row_tiles
+    row = lax.axis_index("row")
+    my_core, my_y = lax.rem(row, 2), row // 2
+    half = n_buckets - 1
+    n_col = 2 * half
+    per_dev = block.shape[0]
+    my_rank = ring_rank(lax.axis_index("col"), n_col)
+
+    def find_place(t, _):
+        ahead = lax.rem(ring_rank(t // per_dev, n_col) - my_rank + n_col, n_col)
+        bucket = jnp.minimum(ahead, n_col - ahead)
+        side = ((ahead > 0) & (ahead < half)).astype(jnp.int32)
+        places[t] = bucket * 256 + side * per_dev + lax.rem(t, per_dev)
+        return 0
+
+    lax.fori_loop(0, places.shape[0], find_place, 0)
     for b in range(n_buckets):
         lists[ends + b] = 0
 
     def tile_row(t, _):
-        head = t * slots * 65536 + tables[first_pos + t] * 256
+        owner = t // (row_tiles // 4)
+        other_core = (lax.rem(owner, 2) != my_core).astype(jnp.int32)
+        other_y = (owner // 2 != my_y).astype(jnp.int32)
+        pos = (other_core * 2 + other_y) * (row_tiles // 4) + lax.rem(t, row_tiles // 4)
+        head = t * slots * 65536 + pos * 256
 
         def slot(s, _):
-            place = tables[first_place + cols[t, s]]
-            bucket = place // 256
+            place = places[cols[t, s]]
+            bucket = place >> 8
             n = lists[ends + bucket]
-            lists[bucket * cap + n] = head + s * 65536 + lax.rem(place, 256)
+            lists[bucket * cap + n] = head + s * 65536 + (place & 255)
             lists[ends + bucket] = n + 1
             return 0
 
@@ -71,7 +91,7 @@
 
 def unit_copies(lists, first, at, values, buffer, sems):
     for u in range(UNIT):
-        yield pltpu.make_async_copy(values.at[lists[first + u] // 65536], buffer.at[at + u], sems.at[at + u])
+        yield pltpu.make_async_copy(values.at[lists[first + u] >> 16], buffer.at[at + u], sems.at[at + u])
 
 
 def stream(lists, buckets, cap, n_buckets, values, buffer, sems, between, use, skip=0):
@@ -112,11 +132,11 @@
 
 
 def destination(entry):
-    return lax.rem(entry // 256, 256)
+    return (entry >> 8) & 255
 
 
 def source(entry):
-    return lax.rem(entry, 256)
+    return entry & 255
 
 
 def forward_kernel(buckets, cap, n_buckets, n_blocks, n_before, role, lists, values, *refs):
@@ -237,11 +257,12 @@
         parts = []
         for u in range(UNIT):
             parts.append(jnp.dot(grads[destination(lists[first + u])], tiles[at + u], preferred_element_type=F32))
-        begin = jnp.where(first // cap == buckets[-1], shift, 0)
+        begin = jnp.where(first < buckets[0] * cap, shift, 0)
         for u in range(UNIT):
             k = source(lists[first + u])
             if sides:
-                k = jnp.where(begin == 0, lax.rem(k + swap, 2 * sides), k)
+                moved = jnp.where(k < sides, k + swap, k - swap)
+                k = jnp.where(begin == 0, moved, k)
             out[k + begin] += parts[u]
 
     def between():
@@ -301,36 +322,21 @@
     my_y, my_core = row // 2, row % 2
 
     n_buckets = half + 1
-    rank = np.zeros(n_col, np.int64)
-    rank[order] = np.arange(n_col)
-    place = np.zeros((n_col, col_tiles), np.int32)
-    for d in range(n_col):
-        for t in range(col_tiles):
-            ahead = (rank[t // per_dev] - rank[d]) % n_col
-            bucket = min(ahead, n_col - ahead)
-            side = 1 if 0 < ahead < half else 0
-            place[d, t] = bucket * 256 + side * per_dev + t % per_dev
-    tiles = np.arange(row_tiles)
-    block = tiles // (row_tiles // 4)
-    pos = [
-        ((block % 2 != r % 2) * 2 + (block // 2 != r // 2)) * (row_tiles // 4) + tiles % (row_tiles // 4)
-        for r in range(4)
-    ]
-    tables = np.concatenate([np.concatenate(pos), place.reshape(-1)]).astype(np.int32)
     cap = row_tiles * slots + UNIT
     mine = features.reshape(per_dev, tile, width)
     lists, kept = pl.pallas_call(
-        functools.partial(lists_kernel, n_buckets, cap, col_tiles, 4 * row_tiles),
-        in_specs=[SMEM] * 3 + [VMEM],
+        functools.partial(lists_kernel, n_buckets, cap),
+        in_specs=[SMEM] * 2 + [VMEM],
         out_specs=[SMEM, VMEM],
         out_shape=[
             jax.ShapeDtypeStruct((n_buckets * cap + n_buckets,), jnp.int32),
             jax.ShapeDtypeStruct((per_dev, tile, width), BF16),
         ],
+        scratch_shapes=[pltpu.SMEM((col_tiles,), jnp.int32)],
         compiler_params=params(8),
         cost_estimate=cost(0, 2**12),
         name="lists",
-    )(tile_cols, tile_counts.reshape(-1), jnp.asarray(tables), mine)
+    )(tile_cols, tile_counts.reshape(-1), mine)
 
     dots = 2 * tile * tile * width
     small = cost(dots, tile * tile * 2)

time: 90.2 us -> 89 us (0.987); the launches traced: 88.8 us -> 88.6 us
  Pallas kernels: 32.4 us -> 29.4 us
  waiting for transfers between devices: 20 us -> 22.5 us
  starting transfers between devices: 31 us -> 32 us
    pallas_call x4, Pallas kernels: 13.4 us -> 11.1 us  [backward(): pl.pallas_call(functools.partial(backward_kernel, buckets, n_tiles - per_...]
    ppermute x3, waiting for transfers between devices: 2.67 us -> 3.84 us  [per_device(): from_left = lax.ppermute(from_left, 'col', right)]
    unnamed x14 -> x12, local copies, waits for them, and re-layouts: 2.98 us -> 2.3 us
  transfers between devices with their start and end apart: 30 -> 30, of which waited for: 9 -> 13; matrix products, arithmetic and copies ran while one was open for 2% -> 2% of each run, Pallas kernels for 33% -> 29%
where the time goes in v7:
time: 89 us; the launch traced here: 88.6 us
  starting transfers between devices  32 us (36%)
  Pallas kernels  29.4 us (33%)
  waiting for transfers between devices  22.5 us (25%)
  local copies, waits for them, and re-layouts  3.06 us (3%)
  between operations  0.94 us (1%)
    pallas_call x4, Pallas kernels, forward(): pl.pallas_call(functools.partial(forward_kernel, buckets, cap, n_buckets,...  12.7 us
    pallas_call x4, Pallas kernels, backward(): pl.pallas_call(functools.partial(backward_kernel, buckets, n_tiles - per_...  11.1 us
    ppermute x4, starting transfers between devices, per_device(): to_right = lax.ppermute(sent[0], axes, first)  7.58 us
    ppermute x1, waiting for transfers between devices, per_device(): came = lax.ppermute(own_away, 'row', across)  6.98 us
    ppermute x3, starting transfers between devices, per_device(): from_left = lax.ppermute(from_left, 'col', right)  6.19 us
    ppermute x3, starting transfers between devices, per_device(): lax.ppermute(w_now, 'col', [(i, i ^ stages[step]) for i in range(n_col)])  5.55 us
    ppermute x3, waiting for transfers between devices, per_device(): from_left = lax.ppermute(from_left, 'col', right)  3.84 us
    ppermute x1, waiting for transfers between devices, per_device(): came_away = lax.ppermute(own, 'row', across)  3.64 us
  transfers between devices with their start and end apart: 30, of which 13 were waited for; matrix products, arithmetic and copies ran while one was open for 2% of the time, Pallas kernels for 29%

profile of v7, /device:TPU:0, one launch (start us, length us, event | category | flops | bytes accessed | tf_op | source)
XLA Modules:
  0.0 88.6 jit_solution(14479639653528375169)
XLA Ops:
  0.6 3.1 %collective-permute-start = (bf16[2,256,256]{2,1,0:T(8,128)(2,1)}, bf16[2,256,256]{2,1,0:T(8,128)(2,1)S(1)}, u32[]{:S(2)}, u32[]{:S(2)}) collective-permute-start(bf16[2,256,256]{2,1,0:T(8,128)(2,1)} %bitcast.16), channel_id=1, source_target_pairs={{0,2},{2,4},{4,6},{6,7},{7,5},{5,3},{3,1},{1,0},{8,10},{10,12},{12... | collective-permute-start | bytes 786440 | tf_op jit(solution)/shard_map/ppermute | solution.py:377
  3.7 2.0 %collective-permute-start.3 = (bf16[512,256]{1,0:T(8,128)(2,1)}, bf16[512,256]{1,0:T(8,128)(2,1)S(1)}, u32[]{:S(2)}, u32[]{:S(2)}) collective-permute-start(bf16[512,256]{1,0:T(8,128)(2,1)} %cot.1), channel_id=1, source_target_pairs={{0,16},{16,0},{8,24},{24,8},{1,17},{17,1},{9,25},{25,9},{2,18},{18... | collective-permute-start | bytes 786440 | tf_op jit(solution)/shard_map/ppermute | solution.py:380
  5.7 0.9 %copy-done.1 = bf16[512,256]{1,0:T(8,128)(2,1)S(1)} copy-done((bf16[512,256]{1,0:T(8,128)(2,1)S(1)}, bf16[512,256]{1,0:T(8,128)(2,1)}, u32[]{:S(2)}) %copy-start.1) | copy-done | bytes 262168
  6.6 0.7 copy-done.3
  7.3 0.7 copy-done.5
  8.0 2.2 %lists.1 = (s32[685]{0:T(1024)S(1)}, bf16[2,256,256]{2,1,0:T(8,128)(2,1)S(1)}) custom-call(s32[8,16]{1,0:T(8,128)S(1)} %copy-done.3, s32[8]{0:T(128)S(1)} %bitcast.23, bf16[2,256,256]{2,1,0:T(8,128)(2,1)S(1)} %bitcast.18), custom_call_target="tpu_custom_call" | custom-call | bytes 4096 | tf_op jit(solution)/shard_map/lists/pallas_call | solution.py:327
  10.2 1.8 %collective-permute-start.1 = (bf16[2,256,256]{2,1,0:T(8,128)(2,1)S(1)}, bf16[2,256,256]{2,1,0:T(8,128)(2,1)S(1)}, u32[]{:S(2)}, u32[]{:S(2)}) collective-permute-start(bf16[2,256,256]{2,1,0:T(8,128)(2,1)S(1)} %collective-permute-done.refs_1_), channel_id=1, source_target_pairs={{0,2},{2,4},{4,6},{6,7},{7,5},{5,3},{3,1},{1,0},{8,10},{10,12},{12... | collective-permute-start | bytes 786440 | tf_op jit(solution)/shard_map/ppermute | solution.py:377
  12.3 3.7 %forward_1.1.refs_2_ = f32[9,256,256]{2,1,0:T(8,128)S(1)} custom-call(s32[685]{0:T(1024)S(1)} %get-tuple-element.87.lists, bf16[128,256,256]{2,1,0:T(8,128)(2,1)} %bitcast.24, bf16[2,256,256]{2,1,0:T(8,128)(2,1)S(1)} %get-tuple-element.56.refs_0_, bf16[2,256,256]{2,1,0:T(8,128)(2,1)S(1)} %collective-permute-done.refs_1_, ...), custom_call_target="tpu_custom_call" | custom-call | flops 33554432 | bytes 131072 | tf_op jit(solution)/shard_map/forward_1/pallas_call | solution.py:362
  16.0 2.1 %collective-permute-done.1.refs_0_ = bf16[2,256,256]{2,1,0:T(8,128)(2,1)S(1)} collective-permute-done((bf16[2,256,256]{2,1,0:T(8,128)(2,1)S(1)}, bf16[2,256,256]{2,1,0:T(8,128)(2,1)S(1)}, u32[]{:S(2)}, u32[]{:S(2)}) %collective-permute-start.1) | collective-permute-done | bytes 262176 | tf_op jit(solution)/shard_map/ppermute | solution.py:377
  18.1 1.4 %collective-permute-start.4 = (bf16[2,256,256]{2,1,0:T(8,128)(2,1)S(1)}, bf16[2,256,256]{2,1,0:T(8,128)(2,1)S(1)}, u32[]{:S(2)}, u32[]{:S(2)}) collective-permute-start(bf16[2,256,256]{2,1,0:T(8,128)(2,1)S(1)} %collective-permute-done.1.refs_0_), channel_id=1, source_target_pairs={{0,2},{2,4},{4,6},{6,7},{7,5},{5,3},{3,1},{1,0},{8,10},{10,12},{12... | collective-permute-start | bytes 786440 | tf_op jit(solution)/shard_map/ppermute | solution.py:377
  19.5 0.7 collective-permute-start.7
  20.1 3.1 %forward_2.1.refs_2_ = f32[9,256,256]{2,1,0:T(8,128)S(1)} custom-call(s32[685]{0:T(1024)S(1)} %get-tuple-element.87.lists, bf16[128,256,256]{2,1,0:T(8,128)(2,1)} %bitcast.25, bf16[2,256,256]{2,1,0:T(8,128)(2,1)S(1)} %collective-permute-done.1.refs_0_, bf16[2,256,256]{2,1,0:T(8,128)(2,1)S(1)} %collective-permute-done.5.refs_1_, ...), custom_call_target="tpu_custom_call" | custom-call | flops 33554432 | bytes 131072 | tf_op jit(solution)/shard_map/forward_2/pallas_call | solution.py:362
  23.3 1.8 %collective-permute-done.4.refs_0_ = bf16[2,256,256]{2,1,0:T(8,128)(2,1)S(1)} collective-permute-done((bf16[2,256,256]{2,1,0:T(8,128)(2,1)S(1)}, bf16[2,256,256]{2,1,0:T(8,128)(2,1)S(1)}, u32[]{:S(2)}, u32[]{:S(2)}) %collective-permute-start.4) | collective-permute-done | bytes 262176 | tf_op jit(solution)/shard_map/ppermute | solution.py:377
  25.0 1.0 %collective-permute-start.6 = (bf16[1,256,256]{2,1,0:T(8,128)(2,1)S(1)}, bf16[1,256,256]{2,1,0:T(8,128)(2,1)S(1)}, u32[]{:S(2)}, u32[]{:S(2)}) collective-permute-start(bf16[1,256,256]{2,1,0:T(8,128)(2,1)S(1)} %slice.56), channel_id=1, source_target_pairs={{0,2},{2,4},{4,6},{6,7},{7,5},{5,3},{3,1},{1,0},{8,10},{10,12},{12... | collective-permute-start | bytes 393224 | tf_op jit(solution)/shard_map/ppermute | solution.py:391
  26.1 1.1 %collective-permute-start.8 = (bf16[1,256,256]{2,1,0:T(8,128)(2,1)S(1)}, bf16[1,256,256]{2,1,0:T(8,128)(2,1)S(1)}, u32[]{:S(2)}, u32[]{:S(2)}) collective-permute-start(bf16[1,256,256]{2,1,0:T(8,128)(2,1)S(1)} %slice.72), channel_id=1, source_target_pairs={{2,0},{4,2},{6,4},{7,6},{5,7},{3,5},{1,3},{0,1},{10,8},{12,10},{14... | collective-permute-start | bytes 393224 | tf_op jit(solution)/shard_map/ppermute | solution.py:392
  27.2 3.8 %forward_3.1 = (f32[9,256,256]{2,1,0:T(8,128)S(1)}, bf16[16,256,256]{2,1,0:T(8,128)(2,1)S(1)}) custom-call(s32[685]{0:T(1024)S(1)} %get-tuple-element.87.lists, bf16[128,256,256]{2,1,0:T(8,128)(2,1)} %bitcast.26, bf16[2,256,256]{2,1,0:T(8,128)(2,1)S(1)} %collective-permute-done.4.refs_0_, bf16[2,256,256]{2,1,0:T(8,128)(2,1)S(1)} %collective-permute-done.7.refs_1_, ...), custom_call_target="tpu_custom_call" | custom-call | flops 33554432 | bytes 131072 | tf_op jit(solution)/shard_map/forward_3/pallas_call | solution.py:362
  31.2 2.0 %forward_4.1 = (bf16[2,256,256]{2,1,0:T(8,128)(2,1)S(1)}, bf16[2,256,256]{2,1,0:T(8,128)(2,1)S(1)}, bf16[2,256,256]{2,1,0:T(8,128)(2,1)S(1)}, bf16[2,256,256]{2,1,0:T(8,128)(2,1)S(1)}) custom-call(s32[685]{0:T(1024)S(1)} %get-tuple-element.87.lists, bf16[128,256,256]{2,1,0:T(8,128)(2,1)} %bitcast.27, ...), custom_call_target="tpu_custom_call" | custom-call | flops 33554432 | bytes 131072 | tf_op jit(solution)/shard_map/forward_4/pallas_call | solution.py:362
  33.3 0.5 collective-permute-start.9
  33.8 1.0 %collective-permute-done.11 = bf16[2,256,256]{2,1,0:T(8,128)(2,1)S(1)} collective-permute-done((bf16[2,256,256]{2,1,0:T(8,128)(2,1)S(1)}, bf16[2,256,256]{2,1,0:T(8,128)(2,1)S(1)}, u32[]{:S(2)}, u32[]{:S(2)}) %collective-permute-start.11) | collective-permute-done | bytes 262176 | tf_op jit(solution)/shard_map/ppermute | solution.py:400
  34.9 1.4 %collective-permute-start.12 = (bf16[2,256,256]{2,1,0:T(8,128)(2,1)S(1)}, bf16[2,256,256]{2,1,0:T(8,128)(2,1)S(1)}, u32[]{:S(2)}, u32[]{:S(2)}) collective-permute-start(bf16[2,256,256]{2,1,0:T(8,128)(2,1)S(1)} %add_convert_fusion.4.near), channel_id=1, source_target_pairs={{0,16},{16,0},{8,24},{24,8},{1,17},{17,1},{9,25},{25,9},{2,18},{18... | collective-permute-start | bytes 786440 | tf_op jit(solution)/shard_map/ppermute | solution.py:403
  36.4 0.8 collective-permute-start.10
  37.1 7.0 %collective-permute-done.12.away = bf16[2,256,256]{2,1,0:T(8,128)(2,1)S(1)} collective-permute-done((bf16[2,256,256]{2,1,0:T(8,128)(2,1)S(1)}, bf16[2,256,256]{2,1,0:T(8,128)(2,1)S(1)}, u32[]{:S(2)}, u32[]{:S(2)}) %collective-permute-start.12) | collective-permute-done | bytes 262176 | tf_op jit(solution)/shard_map/ppermute | solution.py:403
  44.1 1.2 %dense_own.1 = (bf16[512,256]{1,0:T(8,128)(2,1)}, bf16[2,256,256]{2,1,0:T(8,128)(2,1)S(1)}, f32[264,256]{1,0:T(8,128)S(1)}) custom-call(bf16[2,256,256]{2,1,0:T(8,128)(2,1)S(1)} %add_convert_fusion.5.near, bf16[2,256,256]{2,1,0:T(8,128)(2,1)S(1)} %collective-permute-done.12.away, bf16[256,256]{1,0:T(8,128)(2,1)S(1)} %copy-done, f32[1,256]{1,0:T(1,128)S(1)} %bitcast.21, ...), custom_call_target="tpu_custom_call" | custom-call | flops 50331648 | bytes 131072 | tf_op jit(solution)/shard_map/dense_own/pallas_call | solution.py:411
  45.3 3.6 %collective-permute-done.10.away = bf16[2,256,256]{2,1,0:T(8,128)(2,1)S(1)} collective-permute-done((bf16[2,256,256]{2,1,0:T(8,128)(2,1)S(1)}, bf16[2,256,256]{2,1,0:T(8,128)(2,1)S(1)}, u32[]{:S(2)}, u32[]{:S(2)}) %collective-permute-start.10) | collective-permute-done | bytes 262176 | tf_op jit(solution)/shard_map/ppermute | solution.py:405
  48.9 0.7 dense_away.1
  49.7 0.4 collective-permute-start.23
  50.2 1.0 %collective-permute-done.14.refs_4_.refs_3_ = bf16[2,256,256]{2,1,0:T(8,128)(2,1)S(1)} collective-permute-done((bf16[2,256,256]{2,1,0:T(8,128)(2,1)S(1)}, bf16[2,256,256]{2,1,0:T(8,128)(2,1)S(1)}, u32[]{:S(2)}, u32[]{:S(2)}) %collective-permute-start.14) | collective-permute-done | bytes 262176 | tf_op jit(solution)/shard_map/ppermute | solution.py:437
  51.2 1.6 %backward_4.1 = f32[2,256,256]{2,1,0:T(8,128)S(1)} custom-call(s32[685]{0:T(1024)S(1)} %get-tuple-element.87.lists, bf16[128,256,256]{2,1,0:T(8,128)(2,1)} %bitcast.28, bf16[16,256,256]{2,1,0:T(8,128)(2,1)S(1)} %get-tuple-element.62.refs_3_.refs_0_, bf16[2,256,256]{2,1,0:T(8,128)(2,1)S(1)} %get-tuple-element.71.refs_1_.refs_0_, ...), custom_call_target="tpu_custom_call" | custom-call | flops 33554432 | bytes 131072 | tf_op jit(solution)/shard_map/backward_4/pallas_call | solution.py:448
  52.9 1.1 %collective-permute-start.15 = (bf16[1,256,256]{2,1,0:T(8,128)(2,1)S(1)}, bf16[1,256,256]{2,1,0:T(8,128)(2,1)S(1)}, u32[]{:S(2)}, u32[]{:S(2)}) collective-permute-start(bf16[1,256,256]{2,1,0:T(8,128)(2,1)S(1)} %get-tuple-element.77), channel_id=1, source_target_pairs={{0,2},{2,4},{4,6},{6,7},{7,5},{5,3},{3,1},{1,0},{10,8},{12,10},{14... | collective-permute-start | bytes 393224 | tf_op jit(solution)/shard_map/ppermute | solution.py:477
  54.0 1.0 %collective-permute-start.16 = (bf16[1,256,256]{2,1,0:T(8,128)(2,1)S(1)}, bf16[1,256,256]{2,1,0:T(8,128)(2,1)S(1)}, u32[]{:S(2)}, u32[]{:S(2)}) collective-permute-start(bf16[1,256,256]{2,1,0:T(8,128)(2,1)S(1)} %get-tuple-element.78), channel_id=1, source_target_pairs={{2,0},{4,2},{6,4},{7,6},{5,7},{3,5},{1,3},{0,1},{8,10},{10,12},{12... | collective-permute-start | bytes 393224 | tf_op jit(solution)/shard_map/ppermute | solution.py:478
  55.0 1.0 %collective-permute-start.24 = (bf16[80,256]{1,0:T(8,128)(2,1)S(1)}, bf16[80,256]{1,0:T(8,128)(2,1)S(1)}, u32[]{:S(2)}, u32[]{:S(2)}) collective-permute-start(bf16[80,256]{1,0:T(8,128)(2,1)S(1)} %fusion), channel_id=1, source_target_pairs={{0,1},{1,0},{2,3},{3,2},{4,5},{5,4},{6,7},{7,6},{8,9},{9,8},{10,11... | collective-permute-start | bytes 122888 | tf_op jit(solution)/shard_map/ppermute | solution.py:501
  56.0 3.5 %backward_3.1 = f32[6,256,256]{2,1,0:T(8,128)S(1)} custom-call(s32[685]{0:T(1024)S(1)} %get-tuple-element.87.lists, bf16[128,256,256]{2,1,0:T(8,128)(2,1)} %bitcast.29, bf16[2,256,256]{2,1,0:T(8,128)(2,1)S(1)} %get-tuple-element.71.refs_1_.refs_0_, bf16[2,256,256]{2,1,0:T(8,128)(2,1)S(1)} %get-tuple-element.75.refs_2_.refs_1_, ...), custom_call_target="tpu_custom_call" | custom-call | flops 33554432 | bytes 131072 | tf_op jit(solution)/shard_map/backward_3/pallas_call | solution.py:448
  59.8 1.2 %collective-permute-start.18 = (bf16[2,256,256]{2,1,0:T(8,128)(2,1)S(1)}, bf16[2,256,256]{2,1,0:T(8,128)(2,1)S(1)}, u32[]{:S(2)}, u32[]{:S(2)}) collective-permute-start(bf16[2,256,256]{2,1,0:T(8,128)(2,1)S(1)} %pad_maximum_fusion.1), channel_id=1, source_target_pairs={{2,0},{4,2},{6,4},{7,6},{5,7},{3,5},{1,3},{0,1},{8,10},{10,12},{12... | collective-permute-start | bytes 786440 | tf_op jit(solution)/shard_map/ppermute | solution.py:478
  61.0 1.3 %collective-permute-start.17 = (bf16[2,256,256]{2,1,0:T(8,128)(2,1)S(1)}, bf16[2,256,256]{2,1,0:T(8,128)(2,1)S(1)}, u32[]{:S(2)}, u32[]{:S(2)}) collective-permute-start(bf16[2,256,256]{2,1,0:T(8,128)(2,1)S(1)} %pad_maximum_fusion), channel_id=1, source_target_pairs={{0,2},{2,4},{4,6},{6,7},{7,5},{5,3},{3,1},{1,0},{10,8},{12,10},{14... | collective-permute-start | bytes 786440 | tf_op jit(solution)/shard_map/ppermute | solution.py:477
  62.3 2.1 %collective-permute-start.25 = (bf16[80,256]{1,0:T(8,128)(2,1)S(1)}, bf16[80,256]{1,0:T(8,128)(2,1)S(1)}, u32[]{:S(2)}, u32[]{:S(2)}) collective-permute-start(bf16[80,256]{1,0:T(8,128)(2,1)S(1)} %add_convert_fusion.9), channel_id=1, source_target_pairs={{0,2},{1,3},{2,0},{3,1},{4,6},{5,7},{6,4},{7,5},{8,10},{9,11},{10,... | collective-permute-start | bytes 122888 | tf_op jit(solution)/shard_map/ppermute | solution.py:501
  64.4 3.1 %backward_2.1 = f32[4,256,256]{2,1,0:T(8,128)S(1)} custom-call(s32[685]{0:T(1024)S(1)} %get-tuple-element.87.lists, bf16[128,256,256]{2,1,0:T(8,128)(2,1)} %bitcast.30, bf16[2,256,256]{2,1,0:T(8,128)(2,1)S(1)} %get-tuple-element.71.refs_1_.refs_0_, bf16[2,256,256]{2,1,0:T(8,128)(2,1)S(1)} %get-tuple-element.75.refs_2_.refs_1_, ...), custom_call_target="tpu_custom_call" | custom-call | flops 33554432 | bytes 131072 | tf_op jit(solution)/shard_map/backward_2/pallas_call | solution.py:448
  67.5 1.5 %collective-permute-done.18 = bf16[2,256,256]{2,1,0:T(8,128)(2,1)S(1)} collective-permute-done((bf16[2,256,256]{2,1,0:T(8,128)(2,1)S(1)}, bf16[2,256,256]{2,1,0:T(8,128)(2,1)S(1)}, u32[]{:S(2)}, u32[]{:S(2)}) %collective-permute-start.18) | collective-permute-done | bytes 262176 | tf_op jit(solution)/shard_map/ppermute | solution.py:478
  69.2 2.4 %collective-permute-start.19 = (bf16[2,256,256]{2,1,0:T(8,128)(2,1)S(1)}, bf16[2,256,256]{2,1,0:T(8,128)(2,1)S(1)}, u32[]{:S(2)}, u32[]{:S(2)}) collective-permute-start(bf16[2,256,256]{2,1,0:T(8,128)(2,1)S(1)} %get-tuple-element.103), channel_id=1, source_target_pairs={{0,2},{2,4},{4,6},{6,7},{7,5},{5,3},{3,1},{1,0},{10,8},{12,10},{14... | collective-permute-start | bytes 786440 | tf_op jit(solution)/shard_map/ppermute | solution.py:477
  71.6 2.4 %collective-permute-start.26 = (bf16[80,256]{1,0:T(8,128)(2,1)S(1)}, bf16[80,256]{1,0:T(8,128)(2,1)S(1)}, u32[]{:S(2)}, u32[]{:S(2)}) collective-permute-start(bf16[80,256]{1,0:T(8,128)(2,1)S(1)} %add_convert_fusion.8), channel_id=1, source_target_pairs={{0,4},{1,5},{2,6},{3,7},{4,0},{5,1},{6,2},{7,3},{8,12},{9,13},{10,... | collective-permute-start | bytes 122888 | tf_op jit(solution)/shard_map/ppermute | solution.py:501
  74.0 2.9 %backward_1.1 = f32[4,256,256]{2,1,0:T(8,128)S(1)} custom-call(s32[685]{0:T(1024)S(1)} %get-tuple-element.87.lists, bf16[128,256,256]{2,1,0:T(8,128)(2,1)} %bitcast.31, bf16[2,256,256]{2,1,0:T(8,128)(2,1)S(1)} %get-tuple-element.71.refs_1_.refs_0_, bf16[2,256,256]{2,1,0:T(8,128)(2,1)S(1)} %get-tuple-element.75.refs_2_.refs_1_, ...), custom_call_target="tpu_custom_call" | custom-call | flops 33554432 | bytes 131072 | tf_op jit(solution)/shard_map/backward_1/pallas_call | solution.py:448
  76.9 1.3 %collective-permute-done.19 = bf16[2,256,256]{2,1,0:T(8,128)(2,1)S(1)} collective-permute-done((bf16[2,256,256]{2,1,0:T(8,128)(2,1)S(1)}, bf16[2,256,256]{2,1,0:T(8,128)(2,1)S(1)}, u32[]{:S(2)}, u32[]{:S(2)}) %collective-permute-start.19) | collective-permute-done | bytes 262176 | tf_op jit(solution)/shard_map/ppermute | solution.py:477
  78.5 2.9 %collective-permute-start.21 = (bf16[2,256,256]{2,1,0:T(8,128)(2,1)S(1)}, bf16[2,256,256]{2,1,0:T(8,128)(2,1)S(1)}, u32[]{:S(2)}, u32[]{:S(2)}) collective-permute-start(bf16[2,256,256]{2,1,0:T(8,128)(2,1)S(1)} %get-tuple-element.101), channel_id=1, source_target_pairs={{0,2},{2,4},{4,6},{6,7},{7,5},{5,3},{3,1},{1,0},{10,8},{12,10},{14... | collective-permute-start | bytes 786440 | tf_op jit(solution)/shard_map/ppermute | solution.py:477
  81.7 1.9 %collective-permute-start.29 = (f32[64,256]{1,0:T(8,128)S(1)}, f32[64,256]{1,0:T(8,128)S(1)}, u32[]{:S(2)}, u32[]{:S(2)}) collective-permute-start(f32[64,256]{1,0:T(8,128)S(1)} %slice.70.own), channel_id=1, source_target_pairs={{0,24},{24,0},{8,16},{16,8},{1,25},{25,1},{9,17},{17,9},{2,26},{26... | collective-permute-start | bytes 196616 | tf_op jit(solution)/shard_map/ppermute | solution.py:483
  83.6 0.6 slice.71
  84.2 2.0 %collective-permute-done.27.y = f32[64,256]{1,0:T(8,128)S(1)} collective-permute-done((f32[64,256]{1,0:T(8,128)S(1)}, f32[64,256]{1,0:T(8,128)S(1)}, u32[]{:S(2)}, u32[]{:S(2)}) %collective-permute-start.27) | collective-permute-done | bytes 65568 | tf_op jit(solution)/shard_map/ppermute | solution.py:483
  86.3 0.7 quarters.1
  87.3 0.4 collective-permute-done.22
  87.7 0.9 finish.1
  (59 shorter events, 2.4 us)
Async XLA Ops:
  0.6 9.6 %collective-permute-start = (bf16[2,256,256]{2,1,0:T(8,128)(2,1)}, bf16[2,256,256]{2,1,0:T(8,128)(2,1)S(1)}, u32[]{:S(2)}, u32[]{:S(2)}) collective-permute-start(bf16[2,256,256]{2,1,0:T(8,128)(2,1)} %bitcast.16), channel_id=1, source_target_pairs={{0,2},{2,4},{4,6},{6,7},{7,5},{5,3},{3,1},{1,0},{8,10},{10,12},{12... | collective-permute-start | bytes 786440 | tf_op jit(solution)/shard_map/ppermute | solution.py:377
  3.7 8.3 %collective-permute-start.2 = (bf16[2,256,256]{2,1,0:T(8,128)(2,1)}, bf16[2,256,256]{2,1,0:T(8,128)(2,1)S(1)}, u32[]{:S(2)}, u32[]{:S(2)}) collective-permute-start(bf16[2,256,256]{2,1,0:T(8,128)(2,1)} %bitcast.17), channel_id=1, source_target_pairs={{2,0},{4,2},{6,4},{7,6},{5,7},{3,5},{1,3},{0,1},{10,8},{12,10},{14... | collective-permute-start | bytes 786440 | tf_op jit(solution)/shard_map/ppermute | solution.py:378
  3.7 12.3 %collective-permute-start.3 = (bf16[512,256]{1,0:T(8,128)(2,1)}, bf16[512,256]{1,0:T(8,128)(2,1)S(1)}, u32[]{:S(2)}, u32[]{:S(2)}) collective-permute-start(bf16[512,256]{1,0:T(8,128)(2,1)} %cot.1), channel_id=1, source_target_pairs={{0,16},{16,0},{8,24},{24,8},{1,17},{17,1},{9,25},{25,9},{2,18},{18... | collective-permute-start | bytes 786440 | tf_op jit(solution)/shard_map/ppermute | solution.py:380
  5.7 0.9 %copy-start.1 = (bf16[512,256]{1,0:T(8,128)(2,1)S(1)}, bf16[512,256]{1,0:T(8,128)(2,1)}, u32[]{:S(2)}) copy-start(bf16[512,256]{1,0:T(8,128)(2,1)} %param.7) | copy-start | bytes 786436
  6.6 0.7 copy-start.3
  7.3 0.7 copy-start.5
  10.2 7.9 %collective-permute-start.1 = (bf16[2,256,256]{2,1,0:T(8,128)(2,1)S(1)}, bf16[2,256,256]{2,1,0:T(8,128)(2,1)S(1)}, u32[]{:S(2)}, u32[]{:S(2)}) collective-permute-start(bf16[2,256,256]{2,1,0:T(8,128)(2,1)S(1)} %collective-permute-done.refs_1_), channel_id=1, source_target_pairs={{0,2},{2,4},{4,6},{6,7},{7,5},{5,3},{3,1},{1,0},{8,10},{10,12},{12... | collective-permute-start | bytes 786440 | tf_op jit(solution)/shard_map/ppermute | solution.py:377
  12.0 7.5 %collective-permute-start.5 = (bf16[2,256,256]{2,1,0:T(8,128)(2,1)S(1)}, bf16[2,256,256]{2,1,0:T(8,128)(2,1)S(1)}, u32[]{:S(2)}, u32[]{:S(2)}) collective-permute-start(bf16[2,256,256]{2,1,0:T(8,128)(2,1)S(1)} %collective-permute-done.2.refs_2_), channel_id=1, source_target_pairs={{2,0},{4,2},{6,4},{7,6},{5,7},{3,5},{1,3},{0,1},{10,8},{12,10},{14... | collective-permute-start | bytes 786440 | tf_op jit(solution)/shard_map/ppermute | solution.py:378
  18.1 6.9 %collective-permute-start.4 = (bf16[2,256,256]{2,1,0:T(8,128)(2,1)S(1)}, bf16[2,256,256]{2,1,0:T(8,128)(2,1)S(1)}, u32[]{:S(2)}, u32[]{:S(2)}) collective-permute-start(bf16[2,256,256]{2,1,0:T(8,128)(2,1)S(1)} %collective-permute-done.1.refs_0_), channel_id=1, source_target_pairs={{0,2},{2,4},{4,6},{6,7},{7,5},{5,3},{3,1},{1,0},{8,10},{10,12},{12... | collective-permute-start | bytes 786440 | tf_op jit(solution)/shard_map/ppermute | solution.py:377
  19.5 6.6 %collective-permute-start.7 = (bf16[2,256,256]{2,1,0:T(8,128)(2,1)S(1)}, bf16[2,256,256]{2,1,0:T(8,128)(2,1)S(1)}, u32[]{:S(2)}, u32[]{:S(2)}) collective-permute-start(bf16[2,256,256]{2,1,0:T(8,128)(2,1)S(1)} %collective-permute-done.5.refs_1_), channel_id=1, source_target_pairs={{2,0},{4,2},{6,4},{7,6},{5,7},{3,5},{1,3},{0,1},{10,8},{12,10},{14... | collective-permute-start | bytes 786440 | tf_op jit(solution)/shard_map/ppermute | solution.py:378
  25.0 6.0 %collective-permute-start.6 = (bf16[1,256,256]{2,1,0:T(8,128)(2,1)S(1)}, bf16[1,256,256]{2,1,0:T(8,128)(2,1)S(1)}, u32[]{:S(2)}, u32[]{:S(2)}) collective-permute-start(bf16[1,256,256]{2,1,0:T(8,128)(2,1)S(1)} %slice.56), channel_id=1, source_target_pairs={{0,2},{2,4},{4,6},{6,7},{7,5},{5,3},{3,1},{1,0},{8,10},{10,12},{12... | collective-permute-start | bytes 393224 | tf_op jit(solution)/shard_map/ppermute | solution.py:391
  26.1 5.1 %collective-permute-start.8 = (bf16[1,256,256]{2,1,0:T(8,128)(2,1)S(1)}, bf16[1,256,256]{2,1,0:T(8,128)(2,1)S(1)}, u32[]{:S(2)}, u32[]{:S(2)}) collective-permute-start(bf16[1,256,256]{2,1,0:T(8,128)(2,1)S(1)} %slice.72), channel_id=1, source_target_pairs={{2,0},{4,2},{6,4},{7,6},{5,7},{3,5},{1,3},{0,1},{10,8},{12,10},{14... | collective-permute-start | bytes 393224 | tf_op jit(solution)/shard_map/ppermute | solution.py:392
  31.2 12.9 %copy-start = (bf16[256,256]{1,0:T(8,128)(2,1)S(1)}, bf16[256,256]{1,0:T(8,128)(2,1)}, u32[]{:S(2)}) copy-start(bf16[256,256]{1,0:T(8,128)(2,1)} %weight.3) | copy-start | bytes 393220
  31.2 12.9 %copy-start.2 = (bf16[512,256]{1,0:T(8,128)(2,1)S(1)}, bf16[512,256]{1,0:T(8,128)(2,1)}, u32[]{:S(2)}) copy-start(bf16[512,256]{1,0:T(8,128)(2,1)} %cot.1) | copy-start | bytes 786436
  31.2 12.9 %copy-start.4 = (f32[256]{0:T(256)S(1)}, f32[256]{0:T(256)}, u32[]{:S(2)}) copy-start(f32[256]{0:T(256)} %param.12) | copy-start | bytes 3076
  33.2 1.6 %collective-permute-start.11 = (bf16[2,256,256]{2,1,0:T(8,128)(2,1)S(1)}, bf16[2,256,256]{2,1,0:T(8,128)(2,1)S(1)}, u32[]{:S(2)}, u32[]{:S(2)}) collective-permute-start(bf16[2,256,256]{2,1,0:T(8,128)(2,1)S(1)} %get-tuple-element.66), channel_id=1, source_target_pairs={{0,8},{8,0},{16,24},{24,16},{1,9},{9,1},{17,25},{25,17},{2,10},{10... | collective-permute-start | bytes 786440 | tf_op jit(solution)/shard_map/ppermute | solution.py:400
  33.3 3.0 %collective-permute-start.9 = (bf16[2,256,256]{2,1,0:T(8,128)(2,1)S(1)}, bf16[2,256,256]{2,1,0:T(8,128)(2,1)S(1)}, u32[]{:S(2)}, u32[]{:S(2)}) collective-permute-start(bf16[2,256,256]{2,1,0:T(8,128)(2,1)S(1)} %get-tuple-element.64), channel_id=1, source_target_pairs={{0,8},{8,0},{16,24},{24,16},{1,9},{9,1},{17,25},{25,17},{2,10},{10... | collective-permute-start | bytes 786440 | tf_op jit(solution)/shard_map/ppermute | solution.py:401
  34.9 9.2 %collective-permute-start.12 = (bf16[2,256,256]{2,1,0:T(8,128)(2,1)S(1)}, bf16[2,256,256]{2,1,0:T(8,128)(2,1)S(1)}, u32[]{:S(2)}, u32[]{:S(2)}) collective-permute-start(bf16[2,256,256]{2,1,0:T(8,128)(2,1)S(1)} %add_convert_fusion.4.near), channel_id=1, source_target_pairs={{0,16},{16,0},{8,24},{24,8},{1,17},{17,1},{9,25},{25,9},{2,18},{18... | collective-permute-start | bytes 786440 | tf_op jit(solution)/shard_map/ppermute | solution.py:403
  36.4 12.6 %collective-permute-start.10 = (bf16[2,256,256]{2,1,0:T(8,128)(2,1)S(1)}, bf16[2,256,256]{2,1,0:T(8,128)(2,1)S(1)}, u32[]{:S(2)}, u32[]{:S(2)}) collective-permute-start(bf16[2,256,256]{2,1,0:T(8,128)(2,1)S(1)} %add_convert_fusion.5.near), channel_id=1, source_target_pairs={{0,16},{16,0},{8,24},{24,8},{1,17},{17,1},{9,25},{25,9},{2,18},{18... | collective-permute-start | bytes 786440 | tf_op jit(solution)/shard_map/ppermute | solution.py:405
  45.3 3.6 %collective-permute-start.13 = (bf16[2,256,256]{2,1,0:T(8,128)(2,1)S(1)}, bf16[2,256,256]{2,1,0:T(8,128)(2,1)S(1)}, u32[]{:S(2)}, u32[]{:S(2)}) collective-permute-start(bf16[2,256,256]{2,1,0:T(8,128)(2,1)S(1)} %get-tuple-element.71.refs_1_.refs_0_), channel_id=1, source_target_pairs={{0,8},{8,0},{16,24},{24,16},{1,9},{9,1},{17,25},{25,17},{2,10},{10... | collective-permute-start | bytes 786440 | tf_op jit(solution)/shard_map/ppermute | solution.py:424
  49.6 1.6 %collective-permute-start.14 = (bf16[2,256,256]{2,1,0:T(8,128)(2,1)S(1)}, bf16[2,256,256]{2,1,0:T(8,128)(2,1)S(1)}, u32[]{:S(2)}, u32[]{:S(2)}) collective-permute-start(bf16[2,256,256]{2,1,0:T(8,128)(2,1)S(1)} %get-tuple-element.75.refs_2_.refs_1_), channel_id=1, source_target_pairs={{0,8},{8,0},{16,24},{24,16},{1,9},{9,1},{17,25},{25,17},{2,10},{10... | collective-permute-start | bytes 786440 | tf_op jit(solution)/shard_map/ppermute | solution.py:437
  49.7 5.2 %collective-permute-start.23 = (f32[80,256]{1,0:T(8,128)S(1)}, f32[80,256]{1,0:T(8,128)S(1)}, u32[]{:S(2)}, u32[]{:S(2)}) collective-permute-start(f32[80,256]{1,0:T(8,128)S(1)} %dynamic-slice_bitcast_fusion), channel_id=1, source_target_pairs={{0,8},{8,0},{16,24},{24,16},{1,9},{9,1},{17,25},{25,17},{2,10},{10... | collective-permute-start | bytes 245768 | tf_op jit(solution)/shard_map/ppermute | solution.py:444
  52.9 6.7 %collective-permute-start.15 = (bf16[1,256,256]{2,1,0:T(8,128)(2,1)S(1)}, bf16[1,256,256]{2,1,0:T(8,128)(2,1)S(1)}, u32[]{:S(2)}, u32[]{:S(2)}) collective-permute-start(bf16[1,256,256]{2,1,0:T(8,128)(2,1)S(1)} %get-tuple-element.77), channel_id=1, source_target_pairs={{0,2},{2,4},{4,6},{6,7},{7,5},{5,3},{3,1},{1,0},{10,8},{12,10},{14... | collective-permute-start | bytes 393224 | tf_op jit(solution)/shard_map/ppermute | solution.py:477
  54.0 5.6 %collective-permute-start.16 = (bf16[1,256,256]{2,1,0:T(8,128)(2,1)S(1)}, bf16[1,256,256]{2,1,0:T(8,128)(2,1)S(1)}, u32[]{:S(2)}, u32[]{:S(2)}) collective-permute-start(bf16[1,256,256]{2,1,0:T(8,128)(2,1)S(1)} %get-tuple-element.78), channel_id=1, source_target_pairs={{2,0},{4,2},{6,4},{7,6},{5,7},{3,5},{1,3},{0,1},{8,10},{10,12},{12... | collective-permute-start | bytes 393224 | tf_op jit(solution)/shard_map/ppermute | solution.py:478
  55.0 7.3 %collective-permute-start.24 = (bf16[80,256]{1,0:T(8,128)(2,1)S(1)}, bf16[80,256]{1,0:T(8,128)(2,1)S(1)}, u32[]{:S(2)}, u32[]{:S(2)}) collective-permute-start(bf16[80,256]{1,0:T(8,128)(2,1)S(1)} %fusion), channel_id=1, source_target_pairs={{0,1},{1,0},{2,3},{3,2},{4,5},{5,4},{6,7},{7,6},{8,9},{9,8},{10,11... | collective-permute-start | bytes 122888 | tf_op jit(solution)/shard_map/ppermute | solution.py:501
  59.8 9.2 %collective-permute-start.18 = (bf16[2,256,256]{2,1,0:T(8,128)(2,1)S(1)}, bf16[2,256,256]{2,1,0:T(8,128)(2,1)S(1)}, u32[]{:S(2)}, u32[]{:S(2)}) collective-permute-start(bf16[2,256,256]{2,1,0:T(8,128)(2,1)S(1)} %pad_maximum_fusion.1), channel_id=1, source_target_pairs={{2,0},{4,2},{6,4},{7,6},{5,7},{3,5},{1,3},{0,1},{8,10},{10,12},{12... | collective-permute-start | bytes 786440 | tf_op jit(solution)/shard_map/ppermute | solution.py:478
  61.0 8.0 %collective-permute-start.17 = (bf16[2,256,256]{2,1,0:T(8,128)(2,1)S(1)}, bf16[2,256,256]{2,1,0:T(8,128)(2,1)S(1)}, u32[]{:S(2)}, u32[]{:S(2)}) collective-permute-start(bf16[2,256,256]{2,1,0:T(8,128)(2,1)S(1)} %pad_maximum_fusion), channel_id=1, source_target_pairs={{0,2},{2,4},{4,6},{6,7},{7,5},{5,3},{3,1},{1,0},{10,8},{12,10},{14... | collective-permute-start | bytes 786440 | tf_op jit(solution)/shard_map/ppermute | solution.py:477
  62.3 9.3 %collective-permute-start.25 = (bf16[80,256]{1,0:T(8,128)(2,1)S(1)}, bf16[80,256]{1,0:T(8,128)(2,1)S(1)}, u32[]{:S(2)}, u32[]{:S(2)}) collective-permute-start(bf16[80,256]{1,0:T(8,128)(2,1)S(1)} %add_convert_fusion.9), channel_id=1, source_target_pairs={{0,2},{1,3},{2,0},{3,1},{4,6},{5,7},{6,4},{7,5},{8,10},{9,11},{10,... | collective-permute-start | bytes 122888 | tf_op jit(solution)/shard_map/ppermute | solution.py:501
  69.2 9.0 %collective-permute-start.19 = (bf16[2,256,256]{2,1,0:T(8,128)(2,1)S(1)}, bf16[2,256,256]{2,1,0:T(8,128)(2,1)S(1)}, u32[]{:S(2)}, u32[]{:S(2)}) collective-permute-start(bf16[2,256,256]{2,1,0:T(8,128)(2,1)S(1)} %get-tuple-element.103), channel_id=1, source_target_pairs={{0,2},{2,4},{4,6},{6,7},{7,5},{5,3},{3,1},{1,0},{10,8},{12,10},{14... | collective-permute-start | bytes 786440 | tf_op jit(solution)/shard_map/ppermute | solution.py:477
  71.5 6.8 %collective-permute-start.20 = (bf16[2,256,256]{2,1,0:T(8,128)(2,1)S(1)}, bf16[2,256,256]{2,1,0:T(8,128)(2,1)S(1)}, u32[]{:S(2)}, u32[]{:S(2)}) collective-permute-start(bf16[2,256,256]{2,1,0:T(8,128)(2,1)S(1)} %get-tuple-element.102), channel_id=1, source_target_pairs={{2,0},{4,2},{6,4},{7,6},{5,7},{3,5},{1,3},{0,1},{8,10},{10,12},{12... | collective-permute-start | bytes 786440 | tf_op jit(solution)/shard_map/ppermute | solution.py:478
  71.6 9.8 %collective-permute-start.26 = (bf16[80,256]{1,0:T(8,128)(2,1)S(1)}, bf16[80,256]{1,0:T(8,128)(2,1)S(1)}, u32[]{:S(2)}, u32[]{:S(2)}) collective-permute-start(bf16[80,256]{1,0:T(8,128)(2,1)S(1)} %add_convert_fusion.8), channel_id=1, source_target_pairs={{0,4},{1,5},{2,6},{3,7},{4,0},{5,1},{6,2},{7,3},{8,12},{9,13},{10,... | collective-permute-start | bytes 122888 | tf_op jit(solution)/shard_map/ppermute | solution.py:501
  78.5 8.8 %collective-permute-start.21 = (bf16[2,256,256]{2,1,0:T(8,128)(2,1)S(1)}, bf16[2,256,256]{2,1,0:T(8,128)(2,1)S(1)}, u32[]{:S(2)}, u32[]{:S(2)}) collective-permute-start(bf16[2,256,256]{2,1,0:T(8,128)(2,1)S(1)} %get-tuple-element.101), channel_id=1, source_target_pairs={{0,2},{2,4},{4,6},{6,7},{7,5},{5,3},{3,1},{1,0},{10,8},{12,10},{14... | collective-permute-start | bytes 786440 | tf_op jit(solution)/shard_map/ppermute | solution.py:477
  81.4 6.4 %collective-permute-start.22 = (bf16[2,256,256]{2,1,0:T(8,128)(2,1)S(1)}, bf16[2,256,256]{2,1,0:T(8,128)(2,1)S(1)}, u32[]{:S(2)}, u32[]{:S(2)}) collective-permute-start(bf16[2,256,256]{2,1,0:T(8,128)(2,1)S(1)} %get-tuple-element.100), channel_id=1, source_target_pairs={{2,0},{4,2},{6,4},{7,6},{5,7},{3,5},{1,3},{0,1},{8,10},{10,12},{12... | collective-permute-start | bytes 786440 | tf_op jit(solution)/shard_map/ppermute | solution.py:478
  81.4 4.9 %collective-permute-start.27 = (f32[64,256]{1,0:T(8,128)S(1)}, f32[64,256]{1,0:T(8,128)S(1)}, u32[]{:S(2)}, u32[]{:S(2)}) collective-permute-start(f32[64,256]{1,0:T(8,128)S(1)} %slice.70.own), channel_id=1, source_target_pairs={{0,16},{16,0},{8,24},{24,8},{1,17},{17,1},{9,25},{25,9},{2,18},{18... | collective-permute-start | bytes 196616 | tf_op jit(solution)/shard_map/ppermute | solution.py:483
  81.7 4.5 %collective-permute-start.28 = (f32[64,256]{1,0:T(8,128)S(1)}, f32[64,256]{1,0:T(8,128)S(1)}, u32[]{:S(2)}, u32[]{:S(2)}) collective-permute-start(f32[64,256]{1,0:T(8,128)S(1)} %slice.70.own), channel_id=1, source_target_pairs={{0,8},{8,0},{16,24},{24,16},{1,9},{9,1},{17,25},{25,17},{2,10},{10... | collective-permute-start | bytes 196616 | tf_op jit(solution)/shard_map/ppermute | solution.py:483
  81.7 4.5 %collective-permute-start.29 = (f32[64,256]{1,0:T(8,128)S(1)}, f32[64,256]{1,0:T(8,128)S(1)}, u32[]{:S(2)}, u32[]{:S(2)}) collective-permute-start(f32[64,256]{1,0:T(8,128)S(1)} %slice.70.own), channel_id=1, source_target_pairs={{0,24},{24,0},{8,16},{16,8},{1,25},{25,1},{9,17},{17,9},{2,26},{26... | collective-permute-start | bytes 196616 | tf_op jit(solution)/shard_map/ppermute | solution.py:483

commit v8 on v7

--- a/solution.py
+++ b/solution.py
@@ -371,26 +371,24 @@
         )(lists, values, *blocks, *before, *early)
 
     from_left = from_right = mine
-    cot_other = None
     for s in range(1, half):
         now = [from_left, from_right]
         from_left = lax.ppermute(from_left, "col", right)
         from_right = lax.ppermute(from_right, "col", left)
         if s == 1:
-            cot_other = lax.ppermute(cotangent, "row", across)
             from_left, lists, kept = lax.optimization_barrier((from_left, lists, kept))
         else:
             if s == 2:
                 (total,) = forward([0, 1], [kept, *now], [])
             else:
                 (total,) = forward([s - 1], now, [total])
-            if s == 2:
-                from_left, total, cot_other = lax.optimization_barrier((from_left, total, cot_other))
-            else:
-                from_left, total = lax.optimization_barrier((from_left, total))
+            from_left, total = lax.optimization_barrier((from_left, total))
+    cot_sent, total = lax.optimization_barrier((cotangent, total))
+    cot_other = lax.ppermute(cot_sent, "row", across)
     far_near = lax.ppermute(from_left[: per_dev // 2], "col", right)
     far_away = lax.ppermute(from_right[per_dev // 2 :], "col", left)
     total, early = forward([half - 1], [from_left, from_right], [total], "next")
+    far_near, cot_other = lax.optimization_barrier((far_near, cot_other))
     own_1, own_2, other_1, other_2 = forward([half], [far_near, far_away], [total], "last", [early])
 
     def add(local, came):

time: 89 us -> 89.1 us (level)
  starting transfers between devices: 32 us -> 30.7 us
  Pallas kernels: 29.4 us -> 30.5 us
    ppermute x4, starting transfers between devices: 7.58 us -> 5.58 us  [per_device(): to_right = lax.ppermute(sent[0], axes, first)]
    ppermute x4, waiting for transfers between devices: 1.66 us -> 0.42 us  [per_device(): to_right = lax.ppermute(sent[0], axes, first)]
  transfers between devices with their start and end apart: 30 -> 30, of which waited for: 13 -> 12; matrix products, arithmetic and copies ran while one was open for 2% -> 2% of each run, Pallas kernels for 29% -> 30%
where the time goes in v8:
time: 89.1 us; the launch traced here: 89.2 us
  starting transfers between devices  30.7 us (34%)
  Pallas kernels  30.5 us (34%)
  waiting for transfers between devices  23.2 us (26%)
  local copies, waits for them, and re-layouts  3.14 us (4%)
  between operations  0.96 us (1%)
    pallas_call x4, Pallas kernels, forward(): pl.pallas_call(functools.partial(forward_kernel, buckets, cap, n_buckets,...  13 us
    pallas_call x4, Pallas kernels, backward(): pl.pallas_call(functools.partial(backward_kernel, buckets, n_tiles - per_...  11.6 us
    ppermute x1, waiting for transfers between devices, per_device(): came = lax.ppermute(own_away, 'row', across)  6.98 us
    ppermute x3, starting transfers between devices, per_device(): from_left = lax.ppermute(from_left, 'col', right)  6.8 us
    ppermute x4, starting transfers between devices, per_device(): to_right = lax.ppermute(sent[0], axes, first)  5.58 us
    ppermute x3, starting transfers between devices, per_device(): lax.ppermute(w_now, 'col', [(i, i ^ stages[step]) for i in range(n_col)])  4.89 us
    ppermute x3, waiting for transfers between devices, per_device(): from_left = lax.ppermute(from_left, 'col', right)  4.36 us
    ppermute x1, waiting for transfers between devices, per_device(): came_away = lax.ppermute(own, 'row', across)  3.65 us
  transfers between devices with their start and end apart: 30, of which 12 were waited for; matrix products, arithmetic and copies ran while one was open for 2% of the time, Pallas kernels for 30%

profile of v8, /device:TPU:0, one launch (start us, length us, event | category | flops | bytes accessed | tf_op | source)
XLA Modules:
  0.0 89.2 jit_solution(16554951559552530620)
XLA Ops:
  0.6 3.1 %collective-permute-start = (bf16[2,256,256]{2,1,0:T(8,128)(2,1)}, bf16[2,256,256]{2,1,0:T(8,128)(2,1)S(1)}, u32[]{:S(2)}, u32[]{:S(2)}) collective-permute-start(bf16[2,256,256]{2,1,0:T(8,128)(2,1)} %bitcast.16), channel_id=1, source_target_pairs={{0,2},{2,4},{4,6},{6,7},{7,5},{5,3},{3,1},{1,0},{8,10},{10,12},{12... | collective-permute-start | bytes 786440 | tf_op jit(solution)/shard_map/ppermute | solution.py:376
  3.7 1.0 %copy-done.1 = bf16[512,256]{1,0:T(8,128)(2,1)S(1)} copy-done((bf16[512,256]{1,0:T(8,128)(2,1)S(1)}, bf16[512,256]{1,0:T(8,128)(2,1)}, u32[]{:S(2)}) %copy-start.1) | copy-done | bytes 262168
  4.7 0.7 copy-done.3
  5.4 0.7 copy-done.5
  6.1 2.5 %lists.1 = (s32[685]{0:T(1024)S(1)}, bf16[2,256,256]{2,1,0:T(8,128)(2,1)S(1)}) custom-call(s32[8,16]{1,0:T(8,128)S(1)} %copy-done.3, s32[8]{0:T(128)S(1)} %bitcast.23, bf16[2,256,256]{2,1,0:T(8,128)(2,1)S(1)} %bitcast.18), custom_call_target="tpu_custom_call" | custom-call | bytes 4096 | tf_op jit(solution)/shard_map/lists/pallas_call | solution.py:327
  8.6 1.5 %collective-permute-done.refs_1_ = bf16[2,256,256]{2,1,0:T(8,128)(2,1)S(1)} collective-permute-done((bf16[2,256,256]{2,1,0:T(8,128)(2,1)}, bf16[2,256,256]{2,1,0:T(8,128)(2,1)S(1)}, u32[]{:S(2)}, u32[]{:S(2)}) %collective-permute-start) | collective-permute-done | bytes 262176 | tf_op jit(solution)/shard_map/ppermute | solution.py:376
  10.1 1.8 %collective-permute-start.1 = (bf16[2,256,256]{2,1,0:T(8,128)(2,1)S(1)}, bf16[2,256,256]{2,1,0:T(8,128)(2,1)S(1)}, u32[]{:S(2)}, u32[]{:S(2)}) collective-permute-start(bf16[2,256,256]{2,1,0:T(8,128)(2,1)S(1)} %collective-permute-done.refs_1_), channel_id=1, source_target_pairs={{0,2},{2,4},{4,6},{6,7},{7,5},{5,3},{3,1},{1,0},{8,10},{10,12},{12... | collective-permute-start | bytes 786440 | tf_op jit(solution)/shard_map/ppermute | solution.py:376
  12.2 4.4 %forward_1.1.refs_2_ = f32[9,256,256]{2,1,0:T(8,128)S(1)} custom-call(s32[685]{0:T(1024)S(1)} %get-tuple-element.93.lists, bf16[128,256,256]{2,1,0:T(8,128)(2,1)} %bitcast.24, bf16[2,256,256]{2,1,0:T(8,128)(2,1)S(1)} %get-tuple-element.59.refs_0_, bf16[2,256,256]{2,1,0:T(8,128)(2,1)S(1)} %collective-permute-done.refs_1_, ...), custom_call_target="tpu_custom_call" | custom-call | flops 33554432 | bytes 131072 | tf_op jit(solution)/shard_map/forward_1/pallas_call | solution.py:362
  16.6 1.1 %collective-permute-done.1.refs_0_ = bf16[2,256,256]{2,1,0:T(8,128)(2,1)S(1)} collective-permute-done((bf16[2,256,256]{2,1,0:T(8,128)(2,1)S(1)}, bf16[2,256,256]{2,1,0:T(8,128)(2,1)S(1)}, u32[]{:S(2)}, u32[]{:S(2)}) %collective-permute-start.1) | collective-permute-done | bytes 262176 | tf_op jit(solution)/shard_map/ppermute | solution.py:376
  17.6 1.9 %collective-permute-start.3 = (bf16[2,256,256]{2,1,0:T(8,128)(2,1)S(1)}, bf16[2,256,256]{2,1,0:T(8,128)(2,1)S(1)}, u32[]{:S(2)}, u32[]{:S(2)}) collective-permute-start(bf16[2,256,256]{2,1,0:T(8,128)(2,1)S(1)} %collective-permute-done.1.refs_0_), channel_id=1, source_target_pairs={{0,2},{2,4},{4,6},{6,7},{7,5},{5,3},{3,1},{1,0},{8,10},{10,12},{12... | collective-permute-start | bytes 786440 | tf_op jit(solution)/shard_map/ppermute | solution.py:376
  19.7 2.7 %forward_2.1.refs_2_ = f32[9,256,256]{2,1,0:T(8,128)S(1)} custom-call(s32[685]{0:T(1024)S(1)} %get-tuple-element.93.lists, bf16[128,256,256]{2,1,0:T(8,128)(2,1)} %bitcast.25, bf16[2,256,256]{2,1,0:T(8,128)(2,1)S(1)} %collective-permute-done.1.refs_0_, bf16[2,256,256]{2,1,0:T(8,128)(2,1)S(1)} %collective-permute-done.4.refs_1_, ...), custom_call_target="tpu_custom_call" | custom-call | flops 33554432 | bytes 131072 | tf_op jit(solution)/shard_map/forward_2/pallas_call | solution.py:362
  22.4 1.8 %collective-permute-done.3.refs_0_ = bf16[2,256,256]{2,1,0:T(8,128)(2,1)S(1)} collective-permute-done((bf16[2,256,256]{2,1,0:T(8,128)(2,1)S(1)}, bf16[2,256,256]{2,1,0:T(8,128)(2,1)S(1)}, u32[]{:S(2)}, u32[]{:S(2)}) %collective-permute-start.3) | collective-permute-done | bytes 262176 | tf_op jit(solution)/shard_map/ppermute | solution.py:376
  24.2 2.1 %collective-permute-start.6 = (bf16[512,256]{1,0:T(8,128)(2,1)S(1)}, bf16[512,256]{1,0:T(8,128)(2,1)S(1)}, u32[]{:S(2)}, u32[]{:S(2)}) collective-permute-start(bf16[512,256]{1,0:T(8,128)(2,1)S(1)} %copy-done.2), channel_id=1, source_target_pairs={{0,16},{16,0},{8,24},{24,8},{1,17},{17,1},{9,25},{25,9},{2,18},{18... | collective-permute-start | bytes 786440 | tf_op jit(solution)/shard_map/ppermute | solution.py:387
  26.3 0.8 collective-permute-start.5
  27.1 1.3 %collective-permute-start.8 = (bf16[1,256,256]{2,1,0:T(8,128)(2,1)S(1)}, bf16[1,256,256]{2,1,0:T(8,128)(2,1)S(1)}, u32[]{:S(2)}, u32[]{:S(2)}) collective-permute-start(bf16[1,256,256]{2,1,0:T(8,128)(2,1)S(1)} %slice.72), channel_id=1, source_target_pairs={{2,0},{4,2},{6,4},{7,6},{5,7},{3,5},{1,3},{0,1},{10,8},{12,10},{14... | collective-permute-start | bytes 393224 | tf_op jit(solution)/shard_map/ppermute | solution.py:389
  28.4 3.8 %forward_3.1 = (f32[9,256,256]{2,1,0:T(8,128)S(1)}, bf16[16,256,256]{2,1,0:T(8,128)(2,1)S(1)}) custom-call(s32[685]{0:T(1024)S(1)} %get-tuple-element.93.lists, bf16[128,256,256]{2,1,0:T(8,128)(2,1)} %bitcast.26, bf16[2,256,256]{2,1,0:T(8,128)(2,1)S(1)} %collective-permute-done.3.refs_0_, bf16[2,256,256]{2,1,0:T(8,128)(2,1)S(1)} %collective-permute-done.7.refs_1_, ...), custom_call_target="tpu_custom_call" | custom-call | flops 33554432 | bytes 131072 | tf_op jit(solution)/shard_map/forward_3/pallas_call | solution.py:362
  32.3 2.0 %forward_4.1 = (bf16[2,256,256]{2,1,0:T(8,128)(2,1)S(1)}, bf16[2,256,256]{2,1,0:T(8,128)(2,1)S(1)}, bf16[2,256,256]{2,1,0:T(8,128)(2,1)S(1)}, bf16[2,256,256]{2,1,0:T(8,128)(2,1)S(1)}) custom-call(s32[685]{0:T(1024)S(1)} %get-tuple-element.93.lists, bf16[128,256,256]{2,1,0:T(8,128)(2,1)} %bitcast.27, ...), custom_call_target="tpu_custom_call" | custom-call | flops 33554432 | bytes 131072 | tf_op jit(solution)/shard_map/forward_4/pallas_call | solution.py:362
  34.4 0.5 collective-permute-start.9
  34.9 1.0 %collective-permute-done.11 = bf16[2,256,256]{2,1,0:T(8,128)(2,1)S(1)} collective-permute-done((bf16[2,256,256]{2,1,0:T(8,128)(2,1)S(1)}, bf16[2,256,256]{2,1,0:T(8,128)(2,1)S(1)}, u32[]{:S(2)}, u32[]{:S(2)}) %collective-permute-start.11) | collective-permute-done | bytes 262176 | tf_op jit(solution)/shard_map/ppermute | solution.py:398
  36.0 0.8 collective-permute-start.12
  36.9 1.3 %collective-permute-start.10 = (bf16[2,256,256]{2,1,0:T(8,128)(2,1)S(1)}, bf16[2,256,256]{2,1,0:T(8,128)(2,1)S(1)}, u32[]{:S(2)}, u32[]{:S(2)}) collective-permute-start(bf16[2,256,256]{2,1,0:T(8,128)(2,1)S(1)} %add_convert_fusion.5.near), channel_id=1, source_target_pairs={{0,16},{16,0},{8,24},{24,8},{1,17},{17,1},{9,25},{25,9},{2,18},{18... | collective-permute-start | bytes 786440 | tf_op jit(solution)/shard_map/ppermute | solution.py:403
  38.2 7.0 %collective-permute-done.12.away = bf16[2,256,256]{2,1,0:T(8,128)(2,1)S(1)} collective-permute-done((bf16[2,256,256]{2,1,0:T(8,128)(2,1)S(1)}, bf16[2,256,256]{2,1,0:T(8,128)(2,1)S(1)}, u32[]{:S(2)}, u32[]{:S(2)}) %collective-permute-start.12) | collective-permute-done | bytes 262176 | tf_op jit(solution)/shard_map/ppermute | solution.py:401
  45.2 1.2 %dense_own.1 = (bf16[512,256]{1,0:T(8,128)(2,1)}, bf16[2,256,256]{2,1,0:T(8,128)(2,1)S(1)}, f32[264,256]{1,0:T(8,128)S(1)}) custom-call(bf16[2,256,256]{2,1,0:T(8,128)(2,1)S(1)} %add_convert_fusion.5.near, bf16[2,256,256]{2,1,0:T(8,128)(2,1)S(1)} %collective-permute-done.12.away, bf16[256,256]{1,0:T(8,128)(2,1)S(1)} %copy-done, f32[1,256]{1,0:T(1,128)S(1)} %bitcast.21, ...), custom_call_target="tpu_custom_call" | custom-call | flops 50331648 | bytes 131072 | tf_op jit(solution)/shard_map/dense_own/pallas_call | solution.py:409
  46.4 3.6 %collective-permute-done.10.away = bf16[2,256,256]{2,1,0:T(8,128)(2,1)S(1)} collective-permute-done((bf16[2,256,256]{2,1,0:T(8,128)(2,1)S(1)}, bf16[2,256,256]{2,1,0:T(8,128)(2,1)S(1)}, u32[]{:S(2)}, u32[]{:S(2)}) %collective-permute-start.10) | collective-permute-done | bytes 262176 | tf_op jit(solution)/shard_map/ppermute | solution.py:403
  50.0 0.7 dense_away.1
  50.8 0.4 collective-permute-start.23
  51.3 1.0 %collective-permute-done.14.refs_4_.refs_3_ = bf16[2,256,256]{2,1,0:T(8,128)(2,1)S(1)} collective-permute-done((bf16[2,256,256]{2,1,0:T(8,128)(2,1)S(1)}, bf16[2,256,256]{2,1,0:T(8,128)(2,1)S(1)}, u32[]{:S(2)}, u32[]{:S(2)}) %collective-permute-start.14) | collective-permute-done | bytes 262176 | tf_op jit(solution)/shard_map/ppermute | solution.py:435
  52.3 1.6 %backward_4.1 = f32[2,256,256]{2,1,0:T(8,128)S(1)} custom-call(s32[685]{0:T(1024)S(1)} %get-tuple-element.93.lists, bf16[128,256,256]{2,1,0:T(8,128)(2,1)} %bitcast.28, bf16[16,256,256]{2,1,0:T(8,128)(2,1)S(1)} %get-tuple-element.68.refs_3_.refs_0_, bf16[2,256,256]{2,1,0:T(8,128)(2,1)S(1)} %get-tuple-element.77.refs_1_.refs_0_, ...), custom_call_target="tpu_custom_call" | custom-call | flops 33554432 | bytes 131072 | tf_op jit(solution)/shard_map/backward_4/pallas_call | solution.py:446
  54.0 1.6 %collective-permute-start.15 = (bf16[1,256,256]{2,1,0:T(8,128)(2,1)S(1)}, bf16[1,256,256]{2,1,0:T(8,128)(2,1)S(1)}, u32[]{:S(2)}, u32[]{:S(2)}) collective-permute-start(bf16[1,256,256]{2,1,0:T(8,128)(2,1)S(1)} %get-tuple-element.83), channel_id=1, source_target_pairs={{0,2},{2,4},{4,6},{6,7},{7,5},{5,3},{3,1},{1,0},{10,8},{12,10},{14... | collective-permute-start | bytes 393224 | tf_op jit(solution)/shard_map/ppermute | solution.py:475
  55.6 0.4 collective-permute-start.16
  56.1 1.2 %collective-permute-start.24 = (bf16[80,256]{1,0:T(8,128)(2,1)S(1)}, bf16[80,256]{1,0:T(8,128)(2,1)S(1)}, u32[]{:S(2)}, u32[]{:S(2)}) collective-permute-start(bf16[80,256]{1,0:T(8,128)(2,1)S(1)} %fusion), channel_id=1, source_target_pairs={{0,1},{1,0},{2,3},{3,2},{4,5},{5,4},{6,7},{7,6},{8,9},{9,8},{10,11... | collective-permute-start | bytes 122888 | tf_op jit(solution)/shard_map/ppermute | solution.py:499
  57.3 3.9 %backward_3.1 = f32[6,256,256]{2,1,0:T(8,128)S(1)} custom-call(s32[685]{0:T(1024)S(1)} %get-tuple-element.93.lists, bf16[128,256,256]{2,1,0:T(8,128)(2,1)} %bitcast.29, bf16[2,256,256]{2,1,0:T(8,128)(2,1)S(1)} %get-tuple-element.77.refs_1_.refs_0_, bf16[2,256,256]{2,1,0:T(8,128)(2,1)S(1)} %get-tuple-element.81.refs_2_.refs_1_, ...), custom_call_target="tpu_custom_call" | custom-call | flops 33554432 | bytes 131072 | tf_op jit(solution)/shard_map/backward_3/pallas_call | solution.py:446
  61.9 1.7 %collective-permute-start.17 = (bf16[2,256,256]{2,1,0:T(8,128)(2,1)S(1)}, bf16[2,256,256]{2,1,0:T(8,128)(2,1)S(1)}, u32[]{:S(2)}, u32[]{:S(2)}) collective-permute-start(bf16[2,256,256]{2,1,0:T(8,128)(2,1)S(1)} %pad_maximum_fusion), channel_id=1, source_target_pairs={{0,2},{2,4},{4,6},{6,7},{7,5},{5,3},{3,1},{1,0},{10,8},{12,10},{14... | collective-permute-start | bytes 786440 | tf_op jit(solution)/shard_map/ppermute | solution.py:475
  63.7 1.8 %collective-permute-start.25 = (bf16[80,256]{1,0:T(8,128)(2,1)S(1)}, bf16[80,256]{1,0:T(8,128)(2,1)S(1)}, u32[]{:S(2)}, u32[]{:S(2)}) collective-permute-start(bf16[80,256]{1,0:T(8,128)(2,1)S(1)} %add_convert_fusion.9), channel_id=1, source_target_pairs={{0,2},{1,3},{2,0},{3,1},{4,6},{5,7},{6,4},{7,5},{8,10},{9,11},{10,... | collective-permute-start | bytes 122888 | tf_op jit(solution)/shard_map/ppermute | solution.py:499
  65.5 2.8 %backward_2.1 = f32[4,256,256]{2,1,0:T(8,128)S(1)} custom-call(s32[685]{0:T(1024)S(1)} %get-tuple-element.93.lists, bf16[128,256,256]{2,1,0:T(8,128)(2,1)} %bitcast.30, bf16[2,256,256]{2,1,0:T(8,128)(2,1)S(1)} %get-tuple-element.77.refs_1_.refs_0_, bf16[2,256,256]{2,1,0:T(8,128)(2,1)S(1)} %get-tuple-element.81.refs_2_.refs_1_, ...), custom_call_target="tpu_custom_call" | custom-call | flops 33554432 | bytes 131072 | tf_op jit(solution)/shard_map/backward_2/pallas_call | solution.py:446
  68.2 2.4 %collective-permute-done.18 = bf16[2,256,256]{2,1,0:T(8,128)(2,1)S(1)} collective-permute-done((bf16[2,256,256]{2,1,0:T(8,128)(2,1)S(1)}, bf16[2,256,256]{2,1,0:T(8,128)(2,1)S(1)}, u32[]{:S(2)}, u32[]{:S(2)}) %collective-permute-start.18) | collective-permute-done | bytes 262176 | tf_op jit(solution)/shard_map/ppermute | solution.py:476
  70.8 0.6 collective-permute-start.19
  71.4 1.5 %collective-permute-start.20 = (bf16[2,256,256]{2,1,0:T(8,128)(2,1)S(1)}, bf16[2,256,256]{2,1,0:T(8,128)(2,1)S(1)}, u32[]{:S(2)}, u32[]{:S(2)}) collective-permute-start(bf16[2,256,256]{2,1,0:T(8,128)(2,1)S(1)} %get-tuple-element.108), channel_id=1, source_target_pairs={{2,0},{4,2},{6,4},{7,6},{5,7},{3,5},{1,3},{0,1},{8,10},{10,12},{12... | collective-permute-start | bytes 786440 | tf_op jit(solution)/shard_map/ppermute | solution.py:476
  72.9 1.9 %collective-permute-start.26 = (bf16[80,256]{1,0:T(8,128)(2,1)S(1)}, bf16[80,256]{1,0:T(8,128)(2,1)S(1)}, u32[]{:S(2)}, u32[]{:S(2)}) collective-permute-start(bf16[80,256]{1,0:T(8,128)(2,1)S(1)} %add_convert_fusion.8), channel_id=1, source_target_pairs={{0,4},{1,5},{2,6},{3,7},{4,0},{5,1},{6,2},{7,3},{8,12},{9,13},{10,... | collective-permute-start | bytes 122888 | tf_op jit(solution)/shard_map/ppermute | solution.py:499
  74.8 3.3 %backward_1.1 = f32[4,256,256]{2,1,0:T(8,128)S(1)} custom-call(s32[685]{0:T(1024)S(1)} %get-tuple-element.93.lists, bf16[128,256,256]{2,1,0:T(8,128)(2,1)} %bitcast.31, bf16[2,256,256]{2,1,0:T(8,128)(2,1)S(1)} %get-tuple-element.77.refs_1_.refs_0_, bf16[2,256,256]{2,1,0:T(8,128)(2,1)S(1)} %get-tuple-element.81.refs_2_.refs_1_, ...), custom_call_target="tpu_custom_call" | custom-call | flops 33554432 | bytes 131072 | tf_op jit(solution)/shard_map/backward_1/pallas_call | solution.py:446
  79.0 1.6 %collective-permute-start.21 = (bf16[2,256,256]{2,1,0:T(8,128)(2,1)S(1)}, bf16[2,256,256]{2,1,0:T(8,128)(2,1)S(1)}, u32[]{:S(2)}, u32[]{:S(2)}) collective-permute-start(bf16[2,256,256]{2,1,0:T(8,128)(2,1)S(1)} %get-tuple-element.107), channel_id=1, source_target_pairs={{0,2},{2,4},{4,6},{6,7},{7,5},{5,3},{3,1},{1,0},{10,8},{12,10},{14... | collective-permute-start | bytes 786440 | tf_op jit(solution)/shard_map/ppermute | solution.py:475
  80.6 0.5 collective-permute-start.22
  81.1 2.7 %collective-permute-start.27 = (f32[64,256]{1,0:T(8,128)S(1)}, f32[64,256]{1,0:T(8,128)S(1)}, u32[]{:S(2)}, u32[]{:S(2)}) collective-permute-start(f32[64,256]{1,0:T(8,128)S(1)} %slice.70.own), channel_id=1, source_target_pairs={{0,16},{16,0},{8,24},{24,8},{1,17},{17,1},{9,25},{25,9},{2,18},{18... | collective-permute-start | bytes 196616 | tf_op jit(solution)/shard_map/ppermute | solution.py:481
  84.1 0.6 slice.71
  84.7 1.5 %collective-permute-done.27.y = f32[64,256]{1,0:T(8,128)S(1)} collective-permute-done((f32[64,256]{1,0:T(8,128)S(1)}, f32[64,256]{1,0:T(8,128)S(1)}, u32[]{:S(2)}, u32[]{:S(2)}) %collective-permute-start.27) | collective-permute-done | bytes 65568 | tf_op jit(solution)/shard_map/ppermute | solution.py:481
  86.2 1.4 %collective-permute-done.29.both = f32[64,256]{1,0:T(8,128)S(1)} collective-permute-done((f32[64,256]{1,0:T(8,128)S(1)}, f32[64,256]{1,0:T(8,128)S(1)}, u32[]{:S(2)}, u32[]{:S(2)}) %collective-permute-start.29) | collective-permute-done | bytes 65568 | tf_op jit(solution)/shard_map/ppermute | solution.py:481
  87.6 0.7 quarters.1
  88.3 0.9 finish.1
  (59 shorter events, 2.8 us)
Async XLA Ops:
  0.6 9.5 %collective-permute-start = (bf16[2,256,256]{2,1,0:T(8,128)(2,1)}, bf16[2,256,256]{2,1,0:T(8,128)(2,1)S(1)}, u32[]{:S(2)}, u32[]{:S(2)}) collective-permute-start(bf16[2,256,256]{2,1,0:T(8,128)(2,1)} %bitcast.16), channel_id=1, source_target_pairs={{0,2},{2,4},{4,6},{6,7},{7,5},{5,3},{3,1},{1,0},{8,10},{10,12},{12... | collective-permute-start | bytes 786440 | tf_op jit(solution)/shard_map/ppermute | solution.py:376
  3.7 8.3 %collective-permute-start.2 = (bf16[2,256,256]{2,1,0:T(8,128)(2,1)}, bf16[2,256,256]{2,1,0:T(8,128)(2,1)S(1)}, u32[]{:S(2)}, u32[]{:S(2)}) collective-permute-start(bf16[2,256,256]{2,1,0:T(8,128)(2,1)} %bitcast.17), channel_id=1, source_target_pairs={{2,0},{4,2},{6,4},{7,6},{5,7},{3,5},{1,3},{0,1},{10,8},{12,10},{14... | collective-permute-start | bytes 786440 | tf_op jit(solution)/shard_map/ppermute | solution.py:377
  3.7 1.0 %copy-start.1 = (bf16[512,256]{1,0:T(8,128)(2,1)S(1)}, bf16[512,256]{1,0:T(8,128)(2,1)}, u32[]{:S(2)}) copy-start(bf16[512,256]{1,0:T(8,128)(2,1)} %param.7) | copy-start | bytes 786436
  4.7 0.7 copy-start.3
  5.4 0.7 copy-start.5
  10.1 7.5 %collective-permute-start.1 = (bf16[2,256,256]{2,1,0:T(8,128)(2,1)S(1)}, bf16[2,256,256]{2,1,0:T(8,128)(2,1)S(1)}, u32[]{:S(2)}, u32[]{:S(2)}) collective-permute-start(bf16[2,256,256]{2,1,0:T(8,128)(2,1)S(1)} %collective-permute-done.refs_1_), channel_id=1, source_target_pairs={{0,2},{2,4},{4,6},{6,7},{7,5},{5,3},{3,1},{1,0},{8,10},{10,12},{12... | collective-permute-start | bytes 786440 | tf_op jit(solution)/shard_map/ppermute | solution.py:376
  12.0 7.6 %collective-permute-start.4 = (bf16[2,256,256]{2,1,0:T(8,128)(2,1)S(1)}, bf16[2,256,256]{2,1,0:T(8,128)(2,1)S(1)}, u32[]{:S(2)}, u32[]{:S(2)}) collective-permute-start(bf16[2,256,256]{2,1,0:T(8,128)(2,1)S(1)} %collective-permute-done.2.refs_2_), channel_id=1, source_target_pairs={{2,0},{4,2},{6,4},{7,6},{5,7},{3,5},{1,3},{0,1},{10,8},{12,10},{14... | collective-permute-start | bytes 786440 | tf_op jit(solution)/shard_map/ppermute | solution.py:377
  16.6 7.6 %copy-start.2 = (bf16[512,256]{1,0:T(8,128)(2,1)S(1)}, bf16[512,256]{1,0:T(8,128)(2,1)}, u32[]{:S(2)}) copy-start(bf16[512,256]{1,0:T(8,128)(2,1)} %cot.1) | copy-start | bytes 786436
  17.6 6.6 %collective-permute-start.3 = (bf16[2,256,256]{2,1,0:T(8,128)(2,1)S(1)}, bf16[2,256,256]{2,1,0:T(8,128)(2,1)S(1)}, u32[]{:S(2)}, u32[]{:S(2)}) collective-permute-start(bf16[2,256,256]{2,1,0:T(8,128)(2,1)S(1)} %collective-permute-done.1.refs_0_), channel_id=1, source_target_pairs={{0,2},{2,4},{4,6},{6,7},{7,5},{5,3},{3,1},{1,0},{8,10},{10,12},{12... | collective-permute-start | bytes 786440 | tf_op jit(solution)/shard_map/ppermute | solution.py:376
  19.5 7.6 %collective-permute-start.7 = (bf16[2,256,256]{2,1,0:T(8,128)(2,1)S(1)}, bf16[2,256,256]{2,1,0:T(8,128)(2,1)S(1)}, u32[]{:S(2)}, u32[]{:S(2)}) collective-permute-start(bf16[2,256,256]{2,1,0:T(8,128)(2,1)S(1)} %collective-permute-done.4.refs_1_), channel_id=1, source_target_pairs={{2,0},{4,2},{6,4},{7,6},{5,7},{3,5},{1,3},{0,1},{10,8},{12,10},{14... | collective-permute-start | bytes 786440 | tf_op jit(solution)/shard_map/ppermute | solution.py:377
  24.2 8.0 %collective-permute-start.6 = (bf16[512,256]{1,0:T(8,128)(2,1)S(1)}, bf16[512,256]{1,0:T(8,128)(2,1)S(1)}, u32[]{:S(2)}, u32[]{:S(2)}) collective-permute-start(bf16[512,256]{1,0:T(8,128)(2,1)S(1)} %copy-done.2), channel_id=1, source_target_pairs={{0,16},{16,0},{8,24},{24,8},{1,17},{17,1},{9,25},{25,9},{2,18},{18... | collective-permute-start | bytes 786440 | tf_op jit(solution)/shard_map/ppermute | solution.py:387
  26.3 5.9 %collective-permute-start.5 = (bf16[1,256,256]{2,1,0:T(8,128)(2,1)S(1)}, bf16[1,256,256]{2,1,0:T(8,128)(2,1)S(1)}, u32[]{:S(2)}, u32[]{:S(2)}) collective-permute-start(bf16[1,256,256]{2,1,0:T(8,128)(2,1)S(1)} %slice.56), channel_id=1, source_target_pairs={{0,2},{2,4},{4,6},{6,7},{7,5},{5,3},{3,1},{1,0},{8,10},{10,12},{12... | collective-permute-start | bytes 393224 | tf_op jit(solution)/shard_map/ppermute | solution.py:388
  27.1 5.1 %collective-permute-start.8 = (bf16[1,256,256]{2,1,0:T(8,128)(2,1)S(1)}, bf16[1,256,256]{2,1,0:T(8,128)(2,1)S(1)}, u32[]{:S(2)}, u32[]{:S(2)}) collective-permute-start(bf16[1,256,256]{2,1,0:T(8,128)(2,1)S(1)} %slice.72), channel_id=1, source_target_pairs={{2,0},{4,2},{6,4},{7,6},{5,7},{3,5},{1,3},{0,1},{10,8},{12,10},{14... | collective-permute-start | bytes 393224 | tf_op jit(solution)/shard_map/ppermute | solution.py:389
  32.2 13.0 %copy-start = (bf16[256,256]{1,0:T(8,128)(2,1)S(1)}, bf16[256,256]{1,0:T(8,128)(2,1)}, u32[]{:S(2)}) copy-start(bf16[256,256]{1,0:T(8,128)(2,1)} %weight.3) | copy-start | bytes 393220
  32.2 13.0 %copy-start.4 = (f32[256]{0:T(256)S(1)}, f32[256]{0:T(256)}, u32[]{:S(2)}) copy-start(f32[256]{0:T(256)} %param.12) | copy-start | bytes 3076
  34.3 1.6 %collective-permute-start.11 = (bf16[2,256,256]{2,1,0:T(8,128)(2,1)S(1)}, bf16[2,256,256]{2,1,0:T(8,128)(2,1)S(1)}, u32[]{:S(2)}, u32[]{:S(2)}) collective-permute-start(bf16[2,256,256]{2,1,0:T(8,128)(2,1)S(1)} %get-tuple-element.72), channel_id=1, source_target_pairs={{0,8},{8,0},{16,24},{24,16},{1,9},{9,1},{17,25},{25,17},{2,10},{10... | collective-permute-start | bytes 786440 | tf_op jit(solution)/shard_map/ppermute | solution.py:398
  34.4 2.4 %collective-permute-start.9 = (bf16[2,256,256]{2,1,0:T(8,128)(2,1)S(1)}, bf16[2,256,256]{2,1,0:T(8,128)(2,1)S(1)}, u32[]{:S(2)}, u32[]{:S(2)}) collective-permute-start(bf16[2,256,256]{2,1,0:T(8,128)(2,1)S(1)} %get-tuple-element.70), channel_id=1, source_target_pairs={{0,8},{8,0},{16,24},{24,16},{1,9},{9,1},{17,25},{25,17},{2,10},{10... | collective-permute-start | bytes 786440 | tf_op jit(solution)/shard_map/ppermute | solution.py:399
  36.0 9.2 %collective-permute-start.12 = (bf16[2,256,256]{2,1,0:T(8,128)(2,1)S(1)}, bf16[2,256,256]{2,1,0:T(8,128)(2,1)S(1)}, u32[]{:S(2)}, u32[]{:S(2)}) collective-permute-start(bf16[2,256,256]{2,1,0:T(8,128)(2,1)S(1)} %add_convert_fusion.4.near), channel_id=1, source_target_pairs={{0,16},{16,0},{8,24},{24,8},{1,17},{17,1},{9,25},{25,9},{2,18},{18... | collective-permute-start | bytes 786440 | tf_op jit(solution)/shard_map/ppermute | solution.py:401
  36.9 13.1 %collective-permute-start.10 = (bf16[2,256,256]{2,1,0:T(8,128)(2,1)S(1)}, bf16[2,256,256]{2,1,0:T(8,128)(2,1)S(1)}, u32[]{:S(2)}, u32[]{:S(2)}) collective-permute-start(bf16[2,256,256]{2,1,0:T(8,128)(2,1)S(1)} %add_convert_fusion.5.near), channel_id=1, source_target_pairs={{0,16},{16,0},{8,24},{24,8},{1,17},{17,1},{9,25},{25,9},{2,18},{18... | collective-permute-start | bytes 786440 | tf_op jit(solution)/shard_map/ppermute | solution.py:403
  46.4 3.7 %collective-permute-start.13 = (bf16[2,256,256]{2,1,0:T(8,128)(2,1)S(1)}, bf16[2,256,256]{2,1,0:T(8,128)(2,1)S(1)}, u32[]{:S(2)}, u32[]{:S(2)}) collective-permute-start(bf16[2,256,256]{2,1,0:T(8,128)(2,1)S(1)} %get-tuple-element.77.refs_1_.refs_0_), channel_id=1, source_target_pairs={{0,8},{8,0},{16,24},{24,16},{1,9},{9,1},{17,25},{25,17},{2,10},{10... | collective-permute-start | bytes 786440 | tf_op jit(solution)/shard_map/ppermute | solution.py:422
  50.7 1.6 %collective-permute-start.14 = (bf16[2,256,256]{2,1,0:T(8,128)(2,1)S(1)}, bf16[2,256,256]{2,1,0:T(8,128)(2,1)S(1)}, u32[]{:S(2)}, u32[]{:S(2)}) collective-permute-start(bf16[2,256,256]{2,1,0:T(8,128)(2,1)S(1)} %get-tuple-element.81.refs_2_.refs_1_), channel_id=1, source_target_pairs={{0,8},{8,0},{16,24},{24,16},{1,9},{9,1},{17,25},{25,17},{2,10},{10... | collective-permute-start | bytes 786440 | tf_op jit(solution)/shard_map/ppermute | solution.py:435
  50.8 5.2 %collective-permute-start.23 = (f32[80,256]{1,0:T(8,128)S(1)}, f32[80,256]{1,0:T(8,128)S(1)}, u32[]{:S(2)}, u32[]{:S(2)}) collective-permute-start(f32[80,256]{1,0:T(8,128)S(1)} %dynamic-slice_bitcast_fusion), channel_id=1, source_target_pairs={{0,8},{8,0},{16,24},{24,16},{1,9},{9,1},{17,25},{25,17},{2,10},{10... | collective-permute-start | bytes 245768 | tf_op jit(solution)/shard_map/ppermute | solution.py:442
  54.0 7.3 %collective-permute-start.15 = (bf16[1,256,256]{2,1,0:T(8,128)(2,1)S(1)}, bf16[1,256,256]{2,1,0:T(8,128)(2,1)S(1)}, u32[]{:S(2)}, u32[]{:S(2)}) collective-permute-start(bf16[1,256,256]{2,1,0:T(8,128)(2,1)S(1)} %get-tuple-element.83), channel_id=1, source_target_pairs={{0,2},{2,4},{4,6},{6,7},{7,5},{5,3},{3,1},{1,0},{10,8},{12,10},{14... | collective-permute-start | bytes 393224 | tf_op jit(solution)/shard_map/ppermute | solution.py:475
  55.6 5.7 %collective-permute-start.16 = (bf16[1,256,256]{2,1,0:T(8,128)(2,1)S(1)}, bf16[1,256,256]{2,1,0:T(8,128)(2,1)S(1)}, u32[]{:S(2)}, u32[]{:S(2)}) collective-permute-start(bf16[1,256,256]{2,1,0:T(8,128)(2,1)S(1)} %get-tuple-element.84), channel_id=1, source_target_pairs={{2,0},{4,2},{6,4},{7,6},{5,7},{3,5},{1,3},{0,1},{8,10},{10,12},{12... | collective-permute-start | bytes 393224 | tf_op jit(solution)/shard_map/ppermute | solution.py:476
  56.1 7.6 %collective-permute-start.24 = (bf16[80,256]{1,0:T(8,128)(2,1)S(1)}, bf16[80,256]{1,0:T(8,128)(2,1)S(1)}, u32[]{:S(2)}, u32[]{:S(2)}) collective-permute-start(bf16[80,256]{1,0:T(8,128)(2,1)S(1)} %fusion), channel_id=1, source_target_pairs={{0,1},{1,0},{2,3},{3,2},{4,5},{5,4},{6,7},{7,6},{8,9},{9,8},{10,11... | collective-permute-start | bytes 122888 | tf_op jit(solution)/shard_map/ppermute | solution.py:499
  61.5 9.1 %collective-permute-start.18 = (bf16[2,256,256]{2,1,0:T(8,128)(2,1)S(1)}, bf16[2,256,256]{2,1,0:T(8,128)(2,1)S(1)}, u32[]{:S(2)}, u32[]{:S(2)}) collective-permute-start(bf16[2,256,256]{2,1,0:T(8,128)(2,1)S(1)} %pad_maximum_fusion.1), channel_id=1, source_target_pairs={{2,0},{4,2},{6,4},{7,6},{5,7},{3,5},{1,3},{0,1},{8,10},{10,12},{12... | collective-permute-start | bytes 786440 | tf_op jit(solution)/shard_map/ppermute | solution.py:476
  61.9 8.7 %collective-permute-start.17 = (bf16[2,256,256]{2,1,0:T(8,128)(2,1)S(1)}, bf16[2,256,256]{2,1,0:T(8,128)(2,1)S(1)}, u32[]{:S(2)}, u32[]{:S(2)}) collective-permute-start(bf16[2,256,256]{2,1,0:T(8,128)(2,1)S(1)} %pad_maximum_fusion), channel_id=1, source_target_pairs={{0,2},{2,4},{4,6},{6,7},{7,5},{5,3},{3,1},{1,0},{10,8},{12,10},{14... | collective-permute-start | bytes 786440 | tf_op jit(solution)/shard_map/ppermute | solution.py:475
  63.7 9.2 %collective-permute-start.25 = (bf16[80,256]{1,0:T(8,128)(2,1)S(1)}, bf16[80,256]{1,0:T(8,128)(2,1)S(1)}, u32[]{:S(2)}, u32[]{:S(2)}) collective-permute-start(bf16[80,256]{1,0:T(8,128)(2,1)S(1)} %add_convert_fusion.9), channel_id=1, source_target_pairs={{0,2},{1,3},{2,0},{3,1},{4,6},{5,7},{6,4},{7,5},{8,10},{9,11},{10,... | collective-permute-start | bytes 122888 | tf_op jit(solution)/shard_map/ppermute | solution.py:499
  70.8 7.7 %collective-permute-start.19 = (bf16[2,256,256]{2,1,0:T(8,128)(2,1)S(1)}, bf16[2,256,256]{2,1,0:T(8,128)(2,1)S(1)}, u32[]{:S(2)}, u32[]{:S(2)}) collective-permute-start(bf16[2,256,256]{2,1,0:T(8,128)(2,1)S(1)} %get-tuple-element.109), channel_id=1, source_target_pairs={{0,2},{2,4},{4,6},{6,7},{7,5},{5,3},{3,1},{1,0},{10,8},{12,10},{14... | collective-permute-start | bytes 786440 | tf_op jit(solution)/shard_map/ppermute | solution.py:475
  71.4 7.5 %collective-permute-start.20 = (bf16[2,256,256]{2,1,0:T(8,128)(2,1)S(1)}, bf16[2,256,256]{2,1,0:T(8,128)(2,1)S(1)}, u32[]{:S(2)}, u32[]{:S(2)}) collective-permute-start(bf16[2,256,256]{2,1,0:T(8,128)(2,1)S(1)} %get-tuple-element.108), channel_id=1, source_target_pairs={{2,0},{4,2},{6,4},{7,6},{5,7},{3,5},{1,3},{0,1},{8,10},{10,12},{12... | collective-permute-start | bytes 786440 | tf_op jit(solution)/shard_map/ppermute | solution.py:476
  72.9 8.2 %collective-permute-start.26 = (bf16[80,256]{1,0:T(8,128)(2,1)S(1)}, bf16[80,256]{1,0:T(8,128)(2,1)S(1)}, u32[]{:S(2)}, u32[]{:S(2)}) collective-permute-start(bf16[80,256]{1,0:T(8,128)(2,1)S(1)} %add_convert_fusion.8), channel_id=1, source_target_pairs={{0,4},{1,5},{2,6},{3,7},{4,0},{5,1},{6,2},{7,3},{8,12},{9,13},{10,... | collective-permute-start | bytes 122888 | tf_op jit(solution)/shard_map/ppermute | solution.py:499
  79.0 9.3 %collective-permute-start.21 = (bf16[2,256,256]{2,1,0:T(8,128)(2,1)S(1)}, bf16[2,256,256]{2,1,0:T(8,128)(2,1)S(1)}, u32[]{:S(2)}, u32[]{:S(2)}) collective-permute-start(bf16[2,256,256]{2,1,0:T(8,128)(2,1)S(1)} %get-tuple-element.107), channel_id=1, source_target_pairs={{0,2},{2,4},{4,6},{6,7},{7,5},{5,3},{3,1},{1,0},{10,8},{12,10},{14... | collective-permute-start | bytes 786440 | tf_op jit(solution)/shard_map/ppermute | solution.py:475
  80.6 7.7 %collective-permute-start.22 = (bf16[2,256,256]{2,1,0:T(8,128)(2,1)S(1)}, bf16[2,256,256]{2,1,0:T(8,128)(2,1)S(1)}, u32[]{:S(2)}, u32[]{:S(2)}) collective-permute-start(bf16[2,256,256]{2,1,0:T(8,128)(2,1)S(1)} %get-tuple-element.106), channel_id=1, source_target_pairs={{2,0},{4,2},{6,4},{7,6},{5,7},{3,5},{1,3},{0,1},{8,10},{10,12},{12... | collective-permute-start | bytes 786440 | tf_op jit(solution)/shard_map/ppermute | solution.py:476
  81.1 5.0 %collective-permute-start.27 = (f32[64,256]{1,0:T(8,128)S(1)}, f32[64,256]{1,0:T(8,128)S(1)}, u32[]{:S(2)}, u32[]{:S(2)}) collective-permute-start(f32[64,256]{1,0:T(8,128)S(1)} %slice.70.own), channel_id=1, source_target_pairs={{0,16},{16,0},{8,24},{24,8},{1,17},{17,1},{9,25},{25,9},{2,18},{18... | collective-permute-start | bytes 196616 | tf_op jit(solution)/shard_map/ppermute | solution.py:481
  83.9 2.3 %collective-permute-start.28 = (f32[64,256]{1,0:T(8,128)S(1)}, f32[64,256]{1,0:T(8,128)S(1)}, u32[]{:S(2)}, u32[]{:S(2)}) collective-permute-start(f32[64,256]{1,0:T(8,128)S(1)} %slice.70.own), channel_id=1, source_target_pairs={{0,8},{8,0},{16,24},{24,16},{1,9},{9,1},{17,25},{25,17},{2,10},{10... | collective-permute-start | bytes 196616 | tf_op jit(solution)/shard_map/ppermute | solution.py:481
  83.9 3.7 %collective-permute-start.29 = (f32[64,256]{1,0:T(8,128)S(1)}, f32[64,256]{1,0:T(8,128)S(1)}, u32[]{:S(2)}, u32[]{:S(2)}) collective-permute-start(f32[64,256]{1,0:T(8,128)S(1)} %slice.70.own), channel_id=1, source_target_pairs={{0,24},{24,0},{8,16},{16,8},{1,25},{25,1},{9,17},{17,9},{2,26},{26... | collective-permute-start | bytes 196616 | tf_op jit(solution)/shard_map/ppermute | solution.py:481
